TPU v7x, 32 devices: a whole 2x2x4 slice. The times are simulated.
32 devices in a mesh: ingest: 4 (over x, core), run: 8 (over z, y).
Axes of the slice: x: 2, y: 2, z: 4, core: 2. Of those that a mesh axis runs over, the one named last changes fastest.
Arguments:
- embeddings: bfloat16 [32768, 768], P(('ingest', 'run')), may hold values from -2000 to 2000, as said below
- cluster_id: int32 [32768], P(('ingest', 'run')), may hold values from 0 to 11, as said below
- rank: int32 [32768], P(('ingest', 'run')), may hold values from 0 to 4095, as said below
- run_len: int32 [12], replicated, may hold values from 2 to 4, as said below
Outputs:
- best_cosine: float32 [32768], P(('ingest', 'run'))
Inputs may be any that keep to these rules, and one draw needn't show every extreme that they name: All lengths are even. For each ingest index i, the lengths of the 3 clusters c with c // 3 == i are 4, 2 and 2 in some order (sum 8). Cluster c owns the run devices of ingest index c // 3 from the sum of the lengths of the earlier clusters of that index on, for run_len[c] devices. `cluster_id`: cluster c holds exactly run_len[c] * 1024 rows. The ranks of a cluster's rows are 0 up to its row count - 1, each once. A row of cluster c with rank k belongs to owner slot k % 1024 of run device (start of c) + k // 1024 of ingest index c // 3. Every device holds rows of exactly 16 owner devices, exactly 64 rows of each, and those fill one aligned group of 64 slots of that owner. `embeddings`: rows of one cluster share a direction of their cluster; some rows are near copies of an earlier row of their cluster.
All inputs are finite; a program needn't handle non-finite values.
Results may differ from a plain program's by a relative error of at most 0.00059.
Values may be sent and summed in bfloat16 or wider, within the bound.
No kernel may reach another device: no remote copies, remote signals or barrier semaphores. Data moves between devices by JAX's collectives and lax.ppermute only.
A program may use at most 64 MiB of HBM per device.

v0:
```python
import math

import jax
import jax.numpy as jnp
from jax import lax
from jax.sharding import PartitionSpec as P

EPSILON = 1e-06


def from_behind(block, axis, distance):
    devices = range(lax.axis_size(axis))
    route = [(i - distance, i) for i in devices if i - distance in devices]
    return lax.ppermute(block, axis, route)


def unit_rows(embeddings):
    widened = embeddings.astype(jnp.float32)
    return (
        widened * lax.rsqrt(jnp.sum(widened * widened, axis=1, keepdims=True) + EPSILON)
    ).astype(jnp.bfloat16)


def best_update(best_score, owned_rows, key_block, first_row, lowest, mine_rows, upper_row):
    width_rows = key_block.shape[0]

    def compute(current):
        scores = lax.dot_general(
            owned_rows, key_block, (((1,), (1,)), ((), ())), preferred_element_type=jnp.float32
        )
        candidate = first_row + jnp.arange(width_rows, dtype=jnp.int32)
        allowed = (candidate[None, :] >= lowest) & (candidate[None, :] < mine_rows[:, None])
        return jnp.maximum(current, jnp.max(jnp.where(allowed, scores, -2.0), axis=1))

    touches = (first_row + width_rows > lowest) & (first_row < upper_row)
    return lax.cond(touches, compute, lambda current: current, best_score)


def fold_piece(best_score, piece, first_row, owned_rows, lowest, mine_rows, upper_row):
    block_rows = math.gcd(piece.shape[0], owned_rows.shape[0])

    def one_block(number, current):
        return best_update(
            current,
            owned_rows,
            piece,
            first_row + number * block_rows,
            lowest,
            mine_rows,
            upper_row,
        )

    return lax.fori_loop(0, piece.shape[0] // block_rows, one_block, best_score)


def local(embeddings, cluster_id, rank, run_len):
    rows_dev, feature_width = embeddings.shape
    ingest_count = lax.axis_size("ingest")
    run_count = lax.axis_size("run")
    devices = ingest_count * run_count
    clusters = run_len.shape[0]
    per_group = clusters // ingest_count
    capacity = 2 * rows_dev // devices
    run_reach = min(8, run_count // 2)
    unit_vectors = unit_rows(embeddings)
    run_lengths = run_len.reshape(ingest_count, per_group)
    run_starts = (jnp.cumsum(run_lengths, axis=1) - run_lengths).reshape(clusters)
    member = (cluster_id[:, None] == jnp.arange(clusters, dtype=jnp.int32)[None, :]).astype(
        jnp.int32
    )
    own_start = jnp.sum(member * run_starts[None, :], axis=1)
    owner_device = cluster_id // per_group * run_count + own_start + rank // rows_dev
    within = rank % rows_dev
    position = owner_device * capacity + within % capacity
    outgoing = (
        jnp.zeros((devices * capacity, feature_width), jnp.bfloat16).at[position].set(unit_vectors)
    )
    labels = jnp.full((devices * capacity,), -1, jnp.int32).at[position].set(within)
    arrived = lax.all_to_all(outgoing, ("ingest", "run"), split_axis=0, concat_axis=0, tiled=True)
    arrived_slots = lax.all_to_all(
        labels, ("ingest", "run"), split_axis=0, concat_axis=0, tiled=True
    )
    target = jnp.where(arrived_slots >= 0, arrived_slots, rows_dev)
    owned_rows = (
        jnp.zeros((rows_dev, feature_width), jnp.bfloat16).at[target].set(arrived, mode="drop")
    )
    ingest_pos = lax.axis_index("ingest")
    run_pos = lax.axis_index("run")
    group_starts = lax.dynamic_index_in_dim(
        run_starts.reshape(ingest_count, per_group), ingest_pos, 0, keepdims=False
    )
    run_begin = jnp.max(jnp.where(group_starts <= run_pos, group_starts, 0))
    lowest = run_begin * rows_dev
    mine_rows = run_pos * rows_dev + jnp.arange(rows_dev, dtype=jnp.int32)
    upper_row = (run_pos + 1) * rows_dev
    initial = jnp.full((rows_dev,), -1.0, jnp.float32)

    def fold_rows(current, piece, first_row):
        return fold_piece(current, piece, first_row, owned_rows, lowest, mine_rows, upper_row)

    best_score = fold_rows(initial, owned_rows, run_pos * rows_dev)
    moving = owned_rows
    for distance in range(1, run_reach):
        moving = from_behind(moving, "run", 1)
        best_score = fold_rows(best_score, moving, (run_pos - distance) * rows_dev)
    replies = best_score[jnp.clip(arrived_slots, 0, rows_dev - 1)]
    returned = lax.all_to_all(replies, ("ingest", "run"), split_axis=0, concat_axis=0, tiled=True)
    return returned[position]


def solution(mesh):
    return jax.shard_map(
        local,
        mesh=mesh,
        in_specs=(P(("ingest", "run"), None), P(("ingest", "run")), P(("ingest", "run")), P()),
        out_specs=P(("ingest", "run")),
        check_vma=False,
    )
```

profile of v0, /device:TPU:0, one launch (start us, length us, event | category | flops | bytes accessed | tf_op | source)
XLA Modules:
  0.0 262.6 jit_solution(6627637538279545676)
XLA Ops:
  0.0 0.9 reshape.104
  0.9 0.2 reduce_window_sum.13
  1.0 0.1 reduce_window_sum.14
  1.1 0.7 sub.31
  1.8 0.8 select_reduce_fusion.4
  2.6 0.7 broadcast_clamp_fusion.1
  3.3 4.3 %scatter_custom_fusion = s32[2048]{0:T(1024)S(1)} fusion(s32[1024]{0:T(1024)S(1)} %get-tuple-element.200, s32[1024]{0:T(1024)S(1)} %get-tuple-element.203, s32[]{:T(128)} %constant.115.clone.1), kind=kCustom, calls=%fused_computation.52 | custom fusion | bytes 8196 | tf_op jit(solution)/shard_map/scatter | solution.py:78
  7.6 0.7 all_to_all.24
  8.3 7.3 %all-to-all-start = ((s32[32,64,1]{1,2,0:T(1,128)}), s32[32,64,1]{1,2,0:T(1,128)S(1)}, u32[]{:S(2)}, u32[]{:S(2)}) async-start(s32[32,64,1]{1,2,0:T(1,128)} %bitcast.1), calls=%async_computation | async-start | bytes 32768 | tf_op jit(solution)/shard_map/all_to_all | solution.py:80
  15.6 1.8 fusion
  17.4 7.7 %scatter_custom_fusion.1 = bf16[2048,768]{1,0:T(8,128)(2,1)} fusion(s32[1024]{0:T(1024)S(1)} %get-tuple-element.200, bf16[1024,768]{1,0:T(8,128)(2,1)S(1)} %copy-done, f32[1024]{0:T(1024)S(1)} %add_rsqrt_fusion, bf16[]{:T(256)} %constant.117.clone.1), kind=kCustom, calls=%fused_computation.21 | custom fusion | flops 2359296 | bytes 4722690 | tf_op jit(solution)/shard_map/scatter | solution.py:76
  25.1 5.8 %all-to-all-start.1 = ((bf16[32,64,768]{2,1,0:T(8,128)(2,1)}), bf16[32,64,768]{2,1,0:T(8,128)(2,1)S(1)}, u32[]{:S(2)}, u32[]{:S(2)}) async-start(bf16[32,64,768]{2,1,0:T(8,128)(2,1)} %bitcast.3), calls=%async_computation.1 | async-start | bytes 6291456 | tf_op jit(solution)/shard_map/all_to_all | solution.py:79
  31.0 0.5 broadcast.164
  31.5 0.7 reduce.6
  32.2 0.1 all_to_all.26
  32.3 71.8 %all-to-all-done.1 = bf16[32,64,768]{2,1,0:T(8,128)(2,1)S(1)} async-done(((bf16[32,64,768]{2,1,0:T(8,128)(2,1)}), bf16[32,64,768]{2,1,0:T(8,128)(2,1)S(1)}, u32[]{:S(2)}, u32[]{:S(2)}) %all-to-all-start.1) | async-done | bytes 3145760 | tf_op jit(solution)/shard_map/all_to_all | solution.py:79
  104.0 10.9 %scatter_custom_fusion.2 = bf16[1024,768]{1,0:T(8,128)(2,1)} fusion(s32[2048]{0:T(1024)S(1)} %bitcast.21, bf16[2048,768]{1,0:T(8,128)(2,1)S(1)} %bitcast.18, bf16[]{:T(256)} %constant.117.clone.1), kind=kCustom, calls=%fused_computation.24 | custom fusion | bytes 1572866 | tf_op jit(solution)/shard_map/scatter | solution.py:85
  115.0 1.6 collective-permute-start
  116.6 34.8 %collective-permute-done = bf16[1024,768]{1,0:T(8,128)(2,1)S(1)} collective-permute-done((bf16[1024,768]{1,0:T(8,128)(2,1)}, bf16[1024,768]{1,0:T(8,128)(2,1)S(1)}, u32[]{:S(2)}, u32[]{:S(2)}) %collective-permute-start) | collective-permute-done | bytes 1572896 | tf_op jit(solution)/shard_map/ppermute | solution.py:14
  151.4 5.4 %collective-permute-start.1 = (bf16[1024,768]{1,0:T(8,128)(2,1)S(1)}, bf16[1024,768]{1,0:T(8,128)(2,1)}, u32[]{:S(2)}, u32[]{:S(2)}) collective-permute-start(bf16[1024,768]{1,0:T(8,128)(2,1)S(1)} %collective-permute-done), channel_id=1, source_target_pairs={{0,1},{1,2},{2,3},{3,4},{4,5},{5,6},{6,7},{8,9},{9,10},{10,11},{11... | collective-permute-start | bytes 4718600 | tf_op jit(solution)/shard_map/ppermute | solution.py:14
  156.8 32.6 %collective-permute-done.1 = bf16[1024,768]{1,0:T(8,128)(2,1)} collective-permute-done((bf16[1024,768]{1,0:T(8,128)(2,1)S(1)}, bf16[1024,768]{1,0:T(8,128)(2,1)}, u32[]{:S(2)}, u32[]{:S(2)}) %collective-permute-start.1) | collective-permute-done | bytes 1572896 | tf_op jit(solution)/shard_map/ppermute | solution.py:14
  189.4 4.6 %collective-permute-start.2 = (bf16[1024,768]{1,0:T(8,128)(2,1)}, bf16[1024,768]{1,0:T(8,128)(2,1)S(1)}, u32[]{:S(2)}, u32[]{:S(2)}) collective-permute-start(bf16[1024,768]{1,0:T(8,128)(2,1)} %collective-permute-done.1), channel_id=1, source_target_pairs={{0,1},{1,2},{2,3},{3,4},{4,5},{5,6},{6,7},{8,9},{9,10},{10,11},{11... | collective-permute-start | bytes 4718600 | tf_op jit(solution)/shard_map/ppermute | solution.py:14
  194.0 0.7 fusion.19
  195.4 4.0 %conditional.4 = (f32[1024]{0:T(1024)S(1)}) conditional(s32[]{:T(128)} %convert_element_type.26, f32[1024]{0:T(1024)S(1)} %broadcast_in_dim.57, (s32[]{:T(128)}, s32[]{:T(128)}, s32[1024]{0:T(1024)S(1)}, bf16[1024,768]{1,0:T(8,128)(2,1)}, f32[1024]{0:T(1024)S(1)}) %tuple.41), branch_computations={%region_7.8_spmd, %region_8.10_spmd} | conditional | flops 1614810112 | bytes 1603604 | solution.py:36
  195.5 4.0 %select_reduce_fusion = f32[1024]{0:T(1024)S(1)} fusion(s32[1024]{0:T(1024)S(1)} %get-tuple-element.168, s32[1024]{0:T(1024)S(1)} %iota_add_fusion, pred[1024]{0:T(1024)(128)(4,1)S(1)} %broadcast_compare_fusion, bf16[1024,768]{1,0:T(8,128)(2,1)} %get-tuple-element.169), kind=kOutput, calls=%fused_computation.5 | convolution fusion | flops 1614806016 | bytes 1586176 | tf_op jit(solution)/shard_map/while/body/eval_jaxpr/cond/branch_1_fun/dot_general | solution.py:28
  199.5 0.2 conditional.5
  199.7 27.3 %collective-permute-done.2 = bf16[1024,768]{1,0:T(8,128)(2,1)S(1)} collective-permute-done((bf16[1024,768]{1,0:T(8,128)(2,1)}, bf16[1024,768]{1,0:T(8,128)(2,1)S(1)}, u32[]{:S(2)}, u32[]{:S(2)}) %collective-permute-start.2) | collective-permute-done | bytes 1572896 | tf_op jit(solution)/shard_map/ppermute | solution.py:14
  227.0 8.6 %gather_fusion = f32[2048]{0:T(1024)S(1)} fusion(f32[1024]{0:T(1024)S(1)} %get-tuple-element.207, s32[2048]{0:T(1024)S(1)} %broadcast_clamp_fusion), kind=kCustom, calls=%fused_computation | custom fusion | bytes 24576 | tf_op jit(solution)/shard_map/gather | solution.py:106
  235.7 15.2 %all_to_all.36 = f32[32,64,1]{1,2,0:T(1,128)S(1)} all-to-all(f32[32,64,1]{1,2,0:T(1,128)S(1)} %bitcast.19), channel_id=1, replica_groups=mesh['ingest'=4,'run'=8] {'ingest','run'}, dimensions={0} | all-to-all | bytes 16384 | tf_op jit(solution)/shard_map/all_to_all | solution.py:107
  250.8 0.5 broadcast.165
  251.3 0.7 reduce.7
  252.1 10.5 %gather_fusion.1 = f32[1024]{0:T(1024)} fusion(f32[2048]{0:T(1024)S(1)} %all_to_all.32, s32[1024]{0:T(1024)S(1)} %get-tuple-element.199), kind=kCustom, calls=%fused_computation.1 | custom fusion | bytes 12288 | tf_op jit(solution)/shard_map/gather | solution.py:108
  (20 shorter events, 0.2 us)
Async XLA Ops:
  0.0 17.4 %copy-start = (bf16[1024,768]{1,0:T(8,128)(2,1)S(1)}, bf16[1024,768]{1,0:T(8,128)(2,1)}, u32[]{:S(2)}) copy-start(bf16[1024,768]{1,0:T(8,128)(2,1)} %param.12) | copy-start | bytes 4718596
  8.3 16.8 %all-to-all-start = ((s32[32,64,1]{1,2,0:T(1,128)}), s32[32,64,1]{1,2,0:T(1,128)S(1)}, u32[]{:S(2)}, u32[]{:S(2)}) async-start(s32[32,64,1]{1,2,0:T(1,128)} %bitcast.1), calls=%async_computation | async-start | bytes 32768 | tf_op jit(solution)/shard_map/all_to_all | solution.py:80
  25.1 78.9 %all-to-all-start.1 = ((bf16[32,64,768]{2,1,0:T(8,128)(2,1)}), bf16[32,64,768]{2,1,0:T(8,128)(2,1)S(1)}, u32[]{:S(2)}, u32[]{:S(2)}) async-start(bf16[32,64,768]{2,1,0:T(8,128)(2,1)} %bitcast.3), calls=%async_computation.1 | async-start | bytes 6291456 | tf_op jit(solution)/shard_map/all_to_all | solution.py:79
  115.0 36.4 %collective-permute-start = (bf16[1024,768]{1,0:T(8,128)(2,1)}, bf16[1024,768]{1,0:T(8,128)(2,1)S(1)}, u32[]{:S(2)}, u32[]{:S(2)}) collective-permute-start(bf16[1024,768]{1,0:T(8,128)(2,1)} %scatter_custom_fusion.2), channel_id=1, source_target_pairs={{0,1},{1,2},{2,3},{3,4},{4,5},{5,6},{6,7},{8,9},{9,10},{10,11},{11... | collective-permute-start | bytes 4718600 | tf_op jit(solution)/shard_map/ppermute | solution.py:14
  151.4 42.6 %copy-start.1 = (bf16[1024,768]{1,0:T(8,128)(2,1)}, bf16[1024,768]{1,0:T(8,128)(2,1)S(1)}, u32[]{:S(2)}) copy-start(bf16[1024,768]{1,0:T(8,128)(2,1)S(1)} %collective-permute-done) | copy-start | bytes 4718596
  151.4 38.0 %collective-permute-start.1 = (bf16[1024,768]{1,0:T(8,128)(2,1)S(1)}, bf16[1024,768]{1,0:T(8,128)(2,1)}, u32[]{:S(2)}, u32[]{:S(2)}) collective-permute-start(bf16[1024,768]{1,0:T(8,128)(2,1)S(1)} %collective-permute-done), channel_id=1, source_target_pairs={{0,1},{1,2},{2,3},{3,4},{4,5},{5,6},{6,7},{8,9},{9,10},{10,11},{11... | collective-permute-start | bytes 4718600 | tf_op jit(solution)/shard_map/ppermute | solution.py:14
  189.4 37.7 %collective-permute-start.2 = (bf16[1024,768]{1,0:T(8,128)(2,1)}, bf16[1024,768]{1,0:T(8,128)(2,1)S(1)}, u32[]{:S(2)}, u32[]{:S(2)}) collective-permute-start(bf16[1024,768]{1,0:T(8,128)(2,1)} %collective-permute-done.1), channel_id=1, source_target_pairs={{0,1},{1,2},{2,3},{3,4},{4,5},{5,6},{6,7},{8,9},{9,10},{10,11},{11... | collective-permute-start | bytes 4718600 | tf_op jit(solution)/shard_map/ppermute | solution.py:14
  195.4 4.1 %copy-start.2 = (bf16[1024,768]{1,0:T(8,128)(2,1)S(1)}, bf16[1024,768]{1,0:T(8,128)(2,1)}, u32[]{:S(2)}) copy-start(bf16[1024,768]{1,0:T(8,128)(2,1)} %copy-done.1) | copy-start | bytes 4718596
where the time goes:
time: 263 us
  waiting for transfers between devices  166 us (63%)
  local copies, waits for them, and re-layouts  37.2 us (14%)
  starting transfers between devices  24.7 us (9%)
  blocking collectives  15.2 us (6%)
  other arithmetic  14 us (5%)
  matrix products  3.98 us (2%)
    ppermute x3, waiting for transfers between devices, from_behind(): return lax.ppermute(block, axis, route)  94.7 us
    all_to_all x1, waiting for transfers between devices, local(): lax.all_to_all(outgoing, ('ingest', 'run'), split_axis=0, concat_axis=0,...  71.8 us
    all_to_all x1, blocking collectives, local(): lax.all_to_all(replies, ('ingest', 'run'), split_axis=0, concat_axis=0, t...  15.2 us
    ppermute x3, starting transfers between devices, from_behind(): return lax.ppermute(block, axis, route)  11.6 us
    scatter x1, local copies, waits for them, and re-layouts, local(): jnp.zeros((rows_dev, feature_width), jnp.bfloat16).at[target]  10.9 us
    gather x1, local copies, waits for them, and re-layouts, local(): return returned[position]  10.5 us
    gather x1, local copies, waits for them, and re-layouts, local(): replies = best_score[jnp.clip(arrived_slots, 0, rows_dev - 1)]  8.58 us
    scatter x1, other arithmetic, local(): jnp.zeros((devices * capacity, feature_width), jnp.bfloat16).at[position]  7.73 us
  transfers between devices with their start and end apart: 5, of which 4 were waited for; matrix products, arithmetic and copies ran while one was open for 6% of the time, Pallas kernels for 0%

commit v1 on v0

v1 whole, which is shorter than its diff:
```python
import functools

import jax
import jax.numpy as jnp
from jax import lax
from jax.experimental import pallas as pl
from jax.experimental.pallas import tpu as pltpu
from jax.sharding import PartitionSpec as P

EPSILON = 1e-06
AXES = ("ingest", "run")
TILE = 256
MEMORY = 60 * 1024 * 1024


class Plan:
    def __init__(self, ingest, run, clusters, rows):
        self.ingest, self.run, self.clusters, self.rows = ingest, run, clusters, rows
        self.devices = ingest * run
        self.per_group = clusters // ingest
        self.cap = 2 * rows // self.devices
        self.reach = min(8, run // 2)
        self.width = run // ingest
        self.pairs = run // 2

    def device(self, group, slot):
        core, chip = slot % 2, slot // 2
        column, place = chip // self.width, chip % self.width
        odd = column % 2
        place = place + odd * (self.width - 1 - 2 * place)
        return (2 * column + core) * self.run + group * self.width + place

    def slot(self, device_ingest, device_run):
        core, column = device_ingest % 2, device_ingest // 2
        place = device_run % self.width
        place = place + (column % 2) * (self.width - 1 - 2 * place)
        return device_run // self.width, 2 * (column * self.width + place) + core

    def splits(self):
        def parts(total, count, top):
            if count == 0:
                if total == 0:
                    yield ()
                return
            for first in range(min(top, total), 0, -1):
                for rest in parts(total - first, count - 1, first):
                    yield (first, *rest)

        return list(parts(self.pairs, self.per_group, self.reach // 2))

    def links(self):
        found = [set() for _ in range(self.reach // 2)]
        for split in self.splits():
            begin = 0
            for length in split:
                for first in range(length):
                    for second in range(first + 1, length):
                        found[second - first].add(begin + first)
                begin += length
        return [sorted(chips) for chips in found]


def cluster_starts(plan, run_len_ref):
    starts = []
    for cluster in range(plan.clusters):
        base = cluster // plan.per_group * plan.per_group
        mine = run_len_ref[cluster]
        total = jnp.int32(0)
        for other in range(base, base + plan.per_group):
            if other == cluster:
                continue
            theirs = run_len_ref[other]
            ahead = (theirs >= mine) if other < cluster else (theirs > mine)
            total = total + jnp.where(ahead, theirs, 0)
        starts.append(total)
    return starts


def row_owner(plan, run_len_ref, cluster, rank):
    starts = cluster_starts(plan, run_len_ref)
    begin = jnp.zeros_like(cluster)
    group = jnp.zeros_like(cluster)
    for number, start in enumerate(starts):
        here = cluster == number
        begin = jnp.where(here, start, begin)
        group = jnp.where(here, number // plan.per_group, group)
    owner = plan.device(group, begin + rank // plan.rows)
    return owner, rank % plan.rows


def pack_kernel(plan, run_len_ref, cluster_ref, rank_ref, rows_ref, out_ref, group_ref, unit_ref):
    step = 128

    @pl.loop(0, plan.rows // step)
    def _(number):
        here = pl.ds(pl.multiple_of(number * step, step), step)
        widened = rows_ref[here, :].astype(jnp.float32)
        total = jnp.sum(widened * widened, axis=1, keepdims=True) + EPSILON
        unit_ref[here, :] = (widened * lax.rsqrt(total)).astype(jnp.bfloat16)

    owner, within = row_owner(plan, run_len_ref, cluster_ref[...], rank_ref[...])
    number = lax.broadcasted_iota(jnp.int32, (plan.devices, plan.rows), 0)
    group = jnp.max(
        jnp.where(number == owner, within // plan.cap + 1, 0), axis=1, keepdims=True
    )
    group_ref[...] = jnp.broadcast_to(group, group_ref.shape)
    position = owner * plan.cap + within % plan.cap

    @pl.loop(0, plan.devices * plan.cap // TILE)
    def _(tile):
        row = lax.broadcasted_iota(jnp.int32, (TILE, plan.rows), 0) + tile * TILE
        chosen = jnp.where(row == position, 1.0, 0.0).astype(jnp.bfloat16)
        moved = jnp.dot(chosen, unit_ref[...], preferred_element_type=jnp.float32)
        here = pl.ds(pl.multiple_of(tile * TILE, TILE), TILE)
        out_ref[here, :] = moved.astype(jnp.bfloat16)


def sort_kernel(plan, group_ref, arrived_ref, out_ref):
    for source in range(plan.devices):
        group = group_ref[source, 0]

        @pl.when(group > 0)
        def _():
            here = pl.ds(pl.multiple_of((group - 1) * plan.cap, plan.cap), plan.cap)
            out_ref[here, :] = arrived_ref[source * plan.cap : (source + 1) * plan.cap, :]


def block_best(keys_ref, queries_ref, best_ref):
    rows = keys_ref.shape[0]

    @pl.loop(0, rows // TILE)
    def _(tile):
        keys = keys_ref[pl.ds(pl.multiple_of(tile * TILE, TILE), TILE), :]
        scores = lax.dot_general(
            keys, queries_ref[...], (((1,), (1,)), ((), ())), preferred_element_type=jnp.float32
        )
        best_ref[...] = jnp.maximum(best_ref[...], jnp.max(scores, axis=0, keepdims=True))


def triangle_best(rows_ref, best_ref):
    rows = rows_ref.shape[0]
    for first in range(0, rows, TILE):
        scores = lax.dot_general(
            rows_ref[first : first + TILE, :],
            rows_ref[first:, :],
            (((1,), (1,)), ((), ())),
            preferred_element_type=jnp.float32,
        )
        key = lax.broadcasted_iota(jnp.int32, (TILE, TILE), 0)
        query = lax.broadcasted_iota(jnp.int32, (TILE, TILE), 1)
        corner = jnp.max(
            jnp.where(key < query, scores[:, :TILE], -2.0), axis=0, keepdims=True
        )
        here = slice(first, first + TILE)
        best_ref[:, here] = jnp.maximum(best_ref[:, here], corner)
        if first + TILE < rows:
            rest = jnp.max(scores[:, TILE:], axis=0, keepdims=True)
            there = slice(first + TILE, rows)
            best_ref[:, there] = jnp.maximum(best_ref[:, there], rest)


def best_kernel(plan, run_len_ref, place_ref, group_ref, own_ref, mate_ref, *rest):
    behind, (out_ref, best_ref, blocks_ref) = rest[:-3], rest[-3:]
    group, slot = plan.slot(place_ref[0], place_ref[1])
    begin = jnp.int32(0)
    for number, start in enumerate(cluster_starts(plan, run_len_ref)):
        here = (number // plan.per_group == group) & (start <= slot)
        begin = jnp.where(here, jnp.maximum(begin, start), begin)
    best_ref[...] = jnp.full(best_ref.shape, -1.0, jnp.float32)
    triangle_best(own_ref, best_ref)

    @pl.when(slot % 2 == 1)
    def _():
        block_best(mate_ref, own_ref, best_ref)

    for distance in range(1, plan.reach // 2):
        first, second = behind[2 * distance - 2], behind[2 * distance - 1]

        @pl.when(slot - slot % 2 - 2 * distance >= begin)
        def _():
            block_best(first, own_ref, best_ref)
            block_best(second, own_ref, best_ref)

    for number in range(plan.rows // plan.cap):
        part = best_ref[:, number * plan.cap : (number + 1) * plan.cap]
        blocks_ref[number : number + 1, : plan.cap] = part
    for source in range(plan.devices):
        chosen = jnp.maximum(group_ref[source, 0] - 1, 0)
        out_ref[source : source + 1, :] = blocks_ref[pl.ds(chosen, 1), :]


def unpack_kernel(plan, run_len_ref, cluster_ref, rank_ref, reply_ref, out_ref):
    owner, within = row_owner(plan, run_len_ref, cluster_ref[...], rank_ref[...])
    number = lax.broadcasted_iota(jnp.int32, (plan.devices, plan.rows), 0)
    chosen = jnp.where(number == owner, 1.0, 0.0)
    columns = lax.dot_general(
        reply_ref[:, : plan.cap],
        chosen,
        (((0,), (0,)), ((), ())),
        precision=lax.Precision.HIGHEST,
        preferred_element_type=jnp.float32,
    )
    lane = lax.broadcasted_iota(jnp.int32, (plan.cap, plan.rows), 0)
    out_ref[...] = jnp.sum(
        jnp.where(lane == within % plan.cap, columns, 0.0), axis=0, keepdims=True
    )


SMEM = pl.BlockSpec(memory_space=pltpu.SMEM)
VMEM = pl.BlockSpec(memory_space=pltpu.VMEM)


def call(kernel, plan, shapes, specs, scratch=(), flops=0, moved=0):
    return pl.pallas_call(
        functools.partial(kernel, plan),
        out_shape=shapes,
        in_specs=specs,
        out_specs=[VMEM] * len(shapes),
        scratch_shapes=scratch,
        compiler_params=pltpu.CompilerParams(vmem_limit_bytes=MEMORY),
        cost_estimate=pl.CostEstimate(flops=flops, bytes_accessed=moved, transcendentals=0),
    )


def exchange(block):
    return lax.all_to_all(block, AXES, split_axis=0, concat_axis=0, tiled=True)


def local(embeddings, cluster_id, rank, run_len):
    rows, width = embeddings.shape
    plan = Plan(lax.axis_size("ingest"), lax.axis_size("run"), run_len.shape[0], rows)
    clusters, ranks = cluster_id.reshape(1, rows), rank.reshape(1, rows)
    slots = plan.devices * plan.cap
    wide = jax.ShapeDtypeStruct
    outgoing, groups = call(
        pack_kernel,
        plan,
        [wide((slots, width), jnp.bfloat16), wide((plan.devices, 128), jnp.int32)],
        [SMEM, VMEM, VMEM, VMEM],
        [pltpu.VMEM((rows, width), jnp.bfloat16)],
        2 * slots * rows * width,
        3 * rows * width * 2,
    )(run_len, clusters, ranks, embeddings)
    groups = exchange(groups)
    arrived = exchange(outgoing)
    (own,) = call(
        sort_kernel, plan, [wide((rows, width), jnp.bfloat16)], [SMEM, VMEM],
        moved=3 * rows * width * 2,
    )(groups, arrived)

    def swap(block):
        pairs = [
            (i * plan.run + r, (i ^ 1) * plan.run + r)
            for i in range(plan.ingest)
            for r in range(plan.run)
        ]
        return lax.ppermute(block, AXES, pairs)

    mate = swap(own)
    behind = []
    for distance, chips in enumerate(plan.links()):
        if distance == 0:
            continue
        pairs = [
            (plan.device(i, 2 * chip + core), plan.device(i, 2 * (chip + distance) + core))
            for i in range(plan.ingest)
            for chip in chips
            for core in range(2)
        ]
        moved = lax.ppermute(own, AXES, pairs)
        behind += [moved, swap(moved)]
    place = jnp.stack([lax.axis_index("ingest"), lax.axis_index("run")]).astype(jnp.int32)
    (replies,) = call(
        best_kernel,
        plan,
        [wide((plan.devices, 128), jnp.float32)],
        [SMEM, SMEM, SMEM] + [VMEM] * (2 + len(behind)),
        [pltpu.VMEM((1, rows), jnp.float32), pltpu.VMEM((rows // plan.cap, 128), jnp.float32)],
        2 * rows * rows * width * 3,
        4 * rows * width * 2,
    )(run_len, place, groups, own, mate, *behind)
    returned = exchange(replies)
    (best,) = call(
        unpack_kernel, plan, [wide((1, rows), jnp.float32)], [SMEM, VMEM, VMEM, VMEM],
        moved=4 * rows * 4,
    )(run_len, clusters, ranks, returned)
    return best.reshape(rows)


def solution(mesh):
    return jax.shard_map(
        local,
        mesh=mesh,
        in_specs=(P(AXES, None), P(AXES), P(AXES), P()),
        out_specs=P(AXES),
        check_vma=False,
    )
```

time: 263 us -> 168 us (0.64)
  waiting for transfers between devices: 166 us -> 37 us
  blocking collectives: 15.2 us -> 108 us
  local copies, waits for them, and re-layouts: 37.2 us -> 0.01 us
  starting transfers between devices: 24.7 us -> 2.72 us
  Pallas kernels: 0 us -> 19 us
  other arithmetic: 14 us -> 0.64 us
  matrix products: 3.98 us -> 0 us
    all_to_all x1 -> x3, blocking collectives: 15.2 us -> 108 us  [exchange(): return lax.all_to_all(block, AXES, split_axis=0, concat_axis=0, tiled=True)]
    all_to_all x2 -> x0, waiting for transfers between devices: 71.8 us -> none  [the longest x1 71.8 us: local(): lax.all_to_all(outgoing, ('ingest', 'run'), split_axis=0, concat_axis=0,...]
    ppermute x3, waiting for transfers between devices: 94.7 us -> 37 us  [the longest x1 34.1 us: local(): moved = lax.ppermute(own, AXES, pairs)]
    gather x2 -> x0, local copies, waits for them, and re-layouts: 19.1 us -> none  [the longest x1 10.5 us: local(): return returned[position]]
    pallas_call x0 -> x4, Pallas kernels: none -> 19 us  [the longest x1 8.94 us: local(): call(pack_kernel, plan, [wide((slots, width), jnp.bfloat16), wide((plan.d...]
    scatter x2 -> x0, local copies, waits for them, and re-layouts: 15.3 us -> none  [the longest x1 10.9 us: local(): jnp.zeros((rows_dev, feature_width), jnp.bfloat16).at[target]]
    all_to_all x2 -> x0, starting transfers between devices: 13.1 us -> none  [the longest x1 7.3 us: local(): lax.all_to_all(labels, ('ingest', 'run'), split_axis=0, concat_axis=0, ti...]
    ppermute x3, starting transfers between devices: 11.6 us -> 2.72 us  [the longest x1 2.65 us: local(): moved = lax.ppermute(own, AXES, pairs)]
  transfers between devices with their start and end apart: 5 -> 3, of which waited for: 4 -> 2; matrix products, arithmetic and copies ran while one was open for 6% -> 0% of each run, Pallas kernels for 0% -> 0%
where the time goes in v1:
time: 168 us; the launch traced here: 167 us
  blocking collectives  108 us (64%)
  waiting for transfers between devices  37 us (22%)
  Pallas kernels  19 us (11%)
  starting transfers between devices  2.72 us (2%)
    all_to_all x3, blocking collectives, exchange(): return lax.all_to_all(block, AXES, split_axis=0, concat_axis=0, tiled=True)  108 us
    ppermute x1, waiting for transfers between devices, local(): moved = lax.ppermute(own, AXES, pairs)  34.1 us
    pallas_call x1, Pallas kernels, local(): call(pack_kernel, plan, [wide((slots, width), jnp.bfloat16), wide((plan.d...  8.94 us
    pallas_call x1, Pallas kernels, local(): call(best_kernel, plan, [wide((plan.devices, 128), jnp.float32)], [SMEM,...  4.79 us
    pallas_call x1, Pallas kernels, local(): call(sort_kernel, plan, [wide((rows, width), jnp.bfloat16)], [SMEM, VMEM]...  3.41 us
  transfers between devices with their start and end apart: 3, of which 2 were waited for; matrix products, arithmetic and copies ran while one was open for 0% of the time, Pallas kernels for 0%

profile of v1, /device:TPU:0, one launch (start us, length us, event | category | flops | bytes accessed | tf_op | source)
XLA Modules:
  0.0 167.2 jit_solution(17071550505176467267)
XLA Ops:
  0.0 8.9 %shard_map.46 = (bf16[2048,768]{1,0:T(8,128)(2,1)}, s32[32,128]{1,0:T(8,128)}) custom-call(s32[12]{0:T(128)} %run_len_ref.5, s32[1,1024]{1,0:T(1,128)} %bitcast.22, s32[1,1024]{1,0:T(1,128)} %bitcast.24, bf16[1024,768]{1,0:T(8,128)(2,1)} %rows_ref.1), custom_call_target="tpu_custom_call" | custom-call | flops 3221225472 | bytes 4718592 | tf_op jit(solution)/shard_map/pallas_call | solution.py:235
  8.9 14.4 %all_to_all.33 = s32[32,1,128]{2,1,0:T(1,128)} all-to-all(s32[32,1,128]{2,1,0:T(1,128)} %bitcast.21), channel_id=1, replica_groups=mesh['ingest'=4,'run'=8] {'ingest','run'}, dimensions={0} | all-to-all | bytes 32768 | tf_op jit(solution)/shard_map/all_to_all | solution.py:226
  23.3 76.1 %all_to_all.34 = bf16[32,64,768]{2,1,0:T(8,128)(2,1)} all-to-all(bf16[32,64,768]{2,1,0:T(8,128)(2,1)} %bitcast.16), channel_id=1, replica_groups=mesh['ingest'=4,'run'=8] {'ingest','run'}, dimensions={0} | all-to-all | bytes 6291456 | tf_op jit(solution)/shard_map/all_to_all | solution.py:226
  99.4 3.4 %shard_map.47.own_ref = bf16[1024,768]{1,0:T(8,128)(2,1)} custom-call(s32[32,128]{1,0:T(8,128)} %bitcast.17, bf16[2048,768]{1,0:T(8,128)(2,1)} %bitcast.15), custom_call_target="tpu_custom_call" | custom-call | bytes 4718592 | tf_op jit(solution)/shard_map/pallas_call | solution.py:246
  102.8 2.6 %collective-permute-start.1 = (bf16[1024,768]{1,0:T(8,128)(2,1)}, bf16[1024,768]{1,0:T(8,128)(2,1)S(1)}, u32[]{:S(2)}, u32[]{:S(2)}) collective-permute-start(bf16[1024,768]{1,0:T(8,128)(2,1)} %shard_map.47.own_ref), channel_id=1, source_target_pairs={{0,1},{8,9},{2,3},{10,11},{4,5},{12,13},{6,7},{14,15}} | collective-permute-start | bytes 4718600 | tf_op jit(solution)/shard_map/ppermute | solution.py:270
  105.4 0.1 collective-permute-start
  105.5 34.1 %collective-permute-done.1.rest_0_ = bf16[1024,768]{1,0:T(8,128)(2,1)S(1)} collective-permute-done((bf16[1024,768]{1,0:T(8,128)(2,1)}, bf16[1024,768]{1,0:T(8,128)(2,1)S(1)}, u32[]{:S(2)}, u32[]{:S(2)}) %collective-permute-start.1) | collective-permute-done | bytes 1572896 | tf_op jit(solution)/shard_map/ppermute | solution.py:270
  139.6 0.0 copy-start
  139.6 0.0 collective-permute-start.2
  139.6 0.6 pad_add_fusion.place_ref
  140.3 0.0 collective-permute-done.mate_ref
  140.3 0.0 copy-start.1
  140.3 2.9 %collective-permute-done.2.rest_1_ = bf16[1024,768]{1,0:T(8,128)(2,1)} collective-permute-done((bf16[1024,768]{1,0:T(8,128)(2,1)S(1)}, bf16[1024,768]{1,0:T(8,128)(2,1)}, u32[]{:S(2)}, u32[]{:S(2)}) %collective-permute-start.2) | collective-permute-done | bytes 1572896 | tf_op jit(solution)/shard_map/ppermute | solution.py:257
  143.2 0.0 copy-done
  143.2 0.0 copy-done.1
  143.2 4.8 %shard_map.48 = f32[32,128]{1,0:T(8,128)} custom-call(s32[12]{0:T(128)} %run_len_ref.5, s32[2]{0:T(128)} %pad_add_fusion.place_ref, s32[32,128]{1,0:T(8,128)} %bitcast.18, bf16[1024,768]{1,0:T(8,128)(2,1)} %shard_map.47.own_ref, bf16[1024,768]{1,0:T(8,128)(2,1)} %copy-done.1, bf16[1024,768]{1,0:T(8,128)(2,1)} %copy-done, ...), custom_call_target="tpu_custom_call" | custom-call | flops 4831838208 | bytes 6291456 | tf_op jit(solution)/shard_map/pallas_call | solution.py:273
  148.0 17.4 %all_to_all.35 = f32[32,1,128]{2,1,0:T(1,128)} all-to-all(f32[32,1,128]{2,1,0:T(1,128)} %bitcast.20), channel_id=1, replica_groups=mesh['ingest'=4,'run'=8] {'ingest','run'}, dimensions={0} | all-to-all | bytes 32768 | tf_op jit(solution)/shard_map/all_to_all | solution.py:226
  165.3 1.8 %shard_map.49 = f32[1,1024]{1,0:T(1,128)} custom-call(s32[12]{0:T(128)} %run_len_ref.5, s32[1,1024]{1,0:T(1,128)} %bitcast.23, s32[1,1024]{1,0:T(1,128)} %bitcast.25, f32[32,128]{1,0:T(8,128)} %bitcast.19), custom_call_target="tpu_custom_call" | custom-call | bytes 16384 | tf_op jit(solution)/shard_map/pallas_call | solution.py:283
Async XLA Ops:
  102.8 36.8 %collective-permute-start.1 = (bf16[1024,768]{1,0:T(8,128)(2,1)}, bf16[1024,768]{1,0:T(8,128)(2,1)S(1)}, u32[]{:S(2)}, u32[]{:S(2)}) collective-permute-start(bf16[1024,768]{1,0:T(8,128)(2,1)} %shard_map.47.own_ref), channel_id=1, source_target_pairs={{0,1},{8,9},{2,3},{10,11},{4,5},{12,13},{6,7},{14,15}} | collective-permute-start | bytes 4718600 | tf_op jit(solution)/shard_map/ppermute | solution.py:270
  105.4 34.8 %collective-permute-start = (bf16[1024,768]{1,0:T(8,128)(2,1)}, bf16[1024,768]{1,0:T(8,128)(2,1)S(1)}, u32[]{:S(2)}, u32[]{:S(2)}) collective-permute-start(bf16[1024,768]{1,0:T(8,128)(2,1)} %shard_map.47.own_ref), channel_id=1, source_target_pairs={{0,8},{1,9},{2,10},{3,11},{4,12},{5,13},{6,14},{7,15},{8,0},{9,1},... | collective-permute-start | bytes 4718600 | tf_op jit(solution)/shard_map/ppermute | solution.py:257
  139.6 3.5 %copy-start = (bf16[1024,768]{1,0:T(8,128)(2,1)}, bf16[1024,768]{1,0:T(8,128)(2,1)S(1)}, u32[]{:S(2)}) copy-start(bf16[1024,768]{1,0:T(8,128)(2,1)S(1)} %collective-permute-done.1.rest_0_) | copy-start | bytes 4718596
  139.6 3.5 %collective-permute-start.2 = (bf16[1024,768]{1,0:T(8,128)(2,1)S(1)}, bf16[1024,768]{1,0:T(8,128)(2,1)}, u32[]{:S(2)}, u32[]{:S(2)}) collective-permute-start(bf16[1024,768]{1,0:T(8,128)(2,1)S(1)} %collective-permute-done.1.rest_0_), channel_id=1, source_target_pairs={{0,8},{1,9},{2,10},{3,11},{4,12},{5,13},{6,14},{7,15},{8,0},{9,1},... | collective-permute-start | bytes 4718600 | tf_op jit(solution)/shard_map/ppermute | solution.py:257
  140.3 2.9 %copy-start.1 = (bf16[1024,768]{1,0:T(8,128)(2,1)}, bf16[1024,768]{1,0:T(8,128)(2,1)S(1)}, u32[]{:S(2)}) copy-start(bf16[1024,768]{1,0:T(8,128)(2,1)S(1)} %collective-permute-done.mate_ref) | copy-start | bytes 4718596

commit v2 on v1

--- a/solution.py
+++ b/solution.py
@@ -10,11 +10,12 @@
 EPSILON = 1e-06
 AXES = ("ingest", "run")
 TILE = 256
+CHUNKS = 2
 MEMORY = 60 * 1024 * 1024
 
 
 class Plan:
-    def __init__(self, ingest, run, clusters, rows):
+    def __init__(self, ingest, run, clusters, rows, features):
         self.ingest, self.run, self.clusters, self.rows = ingest, run, clusters, rows
         self.devices = ingest * run
         self.per_group = clusters // ingest
@@ -22,6 +23,25 @@
         self.reach = min(8, run // 2)
         self.width = run // ingest
         self.pairs = run // 2
+        self.blocks = rows // self.cap
+        self.layers, self.lanes = ingest, ingest * self.width
+        self.slice = self.cap // self.lanes
+        self.part = self.blocks * self.slice
+        self.chunks = tuple(features // CHUNKS for _ in range(CHUNKS))
+        mean = rows // self.layers
+        self.room = mean + mean // 8
+        self.stride = -(-self.room // 128) * 128
+
+    def staged(self):
+        powers = all(n & (n - 1) == 0 for n in (self.layers, self.lanes, self.width))
+        return (
+            powers
+            and self.cap % (8 * self.lanes) == 0
+            and self.part == 128
+            and self.room % 16 == 0
+            and min(self.chunks) >= self.stride
+            and self.links()[1:] == [[0]]
+        )
 
     def device(self, group, slot):
         core, chip = slot % 2, slot // 2
@@ -76,7 +96,7 @@
     return starts
 
 
-def row_owner(plan, run_len_ref, cluster, rank):
+def row_slot(plan, run_len_ref, cluster, rank):
     starts = cluster_starts(plan, run_len_ref)
     begin = jnp.zeros_like(cluster)
     group = jnp.zeros_like(cluster)
@@ -84,8 +104,12 @@
         here = cluster == number
         begin = jnp.where(here, start, begin)
         group = jnp.where(here, number // plan.per_group, group)
-    owner = plan.device(group, begin + rank // plan.rows)
-    return owner, rank % plan.rows
+    return group, begin + rank // plan.rows, rank % plan.rows
+
+
+def row_owner(plan, run_len_ref, cluster, rank):
+    group, slot, within = row_slot(plan, run_len_ref, cluster, rank)
+    return plan.device(group, slot), within
 
 
 def pack_kernel(plan, run_len_ref, cluster_ref, rank_ref, rows_ref, out_ref, group_ref, unit_ref):
@@ -206,6 +230,290 @@
     )
 
 
+def lane_of(plan, slot):
+    device = plan.device(0, slot)
+    return device // plan.run * plan.width + device % plan.run
+
+
+def lane_device(plan, layer, lane):
+    return lane // plan.width * plan.run + layer * plan.width + lane % plan.width
+
+
+def my_lane(plan):
+    run = lax.axis_index("run")
+    return lax.axis_index("ingest") * plan.width + run % plan.width, run // plan.width
+
+
+def spread_kernel(plan, run_len_ref, cluster_ref, rank_ref, rows_ref, *rest):
+    outs, (unit_ref,) = rest[:-1], rest[-1:]
+    step = 128
+
+    @pl.loop(0, plan.rows // step)
+    def _(number):
+        here = pl.ds(pl.multiple_of(number * step, step), step)
+        widened = rows_ref[here, :].astype(jnp.float32)
+        total = jnp.sum(widened * widened, axis=1, keepdims=True) + EPSILON
+        unit_ref[here, :] = (widened * lax.rsqrt(total)).astype(jnp.bfloat16)
+
+    lane, _ = my_lane(plan)
+    group, slot, within = row_slot(plan, run_len_ref, cluster_ref[...], rank_ref[...])
+    owner = group * plan.run + slot
+    number = lax.broadcasted_iota(jnp.int32, (plan.devices, plan.rows), 0)
+    member = number == owner
+    block = jnp.max(jnp.where(member, within // plan.cap + 1, 0), axis=1, keepdims=True)
+    present = jnp.where(block > 0, 1.0, 0.0)
+    before = lax.broadcasted_iota(jnp.int32, (plan.devices, plan.devices), 0) > (
+        lax.broadcasted_iota(jnp.int32, (plan.devices, plan.devices), 1)
+    )
+    order = jnp.dot(
+        jnp.where(before, 1.0, 0.0),
+        jnp.broadcast_to(present, (plan.devices, 128)),
+        preferred_element_type=jnp.float32,
+    )
+    mine = jnp.sum(jnp.where(member, order[:, :1], 0.0), axis=0, keepdims=True)
+    residue = within % plan.cap
+    target = (
+        (residue // plan.slice ^ lane) * plan.part
+        + mine.astype(jnp.int32) * plan.slice
+        + residue % plan.slice
+    )
+    per = len(outs) // len(plan.chunks)
+    tile = 2 * plan.part
+
+    for pair in range(plan.lanes // 2):
+        row = lax.broadcasted_iota(jnp.int32, (tile, plan.rows), 0) + pair * tile
+        chosen = jnp.where(row == target, 1.0, 0.0).astype(jnp.bfloat16)
+        moved = jnp.dot(chosen, unit_ref[...], preferred_element_type=jnp.float32)
+        moved = moved.astype(jnp.bfloat16)
+        for half in range(2):
+            first = 0
+            for chunk, width in enumerate(plan.chunks):
+                outs[chunk * per + 2 * pair + half][: plan.part, :] = moved[
+                    half * plan.part : (half + 1) * plan.part, first : first + width
+                ]
+                first += width
+
+    place = lax.broadcasted_iota(jnp.int32, (plan.devices, plan.part), 1) // plan.slice
+    here = (place.astype(jnp.float32) == order[:, :1]) & (block > 0)
+    who = lax.broadcasted_iota(jnp.int32, (plan.devices, plan.part), 0)
+    owners = jnp.sum(jnp.where(here, who, 0), axis=0, keepdims=True)
+    blocks = jnp.sum(jnp.where(here, block - 1, 0), axis=0, keepdims=True)
+    line = lax.broadcasted_iota(jnp.int32, (16, plan.part), 0)
+    table = jnp.where(line == 0, owners, jnp.where(line == 1, blocks, 0))
+    for out in outs[:per]:
+        out[plan.part :, : plan.part] = table.astype(jnp.float32).astype(jnp.bfloat16)
+
+
+def permute_into(target, first, inputs_ref, outs, room, stride):
+    columns = inputs_ref.shape[0]
+    for number, out in enumerate(outs):
+        row = lax.broadcasted_iota(jnp.int32, (room, columns), 0) + first + number * stride
+        chosen = jnp.where(row == target, 1.0, 0.0).astype(jnp.bfloat16)
+        moved = jnp.dot(chosen, inputs_ref[...], preferred_element_type=jnp.float32)
+        out[:room, :] = moved.astype(jnp.bfloat16)
+
+
+def route_kernel(plan, *refs):
+    ins, rest = refs[: plan.lanes], refs[plan.lanes :]
+    outs, (target_ref, inputs_ref, owner_ref, block_ref, value_ref) = rest[:-5], rest[-5:]
+    _, layer = my_lane(plan)
+    for number, part in enumerate(ins):
+        inputs_ref[number * plan.part : (number + 1) * plan.part, :] = part[: plan.part, :]
+        table = part[plan.part :, : plan.part].astype(jnp.float32)
+        owner_ref[number : number + 1, :] = table[0:1, :].astype(jnp.int32)
+        block_ref[number : number + 1, :] = table[1:2, :].astype(jnp.int32)
+    owner = owner_ref[...]
+    shape = (plan.part, plan.part)
+    earlier = lax.broadcasted_iota(jnp.int32, shape, 0) < lax.broadcasted_iota(jnp.int32, shape, 1)
+    earlier = jnp.where(earlier, 1.0, 0.0)
+    ones = jnp.ones(shape, jnp.float32)
+    shape = (plan.lanes, plan.lanes)
+    above = lax.broadcasted_iota(jnp.int32, shape, 0) > lax.broadcasted_iota(jnp.int32, shape, 1)
+    above = jnp.where(above, 1.0, 0.0)
+    target = jnp.zeros(owner.shape, jnp.int32)
+    most = jnp.float32(0.0)
+    for other in range(plan.layers):
+        chosen = owner // plan.run == other
+        marks = jnp.where(chosen, 1.0, 0.0)
+        lines = jnp.dot(marks, ones, preferred_element_type=jnp.float32)
+        count = jnp.dot(marks, earlier, preferred_element_type=jnp.float32) + jnp.dot(
+            above, lines, preferred_element_type=jnp.float32
+        )
+        count = count.astype(jnp.int32)
+        there = jnp.where(count < plan.room, (layer ^ other) * plan.stride + count, -1)
+        target = jnp.where(chosen, there, target)
+        most = jnp.maximum(most, jnp.sum(marks))
+    full = jnp.where(most > plan.room, 1.0, 0.0)
+    value = owner % plan.run * plan.blocks + block_ref[...] + 1
+    for number in range(plan.lanes):
+        here = slice(number * plan.part, (number + 1) * plan.part)
+        target_ref[:, here] = target[number : number + 1, :]
+        value_ref[:, here] = value[number : number + 1, :].astype(jnp.float32)
+    target = target_ref[...]
+    values = jnp.broadcast_to(value_ref[...], (8, plan.rows)).astype(jnp.bfloat16)
+    for number, out in enumerate(outs):
+        row = lax.broadcasted_iota(jnp.int32, (plan.stride, plan.rows), 0) + number * plan.stride
+        chosen = jnp.where(row == target, 1.0, 0.0).astype(jnp.bfloat16)
+        moved = jnp.dot(
+            chosen[: plan.room, :], inputs_ref[...], preferred_element_type=jnp.float32
+        )
+        out[: plan.room, :] = moved.astype(jnp.bfloat16)
+        listed = lax.dot_general(
+            values, chosen, (((1,), (1,)), ((), ())), preferred_element_type=jnp.float32
+        )
+        line = lax.broadcasted_iota(jnp.int32, (16, plan.stride), 0)
+        table = jnp.where(line == 0, listed[0:1, :], jnp.where(line == 1, full, 0.0))
+        out[plan.room :, : plan.stride] = table.astype(jnp.bfloat16)
+
+
+def route_more_kernel(plan, target_ref, *refs):
+    ins, outs, inputs_ref = refs[: plan.lanes], refs[plan.lanes : -1], refs[-1]
+    for number, part in enumerate(ins):
+        inputs_ref[number * plan.part : (number + 1) * plan.part, :] = part[...]
+    permute_into(target_ref[...], 0, inputs_ref, outs, plan.room, plan.stride)
+
+
+def gather_rows(plan, ins, inputs_ref):
+    for number, part in enumerate(ins):
+        first = number * plan.stride
+        inputs_ref[first : first + plan.room, :] = part[: plan.room, :]
+        if plan.stride > plan.room:
+            inputs_ref[first + plan.room : first + plan.stride, :] = jnp.zeros(
+                (plan.stride - plan.room, inputs_ref.shape[1]), jnp.bfloat16
+            )
+
+
+def sort_parts(plan, target, inputs_ref, outs, ahead_ref, sorted_ref):
+    tile = 2 * plan.part
+    for pair in range(plan.lanes // 2):
+        row = lax.broadcasted_iota(jnp.int32, (tile, inputs_ref.shape[0]), 0) + pair * tile
+        chosen = jnp.where(row == target, 1.0, 0.0).astype(jnp.bfloat16)
+        moved = jnp.dot(chosen, inputs_ref[...], preferred_element_type=jnp.float32)
+        moved = moved.astype(jnp.bfloat16)
+        sorted_ref[pair * tile : (pair + 1) * tile, :] = moved
+        outs[2 * pair][...] = moved[: plan.part, :]
+        outs[2 * pair + 1][...] = moved[plan.part :, :]
+    lane, _ = my_lane(plan)
+    for slot in range(2):
+        part = lane_of(plan, slot) ^ lane
+        ahead_ref[slot * plan.part : (slot + 1) * plan.part, :] = sorted_ref[
+            pl.ds(pl.multiple_of(part * plan.part, plan.part), plan.part), :
+        ]
+
+
+def deliver_kernel(plan, *refs):
+    ins, rest = refs[: plan.layers], refs[plan.layers :]
+    outs, (ahead_ref, target_ref, full_ref, inputs_ref, sorted_ref) = rest[:-5], rest[-5:]
+    lane, _ = my_lane(plan)
+    gather_rows(plan, ins, inputs_ref)
+    full = jnp.zeros((8, 128), jnp.float32)
+    for number, part in enumerate(ins):
+        table = part[plan.room :, : plan.stride].astype(jnp.float32)
+        value = table[0:1, :].astype(jnp.int32) - 1
+        full = jnp.maximum(full, jnp.broadcast_to(table[1:2, :128], (8, 128)))
+        slot = value // plan.blocks
+        within = lax.broadcasted_iota(jnp.int32, value.shape, 1) % plan.slice
+        target = (lane_of(plan, slot) ^ lane) * plan.part + value % plan.blocks * plan.slice + within
+        target_ref[:, number * plan.stride : (number + 1) * plan.stride] = jnp.where(
+            value >= 0, target, -1
+        )
+    full_ref[...] = full.astype(jnp.int32)
+    sort_parts(plan, target_ref[...], inputs_ref, outs, ahead_ref, sorted_ref)
+
+
+def deliver_more_kernel(plan, target_ref, *refs):
+    ins, rest = refs[: plan.layers], refs[plan.layers :]
+    outs, (ahead_ref, inputs_ref, sorted_ref) = rest[:-3], rest[-3:]
+    gather_rows(plan, ins, inputs_ref)
+    sort_parts(plan, target_ref[...], inputs_ref, outs, ahead_ref, sorted_ref)
+
+
+def join_kernel(plan, *refs):
+    ins, (own_ref, behind_ref) = refs[:-2], refs[-2:]
+    for number, part in enumerate(ins[: plan.lanes]):
+        own_ref[number * plan.part : (number + 1) * plan.part, :] = part[...]
+    for number, part in enumerate(ins[plan.lanes :]):
+        behind_ref[number * 2 * plan.part : (number + 1) * 2 * plan.part, :] = part[...]
+
+
+def wide_best(keys, queries_ref, best_ref):
+    @pl.loop(0, keys[0].shape[0] // TILE)
+    def _(tile):
+        here = pl.ds(pl.multiple_of(tile * TILE, TILE), TILE)
+        block = jnp.concatenate([part[here, :] for part in keys], axis=1)
+        scores = lax.dot_general(
+            block, queries_ref[...], (((1,), (1,)), ((), ())), preferred_element_type=jnp.float32
+        )
+        best_ref[...] = jnp.maximum(best_ref[...], jnp.max(scores, axis=0, keepdims=True))
+
+
+def staged_best_kernel(plan, run_len_ref, *refs):
+    count = len(plan.chunks)
+    own, mate, behind, far = (refs[n * count : (n + 1) * count] for n in range(4))
+    out_ref, best_ref, queries_ref, lines_ref = refs[4 * count :]
+    ingest, run = lax.axis_index("ingest"), lax.axis_index("run")
+    lane, _ = my_lane(plan)
+    group, slot = plan.slot(ingest, run)
+    begin = jnp.int32(0)
+    for number, start in enumerate(cluster_starts(plan, run_len_ref)):
+        here = (number // plan.per_group == group) & (start <= slot)
+        begin = jnp.where(here, jnp.maximum(begin, start), begin)
+    first = 0
+    for part in own:
+        queries_ref[:, first : first + part.shape[1]] = part[...]
+        first += part.shape[1]
+
+    def slots(row):
+        block = row // plan.slice % plan.blocks
+        return block * plan.cap + (row // plan.part ^ lane) * plan.slice + row % plan.slice
+
+    best_ref[...] = jnp.full(best_ref.shape, -1.0, jnp.float32)
+    query = slots(lax.broadcasted_iota(jnp.int32, (1, plan.rows), 1))
+
+    @pl.loop(0, plan.rows // TILE)
+    def _(tile):
+        key = slots(lax.broadcasted_iota(jnp.int32, (TILE, 1), 0) + tile * TILE)
+        block = queries_ref[pl.ds(pl.multiple_of(tile * TILE, TILE), TILE), :]
+        scores = lax.dot_general(
+            block, queries_ref[...], (((1,), (1,)), ((), ())), preferred_element_type=jnp.float32
+        )
+        top = jnp.max(jnp.where(key < query, scores, -2.0), axis=0, keepdims=True)
+        best_ref[...] = jnp.maximum(best_ref[...], top)
+
+    @pl.when(slot % 2 == 1)
+    def _():
+        wide_best(mate, queries_ref, best_ref)
+
+    @pl.when(slot - slot % 2 - 2 >= begin)
+    def _():
+        wide_best(behind, queries_ref, best_ref)
+        wide_best(far, queries_ref, best_ref)
+
+    for number in range(plan.lanes):
+        lines_ref[number : number + 1, :] = best_ref[
+            :, number * plan.part : (number + 1) * plan.part
+        ]
+    for device in range(plan.devices):
+        out_ref[device] = lines_ref[...]
+
+
+def staged_unpack_kernel(plan, run_len_ref, cluster_ref, rank_ref, reply_ref, out_ref):
+    group, slot, within = row_slot(plan, run_len_ref, cluster_ref[...], rank_ref[...])
+    residue = within % plan.cap
+    line = plan.device(group, slot) * plan.lanes + (residue // plan.slice ^ lane_of(plan, slot))
+    column = within // plan.cap * plan.slice + residue % plan.slice
+    number = lax.broadcasted_iota(jnp.int32, (plan.devices * plan.lanes, plan.rows), 0)
+    columns = lax.dot_general(
+        reply_ref[...],
+        jnp.where(number == line, 1.0, 0.0),
+        (((0,), (0,)), ((), ())),
+        precision=lax.Precision.HIGHEST,
+        preferred_element_type=jnp.float32,
+    )
+    place = lax.broadcasted_iota(jnp.int32, (plan.part, plan.rows), 0)
+    out_ref[...] = jnp.sum(jnp.where(place == column, columns, 0.0), axis=0, keepdims=True)
+
+
 SMEM = pl.BlockSpec(memory_space=pltpu.SMEM)
 VMEM = pl.BlockSpec(memory_space=pltpu.VMEM)
 
@@ -226,10 +534,8 @@
     return lax.all_to_all(block, AXES, split_axis=0, concat_axis=0, tiled=True)
 
 
-def local(embeddings, cluster_id, rank, run_len):
+def direct(plan, embeddings, clusters, ranks, run_len):
     rows, width = embeddings.shape
-    plan = Plan(lax.axis_size("ingest"), lax.axis_size("run"), run_len.shape[0], rows)
-    clusters, ranks = cluster_id.reshape(1, rows), rank.reshape(1, rows)
     slots = plan.devices * plan.cap
     wide = jax.ShapeDtypeStruct
     outgoing, groups = call(
@@ -284,6 +590,154 @@
         unpack_kernel, plan, [wide((1, rows), jnp.float32)], [SMEM, VMEM, VMEM, VMEM],
         moved=4 * rows * 4,
     )(run_len, clusters, ranks, returned)
+    return best
+
+
+def staged(plan, embeddings, clusters, ranks, run_len):
+    rows, width = embeddings.shape
+    wide = jax.ShapeDtypeStruct
+    half = jnp.bfloat16
+    lanes, layers = range(plan.lanes), range(plan.layers)
+
+    def along_lanes(block, change):
+        pairs = [
+            (lane_device(plan, layer, lane), lane_device(plan, layer, lane ^ change))
+            for layer in layers
+            for lane in lanes
+        ]
+        return lax.ppermute(block, AXES, pairs)
+
+    def along_layers(block, change):
+        pairs = [
+            (lane_device(plan, layer, lane), lane_device(plan, layer ^ change, lane))
+            for layer in layers
+            for lane in lanes
+        ]
+        return lax.ppermute(block, AXES, pairs)
+
+    def chip_to_chip(block, routes):
+        pairs = [
+            (plan.device(layer, 2 * first + core), plan.device(layer, 2 * second + core))
+            for layer in layers
+            for first, second in routes
+            for core in range(2)
+        ]
+        return lax.ppermute(block, AXES, pairs)
+
+    far_first = sorted(lanes, key=lambda change: -(change & 1) - (change // plan.width // 2))
+
+    def swap_lanes(blocks):
+        return [
+            along_lanes(blocks[change], change) if change else blocks[0] for change in far_first
+        ], far_first
+
+    def by_change(moved):
+        arrays, order = moved
+        return [arrays[order.index(change)] for change in lanes]
+
+    sizes = [plan.part + 16] + [plan.part] * (len(plan.chunks) - 1)
+    spread = call(
+        spread_kernel,
+        plan,
+        [wide((size, f), half) for size, f in zip(sizes, plan.chunks) for _ in lanes],
+        [SMEM, VMEM, VMEM, VMEM],
+        [pltpu.VMEM((rows, width), half)],
+        2 * rows * rows * width,
+        3 * rows * width * 2,
+    )(run_len, clusters, ranks, embeddings)
+    owns, mates, behinds, fars = [], [], [], []
+    table = targets = full = None
+    for chunk, f in enumerate(plan.chunks):
+        spec = dict(flops=2 * rows * rows * f, moved=3 * rows * f * 2)
+        parts = by_change(swap_lanes(spread[chunk * plan.lanes : (chunk + 1) * plan.lanes]))
+        rooms = [wide((plan.room + (0 if chunk else 16), f), half) for _ in layers]
+        inputs = pltpu.VMEM((rows, f), half)
+        if chunk == 0:
+            *routed, table = call(
+                route_kernel,
+                plan,
+                [*rooms, wide((1, rows), jnp.int32)],
+                [VMEM] * plan.lanes,
+                [
+                    inputs,
+                    pltpu.VMEM((plan.lanes, plan.part), jnp.int32),
+                    pltpu.VMEM((plan.lanes, plan.part), jnp.int32),
+                    pltpu.VMEM((1, rows), jnp.float32),
+                ],
+                **spec,
+            )(*parts)
+        else:
+            routed = call(
+                route_more_kernel, plan, rooms, [VMEM] * (1 + plan.lanes), [inputs], **spec
+            )(table, *parts)
+        moved = {change: along_layers(routed[change], change) for change in reversed(layers[1:])}
+        arrived = [routed[0]] + [moved[change] for change in layers[1:]]
+        shapes = [wide((plan.part, f), half) for _ in lanes] + [wide((2 * plan.part, f), half)]
+        scratch = [pltpu.VMEM((plan.layers * plan.stride, f), half), inputs]
+        if chunk == 0:
+            *parts, ahead, targets, full = call(
+                deliver_kernel,
+                plan,
+                [
+                    *shapes,
+                    wide((1, plan.layers * plan.stride), jnp.int32),
+                    wide((8, 128), jnp.int32),
+                ],
+                [VMEM] * plan.layers,
+                scratch,
+                **spec,
+            )(*arrived)
+        else:
+            *parts, ahead = call(
+                deliver_more_kernel, plan, shapes, [VMEM] * (1 + plan.layers), scratch, **spec
+            )(targets, *arrived)
+        near = chip_to_chip(ahead, [(0, 1), (3, 2)])
+        parts = by_change(swap_lanes(parts))
+        side = chip_to_chip(ahead, [(2, 1)])
+        corner = chip_to_chip(near, [(2, 1)])
+        own, behind = call(
+            join_kernel,
+            plan,
+            [wide((rows, f), half)] * 2,
+            [VMEM] * (plan.lanes + 4),
+            moved=4 * rows * f * 2,
+        )(*parts, ahead, near, side, corner)
+        owns.append(own)
+        behinds.append(behind)
+        mates.append(along_lanes(own, plan.width))
+        fars.append(along_lanes(behind, plan.width))
+    (replies,) = call(
+        staged_best_kernel,
+        plan,
+        [wide((plan.devices, plan.lanes, 128), jnp.float32)],
+        [SMEM] + [VMEM] * (4 * len(plan.chunks)),
+        [
+            pltpu.VMEM((1, rows), jnp.float32),
+            pltpu.VMEM((rows, width), half),
+            pltpu.VMEM((plan.lanes, 128), jnp.float32),
+        ],
+        2 * rows * rows * width * 3,
+        4 * rows * width * 2,
+    )(run_len, *owns, *mates, *behinds, *fars)
+    returned = exchange(replies).reshape(plan.devices * plan.lanes, 128)
+    (best,) = call(
+        staged_unpack_kernel,
+        plan,
+        [wide((1, rows), jnp.float32)],
+        [SMEM, VMEM, VMEM, VMEM],
+        moved=4 * rows * 4,
+    )(run_len, clusters, ranks, returned)
+    return best, full[0, 0]
+
+
+def local(embeddings, cluster_id, rank, run_len):
+    rows, width = embeddings.shape
+    plan = Plan(lax.axis_size("ingest"), lax.axis_size("run"), run_len.shape[0], rows, width)
+    given = (embeddings, cluster_id.reshape(1, rows), rank.reshape(1, rows), run_len)
+    if not plan.staged():
+        return direct(plan, *given).reshape(rows)
+    best, full = staged(plan, *given)
+    best = lax.cond(full > 0, lambda: direct(plan, *given), lambda: best)
     return best.reshape(rows)
 
 

time: 168 us -> 156 us (0.929)
  blocking collectives: 108 us -> 0 us
  starting transfers between devices: 2.72 us -> 69.3 us
  Pallas kernels: 19 us -> 35 us
  waiting for transfers between devices: 37 us -> 44.4 us
  local copies, waits for them, and re-layouts: 0.01 us -> 5.69 us
    all_to_all x3 -> x0, blocking collectives: 108 us -> none  [exchange(): return lax.all_to_all(block, AXES, split_axis=0, concat_axis=0, tiled=True)]
    ppermute x3 -> x44, starting transfers between devices: 2.72 us -> 60 us  [the longest x32 39.4 us: along_lanes(): return lax.ppermute(block, AXES, pairs)]
    pallas_call x4 -> x9, Pallas kernels: 19 us -> 35 us  [the longest x1 6.45 us: staged(): call(staged_best_kernel, plan, [wide((plan.devices, plan.lanes, 128), jnp...]
    all_to_all x0 -> x1, starting transfers between devices: none -> 9.29 us  [exchange(): return lax.all_to_all(block, AXES, split_axis=0, concat_axis=0, tiled=True)]
    all_to_all x0 -> x1, waiting for transfers between devices: none -> 5.76 us  [exchange(): return lax.all_to_all(block, AXES, split_axis=0, concat_axis=0, tiled=True)]
    unnamed x4 -> x100, local copies, waits for them, and re-layouts: 0.01 us -> 4.4 us
    ppermute x3 -> x44, waiting for transfers between devices: 37 us -> 38.7 us  [the longest x32 21.3 us: along_lanes(): return lax.ppermute(block, AXES, pairs)]
  transfers between devices with their start and end apart: 3 -> 45, of which waited for: 2 -> 13; matrix products, arithmetic and copies ran while one was open for 0% -> 1% of each run, Pallas kernels for 0% -> 14%
where the time goes in v2:
time: 156 us
  starting transfers between devices  69.3 us (44%)
  waiting for transfers between devices  44.4 us (28%)
  Pallas kernels  35 us (22%)
  local copies, waits for them, and re-layouts  5.69 us (4%)
    ppermute x32, starting transfers between devices, along_lanes(): return lax.ppermute(block, AXES, pairs)  39.4 us
    ppermute x32, waiting for transfers between devices, along_lanes(): return lax.ppermute(block, AXES, pairs)  21.3 us
    ppermute x6, waiting for transfers between devices, along_layers(): return lax.ppermute(block, AXES, pairs)  17.3 us
    ppermute x6, starting transfers between devices, along_layers(): return lax.ppermute(block, AXES, pairs)  11.4 us
    all_to_all x1, starting transfers between devices, exchange(): return lax.all_to_all(block, AXES, split_axis=0, concat_axis=0, tiled=True)  9.29 us
    ppermute x6, starting transfers between devices, chip_to_chip(): return lax.ppermute(block, AXES, pairs)  9.18 us
    pallas_call x1, Pallas kernels, staged(): call(staged_best_kernel, plan, [wide((plan.devices, plan.lanes, 128), jnp...  6.45 us
    all_to_all x1, waiting for transfers between devices, exchange(): return lax.all_to_all(block, AXES, split_axis=0, concat_axis=0, tiled=True)  5.76 us
  transfers between devices with their start and end apart: 45, of which 13 were waited for; matrix products, arithmetic and copies ran while one was open for 1% of the time, Pallas kernels for 14%

profile of v2, /device:TPU:0, one launch (start us, length us, event | category | flops | bytes accessed | tf_op | source)
XLA Modules:
  0.0 155.7 jit_solution(12941037406498868979)
XLA Ops:
  0.0 5.6 %shard_map.48 = (bf16[144,384]{1,0:T(8,128)(2,1)}, bf16[144,384]{1,0:T(8,128)(2,1)}, bf16[144,384]{1,0:T(8,128)(2,1)}, bf16[144,384]{1,0:T(8,128)(2,1)}, bf16[14...) custom-call(s32[12]{0:T(128)} %run_len_ref.5, ...), custom_call_target="tpu_custom_call" | custom-call | flops 1610612736 | bytes 4718592 | tf_op jit(solution)/shard_map/pallas_call | solution.py:639
  5.6 3.0 %collective-permute-start.3 = (bf16[144,384]{1,0:T(8,128)(2,1)}, bf16[144,384]{1,0:T(8,128)(2,1)S(1)}, u32[]{:S(2)}, u32[]{:S(2)}) collective-permute-start(bf16[144,384]{1,0:T(8,128)(2,1)} %get-tuple-element.75), channel_id=1, source_target_pairs={{0,1},{1,0},{8,9},{9,8},{16,17},{17,16},{24,25},{25,24},{2,3},{3,2... | collective-permute-start | bytes 331784 | tf_op jit(solution)/shard_map/ppermute | solution.py:608
  10.8 3.7 %collective-permute-done.23.refs_1_ = bf16[128,384]{1,0:T(8,128)(2,1)S(1)} collective-permute-done((bf16[128,384]{1,0:T(8,128)(2,1)}, bf16[128,384]{1,0:T(8,128)(2,1)S(1)}, u32[]{:S(2)}, u32[]{:S(2)}) %collective-permute-start.23) | collective-permute-done | bytes 98336 | tf_op jit(solution)/shard_map/ppermute | solution.py:608
  16.0 2.3 %collective-permute-start.7 = (bf16[144,384]{1,0:T(8,128)(2,1)}, bf16[144,384]{1,0:T(8,128)(2,1)S(1)}, u32[]{:S(2)}, u32[]{:S(2)}) collective-permute-start(bf16[144,384]{1,0:T(8,128)(2,1)} %get-tuple-element.79), channel_id=1, source_target_pairs={{0,17},{1,16},{8,25},{9,24},{16,1},{17,0},{24,9},{25,8},{2,19},{3,... | collective-permute-start | bytes 331784 | tf_op jit(solution)/shard_map/ppermute | solution.py:608
  21.9 2.1 %collective-permute-done.7.refs_5_ = bf16[144,384]{1,0:T(8,128)(2,1)S(1)} collective-permute-done((bf16[144,384]{1,0:T(8,128)(2,1)}, bf16[144,384]{1,0:T(8,128)(2,1)S(1)}, u32[]{:S(2)}, u32[]{:S(2)}) %collective-permute-start.7) | collective-permute-done | bytes 110624 | tf_op jit(solution)/shard_map/ppermute | solution.py:608
  26.0 2.7 %collective-permute-start.29 = (bf16[128,384]{1,0:T(8,128)(2,1)}, bf16[128,384]{1,0:T(8,128)(2,1)S(1)}, u32[]{:S(2)}, u32[]{:S(2)}) collective-permute-start(bf16[128,384]{1,0:T(8,128)(2,1)} %get-tuple-element.106), channel_id=1, source_target_pairs={{0,25},{1,24},{8,17},{9,16},{16,9},{17,8},{24,1},{25,0},{2,27},{3,... | collective-permute-start | bytes 294920 | tf_op jit(solution)/shard_map/ppermute | solution.py:608
  28.7 4.7 %shard_map.49 = (bf16[304,384]{1,0:T(8,128)(2,1)}, bf16[304,384]{1,0:T(8,128)(2,1)}, bf16[304,384]{1,0:T(8,128)(2,1)}, bf16[304,384]{1,0:T(8,128)(2,1)}, s32[1,1024]{1,0:T(1,128)}) custom-call(bf16[144,384]{1,0:T(8,128)(2,1)} %get-tuple-element.74.refs_0_, bf16[144,384]{1,0:T(8,128)(2,1)} %copy-done.37, bf16[144,384]{1,0:T(8,128)(2,1)} %copy-done.38, ...), custom_call_target="tpu_custom_call" | custom-call | flops 805306368 | bytes 2359296 | tf_op jit(solution)/shard_map/pallas_call | solution.py:656
  35.1 2.6 %collective-permute-start.11 = (bf16[304,384]{1,0:T(8,128)(2,1)}, bf16[304,384]{1,0:T(8,128)(2,1)S(1)}, u32[]{:S(2)}, u32[]{:S(2)}) collective-permute-start(bf16[304,384]{1,0:T(8,128)(2,1)} %get-tuple-element.84), channel_id=1, source_target_pairs={{0,4},{1,5},{8,12},{9,13},{16,20},{17,21},{24,28},{25,29},{2,6},{3... | collective-permute-start | bytes 700424 | tf_op jit(solution)/shard_map/ppermute | solution.py:616
  38.6 3.3 %shard_map.52 = (bf16[288,384]{1,0:T(8,128)(2,1)}, bf16[288,384]{1,0:T(8,128)(2,1)}, bf16[288,384]{1,0:T(8,128)(2,1)}, bf16[288,384]{1,0:T(8,128)(2,1)}) custom-call(s32[1,1024]{1,0:T(1,128)} %get-tuple-element.98.target_ref, bf16[128,384]{1,0:T(8,128)(2,1)} %get-tuple-element.99.refs_0_, bf16[128,384]{1,0:T(8,128)(2,1)} %copy-done.44, ...), custom_call_target="tpu_custom_call" | custom-call | flops 805306368 | bytes 2359296 | tf_op jit(solution)/shard_map/pallas_call | solution.py:670
  42.6 3.5 %collective-permute-start.31 = (bf16[288,384]{1,0:T(8,128)(2,1)}, bf16[288,384]{1,0:T(8,128)(2,1)S(1)}, u32[]{:S(2)}, u32[]{:S(2)}) collective-permute-start(bf16[288,384]{1,0:T(8,128)(2,1)} %get-tuple-element.109), channel_id=1, source_target_pairs={{0,4},{1,5},{8,12},{9,13},{16,20},{17,21},{24,28},{25,29},{2,6},{3... | collective-permute-start | bytes 663560 | tf_op jit(solution)/shard_map/ppermute | solution.py:616
  46.7 2.8 %collective-permute-start.32 = (bf16[288,384]{1,0:T(8,128)(2,1)}, bf16[288,384]{1,0:T(8,128)(2,1)S(1)}, u32[]{:S(2)}, u32[]{:S(2)}) collective-permute-start(bf16[288,384]{1,0:T(8,128)(2,1)} %get-tuple-element.110), channel_id=1, source_target_pairs={{0,6},{1,7},{8,14},{9,15},{16,22},{17,23},{24,30},{25,31},{2,4},{3... | collective-permute-start | bytes 663560 | tf_op jit(solution)/shard_map/ppermute | solution.py:616
  49.5 5.3 %collective-permute-done.11.refs_2_ = bf16[304,384]{1,0:T(8,128)(2,1)S(1)} collective-permute-done((bf16[304,384]{1,0:T(8,128)(2,1)}, bf16[304,384]{1,0:T(8,128)(2,1)S(1)}, u32[]{:S(2)}, u32[]{:S(2)}) %collective-permute-start.11) | collective-permute-done | bytes 233504 | tf_op jit(solution)/shard_map/ppermute | solution.py:616
  55.6 4.0 %shard_map.50 = (bf16[128,384]{1,0:T(8,128)(2,1)}, bf16[128,384]{1,0:T(8,128)(2,1)}, bf16[128,384]{1,0:T(8,128)(2,1)}, bf16[128,384]{1,0:T(8,128)(2,1)}, bf16[12...) custom-call(bf16[304,384]{1,0:T(8,128)(2,1)} %get-tuple-element.82.r, ...), custom_call_target="tpu_custom_call" | custom-call | flops 805306368 | bytes 2359296 | tf_op jit(solution)/shard_map/pallas_call | solution.py:678
  59.6 2.9 %collective-permute-start.13 = (bf16[128,384]{1,0:T(8,128)(2,1)}, bf16[128,384]{1,0:T(8,128)(2,1)S(1)}, u32[]{:S(2)}, u32[]{:S(2)}) collective-permute-start(bf16[128,384]{1,0:T(8,128)(2,1)} %get-tuple-element.88), channel_id=1, source_target_pairs={{0,1},{1,0},{8,9},{9,8},{16,17},{17,16},{24,25},{25,24},{2,3},{3,2... | collective-permute-start | bytes 294920 | tf_op jit(solution)/shard_map/ppermute | solution.py:608
  62.7 11.3 %collective-permute-done.31.refs_2_ = bf16[288,384]{1,0:T(8,128)(2,1)S(1)} collective-permute-done((bf16[288,384]{1,0:T(8,128)(2,1)}, bf16[288,384]{1,0:T(8,128)(2,1)S(1)}, u32[]{:S(2)}, u32[]{:S(2)}) %collective-permute-start.31) | collective-permute-done | bytes 221216 | tf_op jit(solution)/shard_map/ppermute | solution.py:616
  74.0 2.4 %collective-permute-start.16 = (bf16[128,384]{1,0:T(8,128)(2,1)}, bf16[128,384]{1,0:T(8,128)(2,1)S(1)}, u32[]{:S(2)}, u32[]{:S(2)}) collective-permute-start(bf16[128,384]{1,0:T(8,128)(2,1)} %get-tuple-element.91), channel_id=1, source_target_pairs={{0,16},{1,17},{8,24},{9,25},{16,0},{17,1},{24,8},{25,9},{2,18},{3,... | collective-permute-start | bytes 294920 | tf_op jit(solution)/shard_map/ppermute | solution.py:608
  76.4 2.4 %collective-permute-start.20 = (bf16[256,384]{1,0:T(8,128)(2,1)}, bf16[256,384]{1,0:T(8,128)(2,1)S(1)}, u32[]{:S(2)}, u32[]{:S(2)}) collective-permute-start(bf16[256,384]{1,0:T(8,128)(2,1)} %get-tuple-element.95.refs_8_), channel_id=1, source_target_pairs={{0,1},{8,9},{16,17},{24,25},{2,3},{10,11},{18,19},{26,27},{4,5},{1... | collective-permute-start | bytes 589832 | tf_op jit(solution)/shard_map/ppermute | solution.py:625
  79.8 3.8 %collective-permute-start.19 = (bf16[128,384]{1,0:T(8,128)(2,1)}, bf16[128,384]{1,0:T(8,128)(2,1)S(1)}, u32[]{:S(2)}, u32[]{:S(2)}) collective-permute-start(bf16[128,384]{1,0:T(8,128)(2,1)} %get-tuple-element.94), channel_id=1, source_target_pairs={{0,25},{1,24},{8,17},{9,16},{16,9},{17,8},{24,1},{25,0},{2,27},{3,... | collective-permute-start | bytes 294920 | tf_op jit(solution)/shard_map/ppermute | solution.py:608
  83.6 3.9 %shard_map.53 = (bf16[128,384]{1,0:T(8,128)(2,1)}, bf16[128,384]{1,0:T(8,128)(2,1)}, bf16[128,384]{1,0:T(8,128)(2,1)}, bf16[128,384]{1,0:T(8,128)(2,1)}, bf16[12...) custom-call(s32[1,1536]{1,0:T(1,128)} %get-tuple-element.97.target_r, ...), custom_call_target="tpu_custom_call" | custom-call | flops 805306368 | bytes 2359296 | tf_op jit(solution)/shard_map/pallas_call | solution.py:691
  87.6 3.9 %collective-permute-start.40 = (bf16[256,384]{1,0:T(8,128)(2,1)}, bf16[256,384]{1,0:T(8,128)(2,1)S(1)}, u32[]{:S(2)}, u32[]{:S(2)}) collective-permute-start(bf16[256,384]{1,0:T(8,128)(2,1)} %get-tuple-element.119.refs_8_), channel_id=1, source_target_pairs={{0,1},{8,9},{16,17},{24,25},{2,3},{10,11},{18,19},{26,27},{4,5},{1... | collective-permute-start | bytes 589832 | tf_op jit(solution)/shard_map/ppermute | solution.py:625
  93.9 2.4 %collective-permute-start.36 = (bf16[128,384]{1,0:T(8,128)(2,1)}, bf16[128,384]{1,0:T(8,128)(2,1)S(1)}, u32[]{:S(2)}, u32[]{:S(2)}) collective-permute-start(bf16[128,384]{1,0:T(8,128)(2,1)} %get-tuple-element.115), channel_id=1, source_target_pairs={{0,16},{1,17},{8,24},{9,25},{16,0},{17,1},{24,8},{25,9},{2,18},{3,... | collective-permute-start | bytes 294920 | tf_op jit(solution)/shard_map/ppermute | solution.py:608
  99.8 6.2 %collective-permute-start.37 = (bf16[128,384]{1,0:T(8,128)(2,1)}, bf16[128,384]{1,0:T(8,128)(2,1)S(1)}, u32[]{:S(2)}, u32[]{:S(2)}) collective-permute-start(bf16[128,384]{1,0:T(8,128)(2,1)} %get-tuple-element.116), channel_id=1, source_target_pairs={{0,17},{1,16},{8,25},{9,24},{16,1},{17,0},{24,9},{25,8},{2,19},{3,... | collective-permute-start | bytes 294920 | tf_op jit(solution)/shard_map/ppermute | solution.py:608
  108.3 2.7 %shard_map.51 = (bf16[1024,384]{1,0:T(8,128)(2,1)}, bf16[1024,384]{1,0:T(8,128)(2,1)}) custom-call(bf16[128,384]{1,0:T(8,128)(2,1)} %get-tuple-element.87.refs_0_, bf16[128,384]{1,0:T(8,128)(2,1)} %copy-done.8, bf16[128,384]{1,0:T(8,128)(2,1)} %copy-done.9, bf16[128,384]{1,0:T(8,128)(2,1)} %copy-done.10, bf16[128,384]{1,0:T(8,128)(2,1)} %copy-done.11, ...), custom_call_target="tpu_custom_call" | custom-call | bytes 3145728 | tf_op jit(solution)/shard_map/pallas_call | solution.py:698
  110.9 5.9 %collective-permute-done.37.refs_5_ = bf16[128,384]{1,0:T(8,128)(2,1)S(1)} collective-permute-done((bf16[128,384]{1,0:T(8,128)(2,1)}, bf16[128,384]{1,0:T(8,128)(2,1)S(1)}, u32[]{:S(2)}, u32[]{:S(2)}) %collective-permute-start.37) | collective-permute-done | bytes 98336 | tf_op jit(solution)/shard_map/ppermute | solution.py:608
  116.9 3.3 %collective-permute-done.39.refs_7_ = bf16[128,384]{1,0:T(8,128)(2,1)S(1)} collective-permute-done((bf16[128,384]{1,0:T(8,128)(2,1)}, bf16[128,384]{1,0:T(8,128)(2,1)S(1)}, u32[]{:S(2)}, u32[]{:S(2)}) %collective-permute-start.39) | collective-permute-done | bytes 98336 | tf_op jit(solution)/shard_map/ppermute | solution.py:608
  121.0 2.7 %shard_map.54 = (bf16[1024,384]{1,0:T(8,128)(2,1)}, bf16[1024,384]{1,0:T(8,128)(2,1)}) custom-call(bf16[128,384]{1,0:T(8,128)(2,1)} %get-tuple-element.111.refs_0_, bf16[128,384]{1,0:T(8,128)(2,1)} %copy-done.14, bf16[128,384]{1,0:T(8,128)(2,1)} %copy-done.16, bf16[128,384]{1,0:T(8,128)(2,1)} %copy-done.17, bf16[128,384]{1,0:T(8,128)(2,1)} %copy-done.18, ...), custom_call_target="tpu_custom_call" | custom-call | bytes 3145728 | tf_op jit(solution)/shard_map/pallas_call | solution.py:698
  124.5 1.7 %collective-permute-done.44.refs_3_ = bf16[1024,384]{1,0:T(8,128)(2,1)S(1)} collective-permute-done((bf16[1024,384]{1,0:T(8,128)(2,1)}, bf16[1024,384]{1,0:T(8,128)(2,1)S(1)}, u32[]{:S(2)}, u32[]{:S(2)}) %collective-permute-start.44) | collective-permute-done | bytes 786464 | tf_op jit(solution)/shard_map/ppermute | solution.py:608
  126.2 2.0 %collective-permute-done.45.refs_6_ = bf16[1024,384]{1,0:T(8,128)(2,1)S(1)} collective-permute-done((bf16[1024,384]{1,0:T(8,128)(2,1)S(1)}, bf16[1024,384]{1,0:T(8,128)(2,1)S(1)}, u32[]{:S(2)}, u32[]{:S(2)}) %collective-permute-start.45) | collective-permute-done | bytes 786464 | tf_op jit(solution)/shard_map/ppermute | solution.py:608
  129.2 6.5 %shard_map.55 = f32[32,8,128]{2,1,0:T(8,128)} custom-call(s32[12]{0:T(128)S(1)} %copy-done.25, bf16[1024,384]{1,0:T(8,128)(2,1)} %get-tuple-element.96.refs_0_, bf16[1024,384]{1,0:T(8,128)(2,1)} %get-tuple-element.120.refs_1_, bf16[1024,384]{1,0:T(8,128)(2,1)} %collective-permute-done.43.refs_2_, bf16[1024,384]{1,0:T(8,128)(2,1)} %copy-done.29, ...), custom_call_target="tpu_custom_call" | custom-call | flops 4831838208 | bytes 6291456 | tf_op jit(solution)/shard_map/pallas_call | solution.py:709
  135.6 9.3 %all-to-all-start.3 = ((f32[32,8,128]{2,1,0:T(8,128)}), f32[32,8,128]{2,1,0:T(8,128)S(1)}, u32[]{:S(2)}, u32[]{:S(2)}) async-start(f32[32,8,128]{2,1,0:T(8,128)} %shard_map.55), calls=%async_computation.3 | async-start | bytes 262144 | tf_op jit(solution)/shard_map/all_to_all | solution.py:534
  146.9 5.8 %all-to-all-done.3 = f32[32,8,128]{2,1,0:T(8,128)S(1)} async-done(((f32[32,8,128]{2,1,0:T(8,128)}), f32[32,8,128]{2,1,0:T(8,128)S(1)}, u32[]{:S(2)}, u32[]{:S(2)}) %all-to-all-start.3) | async-done | bytes 131104 | tf_op jit(solution)/shard_map/all_to_all | solution.py:534
  153.3 1.8 %shard_map.56 = f32[1,1024]{1,0:T(1,128)S(1)} custom-call(s32[12]{0:T(128)S(1)} %copy-done.25, s32[1,1024]{1,0:T(1,128)S(1)} %bitcast.25, s32[1,1024]{1,0:T(1,128)S(1)} %bitcast.28, f32[256,128]{1,0:T(8,128)} %bitcast.20), custom_call_target="tpu_custom_call" | custom-call | bytes 16384 | tf_op jit(solution)/shard_map/pallas_call | solution.py:723
  (169 shorter events, 28.1 us)
Async XLA Ops:
  5.6 12.8 %collective-permute-start.3 = (bf16[144,384]{1,0:T(8,128)(2,1)}, bf16[144,384]{1,0:T(8,128)(2,1)S(1)}, u32[]{:S(2)}, u32[]{:S(2)}) collective-permute-start(bf16[144,384]{1,0:T(8,128)(2,1)} %get-tuple-element.75), channel_id=1, source_target_pairs={{0,1},{1,0},{8,9},{9,8},{16,17},{17,16},{24,25},{25,24},{2,3},{3,2... | collective-permute-start | bytes 331784 | tf_op jit(solution)/shard_map/ppermute | solution.py:608
  8.6 9.7 %collective-permute-start.4 = (bf16[144,384]{1,0:T(8,128)(2,1)}, bf16[144,384]{1,0:T(8,128)(2,1)S(1)}, u32[]{:S(2)}, u32[]{:S(2)}) collective-permute-start(bf16[144,384]{1,0:T(8,128)(2,1)} %get-tuple-element.76), channel_id=1, source_target_pairs={{0,8},{1,9},{8,0},{9,1},{16,24},{17,25},{24,16},{25,17},{2,10},{3,... | collective-permute-start | bytes 331784 | tf_op jit(solution)/shard_map/ppermute | solution.py:608
  9.1 10.5 %collective-permute-start.5 = (bf16[144,384]{1,0:T(8,128)(2,1)}, bf16[144,384]{1,0:T(8,128)(2,1)S(1)}, u32[]{:S(2)}, u32[]{:S(2)}) collective-permute-start(bf16[144,384]{1,0:T(8,128)(2,1)} %get-tuple-element.77), channel_id=1, source_target_pairs={{0,9},{1,8},{8,1},{9,0},{16,25},{17,24},{24,17},{25,16},{2,11},{3,... | collective-permute-start | bytes 331784 | tf_op jit(solution)/shard_map/ppermute | solution.py:608
  16.0 8.0 %collective-permute-start.7 = (bf16[144,384]{1,0:T(8,128)(2,1)}, bf16[144,384]{1,0:T(8,128)(2,1)S(1)}, u32[]{:S(2)}, u32[]{:S(2)}) collective-permute-start(bf16[144,384]{1,0:T(8,128)(2,1)} %get-tuple-element.79), channel_id=1, source_target_pairs={{0,17},{1,16},{8,25},{9,24},{16,1},{17,0},{24,9},{25,8},{2,19},{3,... | collective-permute-start | bytes 331784 | tf_op jit(solution)/shard_map/ppermute | solution.py:608
  19.7 13.7 %collective-permute-start.25 = (bf16[128,384]{1,0:T(8,128)(2,1)}, bf16[128,384]{1,0:T(8,128)(2,1)S(1)}, u32[]{:S(2)}, u32[]{:S(2)}) collective-permute-start(bf16[128,384]{1,0:T(8,128)(2,1)} %get-tuple-element.102), channel_id=1, source_target_pairs={{0,9},{1,8},{8,1},{9,0},{16,25},{17,24},{24,17},{25,16},{2,11},{3,... | collective-permute-start | bytes 294920 | tf_op jit(solution)/shard_map/ppermute | solution.py:608
  21.2 13.9 %collective-permute-start.26 = (bf16[128,384]{1,0:T(8,128)(2,1)}, bf16[128,384]{1,0:T(8,128)(2,1)S(1)}, u32[]{:S(2)}, u32[]{:S(2)}) collective-permute-start(bf16[128,384]{1,0:T(8,128)(2,1)} %get-tuple-element.103), channel_id=1, source_target_pairs={{0,16},{1,17},{8,24},{9,25},{16,0},{17,1},{24,8},{25,9},{2,18},{3,... | collective-permute-start | bytes 294920 | tf_op jit(solution)/shard_map/ppermute | solution.py:608
  24.0 13.6 %collective-permute-start.27 = (bf16[128,384]{1,0:T(8,128)(2,1)}, bf16[128,384]{1,0:T(8,128)(2,1)S(1)}, u32[]{:S(2)}, u32[]{:S(2)}) collective-permute-start(bf16[128,384]{1,0:T(8,128)(2,1)} %get-tuple-element.104), channel_id=1, source_target_pairs={{0,17},{1,16},{8,25},{9,24},{16,1},{17,0},{24,9},{25,8},{2,19},{3,... | collective-permute-start | bytes 294920 | tf_op jit(solution)/shard_map/ppermute | solution.py:608
  24.5 13.4 %collective-permute-start.28 = (bf16[128,384]{1,0:T(8,128)(2,1)}, bf16[128,384]{1,0:T(8,128)(2,1)S(1)}, u32[]{:S(2)}, u32[]{:S(2)}) collective-permute-start(bf16[128,384]{1,0:T(8,128)(2,1)} %get-tuple-element.105), channel_id=1, source_target_pairs={{0,24},{1,25},{8,16},{9,17},{16,8},{17,9},{24,0},{25,1},{2,26},{3,... | collective-permute-start | bytes 294920 | tf_op jit(solution)/shard_map/ppermute | solution.py:608
  26.0 11.9 %collective-permute-start.29 = (bf16[128,384]{1,0:T(8,128)(2,1)}, bf16[128,384]{1,0:T(8,128)(2,1)S(1)}, u32[]{:S(2)}, u32[]{:S(2)}) collective-permute-start(bf16[128,384]{1,0:T(8,128)(2,1)} %get-tuple-element.106), channel_id=1, source_target_pairs={{0,25},{1,24},{8,17},{9,16},{16,9},{17,8},{24,1},{25,0},{2,27},{3,... | collective-permute-start | bytes 294920 | tf_op jit(solution)/shard_map/ppermute | solution.py:608
  33.4 13.3 %collective-permute-start.10 = (bf16[304,384]{1,0:T(8,128)(2,1)}, bf16[304,384]{1,0:T(8,128)(2,1)S(1)}, u32[]{:S(2)}, u32[]{:S(2)}) collective-permute-start(bf16[304,384]{1,0:T(8,128)(2,1)} %get-tuple-element.83), channel_id=1, source_target_pairs={{0,2},{1,3},{8,10},{9,11},{16,18},{17,19},{24,26},{25,27},{2,0},{3... | collective-permute-start | bytes 700424 | tf_op jit(solution)/shard_map/ppermute | solution.py:616
  35.1 19.7 %collective-permute-start.11 = (bf16[304,384]{1,0:T(8,128)(2,1)}, bf16[304,384]{1,0:T(8,128)(2,1)S(1)}, u32[]{:S(2)}, u32[]{:S(2)}) collective-permute-start(bf16[304,384]{1,0:T(8,128)(2,1)} %get-tuple-element.84), channel_id=1, source_target_pairs={{0,4},{1,5},{8,12},{9,13},{16,20},{17,21},{24,28},{25,29},{2,6},{3... | collective-permute-start | bytes 700424 | tf_op jit(solution)/shard_map/ppermute | solution.py:616
  37.6 17.2 %collective-permute-start.12 = (bf16[304,384]{1,0:T(8,128)(2,1)}, bf16[304,384]{1,0:T(8,128)(2,1)S(1)}, u32[]{:S(2)}, u32[]{:S(2)}) collective-permute-start(bf16[304,384]{1,0:T(8,128)(2,1)} %get-tuple-element.85), channel_id=1, source_target_pairs={{0,6},{1,7},{8,14},{9,15},{16,22},{17,23},{24,30},{25,31},{2,4},{3... | collective-permute-start | bytes 700424 | tf_op jit(solution)/shard_map/ppermute | solution.py:616
  41.9 20.6 %collective-permute-start.30 = (bf16[288,384]{1,0:T(8,128)(2,1)}, bf16[288,384]{1,0:T(8,128)(2,1)S(1)}, u32[]{:S(2)}, u32[]{:S(2)}) collective-permute-start(bf16[288,384]{1,0:T(8,128)(2,1)} %get-tuple-element.108), channel_id=1, source_target_pairs={{0,2},{1,3},{8,10},{9,11},{16,18},{17,19},{24,26},{25,27},{2,0},{3... | collective-permute-start | bytes 663560 | tf_op jit(solution)/shard_map/ppermute | solution.py:616
  42.6 31.5 %collective-permute-start.31 = (bf16[288,384]{1,0:T(8,128)(2,1)}, bf16[288,384]{1,0:T(8,128)(2,1)S(1)}, u32[]{:S(2)}, u32[]{:S(2)}) collective-permute-start(bf16[288,384]{1,0:T(8,128)(2,1)} %get-tuple-element.109), channel_id=1, source_target_pairs={{0,4},{1,5},{8,12},{9,13},{16,20},{17,21},{24,28},{25,29},{2,6},{3... | collective-permute-start | bytes 663560 | tf_op jit(solution)/shard_map/ppermute | solution.py:616
  46.7 29.7 %collective-permute-start.32 = (bf16[288,384]{1,0:T(8,128)(2,1)}, bf16[288,384]{1,0:T(8,128)(2,1)S(1)}, u32[]{:S(2)}, u32[]{:S(2)}) collective-permute-start(bf16[288,384]{1,0:T(8,128)(2,1)} %get-tuple-element.110), channel_id=1, source_target_pairs={{0,6},{1,7},{8,14},{9,15},{16,22},{17,23},{24,30},{25,31},{2,4},{3... | collective-permute-start | bytes 663560 | tf_op jit(solution)/shard_map/ppermute | solution.py:616
  59.6 19.2 %collective-permute-start.13 = (bf16[128,384]{1,0:T(8,128)(2,1)}, bf16[128,384]{1,0:T(8,128)(2,1)S(1)}, u32[]{:S(2)}, u32[]{:S(2)}) collective-permute-start(bf16[128,384]{1,0:T(8,128)(2,1)} %get-tuple-element.88), channel_id=1, source_target_pairs={{0,1},{1,0},{8,9},{9,8},{16,17},{17,16},{24,25},{25,24},{2,3},{3,2... | collective-permute-start | bytes 294920 | tf_op jit(solution)/shard_map/ppermute | solution.py:608
  62.5 17.3 %collective-permute-start.14 = (bf16[128,384]{1,0:T(8,128)(2,1)}, bf16[128,384]{1,0:T(8,128)(2,1)S(1)}, u32[]{:S(2)}, u32[]{:S(2)}) collective-permute-start(bf16[128,384]{1,0:T(8,128)(2,1)} %get-tuple-element.89), channel_id=1, source_target_pairs={{0,8},{1,9},{8,0},{9,1},{16,24},{17,25},{24,16},{25,17},{2,10},{3,... | collective-permute-start | bytes 294920 | tf_op jit(solution)/shard_map/ppermute | solution.py:608
  62.5 17.3 %collective-permute-start.15 = (bf16[128,384]{1,0:T(8,128)(2,1)}, bf16[128,384]{1,0:T(8,128)(2,1)S(1)}, u32[]{:S(2)}, u32[]{:S(2)}) collective-permute-start(bf16[128,384]{1,0:T(8,128)(2,1)} %get-tuple-element.90), channel_id=1, source_target_pairs={{0,9},{1,8},{8,1},{9,0},{16,25},{17,24},{24,17},{25,16},{2,11},{3,... | collective-permute-start | bytes 294920 | tf_op jit(solution)/shard_map/ppermute | solution.py:608
  74.0 13.4 %collective-permute-start.16 = (bf16[128,384]{1,0:T(8,128)(2,1)}, bf16[128,384]{1,0:T(8,128)(2,1)S(1)}, u32[]{:S(2)}, u32[]{:S(2)}) collective-permute-start(bf16[128,384]{1,0:T(8,128)(2,1)} %get-tuple-element.91), channel_id=1, source_target_pairs={{0,16},{1,17},{8,24},{9,25},{16,0},{17,1},{24,8},{25,9},{2,18},{3,... | collective-permute-start | bytes 294920 | tf_op jit(solution)/shard_map/ppermute | solution.py:608
  76.4 15.9 %collective-permute-start.20 = (bf16[256,384]{1,0:T(8,128)(2,1)}, bf16[256,384]{1,0:T(8,128)(2,1)S(1)}, u32[]{:S(2)}, u32[]{:S(2)}) collective-permute-start(bf16[256,384]{1,0:T(8,128)(2,1)} %get-tuple-element.95.refs_8_), channel_id=1, source_target_pairs={{0,1},{8,9},{16,17},{24,25},{2,3},{10,11},{18,19},{26,27},{4,5},{1... | collective-permute-start | bytes 589832 | tf_op jit(solution)/shard_map/ppermute | solution.py:625
  78.9 8.7 %collective-permute-start.17 = (bf16[128,384]{1,0:T(8,128)(2,1)}, bf16[128,384]{1,0:T(8,128)(2,1)S(1)}, u32[]{:S(2)}, u32[]{:S(2)}) collective-permute-start(bf16[128,384]{1,0:T(8,128)(2,1)} %get-tuple-element.92), channel_id=1, source_target_pairs={{0,17},{1,16},{8,25},{9,24},{16,1},{17,0},{24,9},{25,8},{2,19},{3,... | collective-permute-start | bytes 294920 | tf_op jit(solution)/shard_map/ppermute | solution.py:608
  79.8 11.7 %collective-permute-start.18 = (bf16[128,384]{1,0:T(8,128)(2,1)}, bf16[128,384]{1,0:T(8,128)(2,1)S(1)}, u32[]{:S(2)}, u32[]{:S(2)}) collective-permute-start(bf16[128,384]{1,0:T(8,128)(2,1)} %get-tuple-element.93), channel_id=1, source_target_pairs={{0,24},{1,25},{8,16},{9,17},{16,8},{17,9},{24,0},{25,1},{2,26},{3,... | collective-permute-start | bytes 294920 | tf_op jit(solution)/shard_map/ppermute | solution.py:608
  79.8 11.8 %collective-permute-start.19 = (bf16[128,384]{1,0:T(8,128)(2,1)}, bf16[128,384]{1,0:T(8,128)(2,1)S(1)}, u32[]{:S(2)}, u32[]{:S(2)}) collective-permute-start(bf16[128,384]{1,0:T(8,128)(2,1)} %get-tuple-element.94), channel_id=1, source_target_pairs={{0,25},{1,24},{8,17},{9,16},{16,9},{17,8},{24,1},{25,0},{2,27},{3,... | collective-permute-start | bytes 294920 | tf_op jit(solution)/shard_map/ppermute | solution.py:608
  87.6 11.1 %collective-permute-start.40 = (bf16[256,384]{1,0:T(8,128)(2,1)}, bf16[256,384]{1,0:T(8,128)(2,1)S(1)}, u32[]{:S(2)}, u32[]{:S(2)}) collective-permute-start(bf16[256,384]{1,0:T(8,128)(2,1)} %get-tuple-element.119.refs_8_), channel_id=1, source_target_pairs={{0,1},{8,9},{16,17},{24,25},{2,3},{10,11},{18,19},{26,27},{4,5},{1... | collective-permute-start | bytes 589832 | tf_op jit(solution)/shard_map/ppermute | solution.py:625
  91.6 14.4 %collective-permute-start.21 = (bf16[256,384]{1,0:T(8,128)(2,1)S(1)}, bf16[256,384]{1,0:T(8,128)(2,1)S(1)}, u32[]{:S(2)}, u32[]{:S(2)}) collective-permute-start(bf16[256,384]{1,0:T(8,128)(2,1)S(1)} %copy-done.1), channel_id=1, source_target_pairs={{17,1},{25,9},{19,3},{27,11},{21,5},{29,13},{23,7},{31,15}} | collective-permute-start | bytes 589832 | tf_op jit(solution)/shard_map/ppermute | solution.py:625
  92.3 14.6 %collective-permute-start.22 = (bf16[256,384]{1,0:T(8,128)(2,1)S(1)}, bf16[256,384]{1,0:T(8,128)(2,1)S(1)}, u32[]{:S(2)}, u32[]{:S(2)}) collective-permute-start(bf16[256,384]{1,0:T(8,128)(2,1)S(1)} %collective-permute-done.20.refs_9_), channel_id=1, source_target_pairs={{17,1},{25,9},{19,3},{27,11},{21,5},{29,13},{23,7},{31,15}} | collective-permute-start | bytes 589832 | tf_op jit(solution)/shard_map/ppermute | solution.py:625
  98.0 22.3 %collective-permute-start.41 = (bf16[256,384]{1,0:T(8,128)(2,1)}, bf16[256,384]{1,0:T(8,128)(2,1)S(1)}, u32[]{:S(2)}, u32[]{:S(2)}) collective-permute-start(bf16[256,384]{1,0:T(8,128)(2,1)} %get-tuple-element.119.refs_8_), channel_id=1, source_target_pairs={{17,1},{25,9},{19,3},{27,11},{21,5},{29,13},{23,7},{31,15}} | collective-permute-start | bytes 589832 | tf_op jit(solution)/shard_map/ppermute | solution.py:625
  98.6 21.6 %collective-permute-start.42 = (bf16[256,384]{1,0:T(8,128)(2,1)S(1)}, bf16[256,384]{1,0:T(8,128)(2,1)S(1)}, u32[]{:S(2)}, u32[]{:S(2)}) collective-permute-start(bf16[256,384]{1,0:T(8,128)(2,1)S(1)} %collective-permute-done.40.refs_9_), channel_id=1, source_target_pairs={{17,1},{25,9},{19,3},{27,11},{21,5},{29,13},{23,7},{31,15}} | collective-permute-start | bytes 589832 | tf_op jit(solution)/shard_map/ppermute | solution.py:625
  99.8 17.1 %collective-permute-start.37 = (bf16[128,384]{1,0:T(8,128)(2,1)}, bf16[128,384]{1,0:T(8,128)(2,1)S(1)}, u32[]{:S(2)}, u32[]{:S(2)}) collective-permute-start(bf16[128,384]{1,0:T(8,128)(2,1)} %get-tuple-element.116), channel_id=1, source_target_pairs={{0,17},{1,16},{8,25},{9,24},{16,1},{17,0},{24,9},{25,8},{2,19},{3,... | collective-permute-start | bytes 294920 | tf_op jit(solution)/shard_map/ppermute | solution.py:608
  106.0 10.9 %collective-permute-start.38 = (bf16[128,384]{1,0:T(8,128)(2,1)}, bf16[128,384]{1,0:T(8,128)(2,1)S(1)}, u32[]{:S(2)}, u32[]{:S(2)}) collective-permute-start(bf16[128,384]{1,0:T(8,128)(2,1)} %get-tuple-element.117), channel_id=1, source_target_pairs={{0,24},{1,25},{8,16},{9,17},{16,8},{17,9},{24,0},{25,1},{2,26},{3,... | collective-permute-start | bytes 294920 | tf_op jit(solution)/shard_map/ppermute | solution.py:608
  107.0 13.3 %collective-permute-start.39 = (bf16[128,384]{1,0:T(8,128)(2,1)}, bf16[128,384]{1,0:T(8,128)(2,1)S(1)}, u32[]{:S(2)}, u32[]{:S(2)}) collective-permute-start(bf16[128,384]{1,0:T(8,128)(2,1)} %get-tuple-element.118), channel_id=1, source_target_pairs={{0,25},{1,24},{8,17},{9,16},{16,9},{17,8},{24,1},{25,0},{2,27},{3,... | collective-permute-start | bytes 294920 | tf_op jit(solution)/shard_map/ppermute | solution.py:608
  135.6 17.0 %all-to-all-start.3 = ((f32[32,8,128]{2,1,0:T(8,128)}), f32[32,8,128]{2,1,0:T(8,128)S(1)}, u32[]{:S(2)}, u32[]{:S(2)}) async-start(f32[32,8,128]{2,1,0:T(8,128)} %shard_map.55), calls=%async_computation.3 | async-start | bytes 262144 | tf_op jit(solution)/shard_map/all_to_all | solution.py:534
  (63 other events, 689.6 us)

commit v3 on v2

--- a/solution.py
+++ b/solution.py
@@ -11,7 +11,7 @@
 AXES = ("ingest", "run")
 TILE = 256
 CHUNKS = 2
-MEMORY = 60 * 1024 * 1024
+MIB = 1024 * 1024
 
 
 class Plan:
@@ -437,7 +437,7 @@
 
 
 def wide_best(keys, queries_ref, best_ref):
-    @pl.loop(0, keys[0].shape[0] // TILE)
+    @pl.loop(0, keys[0].shape[0] // TILE, unroll=True)
     def _(tile):
         here = pl.ds(pl.multiple_of(tile * TILE, TILE), TILE)
         block = jnp.concatenate([part[here, :] for part in keys], axis=1)
@@ -470,7 +470,7 @@
     best_ref[...] = jnp.full(best_ref.shape, -1.0, jnp.float32)
     query = slots(lax.broadcasted_iota(jnp.int32, (1, plan.rows), 1))
 
-    @pl.loop(0, plan.rows // TILE)
+    @pl.loop(0, plan.rows // TILE, unroll=True)
     def _(tile):
         key = slots(lax.broadcasted_iota(jnp.int32, (TILE, 1), 0) + tile * TILE)
         block = queries_ref[pl.ds(pl.multiple_of(tile * TILE, TILE), TILE), :]
@@ -518,14 +518,14 @@
 VMEM = pl.BlockSpec(memory_space=pltpu.VMEM)
 
 
-def call(kernel, plan, shapes, specs, scratch=(), flops=0, moved=0):
+def call(kernel, plan, shapes, specs, scratch=(), flops=0, moved=0, memory=32):
     return pl.pallas_call(
         functools.partial(kernel, plan),
         out_shape=shapes,
         in_specs=specs,
         out_specs=[VMEM] * len(shapes),
         scratch_shapes=scratch,
-        compiler_params=pltpu.CompilerParams(vmem_limit_bytes=MEMORY),
+        compiler_params=pltpu.CompilerParams(vmem_limit_bytes=memory * MIB),
         cost_estimate=pl.CostEstimate(flops=flops, bytes_accessed=moved, transcendentals=0),
     )
 
@@ -648,7 +648,9 @@
     owns, mates, behinds, fars = [], [], [], []
     table = targets = full = None
     for chunk, f in enumerate(plan.chunks):
-        spec = dict(flops=2 * rows * rows * f, moved=3 * rows * f * 2)
+        if chunk:
+            spread, routed = lax.optimization_barrier((spread, routed))
+        spec = dict(flops=2 * rows * rows * f, moved=3 * rows * f * 2, memory=12)
         parts = by_change(swap_lanes(spread[chunk * plan.lanes : (chunk + 1) * plan.lanes]))
         rooms = [wide((plan.room + (0 if chunk else 16), f), half) for _ in layers]
         inputs = pltpu.VMEM((rows, f), half)
@@ -701,6 +703,7 @@
             [wide((rows, f), half)] * 2,
             [VMEM] * (plan.lanes + 4),
             moved=4 * rows * f * 2,
+            memory=8,
         )(*parts, ahead, near, side, corner)
         owns.append(own)
         behinds.append(behind)
@@ -726,6 +729,7 @@
         [wide((1, rows), jnp.float32)],
         [SMEM, VMEM, VMEM, VMEM],
         moved=4 * rows * 4,
+        memory=8,
     )(run_len, clusters, ranks, returned)
     return best, full[0, 0]
 

time: 156 us -> 140 us (0.90)
  Pallas kernels: 35 us -> 17.4 us
  waiting for transfers between devices: 44.4 us -> 54.5 us
  local copies, waits for them, and re-layouts: 5.69 us -> 1.12 us
  starting transfers between devices: 69.3 us -> 65.6 us
    pallas_call x2, Pallas kernels: 5.37 us -> 0.27 us  [staged(): call(join_kernel, plan, [wide((rows, f), half)] * 2, [VMEM] * (plan.lanes...]
    ppermute x32, starting transfers between devices: 39.4 us -> 34.6 us  [along_lanes(): return lax.ppermute(block, AXES, pairs)]
    ppermute x6, waiting for transfers between devices: 17.3 us -> 22 us  [along_layers(): return lax.ppermute(block, AXES, pairs)]
    ppermute x32, waiting for transfers between devices: 21.3 us -> 25.8 us  [along_lanes(): return lax.ppermute(block, AXES, pairs)]
    unnamed x100 -> x10, local copies, waits for them, and re-layouts: 4.4 us -> 0.6 us
    pallas_call x1, Pallas kernels: 6.45 us -> 3.1 us  [staged(): call(staged_best_kernel, plan, [wide((plan.devices, plan.lanes, 128), jnp...]
    pallas_call x1, Pallas kernels: 3.85 us -> 1.85 us  [staged(): call(deliver_more_kernel, plan, shapes, [VMEM] * (1 + plan.layers), scrat...]
    pallas_call x1, Pallas kernels: 4 us -> 2.02 us  [staged(): call(deliver_kernel, plan, [*shapes, wide((1, plan.layers * plan.stride),...]
  transfers between devices with their start and end apart: 45 -> 45, of which waited for: 13 -> 15; matrix products, arithmetic and copies ran while one was open for 1% -> 0% of each run, Pallas kernels for 14% -> 4%
where the time goes in v3:
time: 140 us; the launch traced here: 139 us
  starting transfers between devices  65.6 us (47%)
  waiting for transfers between devices  54.5 us (39%)
  Pallas kernels  17.4 us (12%)
    ppermute x32, starting transfers between devices, along_lanes(): return lax.ppermute(block, AXES, pairs)  34.6 us
    ppermute x32, waiting for transfers between devices, along_lanes(): return lax.ppermute(block, AXES, pairs)  25.8 us
    ppermute x6, waiting for transfers between devices, along_layers(): return lax.ppermute(block, AXES, pairs)  22 us
    ppermute x6, starting transfers between devices, along_layers(): return lax.ppermute(block, AXES, pairs)  12 us
    ppermute x6, starting transfers between devices, chip_to_chip(): return lax.ppermute(block, AXES, pairs)  10.2 us
    all_to_all x1, starting transfers between devices, exchange(): return lax.all_to_all(block, AXES, split_axis=0, concat_axis=0, tiled=True)  8.77 us
    all_to_all x1, waiting for transfers between devices, exchange(): return lax.all_to_all(block, AXES, split_axis=0, concat_axis=0, tiled=True)  6.57 us
    pallas_call x1, Pallas kernels, staged(): call(spread_kernel, plan, [wide((size, f), half) for size, f in zip(sizes...  4.66 us
  transfers between devices with their start and end apart: 45, of which 15 were waited for; matrix products, arithmetic and copies ran while one was open for 0% of the time, Pallas kernels for 4%

profile of v3, /device:TPU:0, one launch (start us, length us, event | category | flops | bytes accessed | tf_op | source)
XLA Modules:
  0.0 139.5 jit_solution(6848097269566908781)
XLA Ops:
  0.0 4.7 %shard_map.48 = (bf16[144,384]{1,0:T(8,128)(2,1)S(1)}, bf16[144,384]{1,0:T(8,128)(2,1)S(1)}, bf16[144,384]{1,0:T(8,128)(2,1)S(1)}, bf16[144,384]{1,0:T(8,128)(2,...) custom-call(s32[12]{0:T(128)} %run_len_ref.5, ...), custom_call_target="tpu_custom_call" | custom-call | flops 1610612736 | bytes 4718592 | tf_op jit(solution)/shard_map/pallas_call | solution.py:639
  4.7 3.0 %collective-permute-start.3 = (bf16[144,384]{1,0:T(8,128)(2,1)S(1)}, bf16[144,384]{1,0:T(8,128)(2,1)S(1)}, u32[]{:S(2)}, u32[]{:S(2)}) collective-permute-start(bf16[144,384]{1,0:T(8,128)(2,1)S(1)} %get-tuple-element.83), channel_id=1, source_target_pairs={{0,1},{1,0},{8,9},{9,8},{16,17},{17,16},{24,25},{25,24},{2,3},{3,2... | collective-permute-start | bytes 331784 | tf_op jit(solution)/shard_map/ppermute | solution.py:608
  7.9 1.9 %collective-permute-start.6 = (bf16[144,384]{1,0:T(8,128)(2,1)S(1)}, bf16[144,384]{1,0:T(8,128)(2,1)S(1)}, u32[]{:S(2)}, u32[]{:S(2)}) collective-permute-start(bf16[144,384]{1,0:T(8,128)(2,1)S(1)} %get-tuple-element.86), channel_id=1, source_target_pairs={{0,16},{1,17},{8,24},{9,25},{16,0},{17,1},{24,8},{25,9},{2,18},{3,... | collective-permute-start | bytes 331784 | tf_op jit(solution)/shard_map/ppermute | solution.py:608
  11.8 3.0 %collective-permute-start.9 = (bf16[144,384]{1,0:T(8,128)(2,1)S(1)}, bf16[144,384]{1,0:T(8,128)(2,1)S(1)}, u32[]{:S(2)}, u32[]{:S(2)}) collective-permute-start(bf16[144,384]{1,0:T(8,128)(2,1)S(1)} %get-tuple-element.89), channel_id=1, source_target_pairs={{0,25},{1,24},{8,17},{9,16},{16,9},{17,8},{24,1},{25,0},{2,27},{3,... | collective-permute-start | bytes 331784 | tf_op jit(solution)/shard_map/ppermute | solution.py:608
  14.8 2.2 %collective-permute-done.7.refs_5_ = bf16[144,384]{1,0:T(8,128)(2,1)S(1)} collective-permute-done((bf16[144,384]{1,0:T(8,128)(2,1)S(1)}, bf16[144,384]{1,0:T(8,128)(2,1)S(1)}, u32[]{:S(2)}, u32[]{:S(2)}) %collective-permute-start.7) | collective-permute-done | bytes 110624 | tf_op jit(solution)/shard_map/ppermute | solution.py:608
  18.0 2.9 %collective-permute-done.9.refs_7_ = bf16[144,384]{1,0:T(8,128)(2,1)S(1)} collective-permute-done((bf16[144,384]{1,0:T(8,128)(2,1)S(1)}, bf16[144,384]{1,0:T(8,128)(2,1)S(1)}, u32[]{:S(2)}, u32[]{:S(2)}) %collective-permute-start.9) | collective-permute-done | bytes 110624 | tf_op jit(solution)/shard_map/ppermute | solution.py:608
  20.9 2.7 %shard_map.49 = (bf16[304,384]{1,0:T(8,128)(2,1)S(1)}, bf16[304,384]{1,0:T(8,128)(2,1)S(1)}, bf16[304,384]{1,0:T(8,128)(2,1)S(1)}, bf16[304,384]{1,0:T(8,128)(2,1)S(1)}, s32[1,1024]{1,0:T(1,128)S(1)}) custom-call(bf16[144,384]{1,0:T(8,128)(2,1)S(1)} %get-tuple-element.82.refs_0_, bf16[144,384]{1,0:T(8,128)(2,1)S(1)} %collective-permute-done.3.refs_1_, ...), custom_call_target="tpu_custom_call" | custom-call | flops 805306368 | bytes 2359296 | tf_op jit(solution)/shard_map/pallas_call | solution.py:658
  24.0 1.7 %collective-permute-start.25 = (bf16[128,384]{1,0:T(8,128)(2,1)S(1)}, bf16[128,384]{1,0:T(8,128)(2,1)S(1)}, u32[]{:S(2)}, u32[]{:S(2)}) collective-permute-start(bf16[128,384]{1,0:T(8,128)(2,1)S(1)} %get-tuple-element.118), channel_id=1, source_target_pairs={{0,9},{1,8},{8,1},{9,0},{16,25},{17,24},{24,17},{25,16},{2,11},{3,... | collective-permute-start | bytes 294920 | tf_op jit(solution)/shard_map/ppermute | solution.py:608
  27.2 2.0 %collective-permute-done.23.refs_1_ = bf16[128,384]{1,0:T(8,128)(2,1)S(1)} collective-permute-done((bf16[128,384]{1,0:T(8,128)(2,1)S(1)}, bf16[128,384]{1,0:T(8,128)(2,1)S(1)}, u32[]{:S(2)}, u32[]{:S(2)}) %collective-permute-start.23) | collective-permute-done | bytes 98336 | tf_op jit(solution)/shard_map/ppermute | solution.py:608
  32.0 2.6 %collective-permute-start.11 = (bf16[304,384]{1,0:T(8,128)(2,1)S(1)}, bf16[304,384]{1,0:T(8,128)(2,1)S(1)}, u32[]{:S(2)}, u32[]{:S(2)}) collective-permute-start(bf16[304,384]{1,0:T(8,128)(2,1)S(1)} %get-tuple-element.92), channel_id=1, source_target_pairs={{0,4},{1,5},{8,12},{9,13},{16,20},{17,21},{24,28},{25,29},{2,6},{3... | collective-permute-start | bytes 700424 | tf_op jit(solution)/shard_map/ppermute | solution.py:616
  34.7 2.7 %collective-permute-start.12 = (bf16[304,384]{1,0:T(8,128)(2,1)S(1)}, bf16[304,384]{1,0:T(8,128)(2,1)S(1)}, u32[]{:S(2)}, u32[]{:S(2)}) collective-permute-start(bf16[304,384]{1,0:T(8,128)(2,1)S(1)} %get-tuple-element.93), channel_id=1, source_target_pairs={{0,6},{1,7},{8,14},{9,15},{16,22},{17,23},{24,30},{25,31},{2,4},{3... | collective-permute-start | bytes 700424 | tf_op jit(solution)/shard_map/ppermute | solution.py:616
  39.0 2.6 %collective-permute-start.31 = (bf16[288,384]{1,0:T(8,128)(2,1)S(1)}, bf16[288,384]{1,0:T(8,128)(2,1)S(1)}, u32[]{:S(2)}, u32[]{:S(2)}) collective-permute-start(bf16[288,384]{1,0:T(8,128)(2,1)S(1)} %get-tuple-element.125), channel_id=1, source_target_pairs={{0,4},{1,5},{8,12},{9,13},{16,20},{17,21},{24,28},{25,29},{2,6},{3... | collective-permute-start | bytes 663560 | tf_op jit(solution)/shard_map/ppermute | solution.py:616
  41.6 1.6 %collective-permute-done.10.refs_1_ = bf16[304,384]{1,0:T(8,128)(2,1)S(1)} collective-permute-done((bf16[304,384]{1,0:T(8,128)(2,1)S(1)}, bf16[304,384]{1,0:T(8,128)(2,1)S(1)}, u32[]{:S(2)}, u32[]{:S(2)}) %collective-permute-start.10) | collective-permute-done | bytes 233504 | tf_op jit(solution)/shard_map/ppermute | solution.py:616
  43.2 2.3 %collective-permute-start.32 = (bf16[288,384]{1,0:T(8,128)(2,1)S(1)}, bf16[288,384]{1,0:T(8,128)(2,1)S(1)}, u32[]{:S(2)}, u32[]{:S(2)}) collective-permute-start(bf16[288,384]{1,0:T(8,128)(2,1)S(1)} %get-tuple-element.126), channel_id=1, source_target_pairs={{0,6},{1,7},{8,14},{9,15},{16,22},{17,23},{24,30},{25,31},{2,4},{3... | collective-permute-start | bytes 663560 | tf_op jit(solution)/shard_map/ppermute | solution.py:616
  45.5 5.7 %collective-permute-done.11.refs_2_ = bf16[304,384]{1,0:T(8,128)(2,1)S(1)} collective-permute-done((bf16[304,384]{1,0:T(8,128)(2,1)S(1)}, bf16[304,384]{1,0:T(8,128)(2,1)S(1)}, u32[]{:S(2)}, u32[]{:S(2)}) %collective-permute-start.11) | collective-permute-done | bytes 233504 | tf_op jit(solution)/shard_map/ppermute | solution.py:616
  51.2 2.0 %shard_map.50 = (bf16[128,384]{1,0:T(8,128)(2,1)S(1)}, bf16[128,384]{1,0:T(8,128)(2,1)S(1)}, bf16[128,384]{1,0:T(8,128)(2,1)S(1)}, bf16[128,384]{1,0:T(8,128)(2,...) custom-call(bf16[304,384]{1,0:T(8,128)(2,1)S(1)} %get-tuple-element., ...), custom_call_target="tpu_custom_call" | custom-call | flops 805306368 | bytes 2359296 | tf_op jit(solution)/shard_map/pallas_call | solution.py:680
  53.3 2.4 %collective-permute-start.13 = (bf16[128,384]{1,0:T(8,128)(2,1)S(1)}, bf16[128,384]{1,0:T(8,128)(2,1)S(1)}, u32[]{:S(2)}, u32[]{:S(2)}) collective-permute-start(bf16[128,384]{1,0:T(8,128)(2,1)S(1)} %get-tuple-element.96), channel_id=1, source_target_pairs={{0,1},{1,0},{8,9},{9,8},{16,17},{17,16},{24,25},{25,24},{2,3},{3,2... | collective-permute-start | bytes 294920 | tf_op jit(solution)/shard_map/ppermute | solution.py:608
  55.9 14.7 %collective-permute-done.31.refs_2_ = bf16[288,384]{1,0:T(8,128)(2,1)S(1)} collective-permute-done((bf16[288,384]{1,0:T(8,128)(2,1)S(1)}, bf16[288,384]{1,0:T(8,128)(2,1)S(1)}, u32[]{:S(2)}, u32[]{:S(2)}) %collective-permute-start.31) | collective-permute-done | bytes 221216 | tf_op jit(solution)/shard_map/ppermute | solution.py:616
  71.3 4.8 %collective-permute-start.20 = (bf16[256,384]{1,0:T(8,128)(2,1)S(1)}, bf16[256,384]{1,0:T(8,128)(2,1)S(1)}, u32[]{:S(2)}, u32[]{:S(2)}) collective-permute-start(bf16[256,384]{1,0:T(8,128)(2,1)S(1)} %get-tuple-element.103.refs_8_), channel_id=1, source_target_pairs={{0,1},{8,9},{16,17},{24,25},{2,3},{10,11},{18,19},{26,27},{4,5},{1... | collective-permute-start | bytes 589832 | tf_op jit(solution)/shard_map/ppermute | solution.py:625
  76.4 3.1 %collective-permute-start.19 = (bf16[128,384]{1,0:T(8,128)(2,1)S(1)}, bf16[128,384]{1,0:T(8,128)(2,1)S(1)}, u32[]{:S(2)}, u32[]{:S(2)}) collective-permute-start(bf16[128,384]{1,0:T(8,128)(2,1)S(1)} %get-tuple-element.102), channel_id=1, source_target_pairs={{0,25},{1,24},{8,17},{9,16},{16,9},{17,8},{24,1},{25,0},{2,27},{3,... | collective-permute-start | bytes 294920 | tf_op jit(solution)/shard_map/ppermute | solution.py:608
  79.4 1.8 %shard_map.53 = (bf16[128,384]{1,0:T(8,128)(2,1)S(1)}, bf16[128,384]{1,0:T(8,128)(2,1)S(1)}, bf16[128,384]{1,0:T(8,128)(2,1)S(1)}, bf16[128,384]{1,0:T(8,128)(2,...) custom-call(s32[1,1536]{1,0:T(1,128)S(1)} %get-tuple-element.105.tar, ...), custom_call_target="tpu_custom_call" | custom-call | flops 805306368 | bytes 2359296 | tf_op jit(solution)/shard_map/pallas_call | solution.py:693
  82.8 2.5 %collective-permute-start.40 = (bf16[256,384]{1,0:T(8,128)(2,1)S(1)}, bf16[256,384]{1,0:T(8,128)(2,1)S(1)}, u32[]{:S(2)}, u32[]{:S(2)}) collective-permute-start(bf16[256,384]{1,0:T(8,128)(2,1)S(1)} %get-tuple-element.135.refs_8_), channel_id=1, source_target_pairs={{0,1},{8,9},{16,17},{24,25},{2,3},{10,11},{18,19},{26,27},{4,5},{1... | collective-permute-start | bytes 589832 | tf_op jit(solution)/shard_map/ppermute | solution.py:625
  87.9 2.4 %collective-permute-start.36 = (bf16[128,384]{1,0:T(8,128)(2,1)S(1)}, bf16[128,384]{1,0:T(8,128)(2,1)S(1)}, u32[]{:S(2)}, u32[]{:S(2)}) collective-permute-start(bf16[128,384]{1,0:T(8,128)(2,1)S(1)} %get-tuple-element.131), channel_id=1, source_target_pairs={{0,16},{1,17},{8,24},{9,25},{16,0},{17,1},{24,8},{25,9},{2,18},{3,... | collective-permute-start | bytes 294920 | tf_op jit(solution)/shard_map/ppermute | solution.py:608
  90.2 2.4 %collective-permute-done.35.refs_3_ = bf16[128,384]{1,0:T(8,128)(2,1)S(1)} collective-permute-done((bf16[128,384]{1,0:T(8,128)(2,1)S(1)}, bf16[128,384]{1,0:T(8,128)(2,1)S(1)}, u32[]{:S(2)}, u32[]{:S(2)}) %collective-permute-start.35) | collective-permute-done | bytes 98336 | tf_op jit(solution)/shard_map/ppermute | solution.py:608
  94.2 6.4 %collective-permute-start.37 = (bf16[128,384]{1,0:T(8,128)(2,1)S(1)}, bf16[128,384]{1,0:T(8,128)(2,1)S(1)}, u32[]{:S(2)}, u32[]{:S(2)}) collective-permute-start(bf16[128,384]{1,0:T(8,128)(2,1)S(1)} %get-tuple-element.132), channel_id=1, source_target_pairs={{0,17},{1,16},{8,25},{9,24},{16,1},{17,0},{24,9},{25,8},{2,19},{3,... | collective-permute-start | bytes 294920 | tf_op jit(solution)/shard_map/ppermute | solution.py:608
  100.5 2.2 %collective-permute-start.39 = (bf16[128,384]{1,0:T(8,128)(2,1)S(1)}, bf16[128,384]{1,0:T(8,128)(2,1)S(1)}, u32[]{:S(2)}, u32[]{:S(2)}) collective-permute-start(bf16[128,384]{1,0:T(8,128)(2,1)S(1)} %get-tuple-element.134), channel_id=1, source_target_pairs={{0,25},{1,24},{8,17},{9,16},{16,9},{17,8},{24,1},{25,0},{2,27},{3,... | collective-permute-start | bytes 294920 | tf_op jit(solution)/shard_map/ppermute | solution.py:608
  102.9 8.6 %collective-permute-done.37.refs_5_ = bf16[128,384]{1,0:T(8,128)(2,1)S(1)} collective-permute-done((bf16[128,384]{1,0:T(8,128)(2,1)S(1)}, bf16[128,384]{1,0:T(8,128)(2,1)S(1)}, u32[]{:S(2)}, u32[]{:S(2)}) %collective-permute-start.37) | collective-permute-done | bytes 98336 | tf_op jit(solution)/shard_map/ppermute | solution.py:608
  112.0 1.8 %collective-permute-done.39.refs_7_ = bf16[128,384]{1,0:T(8,128)(2,1)S(1)} collective-permute-done((bf16[128,384]{1,0:T(8,128)(2,1)S(1)}, bf16[128,384]{1,0:T(8,128)(2,1)S(1)}, u32[]{:S(2)}, u32[]{:S(2)}) %collective-permute-start.39) | collective-permute-done | bytes 98336 | tf_op jit(solution)/shard_map/ppermute | solution.py:608
  114.9 1.8 %collective-permute-done.44.refs_3_ = bf16[1024,384]{1,0:T(8,128)(2,1)S(1)} collective-permute-done((bf16[1024,384]{1,0:T(8,128)(2,1)S(1)}, bf16[1024,384]{1,0:T(8,128)(2,1)S(1)}, u32[]{:S(2)}, u32[]{:S(2)}) %collective-permute-start.44) | collective-permute-done | bytes 786464 | tf_op jit(solution)/shard_map/ppermute | solution.py:608
  117.8 3.1 %shard_map.55 = f32[32,8,128]{2,1,0:T(8,128)} custom-call(s32[12]{0:T(128)S(1)} %copy-done.3, bf16[1024,384]{1,0:T(8,128)(2,1)S(1)} %get-tuple-element.104.refs_0_, bf16[1024,384]{1,0:T(8,128)(2,1)S(1)} %get-tuple-element.136.refs_1_, bf16[1024,384]{1,0:T(8,128)(2,1)S(1)} %collective-permute-done.43.refs_2_, ...), custom_call_target="tpu_custom_call" | custom-call | flops 4831838208 | bytes 6291456 | tf_op jit(solution)/shard_map/pallas_call | solution.py:712
  121.0 8.8 %all-to-all-start.3 = ((f32[32,8,128]{2,1,0:T(8,128)}), f32[32,8,128]{2,1,0:T(8,128)S(1)}, u32[]{:S(2)}, u32[]{:S(2)}) async-start(f32[32,8,128]{2,1,0:T(8,128)} %shard_map.55), calls=%async_computation.3 | async-start | bytes 262144 | tf_op jit(solution)/shard_map/all_to_all | solution.py:534
  130.9 6.6 %all-to-all-done.3 = f32[32,8,128]{2,1,0:T(8,128)S(1)} async-done(((f32[32,8,128]{2,1,0:T(8,128)}), f32[32,8,128]{2,1,0:T(8,128)S(1)}, u32[]{:S(2)}, u32[]{:S(2)}) %all-to-all-start.3) | async-done | bytes 131104 | tf_op jit(solution)/shard_map/all_to_all | solution.py:534
  (79 shorter events, 21.6 us)
Async XLA Ops:
  4.7 6.6 %collective-permute-start.3 = (bf16[144,384]{1,0:T(8,128)(2,1)S(1)}, bf16[144,384]{1,0:T(8,128)(2,1)S(1)}, u32[]{:S(2)}, u32[]{:S(2)}) collective-permute-start(bf16[144,384]{1,0:T(8,128)(2,1)S(1)} %get-tuple-element.83), channel_id=1, source_target_pairs={{0,1},{1,0},{8,9},{9,8},{16,17},{17,16},{24,25},{25,24},{2,3},{3,2... | collective-permute-start | bytes 331784 | tf_op jit(solution)/shard_map/ppermute | solution.py:608
  7.7 7.1 %collective-permute-start.5 = (bf16[144,384]{1,0:T(8,128)(2,1)S(1)}, bf16[144,384]{1,0:T(8,128)(2,1)S(1)}, u32[]{:S(2)}, u32[]{:S(2)}) collective-permute-start(bf16[144,384]{1,0:T(8,128)(2,1)S(1)} %get-tuple-element.85), channel_id=1, source_target_pairs={{0,9},{1,8},{8,1},{9,0},{16,25},{17,24},{24,17},{25,16},{2,11},{3,... | collective-permute-start | bytes 331784 | tf_op jit(solution)/shard_map/ppermute | solution.py:608
  7.9 6.9 %collective-permute-start.6 = (bf16[144,384]{1,0:T(8,128)(2,1)S(1)}, bf16[144,384]{1,0:T(8,128)(2,1)S(1)}, u32[]{:S(2)}, u32[]{:S(2)}) collective-permute-start(bf16[144,384]{1,0:T(8,128)(2,1)S(1)} %get-tuple-element.86), channel_id=1, source_target_pairs={{0,16},{1,17},{8,24},{9,25},{16,0},{17,1},{24,8},{25,9},{2,18},{3,... | collective-permute-start | bytes 331784 | tf_op jit(solution)/shard_map/ppermute | solution.py:608
  9.8 7.3 %collective-permute-start.7 = (bf16[144,384]{1,0:T(8,128)(2,1)S(1)}, bf16[144,384]{1,0:T(8,128)(2,1)S(1)}, u32[]{:S(2)}, u32[]{:S(2)}) collective-permute-start(bf16[144,384]{1,0:T(8,128)(2,1)S(1)} %get-tuple-element.87), channel_id=1, source_target_pairs={{0,17},{1,16},{8,25},{9,24},{16,1},{17,0},{24,9},{25,8},{2,19},{3,... | collective-permute-start | bytes 331784 | tf_op jit(solution)/shard_map/ppermute | solution.py:608
  11.3 6.7 %collective-permute-start.8 = (bf16[144,384]{1,0:T(8,128)(2,1)S(1)}, bf16[144,384]{1,0:T(8,128)(2,1)S(1)}, u32[]{:S(2)}, u32[]{:S(2)}) collective-permute-start(bf16[144,384]{1,0:T(8,128)(2,1)S(1)} %get-tuple-element.88), channel_id=1, source_target_pairs={{0,24},{1,25},{8,16},{9,17},{16,8},{17,9},{24,0},{25,1},{2,26},{3,... | collective-permute-start | bytes 331784 | tf_op jit(solution)/shard_map/ppermute | solution.py:608
  11.8 9.0 %collective-permute-start.9 = (bf16[144,384]{1,0:T(8,128)(2,1)S(1)}, bf16[144,384]{1,0:T(8,128)(2,1)S(1)}, u32[]{:S(2)}, u32[]{:S(2)}) collective-permute-start(bf16[144,384]{1,0:T(8,128)(2,1)S(1)} %get-tuple-element.89), channel_id=1, source_target_pairs={{0,25},{1,24},{8,17},{9,16},{16,9},{17,8},{24,1},{25,0},{2,27},{3,... | collective-permute-start | bytes 331784 | tf_op jit(solution)/shard_map/ppermute | solution.py:608
  27.2 7.5 %collective-permute-start.27 = (bf16[128,384]{1,0:T(8,128)(2,1)S(1)}, bf16[128,384]{1,0:T(8,128)(2,1)S(1)}, u32[]{:S(2)}, u32[]{:S(2)}) collective-permute-start(bf16[128,384]{1,0:T(8,128)(2,1)S(1)} %get-tuple-element.120), channel_id=1, source_target_pairs={{0,17},{1,16},{8,25},{9,24},{16,1},{17,0},{24,9},{25,8},{2,19},{3,... | collective-permute-start | bytes 294920 | tf_op jit(solution)/shard_map/ppermute | solution.py:608
  29.2 8.1 %collective-permute-start.28 = (bf16[128,384]{1,0:T(8,128)(2,1)S(1)}, bf16[128,384]{1,0:T(8,128)(2,1)S(1)}, u32[]{:S(2)}, u32[]{:S(2)}) collective-permute-start(bf16[128,384]{1,0:T(8,128)(2,1)S(1)} %get-tuple-element.121), channel_id=1, source_target_pairs={{0,24},{1,25},{8,16},{9,17},{16,8},{17,9},{24,0},{25,1},{2,26},{3,... | collective-permute-start | bytes 294920 | tf_op jit(solution)/shard_map/ppermute | solution.py:608
  29.2 8.1 %collective-permute-start.29 = (bf16[128,384]{1,0:T(8,128)(2,1)S(1)}, bf16[128,384]{1,0:T(8,128)(2,1)S(1)}, u32[]{:S(2)}, u32[]{:S(2)}) collective-permute-start(bf16[128,384]{1,0:T(8,128)(2,1)S(1)} %get-tuple-element.122), channel_id=1, source_target_pairs={{0,25},{1,24},{8,17},{9,16},{16,9},{17,8},{24,1},{25,0},{2,27},{3,... | collective-permute-start | bytes 294920 | tf_op jit(solution)/shard_map/ppermute | solution.py:608
  30.5 12.7 %collective-permute-start.10 = (bf16[304,384]{1,0:T(8,128)(2,1)S(1)}, bf16[304,384]{1,0:T(8,128)(2,1)S(1)}, u32[]{:S(2)}, u32[]{:S(2)}) collective-permute-start(bf16[304,384]{1,0:T(8,128)(2,1)S(1)} %get-tuple-element.91), channel_id=1, source_target_pairs={{0,2},{1,3},{8,10},{9,11},{16,18},{17,19},{24,26},{25,27},{2,0},{3... | collective-permute-start | bytes 700424 | tf_op jit(solution)/shard_map/ppermute | solution.py:616
  32.0 19.2 %collective-permute-start.11 = (bf16[304,384]{1,0:T(8,128)(2,1)S(1)}, bf16[304,384]{1,0:T(8,128)(2,1)S(1)}, u32[]{:S(2)}, u32[]{:S(2)}) collective-permute-start(bf16[304,384]{1,0:T(8,128)(2,1)S(1)} %get-tuple-element.92), channel_id=1, source_target_pairs={{0,4},{1,5},{8,12},{9,13},{16,20},{17,21},{24,28},{25,29},{2,6},{3... | collective-permute-start | bytes 700424 | tf_op jit(solution)/shard_map/ppermute | solution.py:616
  34.7 16.6 %collective-permute-start.12 = (bf16[304,384]{1,0:T(8,128)(2,1)S(1)}, bf16[304,384]{1,0:T(8,128)(2,1)S(1)}, u32[]{:S(2)}, u32[]{:S(2)}) collective-permute-start(bf16[304,384]{1,0:T(8,128)(2,1)S(1)} %get-tuple-element.93), channel_id=1, source_target_pairs={{0,6},{1,7},{8,14},{9,15},{16,22},{17,23},{24,30},{25,31},{2,4},{3... | collective-permute-start | bytes 700424 | tf_op jit(solution)/shard_map/ppermute | solution.py:616
  38.7 16.9 %collective-permute-start.30 = (bf16[288,384]{1,0:T(8,128)(2,1)S(1)}, bf16[288,384]{1,0:T(8,128)(2,1)S(1)}, u32[]{:S(2)}, u32[]{:S(2)}) collective-permute-start(bf16[288,384]{1,0:T(8,128)(2,1)S(1)} %get-tuple-element.124), channel_id=1, source_target_pairs={{0,2},{1,3},{8,10},{9,11},{16,18},{17,19},{24,26},{25,27},{2,0},{3... | collective-permute-start | bytes 663560 | tf_op jit(solution)/shard_map/ppermute | solution.py:616
  39.0 31.6 %collective-permute-start.31 = (bf16[288,384]{1,0:T(8,128)(2,1)S(1)}, bf16[288,384]{1,0:T(8,128)(2,1)S(1)}, u32[]{:S(2)}, u32[]{:S(2)}) collective-permute-start(bf16[288,384]{1,0:T(8,128)(2,1)S(1)} %get-tuple-element.125), channel_id=1, source_target_pairs={{0,4},{1,5},{8,12},{9,13},{16,20},{17,21},{24,28},{25,29},{2,6},{3... | collective-permute-start | bytes 663560 | tf_op jit(solution)/shard_map/ppermute | solution.py:616
  43.2 28.1 %collective-permute-start.32 = (bf16[288,384]{1,0:T(8,128)(2,1)S(1)}, bf16[288,384]{1,0:T(8,128)(2,1)S(1)}, u32[]{:S(2)}, u32[]{:S(2)}) collective-permute-start(bf16[288,384]{1,0:T(8,128)(2,1)S(1)} %get-tuple-element.126), channel_id=1, source_target_pairs={{0,6},{1,7},{8,14},{9,15},{16,22},{17,23},{24,30},{25,31},{2,4},{3... | collective-permute-start | bytes 663560 | tf_op jit(solution)/shard_map/ppermute | solution.py:616
  53.3 22.9 %collective-permute-start.13 = (bf16[128,384]{1,0:T(8,128)(2,1)S(1)}, bf16[128,384]{1,0:T(8,128)(2,1)S(1)}, u32[]{:S(2)}, u32[]{:S(2)}) collective-permute-start(bf16[128,384]{1,0:T(8,128)(2,1)S(1)} %get-tuple-element.96), channel_id=1, source_target_pairs={{0,1},{1,0},{8,9},{9,8},{16,17},{17,16},{24,25},{25,24},{2,3},{3,2... | collective-permute-start | bytes 294920 | tf_op jit(solution)/shard_map/ppermute | solution.py:608
  55.7 20.6 %collective-permute-start.14 = (bf16[128,384]{1,0:T(8,128)(2,1)S(1)}, bf16[128,384]{1,0:T(8,128)(2,1)S(1)}, u32[]{:S(2)}, u32[]{:S(2)}) collective-permute-start(bf16[128,384]{1,0:T(8,128)(2,1)S(1)} %get-tuple-element.97), channel_id=1, source_target_pairs={{0,8},{1,9},{8,0},{9,1},{16,24},{17,25},{24,16},{25,17},{2,10},{3,... | collective-permute-start | bytes 294920 | tf_op jit(solution)/shard_map/ppermute | solution.py:608
  55.7 20.7 %collective-permute-start.15 = (bf16[128,384]{1,0:T(8,128)(2,1)S(1)}, bf16[128,384]{1,0:T(8,128)(2,1)S(1)}, u32[]{:S(2)}, u32[]{:S(2)}) collective-permute-start(bf16[128,384]{1,0:T(8,128)(2,1)S(1)} %get-tuple-element.98), channel_id=1, source_target_pairs={{0,9},{1,8},{8,1},{9,0},{16,25},{17,24},{24,17},{25,16},{2,11},{3,... | collective-permute-start | bytes 294920 | tf_op jit(solution)/shard_map/ppermute | solution.py:608
  70.6 10.7 %collective-permute-start.16 = (bf16[128,384]{1,0:T(8,128)(2,1)S(1)}, bf16[128,384]{1,0:T(8,128)(2,1)S(1)}, u32[]{:S(2)}, u32[]{:S(2)}) collective-permute-start(bf16[128,384]{1,0:T(8,128)(2,1)S(1)} %get-tuple-element.99), channel_id=1, source_target_pairs={{0,16},{1,17},{8,24},{9,25},{16,0},{17,1},{24,8},{25,9},{2,18},{3,... | collective-permute-start | bytes 294920 | tf_op jit(solution)/shard_map/ppermute | solution.py:608
  71.3 14.8 %collective-permute-start.20 = (bf16[256,384]{1,0:T(8,128)(2,1)S(1)}, bf16[256,384]{1,0:T(8,128)(2,1)S(1)}, u32[]{:S(2)}, u32[]{:S(2)}) collective-permute-start(bf16[256,384]{1,0:T(8,128)(2,1)S(1)} %get-tuple-element.103.refs_8_), channel_id=1, source_target_pairs={{0,1},{8,9},{16,17},{24,25},{2,3},{10,11},{18,19},{26,27},{4,5},{1... | collective-permute-start | bytes 589832 | tf_op jit(solution)/shard_map/ppermute | solution.py:625
  76.2 6.6 %collective-permute-start.17 = (bf16[128,384]{1,0:T(8,128)(2,1)S(1)}, bf16[128,384]{1,0:T(8,128)(2,1)S(1)}, u32[]{:S(2)}, u32[]{:S(2)}) collective-permute-start(bf16[128,384]{1,0:T(8,128)(2,1)S(1)} %get-tuple-element.100), channel_id=1, source_target_pairs={{0,17},{1,16},{8,25},{9,24},{16,1},{17,0},{24,9},{25,8},{2,19},{3,... | collective-permute-start | bytes 294920 | tf_op jit(solution)/shard_map/ppermute | solution.py:608
  76.3 9.0 %collective-permute-start.18 = (bf16[128,384]{1,0:T(8,128)(2,1)S(1)}, bf16[128,384]{1,0:T(8,128)(2,1)S(1)}, u32[]{:S(2)}, u32[]{:S(2)}) collective-permute-start(bf16[128,384]{1,0:T(8,128)(2,1)S(1)} %get-tuple-element.101), channel_id=1, source_target_pairs={{0,24},{1,25},{8,16},{9,17},{16,8},{17,9},{24,0},{25,1},{2,26},{3,... | collective-permute-start | bytes 294920 | tf_op jit(solution)/shard_map/ppermute | solution.py:608
  76.4 9.0 %collective-permute-start.19 = (bf16[128,384]{1,0:T(8,128)(2,1)S(1)}, bf16[128,384]{1,0:T(8,128)(2,1)S(1)}, u32[]{:S(2)}, u32[]{:S(2)}) collective-permute-start(bf16[128,384]{1,0:T(8,128)(2,1)S(1)} %get-tuple-element.102), channel_id=1, source_target_pairs={{0,25},{1,24},{8,17},{9,16},{16,9},{17,8},{24,1},{25,0},{2,27},{3,... | collective-permute-start | bytes 294920 | tf_op jit(solution)/shard_map/ppermute | solution.py:608
  82.8 10.5 %collective-permute-start.40 = (bf16[256,384]{1,0:T(8,128)(2,1)S(1)}, bf16[256,384]{1,0:T(8,128)(2,1)S(1)}, u32[]{:S(2)}, u32[]{:S(2)}) collective-permute-start(bf16[256,384]{1,0:T(8,128)(2,1)S(1)} %get-tuple-element.135.refs_8_), channel_id=1, source_target_pairs={{0,1},{8,9},{16,17},{24,25},{2,3},{10,11},{18,19},{26,27},{4,5},{1... | collective-permute-start | bytes 589832 | tf_op jit(solution)/shard_map/ppermute | solution.py:625
  85.4 15.1 %collective-permute-start.21 = (bf16[256,384]{1,0:T(8,128)(2,1)S(1)}, bf16[256,384]{1,0:T(8,128)(2,1)S(1)}, u32[]{:S(2)}, u32[]{:S(2)}) collective-permute-start(bf16[256,384]{1,0:T(8,128)(2,1)S(1)} %get-tuple-element.103.refs_8_), channel_id=1, source_target_pairs={{17,1},{25,9},{19,3},{27,11},{21,5},{29,13},{23,7},{31,15}} | collective-permute-start | bytes 589832 | tf_op jit(solution)/shard_map/ppermute | solution.py:625
  86.1 14.4 %collective-permute-start.22 = (bf16[256,384]{1,0:T(8,128)(2,1)S(1)}, bf16[256,384]{1,0:T(8,128)(2,1)S(1)}, u32[]{:S(2)}, u32[]{:S(2)}) collective-permute-start(bf16[256,384]{1,0:T(8,128)(2,1)S(1)} %collective-permute-done.20.refs_9_), channel_id=1, source_target_pairs={{17,1},{25,9},{19,3},{27,11},{21,5},{29,13},{23,7},{31,15}} | collective-permute-start | bytes 589832 | tf_op jit(solution)/shard_map/ppermute | solution.py:625
  92.6 21.2 %collective-permute-start.41 = (bf16[256,384]{1,0:T(8,128)(2,1)S(1)}, bf16[256,384]{1,0:T(8,128)(2,1)S(1)}, u32[]{:S(2)}, u32[]{:S(2)}) collective-permute-start(bf16[256,384]{1,0:T(8,128)(2,1)S(1)} %get-tuple-element.135.refs_8_), channel_id=1, source_target_pairs={{17,1},{25,9},{19,3},{27,11},{21,5},{29,13},{23,7},{31,15}} | collective-permute-start | bytes 589832 | tf_op jit(solution)/shard_map/ppermute | solution.py:625
  93.3 20.5 %collective-permute-start.42 = (bf16[256,384]{1,0:T(8,128)(2,1)S(1)}, bf16[256,384]{1,0:T(8,128)(2,1)S(1)}, u32[]{:S(2)}, u32[]{:S(2)}) collective-permute-start(bf16[256,384]{1,0:T(8,128)(2,1)S(1)} %collective-permute-done.40.refs_9_), channel_id=1, source_target_pairs={{17,1},{25,9},{19,3},{27,11},{21,5},{29,13},{23,7},{31,15}} | collective-permute-start | bytes 589832 | tf_op jit(solution)/shard_map/ppermute | solution.py:625
  94.2 17.3 %collective-permute-start.37 = (bf16[128,384]{1,0:T(8,128)(2,1)S(1)}, bf16[128,384]{1,0:T(8,128)(2,1)S(1)}, u32[]{:S(2)}, u32[]{:S(2)}) collective-permute-start(bf16[128,384]{1,0:T(8,128)(2,1)S(1)} %get-tuple-element.132), channel_id=1, source_target_pairs={{0,17},{1,16},{8,25},{9,24},{16,1},{17,0},{24,9},{25,8},{2,19},{3,... | collective-permute-start | bytes 294920 | tf_op jit(solution)/shard_map/ppermute | solution.py:608
  100.5 11.0 %collective-permute-start.38 = (bf16[128,384]{1,0:T(8,128)(2,1)S(1)}, bf16[128,384]{1,0:T(8,128)(2,1)S(1)}, u32[]{:S(2)}, u32[]{:S(2)}) collective-permute-start(bf16[128,384]{1,0:T(8,128)(2,1)S(1)} %get-tuple-element.133), channel_id=1, source_target_pairs={{0,24},{1,25},{8,16},{9,17},{16,8},{17,9},{24,0},{25,1},{2,26},{3,... | collective-permute-start | bytes 294920 | tf_op jit(solution)/shard_map/ppermute | solution.py:608
  100.5 13.3 %collective-permute-start.39 = (bf16[128,384]{1,0:T(8,128)(2,1)S(1)}, bf16[128,384]{1,0:T(8,128)(2,1)S(1)}, u32[]{:S(2)}, u32[]{:S(2)}) collective-permute-start(bf16[128,384]{1,0:T(8,128)(2,1)S(1)} %get-tuple-element.134), channel_id=1, source_target_pairs={{0,25},{1,24},{8,17},{9,16},{16,9},{17,8},{24,1},{25,0},{2,27},{3,... | collective-permute-start | bytes 294920 | tf_op jit(solution)/shard_map/ppermute | solution.py:608
  121.0 16.5 %all-to-all-start.3 = ((f32[32,8,128]{2,1,0:T(8,128)}), f32[32,8,128]{2,1,0:T(8,128)S(1)}, u32[]{:S(2)}, u32[]{:S(2)}) async-start(f32[32,8,128]{2,1,0:T(8,128)} %shard_map.55), calls=%async_computation.3 | async-start | bytes 262144 | tf_op jit(solution)/shard_map/all_to_all | solution.py:534
  (18 other events, 145.9 us)

commit v4 on v3

--- a/solution.py
+++ b/solution.py
@@ -235,6 +235,16 @@
     return device // plan.run * plan.width + device % plan.run
 
 
+def chip_change(plan, change):
+    width = plan.width
+    return change % width + change // (2 * width) * width, change // width % 2
+
+
+def lane_change(plan, chip, core):
+    width = plan.width
+    return chip % width + core * width + chip // width * 2 * width
+
+
 def lane_device(plan, layer, lane):
     return lane // plan.width * plan.run + layer * plan.width + lane % plan.width
 
@@ -277,7 +287,6 @@
         + mine.astype(jnp.int32) * plan.slice
         + residue % plan.slice
     )
-    per = len(outs) // len(plan.chunks)
     tile = 2 * plan.part
 
     for pair in range(plan.lanes // 2):
@@ -285,13 +294,8 @@
         chosen = jnp.where(row == target, 1.0, 0.0).astype(jnp.bfloat16)
         moved = jnp.dot(chosen, unit_ref[...], preferred_element_type=jnp.float32)
         moved = moved.astype(jnp.bfloat16)
-        for half in range(2):
-            first = 0
-            for chunk, width in enumerate(plan.chunks):
-                outs[chunk * per + 2 * pair + half][: plan.part, :] = moved[
-                    half * plan.part : (half + 1) * plan.part, first : first + width
-                ]
-                first += width
+        outs[2 * pair][: plan.part, :] = moved[: plan.part, :]
+        outs[2 * pair + 1][: plan.part, :] = moved[plan.part :, :]
 
     place = lax.broadcasted_iota(jnp.int32, (plan.devices, plan.part), 1) // plan.slice
     here = (place.astype(jnp.float32) == order[:, :1]) & (block > 0)
@@ -300,7 +304,7 @@
     blocks = jnp.sum(jnp.where(here, block - 1, 0), axis=0, keepdims=True)
     line = lax.broadcasted_iota(jnp.int32, (16, plan.part), 0)
     table = jnp.where(line == 0, owners, jnp.where(line == 1, blocks, 0))
-    for out in outs[:per]:
+    for out in outs:
         out[plan.part :, : plan.part] = table.astype(jnp.float32).astype(jnp.bfloat16)
 
 
@@ -318,7 +322,9 @@
     outs, (target_ref, inputs_ref, owner_ref, block_ref, value_ref) = rest[:-5], rest[-5:]
     _, layer = my_lane(plan)
     for number, part in enumerate(ins):
-        inputs_ref[number * plan.part : (number + 1) * plan.part, :] = part[: plan.part, :]
+        inputs_ref[number * plan.part : (number + 1) * plan.part, :] = part[
+            : plan.part, : plan.chunks[0]
+        ]
         table = part[plan.part :, : plan.part].astype(jnp.float32)
         owner_ref[number : number + 1, :] = table[0:1, :].astype(jnp.int32)
         block_ref[number : number + 1, :] = table[1:2, :].astype(jnp.int32)
@@ -366,10 +372,13 @@
         out[plan.room :, : plan.stride] = table.astype(jnp.bfloat16)
 
 
-def route_more_kernel(plan, target_ref, *refs):
+def route_more_kernel(plan, target_ref, *refs, chunk):
     ins, outs, inputs_ref = refs[: plan.lanes], refs[plan.lanes : -1], refs[-1]
+    first = sum(plan.chunks[:chunk])
     for number, part in enumerate(ins):
-        inputs_ref[number * plan.part : (number + 1) * plan.part, :] = part[...]
+        inputs_ref[number * plan.part : (number + 1) * plan.part, :] = part[
+            : plan.part, first : first + plan.chunks[chunk]
+        ]
     permute_into(target_ref[...], 0, inputs_ref, outs, plan.room, plan.stride)
 
 
@@ -385,20 +394,16 @@
 
 def sort_parts(plan, target, inputs_ref, outs, ahead_ref, sorted_ref):
     tile = 2 * plan.part
-    for pair in range(plan.lanes // 2):
-        row = lax.broadcasted_iota(jnp.int32, (tile, inputs_ref.shape[0]), 0) + pair * tile
+    for chip, out in enumerate(outs):
+        row = lax.broadcasted_iota(jnp.int32, (tile, inputs_ref.shape[0]), 0) + chip * tile
         chosen = jnp.where(row == target, 1.0, 0.0).astype(jnp.bfloat16)
         moved = jnp.dot(chosen, inputs_ref[...], preferred_element_type=jnp.float32)
         moved = moved.astype(jnp.bfloat16)
-        sorted_ref[pair * tile : (pair + 1) * tile, :] = moved
-        outs[2 * pair][...] = moved[: plan.part, :]
-        outs[2 * pair + 1][...] = moved[plan.part :, :]
+        sorted_ref[chip * tile : (chip + 1) * tile, :] = moved
+        out[...] = moved
     lane, _ = my_lane(plan)
-    for slot in range(2):
-        part = lane_of(plan, slot) ^ lane
-        ahead_ref[slot * plan.part : (slot + 1) * plan.part, :] = sorted_ref[
-            pl.ds(pl.multiple_of(part * plan.part, plan.part), plan.part), :
-        ]
+    chip, _ = chip_change(plan, lane_of(plan, 0) ^ lane)
+    ahead_ref[...] = sorted_ref[pl.ds(pl.multiple_of(chip * tile, tile), tile), :]
 
 
 def deliver_kernel(plan, *refs):
@@ -413,7 +418,8 @@
         full = jnp.maximum(full, jnp.broadcast_to(table[1:2, :128], (8, 128)))
         slot = value // plan.blocks
         within = lax.broadcasted_iota(jnp.int32, value.shape, 1) % plan.slice
-        target = (lane_of(plan, slot) ^ lane) * plan.part + value % plan.blocks * plan.slice + within
+        chip, _ = chip_change(plan, lane_of(plan, slot) ^ lane)
+        target = (2 * chip + slot % 2) * plan.part + value % plan.blocks * plan.slice + within
         target_ref[:, number * plan.stride : (number + 1) * plan.stride] = jnp.where(
             value >= 0, target, -1
         )
@@ -429,22 +435,21 @@
 
 
 def join_kernel(plan, *refs):
-    ins, (own_ref, behind_ref) = refs[:-2], refs[-2:]
-    for number, part in enumerate(ins[: plan.lanes]):
-        own_ref[number * plan.part : (number + 1) * plan.part, :] = part[...]
-    for number, part in enumerate(ins[plan.lanes :]):
-        behind_ref[number * 2 * plan.part : (number + 1) * 2 * plan.part, :] = part[...]
-
-
-def wide_best(keys, queries_ref, best_ref):
-    @pl.loop(0, keys[0].shape[0] // TILE, unroll=True)
-    def _(tile):
-        here = pl.ds(pl.multiple_of(tile * TILE, TILE), TILE)
-        block = jnp.concatenate([part[here, :] for part in keys], axis=1)
-        scores = lax.dot_general(
-            block, queries_ref[...], (((1,), (1,)), ((), ())), preferred_element_type=jnp.float32
-        )
-        best_ref[...] = jnp.maximum(best_ref[...], jnp.max(scores, axis=0, keepdims=True))
+    ins, outs = refs[: -(len(refs) // 5)], refs[-(len(refs) // 5) :]
+    tile = 2 * plan.part
+    for number, part in enumerate(ins):
+        out = outs[number // (plan.lanes // 2)]
+        first = number % (plan.lanes // 2) * tile
+        out[first : first + tile, :] = part[...]
+
+
+def add_best(keys, queries_ref, best_ref, allowed=None):
+    scores = lax.dot_general(
+        keys, queries_ref[...], (((1,), (1,)), ((), ())), preferred_element_type=jnp.float32
+    )
+    if allowed is not None:
+        scores = jnp.where(allowed, scores, -2.0)
+    best_ref[...] = jnp.maximum(best_ref[...], jnp.max(scores, axis=0, keepdims=True))
 
 
 def staged_best_kernel(plan, run_len_ref, *refs):
@@ -454,40 +459,49 @@
     ingest, run = lax.axis_index("ingest"), lax.axis_index("run")
     lane, _ = my_lane(plan)
     group, slot = plan.slot(ingest, run)
+    core = slot % 2
     begin = jnp.int32(0)
     for number, start in enumerate(cluster_starts(plan, run_len_ref)):
         here = (number // plan.per_group == group) & (start <= slot)
         begin = jnp.where(here, jnp.maximum(begin, start), begin)
-    first = 0
-    for part in own:
-        queries_ref[:, first : first + part.shape[1]] = part[...]
-        first += part.shape[1]
+    chips = plan.lanes // 2
+    for side, parts in enumerate((own, mate)):
+        for chip in range(chips):
+            there = pl.ds(pl.multiple_of((2 * chip + core) * plan.part, plan.part), plan.part)
+            here = slice((side * chips + chip) * plan.part, (side * chips + chip + 1) * plan.part)
+            first = 0
+            for part in parts:
+                queries_ref[here, first : first + part.shape[1]] = part[there, :]
+                first += part.shape[1]
 
     def slots(row):
+        line = row // plan.part
+        source = lane_change(plan, line % chips, line // chips) ^ lane
         block = row // plan.slice % plan.blocks
-        return block * plan.cap + (row // plan.part ^ lane) * plan.slice + row % plan.slice
+        return block * plan.cap + source * plan.slice + row % plan.slice
 
     best_ref[...] = jnp.full(best_ref.shape, -1.0, jnp.float32)
     query = slots(lax.broadcasted_iota(jnp.int32, (1, plan.rows), 1))
-
-    @pl.loop(0, plan.rows // TILE, unroll=True)
-    def _(tile):
-        key = slots(lax.broadcasted_iota(jnp.int32, (TILE, 1), 0) + tile * TILE)
-        block = queries_ref[pl.ds(pl.multiple_of(tile * TILE, TILE), TILE), :]
-        scores = lax.dot_general(
-            block, queries_ref[...], (((1,), (1,)), ((), ())), preferred_element_type=jnp.float32
-        )
-        top = jnp.max(jnp.where(key < query, scores, -2.0), axis=0, keepdims=True)
-        best_ref[...] = jnp.maximum(best_ref[...], top)
-
-    @pl.when(slot % 2 == 1)
+    for first in range(0, plan.rows, TILE):
+        key = slots(lax.broadcasted_iota(jnp.int32, (TILE, 1), 0) + first)
+        add_best(queries_ref[first : first + TILE, :], queries_ref, best_ref, key < query)
+
+    @pl.when(core == 1)
     def _():
-        wide_best(mate, queries_ref, best_ref)
-
-    @pl.when(slot - slot % 2 - 2 >= begin)
+        for parts in (own, mate):
+            for pair in range(0, chips, 2):
+                keys = [
+                    jnp.concatenate([part[2 * n * plan.part : (2 * n + 1) * plan.part, :] for part in parts], axis=1)
+                    for n in (pair, pair + 1)
+                ]
+                add_best(jnp.concatenate(keys, axis=0), queries_ref, best_ref)
+
+    @pl.when(slot - core - 2 >= begin)
     def _():
-        wide_best(behind, queries_ref, best_ref)
-        wide_best(far, queries_ref, best_ref)
+        for parts in (behind, far):
+            for first in range(0, plan.rows, TILE):
+                keys = [part[first : first + TILE, :] for part in parts]
+                add_best(jnp.concatenate(keys, axis=1), queries_ref, best_ref)
 
     for number in range(plan.lanes):
         lines_ref[number : number + 1, :] = best_ref[
@@ -500,7 +514,8 @@
 def staged_unpack_kernel(plan, run_len_ref, cluster_ref, rank_ref, reply_ref, out_ref):
     group, slot, within = row_slot(plan, run_len_ref, cluster_ref[...], rank_ref[...])
     residue = within % plan.cap
-    line = plan.device(group, slot) * plan.lanes + (residue // plan.slice ^ lane_of(plan, slot))
+    chip, core = chip_change(plan, residue // plan.slice ^ lane_of(plan, slot))
+    line = plan.device(group, slot) * plan.lanes + core * (plan.lanes // 2) + chip
     column = within // plan.cap * plan.slice + residue % plan.slice
     number = lax.broadcasted_iota(jnp.int32, (plan.devices * plan.lanes, plan.rows), 0)
     columns = lax.dot_general(
@@ -626,32 +641,21 @@
 
     far_first = sorted(lanes, key=lambda change: -(change & 1) - (change // plan.width // 2))
 
-    def swap_lanes(blocks):
-        return [
-            along_lanes(blocks[change], change) if change else blocks[0] for change in far_first
-        ], far_first
-
-    def by_change(moved):
-        arrays, order = moved
-        return [arrays[order.index(change)] for change in lanes]
-
-    sizes = [plan.part + 16] + [plan.part] * (len(plan.chunks) - 1)
     spread = call(
         spread_kernel,
         plan,
-        [wide((size, f), half) for size, f in zip(sizes, plan.chunks) for _ in lanes],
+        [wide((plan.part + 16, width), half) for _ in lanes],
         [SMEM, VMEM, VMEM, VMEM],
         [pltpu.VMEM((rows, width), half)],
         2 * rows * rows * width,
         3 * rows * width * 2,
     )(run_len, clusters, ranks, embeddings)
+    swapped = {change: along_lanes(spread[change], change) for change in far_first if change}
+    spread = [spread[0]] + [swapped[change] for change in lanes[1:]]
     owns, mates, behinds, fars = [], [], [], []
     table = targets = full = None
     for chunk, f in enumerate(plan.chunks):
-        if chunk:
-            spread, routed = lax.optimization_barrier((spread, routed))
         spec = dict(flops=2 * rows * rows * f, moved=3 * rows * f * 2, memory=12)
-        parts = by_change(swap_lanes(spread[chunk * plan.lanes : (chunk + 1) * plan.lanes]))
         rooms = [wide((plan.room + (0 if chunk else 16), f), half) for _ in layers]
         inputs = pltpu.VMEM((rows, f), half)
         if chunk == 0:
@@ -667,14 +671,15 @@
                     pltpu.VMEM((1, rows), jnp.float32),
                 ],
                 **spec,
-            )(*parts)
+            )(*spread)
         else:
-            routed = call(
-                route_more_kernel, plan, rooms, [VMEM] * (1 + plan.lanes), [inputs], **spec
-            )(table, *parts)
-        moved = {change: along_layers(routed[change], change) for change in reversed(layers[1:])}
-        arrived = [routed[0]] + [moved[change] for change in layers[1:]]
-        shapes = [wide((plan.part, f), half) for _ in lanes] + [wide((2 * plan.part, f), half)]
+            more = functools.partial(route_more_kernel, chunk=chunk)
+            routed = call(more, plan, rooms, [VMEM] * (1 + plan.lanes), [inputs], **spec)(
+                table, *spread
+            )
+        far = {change: along_layers(routed[change], change) for change in reversed(layers[1:])}
+        arrived = [routed[0]] + [far[change] for change in layers[1:]]
+        shapes = [wide((2 * plan.part, f), half) for _ in range(plan.lanes // 2 + 1)]
         scratch = [pltpu.VMEM((plan.layers * plan.stride, f), half), inputs]
         if chunk == 0:
             *parts, ahead, targets, full = call(
@@ -694,17 +699,17 @@
                 deliver_more_kernel, plan, shapes, [VMEM] * (1 + plan.layers), scratch, **spec
             )(targets, *arrived)
         near = chip_to_chip(ahead, [(0, 1), (3, 2)])
-        parts = by_change(swap_lanes(parts))
+        parts = [
+            along_lanes(part, lane_change(plan, chip, 0)) if chip else part
+            for chip, part in enumerate(parts)
+        ]
         side = chip_to_chip(ahead, [(2, 1)])
         corner = chip_to_chip(near, [(2, 1)])
-        own, behind = call(
-            join_kernel,
-            plan,
-            [wide((rows, f), half)] * 2,
-            [VMEM] * (plan.lanes + 4),
-            moved=4 * rows * f * 2,
-            memory=8,
-        )(*parts, ahead, near, side, corner)
+        spec = dict(moved=4 * rows * f * 2, memory=8)
+        ((own,), (behind,)) = (
+            call(join_kernel, plan, [wide((rows, f), half)], [VMEM] * len(group), **spec)(*group)
+            for group in (parts, (ahead, near, side, corner))
+        )
         owns.append(own)
         behinds.append(behind)
         mates.append(along_lanes(own, plan.width))

time: 140 us -> 132 us (0.943)
  starting transfers between devices: 65.6 us -> 56.3 us
  waiting for transfers between devices: 54.5 us -> 56 us
    ppermute x32 -> x17, starting transfers between devices: 34.6 us -> 16.9 us  [along_lanes(): return lax.ppermute(block, AXES, pairs)]
    all_to_all x1, starting transfers between devices: 8.77 us -> 20.7 us  [exchange(): return lax.all_to_all(block, AXES, split_axis=0, concat_axis=0, tiled=True)]
    ppermute x6, waiting for transfers between devices: 0.02 us -> 7.86 us  [chip_to_chip(): return lax.ppermute(block, AXES, pairs)]
    ppermute x32 -> x17, waiting for transfers between devices: 25.8 us -> 19.5 us  [along_lanes(): return lax.ppermute(block, AXES, pairs)]
    ppermute x6, starting transfers between devices: 10.2 us -> 7.54 us  [chip_to_chip(): return lax.ppermute(block, AXES, pairs)]
    pallas_call x4 -> x6, Pallas kernels: 6.34 us -> 6.34 us  [the longest x1 4.66 us: staged(): call(spread_kernel, plan, [wide((plan.part + 16, width), half) for _ in l...]
  transfers between devices with their start and end apart: 45 -> 30, of which waited for: 15 -> 15; matrix products, arithmetic and copies ran while one was open for 0% -> 0% of each run, Pallas kernels for 4% -> 4%
where the time goes in v4:
time: 132 us
  starting transfers between devices  56.3 us (43%)
  waiting for transfers between devices  56 us (42%)
  Pallas kernels  17.8 us (13%)
    ppermute x6, waiting for transfers between devices, along_layers(): return lax.ppermute(block, AXES, pairs)  22 us
    all_to_all x1, starting transfers between devices, exchange(): return lax.all_to_all(block, AXES, split_axis=0, concat_axis=0, tiled=True)  20.7 us
    ppermute x17, waiting for transfers between devices, along_lanes(): return lax.ppermute(block, AXES, pairs)  19.5 us
    ppermute x17, starting transfers between devices, along_lanes(): return lax.ppermute(block, AXES, pairs)  16.9 us
    ppermute x6, starting transfers between devices, along_layers(): return lax.ppermute(block, AXES, pairs)  11.2 us
    ppermute x6, waiting for transfers between devices, chip_to_chip(): return lax.ppermute(block, AXES, pairs)  7.86 us
    ppermute x6, starting transfers between devices, chip_to_chip(): return lax.ppermute(block, AXES, pairs)  7.54 us
    all_to_all x1, waiting for transfers between devices, exchange(): return lax.all_to_all(block, AXES, split_axis=0, concat_axis=0, tiled=True)  6.57 us
  transfers between devices with their start and end apart: 30, of which 15 were waited for; matrix products, arithmetic and copies ran while one was open for 0% of the time, Pallas kernels for 4%

profile of v4, /device:TPU:0, one launch (start us, length us, event | category | flops | bytes accessed | tf_op | source)
XLA Modules:
  0.0 132.1 jit_solution(3902298614369943279)
XLA Ops:
  0.0 4.7 %shard_map.48 = (bf16[144,768]{1,0:T(8,128)(2,1)S(1)}, bf16[144,768]{1,0:T(8,128)(2,1)S(1)}, bf16[144,768]{1,0:T(8,128)(2,1)S(1)}, bf16[144,768]{1,0:T(8,128)(2,...) custom-call(s32[12]{0:T(128)} %run_len_ref.5, ...), custom_call_target="tpu_custom_call" | custom-call | flops 1610612736 | bytes 4718592 | tf_op jit(solution)/shard_map/pallas_call | solution.py:644
  4.7 3.0 %collective-permute-start.3 = (bf16[144,768]{1,0:T(8,128)(2,1)S(1)}, bf16[144,768]{1,0:T(8,128)(2,1)S(1)}, u32[]{:S(2)}, u32[]{:S(2)}) collective-permute-start(bf16[144,768]{1,0:T(8,128)(2,1)S(1)} %get-tuple-element.55), channel_id=1, source_target_pairs={{0,1},{1,0},{8,9},{9,8},{16,17},{17,16},{24,25},{25,24},{2,3},{3,2... | collective-permute-start | bytes 663560 | tf_op jit(solution)/shard_map/ppermute | solution.py:623
  7.9 1.9 %collective-permute-start.6 = (bf16[144,768]{1,0:T(8,128)(2,1)S(1)}, bf16[144,768]{1,0:T(8,128)(2,1)S(1)}, u32[]{:S(2)}, u32[]{:S(2)}) collective-permute-start(bf16[144,768]{1,0:T(8,128)(2,1)S(1)} %get-tuple-element.58), channel_id=1, source_target_pairs={{0,16},{1,17},{8,24},{9,25},{16,0},{17,1},{24,8},{25,9},{2,18},{3,... | collective-permute-start | bytes 663560 | tf_op jit(solution)/shard_map/ppermute | solution.py:623
  9.8 1.5 %collective-permute-start.7 = (bf16[144,768]{1,0:T(8,128)(2,1)S(1)}, bf16[144,768]{1,0:T(8,128)(2,1)S(1)}, u32[]{:S(2)}, u32[]{:S(2)}) collective-permute-start(bf16[144,768]{1,0:T(8,128)(2,1)S(1)} %get-tuple-element.59), channel_id=1, source_target_pairs={{0,17},{1,16},{8,25},{9,24},{16,1},{17,0},{24,9},{25,8},{2,19},{3,... | collective-permute-start | bytes 663560 | tf_op jit(solution)/shard_map/ppermute | solution.py:623
  11.3 2.7 %collective-permute-done.3.refs_1_ = bf16[144,768]{1,0:T(8,128)(2,1)S(1)} collective-permute-done((bf16[144,768]{1,0:T(8,128)(2,1)S(1)}, bf16[144,768]{1,0:T(8,128)(2,1)S(1)}, u32[]{:S(2)}, u32[]{:S(2)}) %collective-permute-start.3) | collective-permute-done | bytes 221216 | tf_op jit(solution)/shard_map/ppermute | solution.py:623
  14.0 3.2 %collective-permute-start.9 = (bf16[144,768]{1,0:T(8,128)(2,1)S(1)}, bf16[144,768]{1,0:T(8,128)(2,1)S(1)}, u32[]{:S(2)}, u32[]{:S(2)}) collective-permute-start(bf16[144,768]{1,0:T(8,128)(2,1)S(1)} %get-tuple-element.61), channel_id=1, source_target_pairs={{0,25},{1,24},{8,17},{9,16},{16,9},{17,8},{24,1},{25,0},{2,27},{3,... | collective-permute-start | bytes 663560 | tf_op jit(solution)/shard_map/ppermute | solution.py:623
  17.2 4.7 %collective-permute-done.5.refs_3_ = bf16[144,768]{1,0:T(8,128)(2,1)S(1)} collective-permute-done((bf16[144,768]{1,0:T(8,128)(2,1)S(1)}, bf16[144,768]{1,0:T(8,128)(2,1)S(1)}, u32[]{:S(2)}, u32[]{:S(2)}) %collective-permute-start.5) | collective-permute-done | bytes 221216 | tf_op jit(solution)/shard_map/ppermute | solution.py:623
  22.4 2.8 %collective-permute-done.8.refs_6_ = bf16[144,768]{1,0:T(8,128)(2,1)S(1)} collective-permute-done((bf16[144,768]{1,0:T(8,128)(2,1)S(1)}, bf16[144,768]{1,0:T(8,128)(2,1)S(1)}, u32[]{:S(2)}, u32[]{:S(2)}) %collective-permute-start.8) | collective-permute-done | bytes 221216 | tf_op jit(solution)/shard_map/ppermute | solution.py:623
  25.1 4.8 %collective-permute-done.9.refs_7_ = bf16[144,768]{1,0:T(8,128)(2,1)S(1)} collective-permute-done((bf16[144,768]{1,0:T(8,128)(2,1)S(1)}, bf16[144,768]{1,0:T(8,128)(2,1)S(1)}, u32[]{:S(2)}, u32[]{:S(2)}) %collective-permute-start.9) | collective-permute-done | bytes 221216 | tf_op jit(solution)/shard_map/ppermute | solution.py:623
  29.9 2.7 %shard_map.49 = (bf16[304,384]{1,0:T(8,128)(2,1)S(1)}, bf16[304,384]{1,0:T(8,128)(2,1)S(1)}, bf16[304,384]{1,0:T(8,128)(2,1)S(1)}, bf16[304,384]{1,0:T(8,128)(2,1)S(1)}, s32[1,1024]{1,0:T(1,128)S(1)}) custom-call(bf16[144,768]{1,0:T(8,128)(2,1)S(1)} %get-tuple-element.54.refs_0_, bf16[144,768]{1,0:T(8,128)(2,1)S(1)} %collective-permute-done.3.refs_1_, ...), custom_call_target="tpu_custom_call" | custom-call | flops 805306368 | bytes 2359296 | tf_op jit(solution)/shard_map/pallas_call | solution.py:662
  32.6 1.6 %collective-permute-start.10 = (bf16[304,384]{1,0:T(8,128)(2,1)S(1)}, bf16[304,384]{1,0:T(8,128)(2,1)S(1)}, u32[]{:S(2)}, u32[]{:S(2)}) collective-permute-start(bf16[304,384]{1,0:T(8,128)(2,1)S(1)} %get-tuple-element.63), channel_id=1, source_target_pairs={{0,2},{1,3},{8,10},{9,11},{16,18},{17,19},{24,26},{25,27},{2,0},{3... | collective-permute-start | bytes 700424 | tf_op jit(solution)/shard_map/ppermute | solution.py:631
  34.2 2.6 %collective-permute-start.11 = (bf16[304,384]{1,0:T(8,128)(2,1)S(1)}, bf16[304,384]{1,0:T(8,128)(2,1)S(1)}, u32[]{:S(2)}, u32[]{:S(2)}) collective-permute-start(bf16[304,384]{1,0:T(8,128)(2,1)S(1)} %get-tuple-element.64), channel_id=1, source_target_pairs={{0,4},{1,5},{8,12},{9,13},{16,20},{17,21},{24,28},{25,29},{2,6},{3... | collective-permute-start | bytes 700424 | tf_op jit(solution)/shard_map/ppermute | solution.py:631
  37.0 1.4 %shard_map.52 = (bf16[288,384]{1,0:T(8,128)(2,1)S(1)}, bf16[288,384]{1,0:T(8,128)(2,1)S(1)}, bf16[288,384]{1,0:T(8,128)(2,1)S(1)}, bf16[288,384]{1,0:T(8,128)(2,1)S(1)}) custom-call(s32[1,1024]{1,0:T(1,128)S(1)} %get-tuple-element.72.target_ref, bf16[144,768]{1,0:T(8,128)(2,1)S(1)} %get-tuple-element.54.refs_0_, ...), custom_call_target="tpu_custom_call" | custom-call | flops 805306368 | bytes 2359296 | tf_op jit(solution)/shard_map/pallas_call | solution.py:677
  39.1 3.5 %collective-permute-start.17 = (bf16[288,384]{1,0:T(8,128)(2,1)S(1)}, bf16[288,384]{1,0:T(8,128)(2,1)S(1)}, u32[]{:S(2)}, u32[]{:S(2)}) collective-permute-start(bf16[288,384]{1,0:T(8,128)(2,1)S(1)} %get-tuple-element.75), channel_id=1, source_target_pairs={{0,4},{1,5},{8,12},{9,13},{16,20},{17,21},{24,28},{25,29},{2,6},{3... | collective-permute-start | bytes 663560 | tf_op jit(solution)/shard_map/ppermute | solution.py:631
  42.6 3.3 %collective-permute-done.10.refs_1_ = bf16[304,384]{1,0:T(8,128)(2,1)S(1)} collective-permute-done((bf16[304,384]{1,0:T(8,128)(2,1)S(1)}, bf16[304,384]{1,0:T(8,128)(2,1)S(1)}, u32[]{:S(2)}, u32[]{:S(2)}) %collective-permute-start.10) | collective-permute-done | bytes 233504 | tf_op jit(solution)/shard_map/ppermute | solution.py:631
  45.9 2.6 %collective-permute-start.18 = (bf16[288,384]{1,0:T(8,128)(2,1)S(1)}, bf16[288,384]{1,0:T(8,128)(2,1)S(1)}, u32[]{:S(2)}, u32[]{:S(2)}) collective-permute-start(bf16[288,384]{1,0:T(8,128)(2,1)S(1)} %get-tuple-element.76), channel_id=1, source_target_pairs={{0,6},{1,7},{8,14},{9,15},{16,22},{17,23},{24,30},{25,31},{2,4},{3... | collective-permute-start | bytes 663560 | tf_op jit(solution)/shard_map/ppermute | solution.py:631
  48.5 5.1 %collective-permute-done.11.refs_2_ = bf16[304,384]{1,0:T(8,128)(2,1)S(1)} collective-permute-done((bf16[304,384]{1,0:T(8,128)(2,1)S(1)}, bf16[304,384]{1,0:T(8,128)(2,1)S(1)}, u32[]{:S(2)}, u32[]{:S(2)}) %collective-permute-start.11) | collective-permute-done | bytes 233504 | tf_op jit(solution)/shard_map/ppermute | solution.py:631
  53.7 2.1 %shard_map.50 = (bf16[256,384]{1,0:T(8,128)(2,1)S(1)}, bf16[256,384]{1,0:T(8,128)(2,1)S(1)}, bf16[256,384]{1,0:T(8,128)(2,1)S(1)}, bf16[256,384]{1,0:T(8,128)(2,...) custom-call(bf16[304,384]{1,0:T(8,128)(2,1)S(1)} %get-tuple-element.62.refs_0_, ...), custom_call_target="tpu_custom_call" | custom-call | flops 805306368 | bytes 2359296 | tf_op jit(solution)/shard_map/pallas_call | solution.py:685
  56.4 1.5 %collective-permute-start.14 = (bf16[256,384]{1,0:T(8,128)(2,1)S(1)}, bf16[256,384]{1,0:T(8,128)(2,1)S(1)}, u32[]{:S(2)}, u32[]{:S(2)}) collective-permute-start(bf16[256,384]{1,0:T(8,128)(2,1)S(1)} %get-tuple-element.69), channel_id=1, source_target_pairs={{0,16},{1,17},{8,24},{9,25},{16,0},{17,1},{24,8},{25,9},{2,18},{3,... | collective-permute-start | bytes 589832 | tf_op jit(solution)/shard_map/ppermute | solution.py:623
  57.9 1.5 %collective-permute-start.15 = (bf16[256,384]{1,0:T(8,128)(2,1)S(1)}, bf16[256,384]{1,0:T(8,128)(2,1)S(1)}, u32[]{:S(2)}, u32[]{:S(2)}) collective-permute-start(bf16[256,384]{1,0:T(8,128)(2,1)S(1)} %get-tuple-element.70), channel_id=1, source_target_pairs={{0,17},{1,16},{8,25},{9,24},{16,1},{17,0},{24,9},{25,8},{2,19},{3,... | collective-permute-start | bytes 589832 | tf_op jit(solution)/shard_map/ppermute | solution.py:623
  59.3 13.6 %collective-permute-done.17.refs_2_ = bf16[288,384]{1,0:T(8,128)(2,1)S(1)} collective-permute-done((bf16[288,384]{1,0:T(8,128)(2,1)S(1)}, bf16[288,384]{1,0:T(8,128)(2,1)S(1)}, u32[]{:S(2)}, u32[]{:S(2)}) %collective-permute-start.17) | collective-permute-done | bytes 221216 | tf_op jit(solution)/shard_map/ppermute | solution.py:631
  72.9 1.8 %shard_map.53 = (bf16[256,384]{1,0:T(8,128)(2,1)S(1)}, bf16[256,384]{1,0:T(8,128)(2,1)S(1)}, bf16[256,384]{1,0:T(8,128)(2,1)S(1)}, bf16[256,384]{1,0:T(8,128)(2,1)S(1)}, bf16[256,384]{1,0:T(8,128)(2,1)S(1)}) custom-call(s32[1,1536]{1,0:T(1,128)S(1)} %get-tuple-element.71.target_ref, bf16[288,384]{1,0:T(8,128)(2,1)S(1)} %get-tuple-element.73.refs_0_, ...), custom_call_target="tpu_custom_call" | custom-call | flops 805306368 | bytes 2359296 | tf_op jit(solution)/shard_map/pallas_call | solution.py:698
  75.3 3.4 %collective-permute-start.24 = (bf16[256,384]{1,0:T(8,128)(2,1)S(1)}, bf16[256,384]{1,0:T(8,128)(2,1)S(1)}, u32[]{:S(2)}, u32[]{:S(2)}) collective-permute-start(bf16[256,384]{1,0:T(8,128)(2,1)S(1)} %get-tuple-element.81.refs_0_), channel_id=1, source_target_pairs={{0,1},{8,9},{16,17},{24,25},{2,3},{10,11},{18,19},{26,27},{4,5},{1... | collective-permute-start | bytes 589832 | tf_op jit(solution)/shard_map/ppermute | solution.py:640
  78.8 1.5 %collective-permute-start.20 = (bf16[256,384]{1,0:T(8,128)(2,1)S(1)}, bf16[256,384]{1,0:T(8,128)(2,1)S(1)}, u32[]{:S(2)}, u32[]{:S(2)}) collective-permute-start(bf16[256,384]{1,0:T(8,128)(2,1)S(1)} %get-tuple-element.79), channel_id=1, source_target_pairs={{0,16},{1,17},{8,24},{9,25},{16,0},{17,1},{24,8},{25,9},{2,18},{3,... | collective-permute-start | bytes 589832 | tf_op jit(solution)/shard_map/ppermute | solution.py:623
  80.3 1.3 collective-permute-start.27
  82.4 5.9 %collective-permute-done.24.refs_1_ = bf16[256,384]{1,0:T(8,128)(2,1)S(1)} collective-permute-done((bf16[256,384]{1,0:T(8,128)(2,1)S(1)}, bf16[256,384]{1,0:T(8,128)(2,1)S(1)}, u32[]{:S(2)}, u32[]{:S(2)}) %collective-permute-start.24) | collective-permute-done | bytes 196640 | tf_op jit(solution)/shard_map/ppermute | solution.py:640
  89.6 2.0 %collective-permute-done.27.refs_1_ = bf16[256,384]{1,0:T(8,128)(2,1)S(1)} collective-permute-done((bf16[256,384]{1,0:T(8,128)(2,1)S(1)}, bf16[256,384]{1,0:T(8,128)(2,1)S(1)}, u32[]{:S(2)}, u32[]{:S(2)}) %collective-permute-start.27) | collective-permute-done | bytes 196640 | tf_op jit(solution)/shard_map/ppermute | solution.py:640
  94.9 1.1 collective-permute-done.23.refs_3_
  98.3 3.4 %shard_map.57 = f32[32,8,128]{2,1,0:T(8,128)} custom-call(s32[12]{0:T(128)S(1)} %copy-done.3, bf16[1024,384]{1,0:T(8,128)(2,1)S(1)} %shard_map.51.refs_0_, bf16[1024,384]{1,0:T(8,128)(2,1)S(1)} %shard_map.54.refs_1_, bf16[1024,384]{1,0:T(8,128)(2,1)S(1)} %collective-permute-done.22.refs_2_, bf16[1024,384]{1,0:T(8,128)(2,1)S(1)} %collective-permute-done.23.refs_3_, ...), custom_call_target="tpu_custom_call" | custom-call | flops 4831838208 | bytes 6291456 | tf_op jit(solution)/shard_map/pallas_call | solution.py:717
  101.7 20.7 %all-to-all-start.3 = ((f32[32,8,128]{2,1,0:T(8,128)}), f32[32,8,128]{2,1,0:T(8,128)S(1)}, u32[]{:S(2)}, u32[]{:S(2)}) async-start(f32[32,8,128]{2,1,0:T(8,128)} %shard_map.57), calls=%async_computation.3 | async-start | bytes 262144 | tf_op jit(solution)/shard_map/all_to_all | solution.py:549
  123.5 6.6 %all-to-all-done.3 = f32[32,8,128]{2,1,0:T(8,128)S(1)} async-done(((f32[32,8,128]{2,1,0:T(8,128)}), f32[32,8,128]{2,1,0:T(8,128)S(1)}, u32[]{:S(2)}, u32[]{:S(2)}) %all-to-all-start.3) | async-done | bytes 131104 | tf_op jit(solution)/shard_map/all_to_all | solution.py:549
  130.1 1.4 %shard_map.58 = f32[1,1024]{1,0:T(1,128)S(1)} custom-call(s32[12]{0:T(128)S(1)} %copy-done.3, s32[1,1024]{1,0:T(1,128)S(1)} %bitcast.27, s32[1,1024]{1,0:T(1,128)S(1)} %bitcast.30, f32[256,128]{1,0:T(8,128)S(1)} %bitcast.20), custom_call_target="tpu_custom_call" | custom-call | bytes 16384 | tf_op jit(solution)/shard_map/pallas_call | solution.py:731
  (51 shorter events, 11.5 us)
Async XLA Ops:
  4.7 9.3 %collective-permute-start.3 = (bf16[144,768]{1,0:T(8,128)(2,1)S(1)}, bf16[144,768]{1,0:T(8,128)(2,1)S(1)}, u32[]{:S(2)}, u32[]{:S(2)}) collective-permute-start(bf16[144,768]{1,0:T(8,128)(2,1)S(1)} %get-tuple-element.55), channel_id=1, source_target_pairs={{0,1},{1,0},{8,9},{9,8},{16,17},{17,16},{24,25},{25,24},{2,3},{3,2... | collective-permute-start | bytes 663560 | tf_op jit(solution)/shard_map/ppermute | solution.py:623
  7.7 6.3 %collective-permute-start.4 = (bf16[144,768]{1,0:T(8,128)(2,1)S(1)}, bf16[144,768]{1,0:T(8,128)(2,1)S(1)}, u32[]{:S(2)}, u32[]{:S(2)}) collective-permute-start(bf16[144,768]{1,0:T(8,128)(2,1)S(1)} %get-tuple-element.56), channel_id=1, source_target_pairs={{0,8},{1,9},{8,0},{9,1},{16,24},{17,25},{24,16},{25,17},{2,10},{3,... | collective-permute-start | bytes 663560 | tf_op jit(solution)/shard_map/ppermute | solution.py:623
  7.7 14.2 %collective-permute-start.5 = (bf16[144,768]{1,0:T(8,128)(2,1)S(1)}, bf16[144,768]{1,0:T(8,128)(2,1)S(1)}, u32[]{:S(2)}, u32[]{:S(2)}) collective-permute-start(bf16[144,768]{1,0:T(8,128)(2,1)S(1)} %get-tuple-element.57), channel_id=1, source_target_pairs={{0,9},{1,8},{8,1},{9,0},{16,25},{17,24},{24,17},{25,16},{2,11},{3,... | collective-permute-start | bytes 663560 | tf_op jit(solution)/shard_map/ppermute | solution.py:623
  7.9 14.0 %collective-permute-start.6 = (bf16[144,768]{1,0:T(8,128)(2,1)S(1)}, bf16[144,768]{1,0:T(8,128)(2,1)S(1)}, u32[]{:S(2)}, u32[]{:S(2)}) collective-permute-start(bf16[144,768]{1,0:T(8,128)(2,1)S(1)} %get-tuple-element.58), channel_id=1, source_target_pairs={{0,16},{1,17},{8,24},{9,25},{16,0},{17,1},{24,8},{25,9},{2,18},{3,... | collective-permute-start | bytes 663560 | tf_op jit(solution)/shard_map/ppermute | solution.py:623
  9.8 12.6 %collective-permute-start.7 = (bf16[144,768]{1,0:T(8,128)(2,1)S(1)}, bf16[144,768]{1,0:T(8,128)(2,1)S(1)}, u32[]{:S(2)}, u32[]{:S(2)}) collective-permute-start(bf16[144,768]{1,0:T(8,128)(2,1)S(1)} %get-tuple-element.59), channel_id=1, source_target_pairs={{0,17},{1,16},{8,25},{9,24},{16,1},{17,0},{24,9},{25,8},{2,19},{3,... | collective-permute-start | bytes 663560 | tf_op jit(solution)/shard_map/ppermute | solution.py:623
  14.0 11.2 %collective-permute-start.8 = (bf16[144,768]{1,0:T(8,128)(2,1)S(1)}, bf16[144,768]{1,0:T(8,128)(2,1)S(1)}, u32[]{:S(2)}, u32[]{:S(2)}) collective-permute-start(bf16[144,768]{1,0:T(8,128)(2,1)S(1)} %get-tuple-element.60), channel_id=1, source_target_pairs={{0,24},{1,25},{8,16},{9,17},{16,8},{17,9},{24,0},{25,1},{2,26},{3,... | collective-permute-start | bytes 663560 | tf_op jit(solution)/shard_map/ppermute | solution.py:623
  14.0 15.9 %collective-permute-start.9 = (bf16[144,768]{1,0:T(8,128)(2,1)S(1)}, bf16[144,768]{1,0:T(8,128)(2,1)S(1)}, u32[]{:S(2)}, u32[]{:S(2)}) collective-permute-start(bf16[144,768]{1,0:T(8,128)(2,1)S(1)} %get-tuple-element.61), channel_id=1, source_target_pairs={{0,25},{1,24},{8,17},{9,16},{16,9},{17,8},{24,1},{25,0},{2,27},{3,... | collective-permute-start | bytes 663560 | tf_op jit(solution)/shard_map/ppermute | solution.py:623
  32.6 13.3 %collective-permute-start.10 = (bf16[304,384]{1,0:T(8,128)(2,1)S(1)}, bf16[304,384]{1,0:T(8,128)(2,1)S(1)}, u32[]{:S(2)}, u32[]{:S(2)}) collective-permute-start(bf16[304,384]{1,0:T(8,128)(2,1)S(1)} %get-tuple-element.63), channel_id=1, source_target_pairs={{0,2},{1,3},{8,10},{9,11},{16,18},{17,19},{24,26},{25,27},{2,0},{3... | collective-permute-start | bytes 700424 | tf_op jit(solution)/shard_map/ppermute | solution.py:631
  34.2 19.5 %collective-permute-start.11 = (bf16[304,384]{1,0:T(8,128)(2,1)S(1)}, bf16[304,384]{1,0:T(8,128)(2,1)S(1)}, u32[]{:S(2)}, u32[]{:S(2)}) collective-permute-start(bf16[304,384]{1,0:T(8,128)(2,1)S(1)} %get-tuple-element.64), channel_id=1, source_target_pairs={{0,4},{1,5},{8,12},{9,13},{16,20},{17,21},{24,28},{25,29},{2,6},{3... | collective-permute-start | bytes 700424 | tf_op jit(solution)/shard_map/ppermute | solution.py:631
  36.8 16.9 %collective-permute-start.12 = (bf16[304,384]{1,0:T(8,128)(2,1)S(1)}, bf16[304,384]{1,0:T(8,128)(2,1)S(1)}, u32[]{:S(2)}, u32[]{:S(2)}) collective-permute-start(bf16[304,384]{1,0:T(8,128)(2,1)S(1)} %get-tuple-element.65), channel_id=1, source_target_pairs={{0,6},{1,7},{8,14},{9,15},{16,22},{17,23},{24,30},{25,31},{2,4},{3... | collective-permute-start | bytes 700424 | tf_op jit(solution)/shard_map/ppermute | solution.py:631
  38.4 19.5 %collective-permute-start.16 = (bf16[288,384]{1,0:T(8,128)(2,1)S(1)}, bf16[288,384]{1,0:T(8,128)(2,1)S(1)}, u32[]{:S(2)}, u32[]{:S(2)}) collective-permute-start(bf16[288,384]{1,0:T(8,128)(2,1)S(1)} %get-tuple-element.74), channel_id=1, source_target_pairs={{0,2},{1,3},{8,10},{9,11},{16,18},{17,19},{24,26},{25,27},{2,0},{3... | collective-permute-start | bytes 663560 | tf_op jit(solution)/shard_map/ppermute | solution.py:631
  39.1 33.7 %collective-permute-start.17 = (bf16[288,384]{1,0:T(8,128)(2,1)S(1)}, bf16[288,384]{1,0:T(8,128)(2,1)S(1)}, u32[]{:S(2)}, u32[]{:S(2)}) collective-permute-start(bf16[288,384]{1,0:T(8,128)(2,1)S(1)} %get-tuple-element.75), channel_id=1, source_target_pairs={{0,4},{1,5},{8,12},{9,13},{16,20},{17,21},{24,28},{25,29},{2,6},{3... | collective-permute-start | bytes 663560 | tf_op jit(solution)/shard_map/ppermute | solution.py:631
  45.9 27.0 %collective-permute-start.18 = (bf16[288,384]{1,0:T(8,128)(2,1)S(1)}, bf16[288,384]{1,0:T(8,128)(2,1)S(1)}, u32[]{:S(2)}, u32[]{:S(2)}) collective-permute-start(bf16[288,384]{1,0:T(8,128)(2,1)S(1)} %get-tuple-element.76), channel_id=1, source_target_pairs={{0,6},{1,7},{8,14},{9,15},{16,22},{17,23},{24,30},{25,31},{2,4},{3... | collective-permute-start | bytes 663560 | tf_op jit(solution)/shard_map/ppermute | solution.py:631
  55.8 23.0 %collective-permute-start.13 = (bf16[256,384]{1,0:T(8,128)(2,1)S(1)}, bf16[256,384]{1,0:T(8,128)(2,1)S(1)}, u32[]{:S(2)}, u32[]{:S(2)}) collective-permute-start(bf16[256,384]{1,0:T(8,128)(2,1)S(1)} %get-tuple-element.68), channel_id=1, source_target_pairs={{0,1},{1,0},{8,9},{9,8},{16,17},{17,16},{24,25},{25,24},{2,3},{3,2... | collective-permute-start | bytes 589832 | tf_op jit(solution)/shard_map/ppermute | solution.py:623
  56.4 24.0 %collective-permute-start.14 = (bf16[256,384]{1,0:T(8,128)(2,1)S(1)}, bf16[256,384]{1,0:T(8,128)(2,1)S(1)}, u32[]{:S(2)}, u32[]{:S(2)}) collective-permute-start(bf16[256,384]{1,0:T(8,128)(2,1)S(1)} %get-tuple-element.69), channel_id=1, source_target_pairs={{0,16},{1,17},{8,24},{9,25},{16,0},{17,1},{24,8},{25,9},{2,18},{3,... | collective-permute-start | bytes 589832 | tf_op jit(solution)/shard_map/ppermute | solution.py:623
  57.9 23.8 %collective-permute-start.15 = (bf16[256,384]{1,0:T(8,128)(2,1)S(1)}, bf16[256,384]{1,0:T(8,128)(2,1)S(1)}, u32[]{:S(2)}, u32[]{:S(2)}) collective-permute-start(bf16[256,384]{1,0:T(8,128)(2,1)S(1)} %get-tuple-element.70), channel_id=1, source_target_pairs={{0,17},{1,16},{8,25},{9,24},{16,1},{17,0},{24,9},{25,8},{2,19},{3,... | collective-permute-start | bytes 589832 | tf_op jit(solution)/shard_map/ppermute | solution.py:623
  74.7 7.0 %collective-permute-start.19 = (bf16[256,384]{1,0:T(8,128)(2,1)S(1)}, bf16[256,384]{1,0:T(8,128)(2,1)S(1)}, u32[]{:S(2)}, u32[]{:S(2)}) collective-permute-start(bf16[256,384]{1,0:T(8,128)(2,1)S(1)} %get-tuple-element.78), channel_id=1, source_target_pairs={{0,1},{1,0},{8,9},{9,8},{16,17},{17,16},{24,25},{25,24},{2,3},{3,2... | collective-permute-start | bytes 589832 | tf_op jit(solution)/shard_map/ppermute | solution.py:623
  75.3 12.9 %collective-permute-start.24 = (bf16[256,384]{1,0:T(8,128)(2,1)S(1)}, bf16[256,384]{1,0:T(8,128)(2,1)S(1)}, u32[]{:S(2)}, u32[]{:S(2)}) collective-permute-start(bf16[256,384]{1,0:T(8,128)(2,1)S(1)} %get-tuple-element.81.refs_0_), channel_id=1, source_target_pairs={{0,1},{8,9},{16,17},{24,25},{2,3},{10,11},{18,19},{26,27},{4,5},{1... | collective-permute-start | bytes 589832 | tf_op jit(solution)/shard_map/ppermute | solution.py:640
  78.8 10.2 %collective-permute-start.20 = (bf16[256,384]{1,0:T(8,128)(2,1)S(1)}, bf16[256,384]{1,0:T(8,128)(2,1)S(1)}, u32[]{:S(2)}, u32[]{:S(2)}) collective-permute-start(bf16[256,384]{1,0:T(8,128)(2,1)S(1)} %get-tuple-element.79), channel_id=1, source_target_pairs={{0,16},{1,17},{8,24},{9,25},{16,0},{17,1},{24,8},{25,9},{2,18},{3,... | collective-permute-start | bytes 589832 | tf_op jit(solution)/shard_map/ppermute | solution.py:623
  80.3 11.3 %collective-permute-start.27 = (bf16[256,384]{1,0:T(8,128)(2,1)S(1)}, bf16[256,384]{1,0:T(8,128)(2,1)S(1)}, u32[]{:S(2)}, u32[]{:S(2)}) collective-permute-start(bf16[256,384]{1,0:T(8,128)(2,1)S(1)} %get-tuple-element.82.refs_0_), channel_id=1, source_target_pairs={{0,1},{8,9},{16,17},{24,25},{2,3},{10,11},{18,19},{26,27},{4,5},{1... | collective-permute-start | bytes 589832 | tf_op jit(solution)/shard_map/ppermute | solution.py:640
  81.6 10.9 %collective-permute-start.21 = (bf16[256,384]{1,0:T(8,128)(2,1)S(1)}, bf16[256,384]{1,0:T(8,128)(2,1)S(1)}, u32[]{:S(2)}, u32[]{:S(2)}) collective-permute-start(bf16[256,384]{1,0:T(8,128)(2,1)S(1)} %get-tuple-element.80), channel_id=1, source_target_pairs={{0,17},{1,16},{8,25},{9,24},{16,1},{17,0},{24,9},{25,8},{2,19},{3,... | collective-permute-start | bytes 589832 | tf_op jit(solution)/shard_map/ppermute | solution.py:623
  81.7 11.0 %collective-permute-start.25 = (bf16[256,384]{1,0:T(8,128)(2,1)S(1)}, bf16[256,384]{1,0:T(8,128)(2,1)S(1)}, u32[]{:S(2)}, u32[]{:S(2)}) collective-permute-start(bf16[256,384]{1,0:T(8,128)(2,1)S(1)} %get-tuple-element.81.refs_0_), channel_id=1, source_target_pairs={{17,1},{25,9},{19,3},{27,11},{21,5},{29,13},{23,7},{31,15}} | collective-permute-start | bytes 589832 | tf_op jit(solution)/shard_map/ppermute | solution.py:640
  88.2 5.0 %collective-permute-start.26 = (bf16[256,384]{1,0:T(8,128)(2,1)S(1)}, bf16[256,384]{1,0:T(8,128)(2,1)S(1)}, u32[]{:S(2)}, u32[]{:S(2)}) collective-permute-start(bf16[256,384]{1,0:T(8,128)(2,1)S(1)} %collective-permute-done.24.refs_1_), channel_id=1, source_target_pairs={{17,1},{25,9},{19,3},{27,11},{21,5},{29,13},{23,7},{31,15}} | collective-permute-start | bytes 589832 | tf_op jit(solution)/shard_map/ppermute | solution.py:640
  88.9 4.5 %collective-permute-start.28 = (bf16[256,384]{1,0:T(8,128)(2,1)S(1)}, bf16[256,384]{1,0:T(8,128)(2,1)S(1)}, u32[]{:S(2)}, u32[]{:S(2)}) collective-permute-start(bf16[256,384]{1,0:T(8,128)(2,1)S(1)} %get-tuple-element.82.refs_0_), channel_id=1, source_target_pairs={{17,1},{25,9},{19,3},{27,11},{21,5},{29,13},{23,7},{31,15}} | collective-permute-start | bytes 589832 | tf_op jit(solution)/shard_map/ppermute | solution.py:640
  91.6 1.8 %collective-permute-start.29 = (bf16[256,384]{1,0:T(8,128)(2,1)S(1)}, bf16[256,384]{1,0:T(8,128)(2,1)S(1)}, u32[]{:S(2)}, u32[]{:S(2)}) collective-permute-start(bf16[256,384]{1,0:T(8,128)(2,1)S(1)} %collective-permute-done.27.refs_1_), channel_id=1, source_target_pairs={{17,1},{25,9},{19,3},{27,11},{21,5},{29,13},{23,7},{31,15}} | collective-permute-start | bytes 589832 | tf_op jit(solution)/shard_map/ppermute | solution.py:640
  92.5 2.4 %collective-permute-start.22 = (bf16[1024,384]{1,0:T(8,128)(2,1)S(1)}, bf16[1024,384]{1,0:T(8,128)(2,1)S(1)}, u32[]{:S(2)}, u32[]{:S(2)}) collective-permute-start(bf16[1024,384]{1,0:T(8,128)(2,1)S(1)} %shard_map.51.refs_0_), channel_id=1, source_target_pairs={{0,8},{1,9},{8,0},{9,1},{16,24},{17,25},{24,16},{25,17},{2,10},{3,... | collective-permute-start | bytes 2359304 | tf_op jit(solution)/shard_map/ppermute | solution.py:623
  92.7 3.3 %collective-permute-start.23 = (bf16[1024,384]{1,0:T(8,128)(2,1)S(1)}, bf16[1024,384]{1,0:T(8,128)(2,1)S(1)}, u32[]{:S(2)}, u32[]{:S(2)}) collective-permute-start(bf16[1024,384]{1,0:T(8,128)(2,1)S(1)} %shard_map.54.refs_1_), channel_id=1, source_target_pairs={{0,8},{1,9},{8,0},{9,1},{16,24},{17,25},{24,16},{25,17},{2,10},{3,... | collective-permute-start | bytes 2359304 | tf_op jit(solution)/shard_map/ppermute | solution.py:623
  93.4 3.8 %collective-permute-start.30 = (bf16[1024,384]{1,0:T(8,128)(2,1)S(1)}, bf16[1024,384]{1,0:T(8,128)(2,1)S(1)}, u32[]{:S(2)}, u32[]{:S(2)}) collective-permute-start(bf16[1024,384]{1,0:T(8,128)(2,1)S(1)} %shard_map.55.refs_4_), channel_id=1, source_target_pairs={{0,8},{1,9},{8,0},{9,1},{16,24},{17,25},{24,16},{25,17},{2,10},{3,... | collective-permute-start | bytes 2359304 | tf_op jit(solution)/shard_map/ppermute | solution.py:623
  93.5 36.6 %copy-start = (s32[1024]{0:T(1024)S(1)}, s32[1024]{0:T(1024)}, u32[]{:S(2)}) copy-start(s32[1024]{0:T(1024)} %param.7) | copy-start | bytes 12292
  93.6 38.0 %copy-start.4 = (bf16[1024,768]{1,0:T(8,128)(2,1)S(1)}, bf16[1024,768]{1,0:T(8,128)(2,1)}, u32[]{:S(2)}) copy-start(bf16[1024,768]{1,0:T(8,128)(2,1)} %rows_ref.1) | copy-start | bytes 4718596
  93.6 4.7 %collective-permute-start.31 = (bf16[1024,384]{1,0:T(8,128)(2,1)S(1)}, bf16[1024,384]{1,0:T(8,128)(2,1)S(1)}, u32[]{:S(2)}, u32[]{:S(2)}) collective-permute-start(bf16[1024,384]{1,0:T(8,128)(2,1)S(1)} %shard_map.56.refs_5_), channel_id=1, source_target_pairs={{0,8},{1,9},{8,0},{9,1},{16,24},{17,25},{24,16},{25,17},{2,10},{3,... | collective-permute-start | bytes 2359304 | tf_op jit(solution)/shard_map/ppermute | solution.py:623
  101.7 28.4 %all-to-all-start.3 = ((f32[32,8,128]{2,1,0:T(8,128)}), f32[32,8,128]{2,1,0:T(8,128)S(1)}, u32[]{:S(2)}, u32[]{:S(2)}) async-start(f32[32,8,128]{2,1,0:T(8,128)} %shard_map.57), calls=%async_computation.3 | async-start | bytes 262144 | tf_op jit(solution)/shard_map/all_to_all | solution.py:549
  (3 other events, 42.7 us)

commit v5 on v4

--- a/solution.py
+++ b/solution.py
@@ -10,7 +10,7 @@
 EPSILON = 1e-06
 AXES = ("ingest", "run")
 TILE = 256
-CHUNKS = 2
+SHARES = (1, 1, 1)
 MIB = 1024 * 1024
 
 
@@ -27,7 +27,7 @@
         self.layers, self.lanes = ingest, ingest * self.width
         self.slice = self.cap // self.lanes
         self.part = self.blocks * self.slice
-        self.chunks = tuple(features // CHUNKS for _ in range(CHUNKS))
+        self.chunks = tuple(features * share // sum(SHARES) for share in SHARES)
         mean = rows // self.layers
         self.room = mean + mean // 8
         self.stride = -(-self.room // 128) * 128
@@ -39,7 +39,7 @@
             and self.cap % (8 * self.lanes) == 0
             and self.part == 128
             and self.room % 16 == 0
-            and min(self.chunks) >= self.stride
+            and all(width % 128 == 0 for width in self.chunks)
             and self.links()[1:] == [[0]]
         )
 
@@ -367,9 +367,12 @@
         listed = lax.dot_general(
             values, chosen, (((1,), (1,)), ((), ())), preferred_element_type=jnp.float32
         )
-        line = lax.broadcasted_iota(jnp.int32, (16, plan.stride), 0)
-        table = jnp.where(line == 0, listed[0:1, :], jnp.where(line == 1, full, 0.0))
-        out[plan.room :, : plan.stride] = table.astype(jnp.bfloat16)
+        line = lax.broadcasted_iota(jnp.int32, (16, 128), 0)
+        table = jnp.where(line == 15, full, 0.0)
+        for piece in range(plan.stride // 128):
+            here = listed[0:1, piece * 128 : (piece + 1) * 128]
+            table = jnp.where(line == piece, here, table)
+        out[plan.room :, :128] = table.astype(jnp.bfloat16)
 
 
 def route_more_kernel(plan, target_ref, *refs, chunk):
@@ -392,7 +395,7 @@
             )
 
 
-def sort_parts(plan, target, inputs_ref, outs, ahead_ref, sorted_ref):
+def sort_parts(plan, target, inputs_ref, outs, sorted_ref):
     tile = 2 * plan.part
     for chip, out in enumerate(outs):
         row = lax.broadcasted_iota(jnp.int32, (tile, inputs_ref.shape[0]), 0) + chip * tile
@@ -400,22 +403,25 @@
         moved = jnp.dot(chosen, inputs_ref[...], preferred_element_type=jnp.float32)
         moved = moved.astype(jnp.bfloat16)
         sorted_ref[chip * tile : (chip + 1) * tile, :] = moved
-        out[...] = moved
+        out[:tile, :] = moved
     lane, _ = my_lane(plan)
     chip, _ = chip_change(plan, lane_of(plan, 0) ^ lane)
-    ahead_ref[...] = sorted_ref[pl.ds(pl.multiple_of(chip * tile, tile), tile), :]
+    ahead = sorted_ref[pl.ds(pl.multiple_of(chip * tile, tile), tile), :]
+    for out in outs:
+        out[tile:, :] = ahead
 
 
 def deliver_kernel(plan, *refs):
     ins, rest = refs[: plan.layers], refs[plan.layers :]
-    outs, (ahead_ref, target_ref, full_ref, inputs_ref, sorted_ref) = rest[:-5], rest[-5:]
+    outs, (target_ref, full_ref, inputs_ref, sorted_ref) = rest[:-4], rest[-4:]
     lane, _ = my_lane(plan)
     gather_rows(plan, ins, inputs_ref)
     full = jnp.zeros((8, 128), jnp.float32)
     for number, part in enumerate(ins):
-        table = part[plan.room :, : plan.stride].astype(jnp.float32)
-        value = table[0:1, :].astype(jnp.int32) - 1
-        full = jnp.maximum(full, jnp.broadcast_to(table[1:2, :128], (8, 128)))
+        table = part[plan.room :, :128].astype(jnp.float32)
+        lines = [table[piece : piece + 1, :] for piece in range(plan.stride // 128)]
+        value = jnp.concatenate(lines, axis=1).astype(jnp.int32) - 1
+        full = jnp.maximum(full, jnp.broadcast_to(table[15:, :], (8, 128)))
         slot = value // plan.blocks
         within = lax.broadcasted_iota(jnp.int32, value.shape, 1) % plan.slice
         chip, _ = chip_change(plan, lane_of(plan, slot) ^ lane)
@@ -424,23 +430,22 @@
             value >= 0, target, -1
         )
     full_ref[...] = full.astype(jnp.int32)
-    sort_parts(plan, target_ref[...], inputs_ref, outs, ahead_ref, sorted_ref)
+    sort_parts(plan, target_ref[...], inputs_ref, outs, sorted_ref)
 
 
 def deliver_more_kernel(plan, target_ref, *refs):
     ins, rest = refs[: plan.layers], refs[plan.layers :]
-    outs, (ahead_ref, inputs_ref, sorted_ref) = rest[:-3], rest[-3:]
+    outs, (inputs_ref, sorted_ref) = rest[:-2], rest[-2:]
     gather_rows(plan, ins, inputs_ref)
-    sort_parts(plan, target_ref[...], inputs_ref, outs, ahead_ref, sorted_ref)
+    sort_parts(plan, target_ref[...], inputs_ref, outs, sorted_ref)
 
 
 def join_kernel(plan, *refs):
-    ins, outs = refs[: -(len(refs) // 5)], refs[-(len(refs) // 5) :]
+    ins, outs = refs[:-2], refs[-2:]
     tile = 2 * plan.part
     for number, part in enumerate(ins):
-        out = outs[number // (plan.lanes // 2)]
-        first = number % (plan.lanes // 2) * tile
-        out[first : first + tile, :] = part[...]
+        for half, out in enumerate(outs):
+            out[number * tile : (number + 1) * tile, :] = part[half * tile : (half + 1) * tile, :]
 
 
 def add_best(keys, queries_ref, best_ref, allowed=None):
@@ -452,18 +457,13 @@
     best_ref[...] = jnp.maximum(best_ref[...], jnp.max(scores, axis=0, keepdims=True))
 
 
-def staged_best_kernel(plan, run_len_ref, *refs):
+def pair_best_kernel(plan, *refs):
     count = len(plan.chunks)
-    own, mate, behind, far = (refs[n * count : (n + 1) * count] for n in range(4))
-    out_ref, best_ref, queries_ref, lines_ref = refs[4 * count :]
-    ingest, run = lax.axis_index("ingest"), lax.axis_index("run")
+    own, mate = refs[:count], refs[count : 2 * count]
+    queries_ref, out_ref, best_ref = refs[2 * count :]
     lane, _ = my_lane(plan)
-    group, slot = plan.slot(ingest, run)
+    _, slot = plan.slot(lax.axis_index("ingest"), lax.axis_index("run"))
     core = slot % 2
-    begin = jnp.int32(0)
-    for number, start in enumerate(cluster_starts(plan, run_len_ref)):
-        here = (number // plan.per_group == group) & (start <= slot)
-        begin = jnp.where(here, jnp.maximum(begin, start), begin)
     chips = plan.lanes // 2
     for side, parts in enumerate((own, mate)):
         for chip in range(chips):
@@ -490,19 +490,35 @@
     def _():
         for parts in (own, mate):
             for pair in range(0, chips, 2):
-                keys = [
-                    jnp.concatenate([part[2 * n * plan.part : (2 * n + 1) * plan.part, :] for part in parts], axis=1)
-                    for n in (pair, pair + 1)
-                ]
+                keys = []
+                for number in (pair, pair + 1):
+                    here = slice(2 * number * plan.part, (2 * number + 1) * plan.part)
+                    keys.append(jnp.concatenate([part[here, :] for part in parts], axis=1))
                 add_best(jnp.concatenate(keys, axis=0), queries_ref, best_ref)
 
-    @pl.when(slot - core - 2 >= begin)
+    out_ref[...] = best_ref[...]
+
+
+def more_best_kernel(plan, run_len_ref, given_ref, queries_ref, *refs, last):
+    count = len(plan.chunks)
+    behind, (out_ref, best_ref) = refs[:count], refs[count : count + 2]
+    group, slot = plan.slot(lax.axis_index("ingest"), lax.axis_index("run"))
+    begin = jnp.int32(0)
+    for number, start in enumerate(cluster_starts(plan, run_len_ref)):
+        here = (number // plan.per_group == group) & (start <= slot)
+        begin = jnp.where(here, jnp.maximum(begin, start), begin)
+    best_ref[...] = given_ref[...]
+
+    @pl.when(slot - slot % 2 - 2 >= begin)
     def _():
-        for parts in (behind, far):
-            for first in range(0, plan.rows, TILE):
-                keys = [part[first : first + TILE, :] for part in parts]
-                add_best(jnp.concatenate(keys, axis=1), queries_ref, best_ref)
-
+        for first in range(0, plan.rows, TILE):
+            keys = [part[first : first + TILE, :] for part in behind]
+            add_best(jnp.concatenate(keys, axis=1), queries_ref, best_ref)
+
+    if not last:
+        out_ref[...] = best_ref[...]
+        return
+    lines_ref = refs[-1]
     for number in range(plan.lanes):
         lines_ref[number : number + 1, :] = best_ref[
             :, number * plan.part : (number + 1) * plan.part
@@ -630,15 +646,6 @@
         ]
         return lax.ppermute(block, AXES, pairs)
 
-    def chip_to_chip(block, routes):
-        pairs = [
-            (plan.device(layer, 2 * first + core), plan.device(layer, 2 * second + core))
-            for layer in layers
-            for first, second in routes
-            for core in range(2)
-        ]
-        return lax.ppermute(block, AXES, pairs)
-
     far_first = sorted(lanes, key=lambda change: -(change & 1) - (change // plan.width // 2))
 
     spread = call(
@@ -652,8 +659,9 @@
     )(run_len, clusters, ranks, embeddings)
     swapped = {change: along_lanes(spread[change], change) for change in far_first if change}
     spread = [spread[0]] + [swapped[change] for change in lanes[1:]]
-    owns, mates, behinds, fars = [], [], [], []
+    pair, mates, behind, fars = [], [], [], []
     table = targets = full = None
+    arrivals = []
     for chunk, f in enumerate(plan.chunks):
         spec = dict(flops=2 * rows * rows * f, moved=3 * rows * f * 2, memory=12)
         rooms = [wide((plan.room + (0 if chunk else 16), f), half) for _ in layers]
@@ -677,12 +685,19 @@
             routed = call(more, plan, rooms, [VMEM] * (1 + plan.lanes), [inputs], **spec)(
                 table, *spread
             )
-        far = {change: along_layers(routed[change], change) for change in reversed(layers[1:])}
-        arrived = [routed[0]] + [far[change] for change in layers[1:]]
-        shapes = [wide((2 * plan.part, f), half) for _ in range(plan.lanes // 2 + 1)]
+        moved = {change: along_layers(routed[change], change) for change in reversed(layers[1:])}
+        arrived = [routed[0]] + [moved[change] for change in layers[1:]]
+        arrivals.append(arrived)
+    for chunk, f in enumerate(plan.chunks):
+        spec = dict(flops=2 * rows * rows * f, moved=3 * rows * f * 2, memory=12)
+        inputs = pltpu.VMEM((rows, f), half)
+        arrived = arrivals[chunk]
+        if chunk:
+            arrived, _ = lax.optimization_barrier((arrived, parts))
+        shapes = [wide((4 * plan.part, f), half) for _ in range(plan.lanes // 2)]
         scratch = [pltpu.VMEM((plan.layers * plan.stride, f), half), inputs]
         if chunk == 0:
-            *parts, ahead, targets, full = call(
+            *parts, targets, full = call(
                 deliver_kernel,
                 plan,
                 [
@@ -695,38 +710,46 @@
                 **spec,
             )(*arrived)
         else:
-            *parts, ahead = call(
+            parts = call(
                 deliver_more_kernel, plan, shapes, [VMEM] * (1 + plan.layers), scratch, **spec
             )(targets, *arrived)
-        near = chip_to_chip(ahead, [(0, 1), (3, 2)])
         parts = [
             along_lanes(part, lane_change(plan, chip, 0)) if chip else part
             for chip, part in enumerate(parts)
         ]
-        side = chip_to_chip(ahead, [(2, 1)])
-        corner = chip_to_chip(near, [(2, 1)])
-        spec = dict(moved=4 * rows * f * 2, memory=8)
-        ((own,), (behind,)) = (
-            call(join_kernel, plan, [wide((rows, f), half)], [VMEM] * len(group), **spec)(*group)
-            for group in (parts, (ahead, near, side, corner))
-        )
-        owns.append(own)
-        behinds.append(behind)
-        mates.append(along_lanes(own, plan.width))
-        fars.append(along_lanes(behind, plan.width))
+        spec = dict(moved=8 * rows * f * 2, memory=8)
+        joined = call(
+            join_kernel, plan, [wide((rows, f), half)] * 2, [VMEM] * len(parts), **spec
+        )(*parts)
+        for kept, block in zip((pair, behind), joined):
+            kept.append(block)
+        for kept, block in zip((mates, fars), joined):
+            kept.append(along_lanes(block, plan.width))
+    line = wide((1, rows), jnp.float32)
+    kept = pltpu.VMEM((1, rows), jnp.float32)
+    count = len(plan.chunks)
+    spec = dict(flops=4 * rows * rows * width, moved=3 * rows * width * 2, memory=24)
+    queries, best = call(
+        pair_best_kernel,
+        plan,
+        [wide((rows, width), half), line],
+        [VMEM] * (2 * count),
+        [kept],
+        **spec,
+    )(*pair, *mates)
+    spec = dict(flops=2 * rows * rows * width, moved=3 * rows * width * 2, memory=24)
+    places = [SMEM] + [VMEM] * (2 + count)
+    (best,) = call(
+        functools.partial(more_best_kernel, last=False), plan, [line], places, [kept], **spec
+    )(run_len, best, queries, *behind)
     (replies,) = call(
-        staged_best_kernel,
+        functools.partial(more_best_kernel, last=True),
         plan,
         [wide((plan.devices, plan.lanes, 128), jnp.float32)],
-        [SMEM] + [VMEM] * (4 * len(plan.chunks)),
-        [
-            pltpu.VMEM((1, rows), jnp.float32),
-            pltpu.VMEM((rows, width), half),
-            pltpu.VMEM((plan.lanes, 128), jnp.float32),
-        ],
-        2 * rows * rows * width * 3,
-        4 * rows * width * 2,
-    )(run_len, *owns, *mates, *behinds, *fars)
+        places,
+        [kept, pltpu.VMEM((plan.lanes, 128), jnp.float32)],
+        **spec,
+    )(run_len, best, queries, *fars)
     returned = exchange(replies).reshape(plan.devices * plan.lanes, 128)
     (best,) = call(
         staged_unpack_kernel,

time: 132 us -> 125 us (0.947)
  starting transfers between devices: 56.3 us -> 50.3 us
    all_to_all x1, starting transfers between devices: 20.7 us -> 12.2 us  [exchange(): return lax.all_to_all(block, AXES, split_axis=0, concat_axis=0, tiled=True)]
    ppermute x6 -> x0, waiting for transfers between devices: 7.86 us -> none  [chip_to_chip(): return lax.ppermute(block, AXES, pairs)]
    ppermute x6 -> x0, starting transfers between devices: 7.54 us -> none  [chip_to_chip(): return lax.ppermute(block, AXES, pairs)]
    ppermute x17 -> x22, starting transfers between devices: 16.9 us -> 22.2 us  [along_lanes(): return lax.ppermute(block, AXES, pairs)]
    ppermute x6 -> x9, starting transfers between devices: 11.2 us -> 15.9 us  [along_layers(): return lax.ppermute(block, AXES, pairs)]
    ppermute x6 -> x9, waiting for transfers between devices: 22 us -> 25.6 us  [along_layers(): return lax.ppermute(block, AXES, pairs)]
    ppermute x17 -> x22, waiting for transfers between devices: 19.5 us -> 22.6 us  [along_lanes(): return lax.ppermute(block, AXES, pairs)]
    pallas_call x5 -> x6, Pallas kernels: 3.69 us -> 4.52 us  [the longest x1 2.4 us: staged(): call(pair_best_kernel, plan, [wide((rows, width), half), line], [VMEM] *...]
  transfers between devices with their start and end apart: 30 -> 32, of which waited for: 15 -> 13; matrix products, arithmetic and copies ran while one was open for 0% -> 0% of each run, Pallas kernels for 4% -> 6%
where the time goes in v5:
time: 125 us
  waiting for transfers between devices  54.9 us (44%)
  starting transfers between devices  50.3 us (40%)
  Pallas kernels  17.6 us (14%)
    ppermute x9, waiting for transfers between devices, along_layers(): return lax.ppermute(block, AXES, pairs)  25.6 us
    ppermute x22, waiting for transfers between devices, along_lanes(): return lax.ppermute(block, AXES, pairs)  22.6 us
    ppermute x22, starting transfers between devices, along_lanes(): return lax.ppermute(block, AXES, pairs)  22.2 us
    ppermute x9, starting transfers between devices, along_layers(): return lax.ppermute(block, AXES, pairs)  15.9 us
    all_to_all x1, starting transfers between devices, exchange(): return lax.all_to_all(block, AXES, split_axis=0, concat_axis=0, tiled=True)  12.2 us
    all_to_all x1, waiting for transfers between devices, exchange(): return lax.all_to_all(block, AXES, split_axis=0, concat_axis=0, tiled=True)  6.57 us
    pallas_call x1, Pallas kernels, staged(): call(spread_kernel, plan, [wide((plan.part + 16, width), half) for _ in l...  4.66 us
  transfers between devices with their start and end apart: 32, of which 13 were waited for; matrix products, arithmetic and copies ran while one was open for 0% of the time, Pallas kernels for 6%

profile of v5, /device:TPU:0, one launch (start us, length us, event | category | flops | bytes accessed | tf_op | source)
XLA Modules:
  0.0 124.8 jit_solution(12050061570350254017)
XLA Ops:
  0.0 4.7 %shard_map.48 = (bf16[144,768]{1,0:T(8,128)(2,1)S(1)}, bf16[144,768]{1,0:T(8,128)(2,1)S(1)}, bf16[144,768]{1,0:T(8,128)(2,1)S(1)}, bf16[144,768]{1,0:T(8,128)(2,...) custom-call(s32[12]{0:T(128)} %run_len_ref.7, ...), custom_call_target="tpu_custom_call" | custom-call | flops 1610612736 | bytes 4718592 | tf_op jit(solution)/shard_map/pallas_call | solution.py:651
  4.7 3.0 %collective-permute-start.3 = (bf16[144,768]{1,0:T(8,128)(2,1)S(1)}, bf16[144,768]{1,0:T(8,128)(2,1)S(1)}, u32[]{:S(2)}, u32[]{:S(2)}) collective-permute-start(bf16[144,768]{1,0:T(8,128)(2,1)S(1)} %get-tuple-element.77), channel_id=1, source_target_pairs={{0,1},{1,0},{8,9},{9,8},{16,17},{17,16},{24,25},{25,24},{2,3},{3,2... | collective-permute-start | bytes 663560 | tf_op jit(solution)/shard_map/ppermute | solution.py:639
  7.9 1.9 %collective-permute-start.6 = (bf16[144,768]{1,0:T(8,128)(2,1)S(1)}, bf16[144,768]{1,0:T(8,128)(2,1)S(1)}, u32[]{:S(2)}, u32[]{:S(2)}) collective-permute-start(bf16[144,768]{1,0:T(8,128)(2,1)S(1)} %get-tuple-element.80), channel_id=1, source_target_pairs={{0,16},{1,17},{8,24},{9,25},{16,0},{17,1},{24,8},{25,9},{2,18},{3,... | collective-permute-start | bytes 663560 | tf_op jit(solution)/shard_map/ppermute | solution.py:639
  9.8 1.5 %collective-permute-start.7 = (bf16[144,768]{1,0:T(8,128)(2,1)S(1)}, bf16[144,768]{1,0:T(8,128)(2,1)S(1)}, u32[]{:S(2)}, u32[]{:S(2)}) collective-permute-start(bf16[144,768]{1,0:T(8,128)(2,1)S(1)} %get-tuple-element.81), channel_id=1, source_target_pairs={{0,17},{1,16},{8,25},{9,24},{16,1},{17,0},{24,9},{25,8},{2,19},{3,... | collective-permute-start | bytes 663560 | tf_op jit(solution)/shard_map/ppermute | solution.py:639
  11.3 2.7 %collective-permute-done.3.refs_1_ = bf16[144,768]{1,0:T(8,128)(2,1)S(1)} collective-permute-done((bf16[144,768]{1,0:T(8,128)(2,1)S(1)}, bf16[144,768]{1,0:T(8,128)(2,1)S(1)}, u32[]{:S(2)}, u32[]{:S(2)}) %collective-permute-start.3) | collective-permute-done | bytes 221216 | tf_op jit(solution)/shard_map/ppermute | solution.py:639
  14.0 3.2 %collective-permute-start.9 = (bf16[144,768]{1,0:T(8,128)(2,1)S(1)}, bf16[144,768]{1,0:T(8,128)(2,1)S(1)}, u32[]{:S(2)}, u32[]{:S(2)}) collective-permute-start(bf16[144,768]{1,0:T(8,128)(2,1)S(1)} %get-tuple-element.83), channel_id=1, source_target_pairs={{0,25},{1,24},{8,17},{9,16},{16,9},{17,8},{24,1},{25,0},{2,27},{3,... | collective-permute-start | bytes 663560 | tf_op jit(solution)/shard_map/ppermute | solution.py:639
  17.2 4.7 %collective-permute-done.5.refs_3_ = bf16[144,768]{1,0:T(8,128)(2,1)S(1)} collective-permute-done((bf16[144,768]{1,0:T(8,128)(2,1)S(1)}, bf16[144,768]{1,0:T(8,128)(2,1)S(1)}, u32[]{:S(2)}, u32[]{:S(2)}) %collective-permute-start.5) | collective-permute-done | bytes 221216 | tf_op jit(solution)/shard_map/ppermute | solution.py:639
  22.4 2.8 %collective-permute-done.8.refs_6_ = bf16[144,768]{1,0:T(8,128)(2,1)S(1)} collective-permute-done((bf16[144,768]{1,0:T(8,128)(2,1)S(1)}, bf16[144,768]{1,0:T(8,128)(2,1)S(1)}, u32[]{:S(2)}, u32[]{:S(2)}) %collective-permute-start.8) | collective-permute-done | bytes 221216 | tf_op jit(solution)/shard_map/ppermute | solution.py:639
  25.1 4.8 %collective-permute-done.9.refs_7_ = bf16[144,768]{1,0:T(8,128)(2,1)S(1)} collective-permute-done((bf16[144,768]{1,0:T(8,128)(2,1)S(1)}, bf16[144,768]{1,0:T(8,128)(2,1)S(1)}, u32[]{:S(2)}, u32[]{:S(2)}) %collective-permute-start.9) | collective-permute-done | bytes 221216 | tf_op jit(solution)/shard_map/ppermute | solution.py:639
  29.9 2.2 %shard_map.49 = (bf16[304,256]{1,0:T(8,128)(2,1)S(1)}, bf16[304,256]{1,0:T(8,128)(2,1)S(1)}, bf16[304,256]{1,0:T(8,128)(2,1)S(1)}, bf16[304,256]{1,0:T(8,128)(2,1)S(1)}, s32[1,1024]{1,0:T(1,128)S(1)}) custom-call(bf16[144,768]{1,0:T(8,128)(2,1)S(1)} %get-tuple-element.76.refs_0_, bf16[144,768]{1,0:T(8,128)(2,1)S(1)} %collective-permute-done.3.refs_1_, ...), custom_call_target="tpu_custom_call" | custom-call | flops 536870912 | bytes 1572864 | tf_op jit(solution)/shard_map/pallas_call | solution.py:670
  32.1 1.6 %collective-permute-start.10 = (bf16[304,256]{1,0:T(8,128)(2,1)S(1)}, bf16[304,256]{1,0:T(8,128)(2,1)S(1)}, u32[]{:S(2)}, u32[]{:S(2)}) collective-permute-start(bf16[304,256]{1,0:T(8,128)(2,1)S(1)} %get-tuple-element.85), channel_id=1, source_target_pairs={{0,2},{1,3},{8,10},{9,11},{16,18},{17,19},{24,26},{25,27},{2,0},{3... | collective-permute-start | bytes 466952 | tf_op jit(solution)/shard_map/ppermute | solution.py:647
  33.7 2.6 %collective-permute-start.11 = (bf16[304,256]{1,0:T(8,128)(2,1)S(1)}, bf16[304,256]{1,0:T(8,128)(2,1)S(1)}, u32[]{:S(2)}, u32[]{:S(2)}) collective-permute-start(bf16[304,256]{1,0:T(8,128)(2,1)S(1)} %get-tuple-element.86), channel_id=1, source_target_pairs={{0,4},{1,5},{8,12},{9,13},{16,20},{17,21},{24,28},{25,29},{2,6},{3... | collective-permute-start | bytes 466952 | tf_op jit(solution)/shard_map/ppermute | solution.py:647
  38.1 4.1 %collective-permute-done.10.refs_1_ = bf16[304,256]{1,0:T(8,128)(2,1)S(1)} collective-permute-done((bf16[304,256]{1,0:T(8,128)(2,1)S(1)}, bf16[304,256]{1,0:T(8,128)(2,1)S(1)}, u32[]{:S(2)}, u32[]{:S(2)}) %collective-permute-start.10) | collective-permute-done | bytes 155680 | tf_op jit(solution)/shard_map/ppermute | solution.py:647
  42.1 6.1 %collective-permute-done.11.refs_2_ = bf16[304,256]{1,0:T(8,128)(2,1)S(1)} collective-permute-done((bf16[304,256]{1,0:T(8,128)(2,1)S(1)}, bf16[304,256]{1,0:T(8,128)(2,1)S(1)}, u32[]{:S(2)}, u32[]{:S(2)}) %collective-permute-start.11) | collective-permute-done | bytes 155680 | tf_op jit(solution)/shard_map/ppermute | solution.py:647
  50.0 1.5 %collective-permute-start.14 = (bf16[512,256]{1,0:T(8,128)(2,1)S(1)}, bf16[512,256]{1,0:T(8,128)(2,1)S(1)}, u32[]{:S(2)}, u32[]{:S(2)}) collective-permute-start(bf16[512,256]{1,0:T(8,128)(2,1)S(1)} %get-tuple-element.91), channel_id=1, source_target_pairs={{0,16},{1,17},{8,24},{9,25},{16,0},{17,1},{24,8},{25,9},{2,18},{3,... | collective-permute-start | bytes 786440 | tf_op jit(solution)/shard_map/ppermute | solution.py:639
  51.5 1.5 %collective-permute-start.15 = (bf16[512,256]{1,0:T(8,128)(2,1)S(1)}, bf16[512,256]{1,0:T(8,128)(2,1)S(1)}, u32[]{:S(2)}, u32[]{:S(2)}) collective-permute-start(bf16[512,256]{1,0:T(8,128)(2,1)S(1)} %get-tuple-element.92), channel_id=1, source_target_pairs={{0,17},{1,16},{8,25},{9,24},{16,1},{17,0},{24,9},{25,8},{2,19},{3,... | collective-permute-start | bytes 786440 | tf_op jit(solution)/shard_map/ppermute | solution.py:639
  53.0 4.5 %collective-permute-start.17 = (bf16[288,256]{1,0:T(8,128)(2,1)S(1)}, bf16[288,256]{1,0:T(8,128)(2,1)S(1)}, u32[]{:S(2)}, u32[]{:S(2)}) collective-permute-start(bf16[288,256]{1,0:T(8,128)(2,1)S(1)} %get-tuple-element.98), channel_id=1, source_target_pairs={{0,4},{1,5},{8,12},{9,13},{16,20},{17,21},{24,28},{25,29},{2,6},{3... | collective-permute-start | bytes 442376 | tf_op jit(solution)/shard_map/ppermute | solution.py:647
  57.5 1.4 %collective-permute-start.18 = (bf16[288,256]{1,0:T(8,128)(2,1)S(1)}, bf16[288,256]{1,0:T(8,128)(2,1)S(1)}, u32[]{:S(2)}, u32[]{:S(2)}) collective-permute-start(bf16[288,256]{1,0:T(8,128)(2,1)S(1)} %get-tuple-element.99), channel_id=1, source_target_pairs={{0,6},{1,7},{8,14},{9,15},{16,22},{17,23},{24,30},{25,31},{2,4},{3... | collective-permute-start | bytes 442376 | tf_op jit(solution)/shard_map/ppermute | solution.py:647
  59.6 8.3 %collective-permute-done.17.refs_2_ = bf16[288,256]{1,0:T(8,128)(2,1)S(1)} collective-permute-done((bf16[288,256]{1,0:T(8,128)(2,1)S(1)}, bf16[288,256]{1,0:T(8,128)(2,1)S(1)}, u32[]{:S(2)}, u32[]{:S(2)}) %collective-permute-start.17) | collective-permute-done | bytes 147488 | tf_op jit(solution)/shard_map/ppermute | solution.py:647
  69.5 1.5 %collective-permute-start.20 = (bf16[512,256]{1,0:T(8,128)(2,1)S(1)}, bf16[512,256]{1,0:T(8,128)(2,1)S(1)}, u32[]{:S(2)}, u32[]{:S(2)}) collective-permute-start(bf16[512,256]{1,0:T(8,128)(2,1)S(1)} %get-tuple-element.106), channel_id=1, source_target_pairs={{0,16},{1,17},{8,24},{9,25},{16,0},{17,1},{24,8},{25,9},{2,18},{3,... | collective-permute-start | bytes 786440 | tf_op jit(solution)/shard_map/ppermute | solution.py:639
  71.1 1.5 %collective-permute-start.21 = (bf16[512,256]{1,0:T(8,128)(2,1)S(1)}, bf16[512,256]{1,0:T(8,128)(2,1)S(1)}, u32[]{:S(2)}, u32[]{:S(2)}) collective-permute-start(bf16[512,256]{1,0:T(8,128)(2,1)S(1)} %get-tuple-element.107), channel_id=1, source_target_pairs={{0,17},{1,16},{8,25},{9,24},{16,1},{17,0},{24,9},{25,8},{2,19},{3,... | collective-permute-start | bytes 786440 | tf_op jit(solution)/shard_map/ppermute | solution.py:639
  72.5 2.4 %collective-permute-start.23 = (bf16[288,256]{1,0:T(8,128)(2,1)S(1)}, bf16[288,256]{1,0:T(8,128)(2,1)S(1)}, u32[]{:S(2)}, u32[]{:S(2)}) collective-permute-start(bf16[288,256]{1,0:T(8,128)(2,1)S(1)} %get-tuple-element.111), channel_id=1, source_target_pairs={{0,4},{1,5},{8,12},{9,13},{16,20},{17,21},{24,28},{25,29},{2,6},{3... | collective-permute-start | bytes 442376 | tf_op jit(solution)/shard_map/ppermute | solution.py:647
  75.0 2.4 %collective-permute-start.24 = (bf16[288,256]{1,0:T(8,128)(2,1)S(1)}, bf16[288,256]{1,0:T(8,128)(2,1)S(1)}, u32[]{:S(2)}, u32[]{:S(2)}) collective-permute-start(bf16[288,256]{1,0:T(8,128)(2,1)S(1)} %get-tuple-element.112), channel_id=1, source_target_pairs={{0,6},{1,7},{8,14},{9,15},{16,22},{17,23},{24,30},{25,31},{2,4},{3... | collective-permute-start | bytes 442376 | tf_op jit(solution)/shard_map/ppermute | solution.py:647
  77.4 7.2 %collective-permute-done.23.refs_2_ = bf16[288,256]{1,0:T(8,128)(2,1)S(1)} collective-permute-done((bf16[288,256]{1,0:T(8,128)(2,1)S(1)}, bf16[288,256]{1,0:T(8,128)(2,1)S(1)}, u32[]{:S(2)}, u32[]{:S(2)}) %collective-permute-start.23) | collective-permute-done | bytes 147488 | tf_op jit(solution)/shard_map/ppermute | solution.py:647
  86.1 1.6 %collective-permute-start.26 = (bf16[512,256]{1,0:T(8,128)(2,1)S(1)}, bf16[512,256]{1,0:T(8,128)(2,1)S(1)}, u32[]{:S(2)}, u32[]{:S(2)}) collective-permute-start(bf16[512,256]{1,0:T(8,128)(2,1)S(1)} %get-tuple-element.119), channel_id=1, source_target_pairs={{0,16},{1,17},{8,24},{9,25},{16,0},{17,1},{24,8},{25,9},{2,18},{3,... | collective-permute-start | bytes 786440 | tf_op jit(solution)/shard_map/ppermute | solution.py:639
  87.7 1.5 %collective-permute-start.27 = (bf16[512,256]{1,0:T(8,128)(2,1)S(1)}, bf16[512,256]{1,0:T(8,128)(2,1)S(1)}, u32[]{:S(2)}, u32[]{:S(2)}) collective-permute-start(bf16[512,256]{1,0:T(8,128)(2,1)S(1)} %get-tuple-element.120), channel_id=1, source_target_pairs={{0,17},{1,16},{8,25},{9,24},{16,1},{17,0},{24,9},{25,8},{2,19},{3,... | collective-permute-start | bytes 786440 | tf_op jit(solution)/shard_map/ppermute | solution.py:639
  90.0 2.6 %collective-permute-done.25.refs_1_ = bf16[512,256]{1,0:T(8,128)(2,1)S(1)} collective-permute-done((bf16[512,256]{1,0:T(8,128)(2,1)S(1)}, bf16[512,256]{1,0:T(8,128)(2,1)S(1)}, u32[]{:S(2)}, u32[]{:S(2)}) %collective-permute-start.25) | collective-permute-done | bytes 262176 | tf_op jit(solution)/shard_map/ppermute | solution.py:639
  92.6 3.8 %collective-permute-done.27.refs_3_ = bf16[512,256]{1,0:T(8,128)(2,1)S(1)} collective-permute-done((bf16[512,256]{1,0:T(8,128)(2,1)S(1)}, bf16[512,256]{1,0:T(8,128)(2,1)S(1)}, u32[]{:S(2)}, u32[]{:S(2)}) %collective-permute-start.27) | collective-permute-done | bytes 262176 | tf_op jit(solution)/shard_map/ppermute | solution.py:639
  98.4 2.4 %shard_map.58 = (bf16[1024,768]{1,0:T(8,128)(2,1)S(1)}, f32[1,1024]{1,0:T(1,128)S(1)}) custom-call(bf16[1024,256]{1,0:T(8,128)(2,1)S(1)} %get-tuple-element.93.refs_0_, bf16[1024,256]{1,0:T(8,128)(2,1)S(1)} %get-tuple-element.108.refs_1_, bf16[1024,256]{1,0:T(8,128)(2,1)S(1)} %get-tuple-element.121.refs_2_, ...), custom_call_target="tpu_custom_call" | custom-call | flops 3221225472 | bytes 4718592 | tf_op jit(solution)/shard_map/pallas_call | solution.py:732
  102.8 12.2 %all-to-all-start.3 = ((f32[32,8,128]{2,1,0:T(8,128)}), f32[32,8,128]{2,1,0:T(8,128)S(1)}, u32[]{:S(2)}, u32[]{:S(2)}) async-start(f32[32,8,128]{2,1,0:T(8,128)} %shard_map.60), calls=%async_computation.3 | async-start | bytes 262144 | tf_op jit(solution)/shard_map/all_to_all | solution.py:565
  116.2 6.6 %all-to-all-done.3 = f32[32,8,128]{2,1,0:T(8,128)S(1)} async-done(((f32[32,8,128]{2,1,0:T(8,128)}), f32[32,8,128]{2,1,0:T(8,128)S(1)}, u32[]{:S(2)}, u32[]{:S(2)}) %all-to-all-start.3) | async-done | bytes 131104 | tf_op jit(solution)/shard_map/all_to_all | solution.py:565
  122.7 1.4 %shard_map.61 = f32[1,1024]{1,0:T(1,128)S(1)} custom-call(s32[12]{0:T(128)S(1)} %copy-done.3, s32[1,1024]{1,0:T(1,128)S(1)} %bitcast.27, s32[1,1024]{1,0:T(1,128)S(1)} %bitcast.30, f32[256,128]{1,0:T(8,128)S(1)} %bitcast.20), custom_call_target="tpu_custom_call" | custom-call | bytes 16384 | tf_op jit(solution)/shard_map/pallas_call | solution.py:754
  (58 shorter events, 14.0 us)
Async XLA Ops:
  4.7 9.3 %collective-permute-start.3 = (bf16[144,768]{1,0:T(8,128)(2,1)S(1)}, bf16[144,768]{1,0:T(8,128)(2,1)S(1)}, u32[]{:S(2)}, u32[]{:S(2)}) collective-permute-start(bf16[144,768]{1,0:T(8,128)(2,1)S(1)} %get-tuple-element.77), channel_id=1, source_target_pairs={{0,1},{1,0},{8,9},{9,8},{16,17},{17,16},{24,25},{25,24},{2,3},{3,2... | collective-permute-start | bytes 663560 | tf_op jit(solution)/shard_map/ppermute | solution.py:639
  7.7 6.3 %collective-permute-start.4 = (bf16[144,768]{1,0:T(8,128)(2,1)S(1)}, bf16[144,768]{1,0:T(8,128)(2,1)S(1)}, u32[]{:S(2)}, u32[]{:S(2)}) collective-permute-start(bf16[144,768]{1,0:T(8,128)(2,1)S(1)} %get-tuple-element.78), channel_id=1, source_target_pairs={{0,8},{1,9},{8,0},{9,1},{16,24},{17,25},{24,16},{25,17},{2,10},{3,... | collective-permute-start | bytes 663560 | tf_op jit(solution)/shard_map/ppermute | solution.py:639
  7.7 14.2 %collective-permute-start.5 = (bf16[144,768]{1,0:T(8,128)(2,1)S(1)}, bf16[144,768]{1,0:T(8,128)(2,1)S(1)}, u32[]{:S(2)}, u32[]{:S(2)}) collective-permute-start(bf16[144,768]{1,0:T(8,128)(2,1)S(1)} %get-tuple-element.79), channel_id=1, source_target_pairs={{0,9},{1,8},{8,1},{9,0},{16,25},{17,24},{24,17},{25,16},{2,11},{3,... | collective-permute-start | bytes 663560 | tf_op jit(solution)/shard_map/ppermute | solution.py:639
  7.9 14.0 %collective-permute-start.6 = (bf16[144,768]{1,0:T(8,128)(2,1)S(1)}, bf16[144,768]{1,0:T(8,128)(2,1)S(1)}, u32[]{:S(2)}, u32[]{:S(2)}) collective-permute-start(bf16[144,768]{1,0:T(8,128)(2,1)S(1)} %get-tuple-element.80), channel_id=1, source_target_pairs={{0,16},{1,17},{8,24},{9,25},{16,0},{17,1},{24,8},{25,9},{2,18},{3,... | collective-permute-start | bytes 663560 | tf_op jit(solution)/shard_map/ppermute | solution.py:639
  9.8 12.6 %collective-permute-start.7 = (bf16[144,768]{1,0:T(8,128)(2,1)S(1)}, bf16[144,768]{1,0:T(8,128)(2,1)S(1)}, u32[]{:S(2)}, u32[]{:S(2)}) collective-permute-start(bf16[144,768]{1,0:T(8,128)(2,1)S(1)} %get-tuple-element.81), channel_id=1, source_target_pairs={{0,17},{1,16},{8,25},{9,24},{16,1},{17,0},{24,9},{25,8},{2,19},{3,... | collective-permute-start | bytes 663560 | tf_op jit(solution)/shard_map/ppermute | solution.py:639
  14.0 11.2 %collective-permute-start.8 = (bf16[144,768]{1,0:T(8,128)(2,1)S(1)}, bf16[144,768]{1,0:T(8,128)(2,1)S(1)}, u32[]{:S(2)}, u32[]{:S(2)}) collective-permute-start(bf16[144,768]{1,0:T(8,128)(2,1)S(1)} %get-tuple-element.82), channel_id=1, source_target_pairs={{0,24},{1,25},{8,16},{9,17},{16,8},{17,9},{24,0},{25,1},{2,26},{3,... | collective-permute-start | bytes 663560 | tf_op jit(solution)/shard_map/ppermute | solution.py:639
  14.0 15.9 %collective-permute-start.9 = (bf16[144,768]{1,0:T(8,128)(2,1)S(1)}, bf16[144,768]{1,0:T(8,128)(2,1)S(1)}, u32[]{:S(2)}, u32[]{:S(2)}) collective-permute-start(bf16[144,768]{1,0:T(8,128)(2,1)S(1)} %get-tuple-element.83), channel_id=1, source_target_pairs={{0,25},{1,24},{8,17},{9,16},{16,9},{17,8},{24,1},{25,0},{2,27},{3,... | collective-permute-start | bytes 663560 | tf_op jit(solution)/shard_map/ppermute | solution.py:639
  32.1 10.0 %collective-permute-start.10 = (bf16[304,256]{1,0:T(8,128)(2,1)S(1)}, bf16[304,256]{1,0:T(8,128)(2,1)S(1)}, u32[]{:S(2)}, u32[]{:S(2)}) collective-permute-start(bf16[304,256]{1,0:T(8,128)(2,1)S(1)} %get-tuple-element.85), channel_id=1, source_target_pairs={{0,2},{1,3},{8,10},{9,11},{16,18},{17,19},{24,26},{25,27},{2,0},{3... | collective-permute-start | bytes 466952 | tf_op jit(solution)/shard_map/ppermute | solution.py:647
  33.7 14.5 %collective-permute-start.11 = (bf16[304,256]{1,0:T(8,128)(2,1)S(1)}, bf16[304,256]{1,0:T(8,128)(2,1)S(1)}, u32[]{:S(2)}, u32[]{:S(2)}) collective-permute-start(bf16[304,256]{1,0:T(8,128)(2,1)S(1)} %get-tuple-element.86), channel_id=1, source_target_pairs={{0,4},{1,5},{8,12},{9,13},{16,20},{17,21},{24,28},{25,29},{2,6},{3... | collective-permute-start | bytes 466952 | tf_op jit(solution)/shard_map/ppermute | solution.py:647
  36.3 11.9 %collective-permute-start.12 = (bf16[304,256]{1,0:T(8,128)(2,1)S(1)}, bf16[304,256]{1,0:T(8,128)(2,1)S(1)}, u32[]{:S(2)}, u32[]{:S(2)}) collective-permute-start(bf16[304,256]{1,0:T(8,128)(2,1)S(1)} %get-tuple-element.87), channel_id=1, source_target_pairs={{0,6},{1,7},{8,14},{9,15},{16,22},{17,23},{24,30},{25,31},{2,4},{3... | collective-permute-start | bytes 466952 | tf_op jit(solution)/shard_map/ppermute | solution.py:647
  37.3 20.2 %collective-permute-start.16 = (bf16[288,256]{1,0:T(8,128)(2,1)S(1)}, bf16[288,256]{1,0:T(8,128)(2,1)S(1)}, u32[]{:S(2)}, u32[]{:S(2)}) collective-permute-start(bf16[288,256]{1,0:T(8,128)(2,1)S(1)} %get-tuple-element.97), channel_id=1, source_target_pairs={{0,2},{1,3},{8,10},{9,11},{16,18},{17,19},{24,26},{25,27},{2,0},{3... | collective-permute-start | bytes 442376 | tf_op jit(solution)/shard_map/ppermute | solution.py:647
  49.4 18.5 %collective-permute-start.13 = (bf16[512,256]{1,0:T(8,128)(2,1)S(1)}, bf16[512,256]{1,0:T(8,128)(2,1)S(1)}, u32[]{:S(2)}, u32[]{:S(2)}) collective-permute-start(bf16[512,256]{1,0:T(8,128)(2,1)S(1)} %get-tuple-element.90), channel_id=1, source_target_pairs={{0,1},{1,0},{8,9},{9,8},{16,17},{17,16},{24,25},{25,24},{2,3},{3,2... | collective-permute-start | bytes 786440 | tf_op jit(solution)/shard_map/ppermute | solution.py:639
  50.0 17.9 %collective-permute-start.14 = (bf16[512,256]{1,0:T(8,128)(2,1)S(1)}, bf16[512,256]{1,0:T(8,128)(2,1)S(1)}, u32[]{:S(2)}, u32[]{:S(2)}) collective-permute-start(bf16[512,256]{1,0:T(8,128)(2,1)S(1)} %get-tuple-element.91), channel_id=1, source_target_pairs={{0,16},{1,17},{8,24},{9,25},{16,0},{17,1},{24,8},{25,9},{2,18},{3,... | collective-permute-start | bytes 786440 | tf_op jit(solution)/shard_map/ppermute | solution.py:639
  51.5 16.5 %collective-permute-start.15 = (bf16[512,256]{1,0:T(8,128)(2,1)S(1)}, bf16[512,256]{1,0:T(8,128)(2,1)S(1)}, u32[]{:S(2)}, u32[]{:S(2)}) collective-permute-start(bf16[512,256]{1,0:T(8,128)(2,1)S(1)} %get-tuple-element.92), channel_id=1, source_target_pairs={{0,17},{1,16},{8,25},{9,24},{16,1},{17,0},{24,9},{25,8},{2,19},{3,... | collective-permute-start | bytes 786440 | tf_op jit(solution)/shard_map/ppermute | solution.py:639
  53.0 15.0 %collective-permute-start.17 = (bf16[288,256]{1,0:T(8,128)(2,1)S(1)}, bf16[288,256]{1,0:T(8,128)(2,1)S(1)}, u32[]{:S(2)}, u32[]{:S(2)}) collective-permute-start(bf16[288,256]{1,0:T(8,128)(2,1)S(1)} %get-tuple-element.98), channel_id=1, source_target_pairs={{0,4},{1,5},{8,12},{9,13},{16,20},{17,21},{24,28},{25,29},{2,6},{3... | collective-permute-start | bytes 442376 | tf_op jit(solution)/shard_map/ppermute | solution.py:647
  57.5 10.5 %collective-permute-start.18 = (bf16[288,256]{1,0:T(8,128)(2,1)S(1)}, bf16[288,256]{1,0:T(8,128)(2,1)S(1)}, u32[]{:S(2)}, u32[]{:S(2)}) collective-permute-start(bf16[288,256]{1,0:T(8,128)(2,1)S(1)} %get-tuple-element.99), channel_id=1, source_target_pairs={{0,6},{1,7},{8,14},{9,15},{16,22},{17,23},{24,30},{25,31},{2,4},{3... | collective-permute-start | bytes 442376 | tf_op jit(solution)/shard_map/ppermute | solution.py:647
  67.9 7.0 %collective-permute-start.22 = (bf16[288,256]{1,0:T(8,128)(2,1)S(1)}, bf16[288,256]{1,0:T(8,128)(2,1)S(1)}, u32[]{:S(2)}, u32[]{:S(2)}) collective-permute-start(bf16[288,256]{1,0:T(8,128)(2,1)S(1)} %get-tuple-element.110), channel_id=1, source_target_pairs={{0,2},{1,3},{8,10},{9,11},{16,18},{17,19},{24,26},{25,27},{2,0},{3... | collective-permute-start | bytes 442376 | tf_op jit(solution)/shard_map/ppermute | solution.py:647
  69.0 15.6 %collective-permute-start.19 = (bf16[512,256]{1,0:T(8,128)(2,1)S(1)}, bf16[512,256]{1,0:T(8,128)(2,1)S(1)}, u32[]{:S(2)}, u32[]{:S(2)}) collective-permute-start(bf16[512,256]{1,0:T(8,128)(2,1)S(1)} %get-tuple-element.105), channel_id=1, source_target_pairs={{0,1},{1,0},{8,9},{9,8},{16,17},{17,16},{24,25},{25,24},{2,3},{3,2... | collective-permute-start | bytes 786440 | tf_op jit(solution)/shard_map/ppermute | solution.py:639
  69.5 15.1 %collective-permute-start.20 = (bf16[512,256]{1,0:T(8,128)(2,1)S(1)}, bf16[512,256]{1,0:T(8,128)(2,1)S(1)}, u32[]{:S(2)}, u32[]{:S(2)}) collective-permute-start(bf16[512,256]{1,0:T(8,128)(2,1)S(1)} %get-tuple-element.106), channel_id=1, source_target_pairs={{0,16},{1,17},{8,24},{9,25},{16,0},{17,1},{24,8},{25,9},{2,18},{3,... | collective-permute-start | bytes 786440 | tf_op jit(solution)/shard_map/ppermute | solution.py:639
  71.1 13.5 %collective-permute-start.21 = (bf16[512,256]{1,0:T(8,128)(2,1)S(1)}, bf16[512,256]{1,0:T(8,128)(2,1)S(1)}, u32[]{:S(2)}, u32[]{:S(2)}) collective-permute-start(bf16[512,256]{1,0:T(8,128)(2,1)S(1)} %get-tuple-element.107), channel_id=1, source_target_pairs={{0,17},{1,16},{8,25},{9,24},{16,1},{17,0},{24,9},{25,8},{2,19},{3,... | collective-permute-start | bytes 786440 | tf_op jit(solution)/shard_map/ppermute | solution.py:639
  72.5 12.0 %collective-permute-start.23 = (bf16[288,256]{1,0:T(8,128)(2,1)S(1)}, bf16[288,256]{1,0:T(8,128)(2,1)S(1)}, u32[]{:S(2)}, u32[]{:S(2)}) collective-permute-start(bf16[288,256]{1,0:T(8,128)(2,1)S(1)} %get-tuple-element.111), channel_id=1, source_target_pairs={{0,4},{1,5},{8,12},{9,13},{16,20},{17,21},{24,28},{25,29},{2,6},{3... | collective-permute-start | bytes 442376 | tf_op jit(solution)/shard_map/ppermute | solution.py:647
  75.0 9.6 %collective-permute-start.24 = (bf16[288,256]{1,0:T(8,128)(2,1)S(1)}, bf16[288,256]{1,0:T(8,128)(2,1)S(1)}, u32[]{:S(2)}, u32[]{:S(2)}) collective-permute-start(bf16[288,256]{1,0:T(8,128)(2,1)S(1)} %get-tuple-element.112), channel_id=1, source_target_pairs={{0,6},{1,7},{8,14},{9,15},{16,22},{17,23},{24,30},{25,31},{2,4},{3... | collective-permute-start | bytes 442376 | tf_op jit(solution)/shard_map/ppermute | solution.py:647
  85.6 7.0 %collective-permute-start.25 = (bf16[512,256]{1,0:T(8,128)(2,1)S(1)}, bf16[512,256]{1,0:T(8,128)(2,1)S(1)}, u32[]{:S(2)}, u32[]{:S(2)}) collective-permute-start(bf16[512,256]{1,0:T(8,128)(2,1)S(1)} %get-tuple-element.118), channel_id=1, source_target_pairs={{0,1},{1,0},{8,9},{9,8},{16,17},{17,16},{24,25},{25,24},{2,3},{3,2... | collective-permute-start | bytes 786440 | tf_op jit(solution)/shard_map/ppermute | solution.py:639
  86.1 6.4 %collective-permute-start.26 = (bf16[512,256]{1,0:T(8,128)(2,1)S(1)}, bf16[512,256]{1,0:T(8,128)(2,1)S(1)}, u32[]{:S(2)}, u32[]{:S(2)}) collective-permute-start(bf16[512,256]{1,0:T(8,128)(2,1)S(1)} %get-tuple-element.119), channel_id=1, source_target_pairs={{0,16},{1,17},{8,24},{9,25},{16,0},{17,1},{24,8},{25,9},{2,18},{3,... | collective-permute-start | bytes 786440 | tf_op jit(solution)/shard_map/ppermute | solution.py:639
  87.7 8.6 %collective-permute-start.27 = (bf16[512,256]{1,0:T(8,128)(2,1)S(1)}, bf16[512,256]{1,0:T(8,128)(2,1)S(1)}, u32[]{:S(2)}, u32[]{:S(2)}) collective-permute-start(bf16[512,256]{1,0:T(8,128)(2,1)S(1)} %get-tuple-element.120), channel_id=1, source_target_pairs={{0,17},{1,16},{8,25},{9,24},{16,1},{17,0},{24,9},{25,8},{2,19},{3,... | collective-permute-start | bytes 786440 | tf_op jit(solution)/shard_map/ppermute | solution.py:639
  89.2 7.8 %collective-permute-start.28 = (bf16[1024,256]{1,0:T(8,128)(2,1)S(1)}, bf16[1024,256]{1,0:T(8,128)(2,1)S(1)}, u32[]{:S(2)}, u32[]{:S(2)}) collective-permute-start(bf16[1024,256]{1,0:T(8,128)(2,1)S(1)} %get-tuple-element.93.refs_0_), channel_id=1, source_target_pairs={{0,8},{1,9},{8,0},{9,1},{16,24},{17,25},{24,16},{25,17},{2,10},{3,... | collective-permute-start | bytes 1572872 | tf_op jit(solution)/shard_map/ppermute | solution.py:639
  89.4 8.1 %collective-permute-start.29 = (bf16[1024,256]{1,0:T(8,128)(2,1)S(1)}, bf16[1024,256]{1,0:T(8,128)(2,1)S(1)}, u32[]{:S(2)}, u32[]{:S(2)}) collective-permute-start(bf16[1024,256]{1,0:T(8,128)(2,1)S(1)} %get-tuple-element.108.refs_1_), channel_id=1, source_target_pairs={{0,8},{1,9},{8,0},{9,1},{16,24},{17,25},{24,16},{25,17},{2,10},{3,... | collective-permute-start | bytes 1572872 | tf_op jit(solution)/shard_map/ppermute | solution.py:639
  96.4 2.0 %collective-permute-start.30 = (bf16[1024,256]{1,0:T(8,128)(2,1)S(1)}, bf16[1024,256]{1,0:T(8,128)(2,1)S(1)}, u32[]{:S(2)}, u32[]{:S(2)}) collective-permute-start(bf16[1024,256]{1,0:T(8,128)(2,1)S(1)} %get-tuple-element.121.refs_2_), channel_id=1, source_target_pairs={{0,8},{1,9},{8,0},{9,1},{16,24},{17,25},{24,16},{25,17},{2,10},{3,... | collective-permute-start | bytes 1572872 | tf_op jit(solution)/shard_map/ppermute | solution.py:639
  96.5 5.0 %collective-permute-start.31 = (bf16[1024,256]{1,0:T(8,128)(2,1)S(1)}, bf16[1024,256]{1,0:T(8,128)(2,1)S(1)}, u32[]{:S(2)}, u32[]{:S(2)}) collective-permute-start(bf16[1024,256]{1,0:T(8,128)(2,1)S(1)} %get-tuple-element.124.refs_0_), channel_id=1, source_target_pairs={{0,8},{1,9},{8,0},{9,1},{16,24},{17,25},{24,16},{25,17},{2,10},{3,... | collective-permute-start | bytes 1572872 | tf_op jit(solution)/shard_map/ppermute | solution.py:639
  97.0 4.5 %collective-permute-start.32 = (bf16[1024,256]{1,0:T(8,128)(2,1)S(1)}, bf16[1024,256]{1,0:T(8,128)(2,1)S(1)}, u32[]{:S(2)}, u32[]{:S(2)}) collective-permute-start(bf16[1024,256]{1,0:T(8,128)(2,1)S(1)} %get-tuple-element.125.refs_1_), channel_id=1, source_target_pairs={{0,8},{1,9},{8,0},{9,1},{16,24},{17,25},{24,16},{25,17},{2,10},{3,... | collective-permute-start | bytes 1572872 | tf_op jit(solution)/shard_map/ppermute | solution.py:639
  97.1 4.4 %collective-permute-start.33 = (bf16[1024,256]{1,0:T(8,128)(2,1)S(1)}, bf16[1024,256]{1,0:T(8,128)(2,1)S(1)}, u32[]{:S(2)}, u32[]{:S(2)}) collective-permute-start(bf16[1024,256]{1,0:T(8,128)(2,1)S(1)} %get-tuple-element.126.refs_2_), channel_id=1, source_target_pairs={{0,8},{1,9},{8,0},{9,1},{16,24},{17,25},{24,16},{25,17},{2,10},{3,... | collective-permute-start | bytes 1572872 | tf_op jit(solution)/shard_map/ppermute | solution.py:639
  102.8 20.0 %all-to-all-start.3 = ((f32[32,8,128]{2,1,0:T(8,128)}), f32[32,8,128]{2,1,0:T(8,128)S(1)}, u32[]{:S(2)}, u32[]{:S(2)}) async-start(f32[32,8,128]{2,1,0:T(8,128)} %shard_map.60), calls=%async_computation.3 | async-start | bytes 262144 | tf_op jit(solution)/shard_map/all_to_all | solution.py:565
  (5 other events, 69.7 us)

commit v6 on v5

--- a/solution.py
+++ b/solution.py
@@ -294,8 +294,12 @@
         chosen = jnp.where(row == target, 1.0, 0.0).astype(jnp.bfloat16)
         moved = jnp.dot(chosen, unit_ref[...], preferred_element_type=jnp.float32)
         moved = moved.astype(jnp.bfloat16)
-        outs[2 * pair][: plan.part, :] = moved[: plan.part, :]
-        outs[2 * pair + 1][: plan.part, :] = moved[plan.part :, :]
+        for number in range(2):
+            here = moved[number * plan.part : (number + 1) * plan.part, :]
+            outs[2 * pair + number][: plan.part, :] = here[:, : plan.chunks[0]]
+            whole = (2 * pair + number ^ lane) * plan.part
+            there = pl.ds(pl.multiple_of(whole, plan.part), plan.part)
+            outs[plan.lanes][there, :] = here[:, plan.chunks[0] :]
 
     place = lax.broadcasted_iota(jnp.int32, (plan.devices, plan.part), 1) // plan.slice
     here = (place.astype(jnp.float32) == order[:, :1]) & (block > 0)
@@ -304,7 +308,7 @@
     blocks = jnp.sum(jnp.where(here, block - 1, 0), axis=0, keepdims=True)
     line = lax.broadcasted_iota(jnp.int32, (16, plan.part), 0)
     table = jnp.where(line == 0, owners, jnp.where(line == 1, blocks, 0))
-    for out in outs:
+    for out in outs[: plan.lanes]:
         out[plan.part :, : plan.part] = table.astype(jnp.float32).astype(jnp.bfloat16)
 
 
@@ -322,9 +326,7 @@
     outs, (target_ref, inputs_ref, owner_ref, block_ref, value_ref) = rest[:-5], rest[-5:]
     _, layer = my_lane(plan)
     for number, part in enumerate(ins):
-        inputs_ref[number * plan.part : (number + 1) * plan.part, :] = part[
-            : plan.part, : plan.chunks[0]
-        ]
+        inputs_ref[number * plan.part : (number + 1) * plan.part, :] = part[: plan.part, :]
         table = part[plan.part :, : plan.part].astype(jnp.float32)
         owner_ref[number : number + 1, :] = table[0:1, :].astype(jnp.int32)
         block_ref[number : number + 1, :] = table[1:2, :].astype(jnp.int32)
@@ -375,12 +377,14 @@
         out[plan.room :, :128] = table.astype(jnp.bfloat16)
 
 
-def route_more_kernel(plan, target_ref, *refs, chunk):
-    ins, outs, inputs_ref = refs[: plan.lanes], refs[plan.lanes : -1], refs[-1]
-    first = sum(plan.chunks[:chunk])
-    for number, part in enumerate(ins):
-        inputs_ref[number * plan.part : (number + 1) * plan.part, :] = part[
-            : plan.part, first : first + plan.chunks[chunk]
+def route_more_kernel(plan, target_ref, rows_ref, *refs, chunk):
+    outs, inputs_ref = refs[:-1], refs[-1]
+    lane, _ = my_lane(plan)
+    first = sum(plan.chunks[1:chunk])
+    for number in range(plan.lanes):
+        whole = pl.multiple_of((number ^ lane) * plan.part, plan.part)
+        inputs_ref[number * plan.part : (number + 1) * plan.part, :] = rows_ref[
+            pl.ds(whole, plan.part), first : first + plan.chunks[chunk]
         ]
     permute_into(target_ref[...], 0, inputs_ref, outs, plan.room, plan.stride)
 
@@ -646,18 +650,20 @@
         ]
         return lax.ppermute(block, AXES, pairs)
 
-    far_first = sorted(lanes, key=lambda change: -(change & 1) - (change // plan.width // 2))
+    far_first = sorted(lanes[1:], key=lambda change: -(change & 1) - (change // plan.width // 2))
 
     spread = call(
         spread_kernel,
         plan,
-        [wide((plan.part + 16, width), half) for _ in lanes],
+        [wide((plan.part + 16, plan.chunks[0]), half) for _ in lanes]
+        + [wide((rows, width - plan.chunks[0]), half)],
         [SMEM, VMEM, VMEM, VMEM],
         [pltpu.VMEM((rows, width), half)],
         2 * rows * rows * width,
         3 * rows * width * 2,
     )(run_len, clusters, ranks, embeddings)
-    swapped = {change: along_lanes(spread[change], change) for change in far_first if change}
+    *spread, later = spread
+    swapped = {change: along_lanes(spread[change], change) for change in far_first}
     spread = [spread[0]] + [swapped[change] for change in lanes[1:]]
     pair, mates, behind, fars = [], [], [], []
     table = targets = full = None
@@ -681,10 +687,14 @@
                 **spec,
             )(*spread)
         else:
+            if chunk == 1:
+                later, _ = lax.optimization_barrier((later, table))
+                groups = [[lane_device(plan, layer, lane) for lane in lanes] for layer in layers]
+                later = lax.all_to_all(
+                    later, AXES, 0, 0, tiled=True, axis_index_groups=groups
+                )
             more = functools.partial(route_more_kernel, chunk=chunk)
-            routed = call(more, plan, rooms, [VMEM] * (1 + plan.lanes), [inputs], **spec)(
-                table, *spread
-            )
+            routed = call(more, plan, rooms, [VMEM] * 2, [inputs], **spec)(table, later)
         moved = {change: along_layers(routed[change], change) for change in reversed(layers[1:])}
         arrived = [routed[0]] + [moved[change] for change in layers[1:]]
         arrivals.append(arrived)

time: 125 us -> 120 us (0.960)
  waiting for transfers between devices: 54.9 us -> 46.5 us
  starting transfers between devices: 50.3 us -> 53 us
    ppermute x22, waiting for transfers between devices: 22.6 us -> 13.9 us  [along_lanes(): return lax.ppermute(block, AXES, pairs)]
    all_to_all x0 -> x1, starting transfers between devices: none -> 3.56 us  [staged(): lax.all_to_all(later, AXES, 0, 0, tiled=True, axis_index_groups=groups)]
    all_to_all x1, starting transfers between devices: 12.2 us -> 10.2 us  [exchange(): return lax.all_to_all(block, AXES, split_axis=0, concat_axis=0, tiled=True)]
    ppermute x9, starting transfers between devices: 15.9 us -> 17.8 us  [along_layers(): return lax.ppermute(block, AXES, pairs)]
  transfers between devices with their start and end apart: 32 -> 33, of which waited for: 13 -> 12; matrix products, arithmetic and copies ran while one was open for 0% -> 0% of each run, Pallas kernels for 6% -> 6%
where the time goes in v6:
time: 120 us
  starting transfers between devices  53 us (44%)
  waiting for transfers between devices  46.5 us (39%)
  Pallas kernels  18.6 us (16%)
    ppermute x9, waiting for transfers between devices, along_layers(): return lax.ppermute(block, AXES, pairs)  26 us
    ppermute x22, starting transfers between devices, along_lanes(): return lax.ppermute(block, AXES, pairs)  21.5 us
    ppermute x9, starting transfers between devices, along_layers(): return lax.ppermute(block, AXES, pairs)  17.8 us
    ppermute x22, waiting for transfers between devices, along_lanes(): return lax.ppermute(block, AXES, pairs)  13.9 us
    all_to_all x1, starting transfers between devices, exchange(): return lax.all_to_all(block, AXES, split_axis=0, concat_axis=0, tiled=True)  10.2 us
    all_to_all x1, waiting for transfers between devices, exchange(): return lax.all_to_all(block, AXES, split_axis=0, concat_axis=0, tiled=True)  6.57 us
    pallas_call x1, Pallas kernels, staged(): call(spread_kernel, plan, [wide((plan.part + 16, plan.chunks[0]), half) f...  5.66 us
    all_to_all x1, starting transfers between devices, staged(): lax.all_to_all(later, AXES, 0, 0, tiled=True, axis_index_groups=groups)  3.56 us
  transfers between devices with their start and end apart: 33, of which 12 were waited for; matrix products, arithmetic and copies ran while one was open for 0% of the time, Pallas kernels for 6%

profile of v6, /device:TPU:0, one launch (start us, length us, event | category | flops | bytes accessed | tf_op | source)
XLA Modules:
  0.0 120.1 jit_solution(4504379664319362820)
XLA Ops:
  0.0 5.7 %shard_map.48 = (bf16[144,256]{1,0:T(8,128)(2,1)S(1)}, bf16[144,256]{1,0:T(8,128)(2,1)S(1)}, bf16[144,256]{1,0:T(8,128)(2,1)S(1)}, bf16[144,256]{1,0:T(8,128)(2,...) custom-call(s32[12]{0:T(128)} %run_len_ref.7, ...), custom_call_target="tpu_custom_call" | custom-call | flops 1610612736 | bytes 4718592 | tf_op jit(solution)/shard_map/pallas_call | solution.py:655
  5.7 3.0 %collective-permute-start.3 = (bf16[144,256]{1,0:T(8,128)(2,1)S(1)}, bf16[144,256]{1,0:T(8,128)(2,1)S(1)}, u32[]{:S(2)}, u32[]{:S(2)}) collective-permute-start(bf16[144,256]{1,0:T(8,128)(2,1)S(1)} %get-tuple-element.79), channel_id=1, source_target_pairs={{0,1},{1,0},{8,9},{9,8},{16,17},{17,16},{24,25},{25,24},{2,3},{3,2... | collective-permute-start | bytes 221192 | tf_op jit(solution)/shard_map/ppermute | solution.py:643
  8.7 2.0 %collective-permute-start.6 = (bf16[144,256]{1,0:T(8,128)(2,1)S(1)}, bf16[144,256]{1,0:T(8,128)(2,1)S(1)}, u32[]{:S(2)}, u32[]{:S(2)}) collective-permute-start(bf16[144,256]{1,0:T(8,128)(2,1)S(1)} %get-tuple-element.82), channel_id=1, source_target_pairs={{0,16},{1,17},{8,24},{9,25},{16,0},{17,1},{24,8},{25,9},{2,18},{3,... | collective-permute-start | bytes 221192 | tf_op jit(solution)/shard_map/ppermute | solution.py:643
  10.7 1.5 %collective-permute-start.7 = (bf16[144,256]{1,0:T(8,128)(2,1)S(1)}, bf16[144,256]{1,0:T(8,128)(2,1)S(1)}, u32[]{:S(2)}, u32[]{:S(2)}) collective-permute-start(bf16[144,256]{1,0:T(8,128)(2,1)S(1)} %get-tuple-element.83), channel_id=1, source_target_pairs={{0,17},{1,16},{8,25},{9,24},{16,1},{17,0},{24,9},{25,8},{2,19},{3,... | collective-permute-start | bytes 221192 | tf_op jit(solution)/shard_map/ppermute | solution.py:643
  12.8 2.0 %collective-permute-start.9 = (bf16[144,256]{1,0:T(8,128)(2,1)S(1)}, bf16[144,256]{1,0:T(8,128)(2,1)S(1)}, u32[]{:S(2)}, u32[]{:S(2)}) collective-permute-start(bf16[144,256]{1,0:T(8,128)(2,1)S(1)} %get-tuple-element.85), channel_id=1, source_target_pairs={{0,25},{1,24},{8,17},{9,16},{16,9},{17,8},{24,1},{25,0},{2,27},{3,... | collective-permute-start | bytes 221192 | tf_op jit(solution)/shard_map/ppermute | solution.py:643
  14.8 1.5 %collective-permute-done.7.refs_5_ = bf16[144,256]{1,0:T(8,128)(2,1)S(1)} collective-permute-done((bf16[144,256]{1,0:T(8,128)(2,1)S(1)}, bf16[144,256]{1,0:T(8,128)(2,1)S(1)}, u32[]{:S(2)}, u32[]{:S(2)}) %collective-permute-start.7) | collective-permute-done | bytes 73760 | tf_op jit(solution)/shard_map/ppermute | solution.py:643
  16.8 2.3 %collective-permute-done.9.refs_7_ = bf16[144,256]{1,0:T(8,128)(2,1)S(1)} collective-permute-done((bf16[144,256]{1,0:T(8,128)(2,1)S(1)}, bf16[144,256]{1,0:T(8,128)(2,1)S(1)}, u32[]{:S(2)}, u32[]{:S(2)}) %collective-permute-start.9) | collective-permute-done | bytes 73760 | tf_op jit(solution)/shard_map/ppermute | solution.py:643
  19.0 2.2 %shard_map.49 = (bf16[304,256]{1,0:T(8,128)(2,1)S(1)}, bf16[304,256]{1,0:T(8,128)(2,1)S(1)}, bf16[304,256]{1,0:T(8,128)(2,1)S(1)}, bf16[304,256]{1,0:T(8,128)(2,1)S(1)}, s32[1,1024]{1,0:T(1,128)S(1)}) custom-call(bf16[144,256]{1,0:T(8,128)(2,1)S(1)} %get-tuple-element.78.refs_0_, bf16[144,256]{1,0:T(8,128)(2,1)S(1)} %collective-permute-done.3.refs_1_, ...), custom_call_target="tpu_custom_call" | custom-call | flops 536870912 | bytes 1572864 | tf_op jit(solution)/shard_map/pallas_call | solution.py:676
  21.2 3.6 %all-to-all-start.3 = ((bf16[8,128,512]{2,1,0:T(8,128)(2,1)}), bf16[8,128,512]{2,1,0:T(8,128)(2,1)S(1)}, u32[]{:S(2)}, u32[]{:S(2)}) async-start(bf16[8,128,512]{2,1,0:T(8,128)(2,1)} %bitcast.17), calls=%async_computation.3 | async-start | bytes 2097152 | tf_op jit(solution)/shard_map/all_to_all | solution.py:693
  24.8 1.7 %collective-permute-start.10 = (bf16[304,256]{1,0:T(8,128)(2,1)S(1)}, bf16[304,256]{1,0:T(8,128)(2,1)S(1)}, u32[]{:S(2)}, u32[]{:S(2)}) collective-permute-start(bf16[304,256]{1,0:T(8,128)(2,1)S(1)} %get-tuple-element.87), channel_id=1, source_target_pairs={{0,2},{1,3},{8,10},{9,11},{16,18},{17,19},{24,26},{25,27},{2,0},{3... | collective-permute-start | bytes 466952 | tf_op jit(solution)/shard_map/ppermute | solution.py:651
  26.5 2.5 %collective-permute-start.11 = (bf16[304,256]{1,0:T(8,128)(2,1)S(1)}, bf16[304,256]{1,0:T(8,128)(2,1)S(1)}, u32[]{:S(2)}, u32[]{:S(2)}) collective-permute-start(bf16[304,256]{1,0:T(8,128)(2,1)S(1)} %get-tuple-element.88), channel_id=1, source_target_pairs={{0,4},{1,5},{8,12},{9,13},{16,20},{17,21},{24,28},{25,29},{2,6},{3... | collective-permute-start | bytes 466952 | tf_op jit(solution)/shard_map/ppermute | solution.py:651
  29.3 4.7 %collective-permute-done.10.refs_1_ = bf16[304,256]{1,0:T(8,128)(2,1)S(1)} collective-permute-done((bf16[304,256]{1,0:T(8,128)(2,1)S(1)}, bf16[304,256]{1,0:T(8,128)(2,1)S(1)}, u32[]{:S(2)}, u32[]{:S(2)}) %collective-permute-start.10) | collective-permute-done | bytes 155680 | tf_op jit(solution)/shard_map/ppermute | solution.py:651
  34.0 7.0 %collective-permute-done.11.refs_2_ = bf16[304,256]{1,0:T(8,128)(2,1)S(1)} collective-permute-done((bf16[304,256]{1,0:T(8,128)(2,1)S(1)}, bf16[304,256]{1,0:T(8,128)(2,1)S(1)}, u32[]{:S(2)}, u32[]{:S(2)}) %collective-permute-start.11) | collective-permute-done | bytes 155680 | tf_op jit(solution)/shard_map/ppermute | solution.py:651
  42.2 1.9 %collective-permute-start.13 = (bf16[512,256]{1,0:T(8,128)(2,1)S(1)}, bf16[512,256]{1,0:T(8,128)(2,1)S(1)}, u32[]{:S(2)}, u32[]{:S(2)}) collective-permute-start(bf16[512,256]{1,0:T(8,128)(2,1)S(1)} %get-tuple-element.92), channel_id=1, source_target_pairs={{0,1},{1,0},{8,9},{9,8},{16,17},{17,16},{24,25},{25,24},{2,3},{3,2... | collective-permute-start | bytes 786440 | tf_op jit(solution)/shard_map/ppermute | solution.py:643
  44.1 1.5 %collective-permute-start.14 = (bf16[512,256]{1,0:T(8,128)(2,1)S(1)}, bf16[512,256]{1,0:T(8,128)(2,1)S(1)}, u32[]{:S(2)}, u32[]{:S(2)}) collective-permute-start(bf16[512,256]{1,0:T(8,128)(2,1)S(1)} %get-tuple-element.93), channel_id=1, source_target_pairs={{0,16},{1,17},{8,24},{9,25},{16,0},{17,1},{24,8},{25,9},{2,18},{3,... | collective-permute-start | bytes 786440 | tf_op jit(solution)/shard_map/ppermute | solution.py:643
  46.5 3.1 %collective-permute-start.16 = (bf16[288,256]{1,0:T(8,128)(2,1)S(1)}, bf16[288,256]{1,0:T(8,128)(2,1)S(1)}, u32[]{:S(2)}, u32[]{:S(2)}) collective-permute-start(bf16[288,256]{1,0:T(8,128)(2,1)S(1)} %get-tuple-element.101), channel_id=1, source_target_pairs={{0,2},{1,3},{8,10},{9,11},{16,18},{17,19},{24,26},{25,27},{2,0},{3... | collective-permute-start | bytes 442376 | tf_op jit(solution)/shard_map/ppermute | solution.py:651
  50.7 2.4 %collective-permute-start.18 = (bf16[288,256]{1,0:T(8,128)(2,1)S(1)}, bf16[288,256]{1,0:T(8,128)(2,1)S(1)}, u32[]{:S(2)}, u32[]{:S(2)}) collective-permute-start(bf16[288,256]{1,0:T(8,128)(2,1)S(1)} %get-tuple-element.103), channel_id=1, source_target_pairs={{0,6},{1,7},{8,14},{9,15},{16,22},{17,23},{24,30},{25,31},{2,4},{3... | collective-permute-start | bytes 442376 | tf_op jit(solution)/shard_map/ppermute | solution.py:651
  53.9 2.3 %collective-permute-start.22 = (bf16[288,256]{1,0:T(8,128)(2,1)S(1)}, bf16[288,256]{1,0:T(8,128)(2,1)S(1)}, u32[]{:S(2)}, u32[]{:S(2)}) collective-permute-start(bf16[288,256]{1,0:T(8,128)(2,1)S(1)} %get-tuple-element.114), channel_id=1, source_target_pairs={{0,2},{1,3},{8,10},{9,11},{16,18},{17,19},{24,26},{25,27},{2,0},{3... | collective-permute-start | bytes 442376 | tf_op jit(solution)/shard_map/ppermute | solution.py:651
  56.2 6.1 %collective-permute-done.17.refs_2_ = bf16[288,256]{1,0:T(8,128)(2,1)S(1)} collective-permute-done((bf16[288,256]{1,0:T(8,128)(2,1)S(1)}, bf16[288,256]{1,0:T(8,128)(2,1)S(1)}, u32[]{:S(2)}, u32[]{:S(2)}) %collective-permute-start.17) | collective-permute-done | bytes 147488 | tf_op jit(solution)/shard_map/ppermute | solution.py:651
  63.3 1.5 %collective-permute-start.19 = (bf16[512,256]{1,0:T(8,128)(2,1)S(1)}, bf16[512,256]{1,0:T(8,128)(2,1)S(1)}, u32[]{:S(2)}, u32[]{:S(2)}) collective-permute-start(bf16[512,256]{1,0:T(8,128)(2,1)S(1)} %get-tuple-element.109), channel_id=1, source_target_pairs={{0,1},{1,0},{8,9},{9,8},{16,17},{17,16},{24,25},{25,24},{2,3},{3,2... | collective-permute-start | bytes 786440 | tf_op jit(solution)/shard_map/ppermute | solution.py:643
  64.8 1.5 %collective-permute-start.20 = (bf16[512,256]{1,0:T(8,128)(2,1)S(1)}, bf16[512,256]{1,0:T(8,128)(2,1)S(1)}, u32[]{:S(2)}, u32[]{:S(2)}) collective-permute-start(bf16[512,256]{1,0:T(8,128)(2,1)S(1)} %get-tuple-element.110), channel_id=1, source_target_pairs={{0,16},{1,17},{8,24},{9,25},{16,0},{17,1},{24,8},{25,9},{2,18},{3,... | collective-permute-start | bytes 786440 | tf_op jit(solution)/shard_map/ppermute | solution.py:643
  66.9 3.2 %collective-permute-start.23 = (bf16[288,256]{1,0:T(8,128)(2,1)S(1)}, bf16[288,256]{1,0:T(8,128)(2,1)S(1)}, u32[]{:S(2)}, u32[]{:S(2)}) collective-permute-start(bf16[288,256]{1,0:T(8,128)(2,1)S(1)} %get-tuple-element.115), channel_id=1, source_target_pairs={{0,4},{1,5},{8,12},{9,13},{16,20},{17,21},{24,28},{25,29},{2,6},{3... | collective-permute-start | bytes 442376 | tf_op jit(solution)/shard_map/ppermute | solution.py:651
  71.4 8.1 %collective-permute-done.23.refs_2_ = bf16[288,256]{1,0:T(8,128)(2,1)S(1)} collective-permute-done((bf16[288,256]{1,0:T(8,128)(2,1)S(1)}, bf16[288,256]{1,0:T(8,128)(2,1)S(1)}, u32[]{:S(2)}, u32[]{:S(2)}) %collective-permute-start.23) | collective-permute-done | bytes 147488 | tf_op jit(solution)/shard_map/ppermute | solution.py:651
  80.6 1.5 %collective-permute-start.25 = (bf16[512,256]{1,0:T(8,128)(2,1)S(1)}, bf16[512,256]{1,0:T(8,128)(2,1)S(1)}, u32[]{:S(2)}, u32[]{:S(2)}) collective-permute-start(bf16[512,256]{1,0:T(8,128)(2,1)S(1)} %get-tuple-element.122), channel_id=1, source_target_pairs={{0,1},{1,0},{8,9},{9,8},{16,17},{17,16},{24,25},{25,24},{2,3},{3,2... | collective-permute-start | bytes 786440 | tf_op jit(solution)/shard_map/ppermute | solution.py:643
  82.1 1.5 %collective-permute-start.26 = (bf16[512,256]{1,0:T(8,128)(2,1)S(1)}, bf16[512,256]{1,0:T(8,128)(2,1)S(1)}, u32[]{:S(2)}, u32[]{:S(2)}) collective-permute-start(bf16[512,256]{1,0:T(8,128)(2,1)S(1)} %get-tuple-element.123), channel_id=1, source_target_pairs={{0,16},{1,17},{8,24},{9,25},{16,0},{17,1},{24,8},{25,9},{2,18},{3,... | collective-permute-start | bytes 786440 | tf_op jit(solution)/shard_map/ppermute | solution.py:643
  84.9 4.3 %collective-permute-done.25.refs_1_ = bf16[512,256]{1,0:T(8,128)(2,1)S(1)} collective-permute-done((bf16[512,256]{1,0:T(8,128)(2,1)S(1)}, bf16[512,256]{1,0:T(8,128)(2,1)S(1)}, u32[]{:S(2)}, u32[]{:S(2)}) %collective-permute-start.25) | collective-permute-done | bytes 262176 | tf_op jit(solution)/shard_map/ppermute | solution.py:643
  89.3 1.6 %collective-permute-done.26.refs_2_ = bf16[512,256]{1,0:T(8,128)(2,1)S(1)} collective-permute-done((bf16[512,256]{1,0:T(8,128)(2,1)S(1)}, bf16[512,256]{1,0:T(8,128)(2,1)S(1)}, u32[]{:S(2)}, u32[]{:S(2)}) %collective-permute-start.26) | collective-permute-done | bytes 262176 | tf_op jit(solution)/shard_map/ppermute | solution.py:643
  90.9 2.8 %collective-permute-done.27.refs_3_ = bf16[512,256]{1,0:T(8,128)(2,1)S(1)} collective-permute-done((bf16[512,256]{1,0:T(8,128)(2,1)S(1)}, bf16[512,256]{1,0:T(8,128)(2,1)S(1)}, u32[]{:S(2)}, u32[]{:S(2)}) %collective-permute-start.27) | collective-permute-done | bytes 262176 | tf_op jit(solution)/shard_map/ppermute | solution.py:643
  95.8 2.4 %shard_map.58 = (bf16[1024,768]{1,0:T(8,128)(2,1)S(1)}, f32[1,1024]{1,0:T(1,128)S(1)}) custom-call(bf16[1024,256]{1,0:T(8,128)(2,1)S(1)} %get-tuple-element.95.refs_0_, bf16[1024,256]{1,0:T(8,128)(2,1)S(1)} %get-tuple-element.112.refs_1_, bf16[1024,256]{1,0:T(8,128)(2,1)S(1)} %get-tuple-element.125.refs_2_, ...), custom_call_target="tpu_custom_call" | custom-call | flops 3221225472 | bytes 4718592 | tf_op jit(solution)/shard_map/pallas_call | solution.py:742
  100.2 10.2 %all-to-all-start.4 = ((f32[32,8,128]{2,1,0:T(8,128)}), f32[32,8,128]{2,1,0:T(8,128)S(1)}, u32[]{:S(2)}, u32[]{:S(2)}) async-start(f32[32,8,128]{2,1,0:T(8,128)} %shard_map.60), calls=%async_computation.4 | async-start | bytes 262144 | tf_op jit(solution)/shard_map/all_to_all | solution.py:569
  111.5 6.6 %all-to-all-done.4 = f32[32,8,128]{2,1,0:T(8,128)S(1)} async-done(((f32[32,8,128]{2,1,0:T(8,128)}), f32[32,8,128]{2,1,0:T(8,128)S(1)}, u32[]{:S(2)}, u32[]{:S(2)}) %all-to-all-start.4) | async-done | bytes 131104 | tf_op jit(solution)/shard_map/all_to_all | solution.py:569
  118.1 1.4 %shard_map.61 = f32[1,1024]{1,0:T(1,128)S(1)} custom-call(s32[12]{0:T(128)S(1)} %copy-done.3, s32[1,1024]{1,0:T(1,128)S(1)} %bitcast.31, s32[1,1024]{1,0:T(1,128)S(1)} %bitcast.34, f32[256,128]{1,0:T(8,128)S(1)} %bitcast.24), custom_call_target="tpu_custom_call" | custom-call | bytes 16384 | tf_op jit(solution)/shard_map/pallas_call | solution.py:764
  (60 shorter events, 15.8 us)
Async XLA Ops:
  5.7 6.6 %collective-permute-start.3 = (bf16[144,256]{1,0:T(8,128)(2,1)S(1)}, bf16[144,256]{1,0:T(8,128)(2,1)S(1)}, u32[]{:S(2)}, u32[]{:S(2)}) collective-permute-start(bf16[144,256]{1,0:T(8,128)(2,1)S(1)} %get-tuple-element.79), channel_id=1, source_target_pairs={{0,1},{1,0},{8,9},{9,8},{16,17},{17,16},{24,25},{25,24},{2,3},{3,2... | collective-permute-start | bytes 221192 | tf_op jit(solution)/shard_map/ppermute | solution.py:643
  8.6 4.1 %collective-permute-start.4 = (bf16[144,256]{1,0:T(8,128)(2,1)S(1)}, bf16[144,256]{1,0:T(8,128)(2,1)S(1)}, u32[]{:S(2)}, u32[]{:S(2)}) collective-permute-start(bf16[144,256]{1,0:T(8,128)(2,1)S(1)} %get-tuple-element.80), channel_id=1, source_target_pairs={{0,8},{1,9},{8,0},{9,1},{16,24},{17,25},{24,16},{25,17},{2,10},{3,... | collective-permute-start | bytes 221192 | tf_op jit(solution)/shard_map/ppermute | solution.py:643
  8.6 6.2 %collective-permute-start.5 = (bf16[144,256]{1,0:T(8,128)(2,1)S(1)}, bf16[144,256]{1,0:T(8,128)(2,1)S(1)}, u32[]{:S(2)}, u32[]{:S(2)}) collective-permute-start(bf16[144,256]{1,0:T(8,128)(2,1)S(1)} %get-tuple-element.81), channel_id=1, source_target_pairs={{0,9},{1,8},{8,1},{9,0},{16,25},{17,24},{24,17},{25,16},{2,11},{3,... | collective-permute-start | bytes 221192 | tf_op jit(solution)/shard_map/ppermute | solution.py:643
  8.7 6.0 %collective-permute-start.6 = (bf16[144,256]{1,0:T(8,128)(2,1)S(1)}, bf16[144,256]{1,0:T(8,128)(2,1)S(1)}, u32[]{:S(2)}, u32[]{:S(2)}) collective-permute-start(bf16[144,256]{1,0:T(8,128)(2,1)S(1)} %get-tuple-element.82), channel_id=1, source_target_pairs={{0,16},{1,17},{8,24},{9,25},{16,0},{17,1},{24,8},{25,9},{2,18},{3,... | collective-permute-start | bytes 221192 | tf_op jit(solution)/shard_map/ppermute | solution.py:643
  10.7 5.5 %collective-permute-start.7 = (bf16[144,256]{1,0:T(8,128)(2,1)S(1)}, bf16[144,256]{1,0:T(8,128)(2,1)S(1)}, u32[]{:S(2)}, u32[]{:S(2)}) collective-permute-start(bf16[144,256]{1,0:T(8,128)(2,1)S(1)} %get-tuple-element.83), channel_id=1, source_target_pairs={{0,17},{1,16},{8,25},{9,24},{16,1},{17,0},{24,9},{25,8},{2,19},{3,... | collective-permute-start | bytes 221192 | tf_op jit(solution)/shard_map/ppermute | solution.py:643
  12.2 4.5 %collective-permute-start.8 = (bf16[144,256]{1,0:T(8,128)(2,1)S(1)}, bf16[144,256]{1,0:T(8,128)(2,1)S(1)}, u32[]{:S(2)}, u32[]{:S(2)}) collective-permute-start(bf16[144,256]{1,0:T(8,128)(2,1)S(1)} %get-tuple-element.84), channel_id=1, source_target_pairs={{0,24},{1,25},{8,16},{9,17},{16,8},{17,9},{24,0},{25,1},{2,26},{3,... | collective-permute-start | bytes 221192 | tf_op jit(solution)/shard_map/ppermute | solution.py:643
  12.8 6.3 %collective-permute-start.9 = (bf16[144,256]{1,0:T(8,128)(2,1)S(1)}, bf16[144,256]{1,0:T(8,128)(2,1)S(1)}, u32[]{:S(2)}, u32[]{:S(2)}) collective-permute-start(bf16[144,256]{1,0:T(8,128)(2,1)S(1)} %get-tuple-element.85), channel_id=1, source_target_pairs={{0,25},{1,24},{8,17},{9,16},{16,9},{17,8},{24,1},{25,0},{2,27},{3,... | collective-permute-start | bytes 221192 | tf_op jit(solution)/shard_map/ppermute | solution.py:643
  21.2 24.5 %all-to-all-start.3 = ((bf16[8,128,512]{2,1,0:T(8,128)(2,1)}), bf16[8,128,512]{2,1,0:T(8,128)(2,1)S(1)}, u32[]{:S(2)}, u32[]{:S(2)}) async-start(bf16[8,128,512]{2,1,0:T(8,128)(2,1)} %bitcast.17), calls=%async_computation.3 | async-start | bytes 2097152 | tf_op jit(solution)/shard_map/all_to_all | solution.py:693
  24.8 9.2 %collective-permute-start.10 = (bf16[304,256]{1,0:T(8,128)(2,1)S(1)}, bf16[304,256]{1,0:T(8,128)(2,1)S(1)}, u32[]{:S(2)}, u32[]{:S(2)}) collective-permute-start(bf16[304,256]{1,0:T(8,128)(2,1)S(1)} %get-tuple-element.87), channel_id=1, source_target_pairs={{0,2},{1,3},{8,10},{9,11},{16,18},{17,19},{24,26},{25,27},{2,0},{3... | collective-permute-start | bytes 466952 | tf_op jit(solution)/shard_map/ppermute | solution.py:651
  26.5 14.5 %collective-permute-start.11 = (bf16[304,256]{1,0:T(8,128)(2,1)S(1)}, bf16[304,256]{1,0:T(8,128)(2,1)S(1)}, u32[]{:S(2)}, u32[]{:S(2)}) collective-permute-start(bf16[304,256]{1,0:T(8,128)(2,1)S(1)} %get-tuple-element.88), channel_id=1, source_target_pairs={{0,4},{1,5},{8,12},{9,13},{16,20},{17,21},{24,28},{25,29},{2,6},{3... | collective-permute-start | bytes 466952 | tf_op jit(solution)/shard_map/ppermute | solution.py:651
  29.0 11.9 %collective-permute-start.12 = (bf16[304,256]{1,0:T(8,128)(2,1)S(1)}, bf16[304,256]{1,0:T(8,128)(2,1)S(1)}, u32[]{:S(2)}, u32[]{:S(2)}) collective-permute-start(bf16[304,256]{1,0:T(8,128)(2,1)S(1)} %get-tuple-element.89), channel_id=1, source_target_pairs={{0,6},{1,7},{8,14},{9,15},{16,22},{17,23},{24,30},{25,31},{2,4},{3... | collective-permute-start | bytes 466952 | tf_op jit(solution)/shard_map/ppermute | solution.py:651
  42.2 8.5 %collective-permute-start.13 = (bf16[512,256]{1,0:T(8,128)(2,1)S(1)}, bf16[512,256]{1,0:T(8,128)(2,1)S(1)}, u32[]{:S(2)}, u32[]{:S(2)}) collective-permute-start(bf16[512,256]{1,0:T(8,128)(2,1)S(1)} %get-tuple-element.92), channel_id=1, source_target_pairs={{0,1},{1,0},{8,9},{9,8},{16,17},{17,16},{24,25},{25,24},{2,3},{3,2... | collective-permute-start | bytes 786440 | tf_op jit(solution)/shard_map/ppermute | solution.py:643
  44.1 9.8 %collective-permute-start.14 = (bf16[512,256]{1,0:T(8,128)(2,1)S(1)}, bf16[512,256]{1,0:T(8,128)(2,1)S(1)}, u32[]{:S(2)}, u32[]{:S(2)}) collective-permute-start(bf16[512,256]{1,0:T(8,128)(2,1)S(1)} %get-tuple-element.93), channel_id=1, source_target_pairs={{0,16},{1,17},{8,24},{9,25},{16,0},{17,1},{24,8},{25,9},{2,18},{3,... | collective-permute-start | bytes 786440 | tf_op jit(solution)/shard_map/ppermute | solution.py:643
  45.6 10.6 %collective-permute-start.15 = (bf16[512,256]{1,0:T(8,128)(2,1)S(1)}, bf16[512,256]{1,0:T(8,128)(2,1)S(1)}, u32[]{:S(2)}, u32[]{:S(2)}) collective-permute-start(bf16[512,256]{1,0:T(8,128)(2,1)S(1)} %get-tuple-element.94), channel_id=1, source_target_pairs={{0,17},{1,16},{8,25},{9,24},{16,1},{17,0},{24,9},{25,8},{2,19},{3,... | collective-permute-start | bytes 786440 | tf_op jit(solution)/shard_map/ppermute | solution.py:643
  46.5 9.6 %collective-permute-start.16 = (bf16[288,256]{1,0:T(8,128)(2,1)S(1)}, bf16[288,256]{1,0:T(8,128)(2,1)S(1)}, u32[]{:S(2)}, u32[]{:S(2)}) collective-permute-start(bf16[288,256]{1,0:T(8,128)(2,1)S(1)} %get-tuple-element.101), channel_id=1, source_target_pairs={{0,2},{1,3},{8,10},{9,11},{16,18},{17,19},{24,26},{25,27},{2,0},{3... | collective-permute-start | bytes 442376 | tf_op jit(solution)/shard_map/ppermute | solution.py:651
  49.6 12.7 %collective-permute-start.17 = (bf16[288,256]{1,0:T(8,128)(2,1)S(1)}, bf16[288,256]{1,0:T(8,128)(2,1)S(1)}, u32[]{:S(2)}, u32[]{:S(2)}) collective-permute-start(bf16[288,256]{1,0:T(8,128)(2,1)S(1)} %get-tuple-element.102), channel_id=1, source_target_pairs={{0,4},{1,5},{8,12},{9,13},{16,20},{17,21},{24,28},{25,29},{2,6},{3... | collective-permute-start | bytes 442376 | tf_op jit(solution)/shard_map/ppermute | solution.py:651
  50.7 11.6 %collective-permute-start.18 = (bf16[288,256]{1,0:T(8,128)(2,1)S(1)}, bf16[288,256]{1,0:T(8,128)(2,1)S(1)}, u32[]{:S(2)}, u32[]{:S(2)}) collective-permute-start(bf16[288,256]{1,0:T(8,128)(2,1)S(1)} %get-tuple-element.103), channel_id=1, source_target_pairs={{0,6},{1,7},{8,14},{9,15},{16,22},{17,23},{24,30},{25,31},{2,4},{3... | collective-permute-start | bytes 442376 | tf_op jit(solution)/shard_map/ppermute | solution.py:651
  53.9 16.2 %collective-permute-start.22 = (bf16[288,256]{1,0:T(8,128)(2,1)S(1)}, bf16[288,256]{1,0:T(8,128)(2,1)S(1)}, u32[]{:S(2)}, u32[]{:S(2)}) collective-permute-start(bf16[288,256]{1,0:T(8,128)(2,1)S(1)} %get-tuple-element.114), channel_id=1, source_target_pairs={{0,2},{1,3},{8,10},{9,11},{16,18},{17,19},{24,26},{25,27},{2,0},{3... | collective-permute-start | bytes 442376 | tf_op jit(solution)/shard_map/ppermute | solution.py:651
  63.3 16.2 %collective-permute-start.19 = (bf16[512,256]{1,0:T(8,128)(2,1)S(1)}, bf16[512,256]{1,0:T(8,128)(2,1)S(1)}, u32[]{:S(2)}, u32[]{:S(2)}) collective-permute-start(bf16[512,256]{1,0:T(8,128)(2,1)S(1)} %get-tuple-element.109), channel_id=1, source_target_pairs={{0,1},{1,0},{8,9},{9,8},{16,17},{17,16},{24,25},{25,24},{2,3},{3,2... | collective-permute-start | bytes 786440 | tf_op jit(solution)/shard_map/ppermute | solution.py:643
  64.8 14.7 %collective-permute-start.20 = (bf16[512,256]{1,0:T(8,128)(2,1)S(1)}, bf16[512,256]{1,0:T(8,128)(2,1)S(1)}, u32[]{:S(2)}, u32[]{:S(2)}) collective-permute-start(bf16[512,256]{1,0:T(8,128)(2,1)S(1)} %get-tuple-element.110), channel_id=1, source_target_pairs={{0,16},{1,17},{8,24},{9,25},{16,0},{17,1},{24,8},{25,9},{2,18},{3,... | collective-permute-start | bytes 786440 | tf_op jit(solution)/shard_map/ppermute | solution.py:643
  66.3 13.2 %collective-permute-start.21 = (bf16[512,256]{1,0:T(8,128)(2,1)S(1)}, bf16[512,256]{1,0:T(8,128)(2,1)S(1)}, u32[]{:S(2)}, u32[]{:S(2)}) collective-permute-start(bf16[512,256]{1,0:T(8,128)(2,1)S(1)} %get-tuple-element.111), channel_id=1, source_target_pairs={{0,17},{1,16},{8,25},{9,24},{16,1},{17,0},{24,9},{25,8},{2,19},{3,... | collective-permute-start | bytes 786440 | tf_op jit(solution)/shard_map/ppermute | solution.py:643
  66.9 12.7 %collective-permute-start.23 = (bf16[288,256]{1,0:T(8,128)(2,1)S(1)}, bf16[288,256]{1,0:T(8,128)(2,1)S(1)}, u32[]{:S(2)}, u32[]{:S(2)}) collective-permute-start(bf16[288,256]{1,0:T(8,128)(2,1)S(1)} %get-tuple-element.115), channel_id=1, source_target_pairs={{0,4},{1,5},{8,12},{9,13},{16,20},{17,21},{24,28},{25,29},{2,6},{3... | collective-permute-start | bytes 442376 | tf_op jit(solution)/shard_map/ppermute | solution.py:651
  70.1 9.5 %collective-permute-start.24 = (bf16[288,256]{1,0:T(8,128)(2,1)S(1)}, bf16[288,256]{1,0:T(8,128)(2,1)S(1)}, u32[]{:S(2)}, u32[]{:S(2)}) collective-permute-start(bf16[288,256]{1,0:T(8,128)(2,1)S(1)} %get-tuple-element.116), channel_id=1, source_target_pairs={{0,6},{1,7},{8,14},{9,15},{16,22},{17,23},{24,30},{25,31},{2,4},{3... | collective-permute-start | bytes 442376 | tf_op jit(solution)/shard_map/ppermute | solution.py:651
  80.6 8.7 %collective-permute-start.25 = (bf16[512,256]{1,0:T(8,128)(2,1)S(1)}, bf16[512,256]{1,0:T(8,128)(2,1)S(1)}, u32[]{:S(2)}, u32[]{:S(2)}) collective-permute-start(bf16[512,256]{1,0:T(8,128)(2,1)S(1)} %get-tuple-element.122), channel_id=1, source_target_pairs={{0,1},{1,0},{8,9},{9,8},{16,17},{17,16},{24,25},{25,24},{2,3},{3,2... | collective-permute-start | bytes 786440 | tf_op jit(solution)/shard_map/ppermute | solution.py:643
  82.1 8.8 %collective-permute-start.26 = (bf16[512,256]{1,0:T(8,128)(2,1)S(1)}, bf16[512,256]{1,0:T(8,128)(2,1)S(1)}, u32[]{:S(2)}, u32[]{:S(2)}) collective-permute-start(bf16[512,256]{1,0:T(8,128)(2,1)S(1)} %get-tuple-element.123), channel_id=1, source_target_pairs={{0,16},{1,17},{8,24},{9,25},{16,0},{17,1},{24,8},{25,9},{2,18},{3,... | collective-permute-start | bytes 786440 | tf_op jit(solution)/shard_map/ppermute | solution.py:643
  83.6 10.1 %collective-permute-start.27 = (bf16[512,256]{1,0:T(8,128)(2,1)S(1)}, bf16[512,256]{1,0:T(8,128)(2,1)S(1)}, u32[]{:S(2)}, u32[]{:S(2)}) collective-permute-start(bf16[512,256]{1,0:T(8,128)(2,1)S(1)} %get-tuple-element.124), channel_id=1, source_target_pairs={{0,17},{1,16},{8,25},{9,24},{16,1},{17,0},{24,9},{25,8},{2,19},{3,... | collective-permute-start | bytes 786440 | tf_op jit(solution)/shard_map/ppermute | solution.py:643
  84.2 10.2 %collective-permute-start.28 = (bf16[1024,256]{1,0:T(8,128)(2,1)S(1)}, bf16[1024,256]{1,0:T(8,128)(2,1)S(1)}, u32[]{:S(2)}, u32[]{:S(2)}) collective-permute-start(bf16[1024,256]{1,0:T(8,128)(2,1)S(1)} %get-tuple-element.95.refs_0_), channel_id=1, source_target_pairs={{0,8},{1,9},{8,0},{9,1},{16,24},{17,25},{24,16},{25,17},{2,10},{3,... | collective-permute-start | bytes 1572872 | tf_op jit(solution)/shard_map/ppermute | solution.py:643
  84.4 10.5 %collective-permute-start.29 = (bf16[1024,256]{1,0:T(8,128)(2,1)S(1)}, bf16[1024,256]{1,0:T(8,128)(2,1)S(1)}, u32[]{:S(2)}, u32[]{:S(2)}) collective-permute-start(bf16[1024,256]{1,0:T(8,128)(2,1)S(1)} %get-tuple-element.112.refs_1_), channel_id=1, source_target_pairs={{0,8},{1,9},{8,0},{9,1},{16,24},{17,25},{24,16},{25,17},{2,10},{3,... | collective-permute-start | bytes 1572872 | tf_op jit(solution)/shard_map/ppermute | solution.py:643
  93.9 5.0 %collective-permute-start.31 = (bf16[1024,256]{1,0:T(8,128)(2,1)S(1)}, bf16[1024,256]{1,0:T(8,128)(2,1)S(1)}, u32[]{:S(2)}, u32[]{:S(2)}) collective-permute-start(bf16[1024,256]{1,0:T(8,128)(2,1)S(1)} %get-tuple-element.128.refs_0_), channel_id=1, source_target_pairs={{0,8},{1,9},{8,0},{9,1},{16,24},{17,25},{24,16},{25,17},{2,10},{3,... | collective-permute-start | bytes 1572872 | tf_op jit(solution)/shard_map/ppermute | solution.py:643
  94.4 4.5 %collective-permute-start.32 = (bf16[1024,256]{1,0:T(8,128)(2,1)S(1)}, bf16[1024,256]{1,0:T(8,128)(2,1)S(1)}, u32[]{:S(2)}, u32[]{:S(2)}) collective-permute-start(bf16[1024,256]{1,0:T(8,128)(2,1)S(1)} %get-tuple-element.129.refs_1_), channel_id=1, source_target_pairs={{0,8},{1,9},{8,0},{9,1},{16,24},{17,25},{24,16},{25,17},{2,10},{3,... | collective-permute-start | bytes 1572872 | tf_op jit(solution)/shard_map/ppermute | solution.py:643
  94.4 4.4 %collective-permute-start.33 = (bf16[1024,256]{1,0:T(8,128)(2,1)S(1)}, bf16[1024,256]{1,0:T(8,128)(2,1)S(1)}, u32[]{:S(2)}, u32[]{:S(2)}) collective-permute-start(bf16[1024,256]{1,0:T(8,128)(2,1)S(1)} %get-tuple-element.130.refs_2_), channel_id=1, source_target_pairs={{0,8},{1,9},{8,0},{9,1},{16,24},{17,25},{24,16},{25,17},{2,10},{3,... | collective-permute-start | bytes 1572872 | tf_op jit(solution)/shard_map/ppermute | solution.py:643
  100.2 18.0 %all-to-all-start.4 = ((f32[32,8,128]{2,1,0:T(8,128)}), f32[32,8,128]{2,1,0:T(8,128)S(1)}, u32[]{:S(2)}, u32[]{:S(2)}) async-start(f32[32,8,128]{2,1,0:T(8,128)} %shard_map.60), calls=%async_computation.4 | async-start | bytes 262144 | tf_op jit(solution)/shard_map/all_to_all | solution.py:569
  (6 other events, 65.6 us)

commit v7 on v6

--- a/solution.py
+++ b/solution.py
@@ -254,8 +254,24 @@
     return lax.axis_index("ingest") * plan.width + run % plan.width, run // plan.width
 
 
+def spread_pair(plan, part, target, rows):
+    row = lax.broadcasted_iota(jnp.int32, (2 * plan.part, plan.rows), 0) + part * plan.part
+    chosen = jnp.where(row == target, 1.0, 0.0).astype(jnp.bfloat16)
+    return jnp.dot(chosen, rows, preferred_element_type=jnp.float32).astype(jnp.bfloat16)
+
+
+def spread_more_kernel(plan, unit_ref, target_ref, out_ref):
+    lane, _ = my_lane(plan)
+    for part in range(0, plan.lanes, 2):
+        moved = spread_pair(plan, part, target_ref[...], unit_ref[:, plan.chunks[0] :])
+        for number in range(2):
+            whole = pl.multiple_of((part + number ^ lane) * plan.part, plan.part)
+            here = moved[number * plan.part : (number + 1) * plan.part, :]
+            out_ref[pl.ds(whole, plan.part), :] = here
+
+
 def spread_kernel(plan, run_len_ref, cluster_ref, rank_ref, rows_ref, *rest):
-    outs, (unit_ref,) = rest[:-1], rest[-1:]
+    outs, (unit_ref, target_ref) = rest[:-2], rest[-2:]
     step = 128
 
     @pl.loop(0, plan.rows // step)
@@ -287,19 +303,11 @@
         + mine.astype(jnp.int32) * plan.slice
         + residue % plan.slice
     )
-    tile = 2 * plan.part
-
-    for pair in range(plan.lanes // 2):
-        row = lax.broadcasted_iota(jnp.int32, (tile, plan.rows), 0) + pair * tile
-        chosen = jnp.where(row == target, 1.0, 0.0).astype(jnp.bfloat16)
-        moved = jnp.dot(chosen, unit_ref[...], preferred_element_type=jnp.float32)
-        moved = moved.astype(jnp.bfloat16)
-        for number in range(2):
-            here = moved[number * plan.part : (number + 1) * plan.part, :]
-            outs[2 * pair + number][: plan.part, :] = here[:, : plan.chunks[0]]
-            whole = (2 * pair + number ^ lane) * plan.part
-            there = pl.ds(pl.multiple_of(whole, plan.part), plan.part)
-            outs[plan.lanes][there, :] = here[:, plan.chunks[0] :]
+    target_ref[...] = target
+    for part in range(0, plan.lanes, 2):
+        moved = spread_pair(plan, part, target, unit_ref[:, : plan.chunks[0]])
+        outs[part][: plan.part, :] = moved[: plan.part, :]
+        outs[part + 1][: plan.part, :] = moved[plan.part :, :]
 
     place = lax.broadcasted_iota(jnp.int32, (plan.devices, plan.part), 1) // plan.slice
     here = (place.astype(jnp.float32) == order[:, :1]) & (block > 0)
@@ -308,7 +316,7 @@
     blocks = jnp.sum(jnp.where(here, block - 1, 0), axis=0, keepdims=True)
     line = lax.broadcasted_iota(jnp.int32, (16, plan.part), 0)
     table = jnp.where(line == 0, owners, jnp.where(line == 1, blocks, 0))
-    for out in outs[: plan.lanes]:
+    for out in outs:
         out[plan.part :, : plan.part] = table.astype(jnp.float32).astype(jnp.bfloat16)
 
 
@@ -461,13 +469,17 @@
     best_ref[...] = jnp.maximum(best_ref[...], jnp.max(scores, axis=0, keepdims=True))
 
 
-def pair_best_kernel(plan, *refs):
+def staged_best_kernel(plan, run_len_ref, *refs):
     count = len(plan.chunks)
-    own, mate = refs[:count], refs[count : 2 * count]
-    queries_ref, out_ref, best_ref = refs[2 * count :]
+    own, mate, behind, far = (refs[n * count : (n + 1) * count] for n in range(4))
+    out_ref, best_ref, queries_ref, lines_ref = refs[4 * count :]
     lane, _ = my_lane(plan)
-    _, slot = plan.slot(lax.axis_index("ingest"), lax.axis_index("run"))
+    group, slot = plan.slot(lax.axis_index("ingest"), lax.axis_index("run"))
     core = slot % 2
+    begin = jnp.int32(0)
+    for number, start in enumerate(cluster_starts(plan, run_len_ref)):
+        here = (number // plan.per_group == group) & (start <= slot)
+        begin = jnp.where(here, jnp.maximum(begin, start), begin)
     chips = plan.lanes // 2
     for side, parts in enumerate((own, mate)):
         for chip in range(chips):
@@ -500,29 +512,13 @@
                     keys.append(jnp.concatenate([part[here, :] for part in parts], axis=1))
                 add_best(jnp.concatenate(keys, axis=0), queries_ref, best_ref)
 
-    out_ref[...] = best_ref[...]
-
-
-def more_best_kernel(plan, run_len_ref, given_ref, queries_ref, *refs, last):
-    count = len(plan.chunks)
-    behind, (out_ref, best_ref) = refs[:count], refs[count : count + 2]
-    group, slot = plan.slot(lax.axis_index("ingest"), lax.axis_index("run"))
-    begin = jnp.int32(0)
-    for number, start in enumerate(cluster_starts(plan, run_len_ref)):
-        here = (number // plan.per_group == group) & (start <= slot)
-        begin = jnp.where(here, jnp.maximum(begin, start), begin)
-    best_ref[...] = given_ref[...]
-
-    @pl.when(slot - slot % 2 - 2 >= begin)
+    @pl.when(slot - core - 2 >= begin)
     def _():
-        for first in range(0, plan.rows, TILE):
-            keys = [part[first : first + TILE, :] for part in behind]
-            add_best(jnp.concatenate(keys, axis=1), queries_ref, best_ref)
-
-    if not last:
-        out_ref[...] = best_ref[...]
-        return
-    lines_ref = refs[-1]
+        for parts in (behind, far):
+            for first in range(0, plan.rows, TILE):
+                keys = [part[first : first + TILE, :] for part in parts]
+                add_best(jnp.concatenate(keys, axis=1), queries_ref, best_ref)
+
     for number in range(plan.lanes):
         lines_ref[number : number + 1, :] = best_ref[
             :, number * plan.part : (number + 1) * plan.part
@@ -652,22 +648,32 @@
 
     far_first = sorted(lanes[1:], key=lambda change: -(change & 1) - (change // plan.width // 2))
 
-    spread = call(
+    *spread, unit, target = call(
         spread_kernel,
         plan,
         [wide((plan.part + 16, plan.chunks[0]), half) for _ in lanes]
-        + [wide((rows, width - plan.chunks[0]), half)],
+        + [wide((rows, width), half), wide((1, rows), jnp.int32)],
         [SMEM, VMEM, VMEM, VMEM],
-        [pltpu.VMEM((rows, width), half)],
-        2 * rows * rows * width,
+        (),
+        2 * rows * rows * plan.chunks[0],
         3 * rows * width * 2,
+        memory=24,
     )(run_len, clusters, ranks, embeddings)
-    *spread, later = spread
+    (later,) = call(
+        spread_more_kernel,
+        plan,
+        [wide((rows, width - plan.chunks[0]), half)],
+        [VMEM, VMEM],
+        (),
+        2 * rows * rows * (width - plan.chunks[0]),
+        3 * rows * width * 2,
+        memory=16,
+    )(unit, target)
     swapped = {change: along_lanes(spread[change], change) for change in far_first}
     spread = [spread[0]] + [swapped[change] for change in lanes[1:]]
     pair, mates, behind, fars = [], [], [], []
     table = targets = full = None
-    arrivals = []
+    arrivals, routes = [], []
     for chunk, f in enumerate(plan.chunks):
         spec = dict(flops=2 * rows * rows * f, moved=3 * rows * f * 2, memory=12)
         rooms = [wide((plan.room + (0 if chunk else 16), f), half) for _ in layers]
@@ -698,12 +704,16 @@
         moved = {change: along_layers(routed[change], change) for change in reversed(layers[1:])}
         arrived = [routed[0]] + [moved[change] for change in layers[1:]]
         arrivals.append(arrived)
+        routes.append(routed)
     for chunk, f in enumerate(plan.chunks):
         spec = dict(flops=2 * rows * rows * f, moved=3 * rows * f * 2, memory=12)
         inputs = pltpu.VMEM((rows, f), half)
         arrived = arrivals[chunk]
+        ahead = chunk + 1
         if chunk:
             arrived, _ = lax.optimization_barrier((arrived, parts))
+        if ahead < len(plan.chunks):
+            arrived, _ = lax.optimization_barrier((arrived, arrivals[ahead][1] if ahead == 2 else routes[ahead]))
         shapes = [wide((4 * plan.part, f), half) for _ in range(plan.lanes // 2)]
         scratch = [pltpu.VMEM((plan.layers * plan.stride, f), half), inputs]
         if chunk == 0:
@@ -735,31 +745,21 @@
             kept.append(block)
         for kept, block in zip((mates, fars), joined):
             kept.append(along_lanes(block, plan.width))
-    line = wide((1, rows), jnp.float32)
-    kept = pltpu.VMEM((1, rows), jnp.float32)
     count = len(plan.chunks)
-    spec = dict(flops=4 * rows * rows * width, moved=3 * rows * width * 2, memory=24)
-    queries, best = call(
-        pair_best_kernel,
-        plan,
-        [wide((rows, width), half), line],
-        [VMEM] * (2 * count),
-        [kept],
-        **spec,
-    )(*pair, *mates)
-    spec = dict(flops=2 * rows * rows * width, moved=3 * rows * width * 2, memory=24)
-    places = [SMEM] + [VMEM] * (2 + count)
-    (best,) = call(
-        functools.partial(more_best_kernel, last=False), plan, [line], places, [kept], **spec
-    )(run_len, best, queries, *behind)
     (replies,) = call(
-        functools.partial(more_best_kernel, last=True),
+        staged_best_kernel,
         plan,
         [wide((plan.devices, plan.lanes, 128), jnp.float32)],
-        places,
-        [kept, pltpu.VMEM((plan.lanes, 128), jnp.float32)],
-        **spec,
-    )(run_len, best, queries, *fars)
+        [SMEM] + [VMEM] * (4 * count),
+        [
+            pltpu.VMEM((1, rows), jnp.float32),
+            pltpu.VMEM((rows, width), half),
+            pltpu.VMEM((plan.lanes, 128), jnp.float32),
+        ],
+        2 * rows * rows * width * 3,
+        4 * rows * width * 2,
+        memory=24,
+    )(run_len, *pair, *mates, *behind, *fars)
     returned = exchange(replies).reshape(plan.devices * plan.lanes, 128)
     (best,) = call(
         staged_unpack_kernel,

time: 120 us -> 112 us (0.933)
  waiting for transfers between devices: 46.5 us -> 42.6 us
  starting transfers between devices: 53 us -> 49.2 us
    ppermute x9, waiting for transfers between devices: 26 us -> 10 us  [along_layers(): return lax.ppermute(block, AXES, pairs)]
    all_to_all x1, waiting for transfers between devices: 0.01 us -> 10 us  [staged(): lax.all_to_all(later, AXES, 0, 0, tiled=True, axis_index_groups=groups)]
    pallas_call x1, Pallas kernels: 5.66 us -> 3.54 us  [staged(): call(spread_kernel, plan, [wide((plan.part + 16, plan.chunks[0]), half) f...]
    ppermute x22, waiting for transfers between devices: 13.9 us -> 16 us  [along_lanes(): return lax.ppermute(block, AXES, pairs)]
    ppermute x9, starting transfers between devices: 17.8 us -> 16.1 us  [along_layers(): return lax.ppermute(block, AXES, pairs)]
    pallas_call x3 -> x2, Pallas kernels: 4.31 us -> 5.9 us  [the longest x1 3.64 us: staged(): call(staged_best_kernel, plan, [wide((plan.devices, plan.lanes, 128), jnp...]
    all_to_all x1, starting transfers between devices: 10.2 us -> 8.98 us  [exchange(): return lax.all_to_all(block, AXES, split_axis=0, concat_axis=0, tiled=True)]
where the time goes in v7:
time: 112 us
  starting transfers between devices  49.2 us (44%)
  waiting for transfers between devices  42.6 us (38%)
  Pallas kernels  18.1 us (16%)
  local copies, waits for them, and re-layouts  1.12 us (1%)
    ppermute x22, starting transfers between devices, along_lanes(): return lax.ppermute(block, AXES, pairs)  20.5 us
    ppermute x9, starting transfers between devices, along_layers(): return lax.ppermute(block, AXES, pairs)  16.1 us
    ppermute x22, waiting for transfers between devices, along_lanes(): return lax.ppermute(block, AXES, pairs)  16 us
    ppermute x9, waiting for transfers between devices, along_layers(): return lax.ppermute(block, AXES, pairs)  10 us
    all_to_all x1, waiting for transfers between devices, staged(): lax.all_to_all(later, AXES, 0, 0, tiled=True, axis_index_groups=groups)  10 us
    all_to_all x1, starting transfers between devices, exchange(): return lax.all_to_all(block, AXES, split_axis=0, concat_axis=0, tiled=True)  8.98 us
    all_to_all x1, waiting for transfers between devices, exchange(): return lax.all_to_all(block, AXES, split_axis=0, concat_axis=0, tiled=True)  6.57 us
    pallas_call x1, Pallas kernels, staged(): call(staged_best_kernel, plan, [wide((plan.devices, plan.lanes, 128), jnp...  3.64 us
  transfers between devices with their start and end apart: 33, of which 12 were waited for; matrix products, arithmetic and copies ran while one was open for 0% of the time, Pallas kernels for 6%

profile of v7, /device:TPU:0, one launch (start us, length us, event | category | flops | bytes accessed | tf_op | source)
XLA Modules:
  0.0 111.8 jit_solution(4655530541837487857)
XLA Ops:
  0.0 3.5 %shard_map.48 = (bf16[144,256]{1,0:T(8,128)(2,1)S(1)}, bf16[144,256]{1,0:T(8,128)(2,1)S(1)}, bf16[144,256]{1,0:T(8,128)(2,1)S(1)}, bf16[144,256]{1,0:T(8,128)(2,...) custom-call(s32[12]{0:T(128)} %run_len_ref.5, ...), custom_call_target="tpu_custom_call" | custom-call | flops 536870912 | bytes 4718592 | tf_op jit(solution)/shard_map/pallas_call | solution.py:651
  3.5 3.0 %collective-permute-start.3 = (bf16[144,256]{1,0:T(8,128)(2,1)S(1)}, bf16[144,256]{1,0:T(8,128)(2,1)S(1)}, u32[]{:S(2)}, u32[]{:S(2)}) collective-permute-start(bf16[144,256]{1,0:T(8,128)(2,1)S(1)} %get-tuple-element.86), channel_id=1, source_target_pairs={{0,1},{1,0},{8,9},{9,8},{16,17},{17,16},{24,25},{25,24},{2,3},{3,2... | collective-permute-start | bytes 221192 | tf_op jit(solution)/shard_map/ppermute | solution.py:639
  6.8 1.9 %collective-permute-start.6 = (bf16[144,256]{1,0:T(8,128)(2,1)S(1)}, bf16[144,256]{1,0:T(8,128)(2,1)S(1)}, u32[]{:S(2)}, u32[]{:S(2)}) collective-permute-start(bf16[144,256]{1,0:T(8,128)(2,1)S(1)} %get-tuple-element.89), channel_id=1, source_target_pairs={{0,16},{1,17},{8,24},{9,25},{16,0},{17,1},{24,8},{25,9},{2,18},{3,... | collective-permute-start | bytes 221192 | tf_op jit(solution)/shard_map/ppermute | solution.py:639
  8.7 1.5 %collective-permute-start.7 = (bf16[144,256]{1,0:T(8,128)(2,1)S(1)}, bf16[144,256]{1,0:T(8,128)(2,1)S(1)}, u32[]{:S(2)}, u32[]{:S(2)}) collective-permute-start(bf16[144,256]{1,0:T(8,128)(2,1)S(1)} %get-tuple-element.90), channel_id=1, source_target_pairs={{0,17},{1,16},{8,25},{9,24},{16,1},{17,0},{24,9},{25,8},{2,19},{3,... | collective-permute-start | bytes 221192 | tf_op jit(solution)/shard_map/ppermute | solution.py:639
  10.7 2.0 %collective-permute-start.9 = (bf16[144,256]{1,0:T(8,128)(2,1)S(1)}, bf16[144,256]{1,0:T(8,128)(2,1)S(1)}, u32[]{:S(2)}, u32[]{:S(2)}) collective-permute-start(bf16[144,256]{1,0:T(8,128)(2,1)S(1)} %get-tuple-element.92), channel_id=1, source_target_pairs={{0,25},{1,24},{8,17},{9,16},{16,9},{17,8},{24,1},{25,0},{2,27},{3,... | collective-permute-start | bytes 221192 | tf_op jit(solution)/shard_map/ppermute | solution.py:639
  12.7 2.3 %shard_map.50 = bf16[1024,512]{1,0:T(8,128)(2,1)} custom-call(bf16[1024,768]{1,0:T(8,128)(2,1)S(1)} %get-tuple-element.98.unit_ref, s32[1,1024]{1,0:T(1,128)S(1)} %get-tuple-element.99.target_ref), custom_call_target="tpu_custom_call" | custom-call | flops 1073741824 | bytes 4718592 | tf_op jit(solution)/shard_map/pallas_call | solution.py:662
  15.0 2.0 %collective-permute-done.9.refs_7_ = bf16[144,256]{1,0:T(8,128)(2,1)S(1)} collective-permute-done((bf16[144,256]{1,0:T(8,128)(2,1)S(1)}, bf16[144,256]{1,0:T(8,128)(2,1)S(1)}, u32[]{:S(2)}, u32[]{:S(2)}) %collective-permute-start.9) | collective-permute-done | bytes 73760 | tf_op jit(solution)/shard_map/ppermute | solution.py:639
  17.0 2.2 %shard_map.49 = (bf16[304,256]{1,0:T(8,128)(2,1)S(1)}, bf16[304,256]{1,0:T(8,128)(2,1)S(1)}, bf16[304,256]{1,0:T(8,128)(2,1)S(1)}, bf16[304,256]{1,0:T(8,128)(2,1)S(1)}, s32[1,1024]{1,0:T(1,128)S(1)}) custom-call(bf16[144,256]{1,0:T(8,128)(2,1)S(1)} %get-tuple-element.85.refs_0_, bf16[144,256]{1,0:T(8,128)(2,1)S(1)} %collective-permute-done.3.refs_1_, ...), custom_call_target="tpu_custom_call" | custom-call | flops 536870912 | bytes 1572864 | tf_op jit(solution)/shard_map/pallas_call | solution.py:682
  19.2 3.6 %all-to-all-start.3 = ((bf16[8,128,512]{2,1,0:T(8,128)(2,1)}), bf16[8,128,512]{2,1,0:T(8,128)(2,1)S(1)}, u32[]{:S(2)}, u32[]{:S(2)}) async-start(bf16[8,128,512]{2,1,0:T(8,128)(2,1)} %bitcast.16), calls=%async_computation.3 | async-start | bytes 2097152 | tf_op jit(solution)/shard_map/all_to_all | solution.py:699
  22.8 1.6 %collective-permute-start.10 = (bf16[304,256]{1,0:T(8,128)(2,1)S(1)}, bf16[304,256]{1,0:T(8,128)(2,1)S(1)}, u32[]{:S(2)}, u32[]{:S(2)}) collective-permute-start(bf16[304,256]{1,0:T(8,128)(2,1)S(1)} %get-tuple-element.94), channel_id=1, source_target_pairs={{0,2},{1,3},{8,10},{9,11},{16,18},{17,19},{24,26},{25,27},{2,0},{3... | collective-permute-start | bytes 466952 | tf_op jit(solution)/shard_map/ppermute | solution.py:647
  24.4 2.6 %collective-permute-start.11 = (bf16[304,256]{1,0:T(8,128)(2,1)S(1)}, bf16[304,256]{1,0:T(8,128)(2,1)S(1)}, u32[]{:S(2)}, u32[]{:S(2)}) collective-permute-start(bf16[304,256]{1,0:T(8,128)(2,1)S(1)} %get-tuple-element.95), channel_id=1, source_target_pairs={{0,4},{1,5},{8,12},{9,13},{16,20},{17,21},{24,28},{25,29},{2,6},{3... | collective-permute-start | bytes 466952 | tf_op jit(solution)/shard_map/ppermute | solution.py:647
  27.2 10.0 %all-to-all-done.3 = bf16[8,128,512]{2,1,0:T(8,128)(2,1)S(1)} async-done(((bf16[8,128,512]{2,1,0:T(8,128)(2,1)}), bf16[8,128,512]{2,1,0:T(8,128)(2,1)S(1)}, u32[]{:S(2)}, u32[]{:S(2)}) %all-to-all-start.3) | async-done | bytes 1048608 | tf_op jit(solution)/shard_map/all_to_all | solution.py:699
  38.0 1.6 %collective-permute-start.16 = (bf16[288,256]{1,0:T(8,128)(2,1)S(1)}, bf16[288,256]{1,0:T(8,128)(2,1)S(1)}, u32[]{:S(2)}, u32[]{:S(2)}) collective-permute-start(bf16[288,256]{1,0:T(8,128)(2,1)S(1)} %get-tuple-element.102), channel_id=1, source_target_pairs={{0,2},{1,3},{8,10},{9,11},{16,18},{17,19},{24,26},{25,27},{2,0},{3... | collective-permute-start | bytes 442376 | tf_op jit(solution)/shard_map/ppermute | solution.py:647
  39.7 2.6 %collective-permute-start.17 = (bf16[288,256]{1,0:T(8,128)(2,1)S(1)}, bf16[288,256]{1,0:T(8,128)(2,1)S(1)}, u32[]{:S(2)}, u32[]{:S(2)}) collective-permute-start(bf16[288,256]{1,0:T(8,128)(2,1)S(1)} %get-tuple-element.103), channel_id=1, source_target_pairs={{0,4},{1,5},{8,12},{9,13},{16,20},{17,21},{24,28},{25,29},{2,6},{3... | collective-permute-start | bytes 442376 | tf_op jit(solution)/shard_map/ppermute | solution.py:647
  43.5 1.5 %collective-permute-start.13 = (bf16[512,256]{1,0:T(8,128)(2,1)S(1)}, bf16[512,256]{1,0:T(8,128)(2,1)S(1)}, u32[]{:S(2)}, u32[]{:S(2)}) collective-permute-start(bf16[512,256]{1,0:T(8,128)(2,1)S(1)} %get-tuple-element.111), channel_id=1, source_target_pairs={{0,1},{1,0},{8,9},{9,8},{16,17},{17,16},{24,25},{25,24},{2,3},{3,2... | collective-permute-start | bytes 786440 | tf_op jit(solution)/shard_map/ppermute | solution.py:639
  45.6 1.5 %collective-permute-start.15 = (bf16[512,256]{1,0:T(8,128)(2,1)S(1)}, bf16[512,256]{1,0:T(8,128)(2,1)S(1)}, u32[]{:S(2)}, u32[]{:S(2)}) collective-permute-start(bf16[512,256]{1,0:T(8,128)(2,1)S(1)} %get-tuple-element.113), channel_id=1, source_target_pairs={{0,17},{1,16},{8,25},{9,24},{16,1},{17,0},{24,9},{25,8},{2,19},{3,... | collective-permute-start | bytes 786440 | tf_op jit(solution)/shard_map/ppermute | solution.py:639
  47.0 2.3 %collective-permute-start.18 = (bf16[288,256]{1,0:T(8,128)(2,1)S(1)}, bf16[288,256]{1,0:T(8,128)(2,1)S(1)}, u32[]{:S(2)}, u32[]{:S(2)}) collective-permute-start(bf16[288,256]{1,0:T(8,128)(2,1)S(1)} %get-tuple-element.104), channel_id=1, source_target_pairs={{0,6},{1,7},{8,14},{9,15},{16,22},{17,23},{24,30},{25,31},{2,4},{3... | collective-permute-start | bytes 442376 | tf_op jit(solution)/shard_map/ppermute | solution.py:647
  50.3 4.7 %collective-permute-done.18.refs_3_ = bf16[288,256]{1,0:T(8,128)(2,1)S(1)} collective-permute-done((bf16[288,256]{1,0:T(8,128)(2,1)S(1)}, bf16[288,256]{1,0:T(8,128)(2,1)S(1)}, u32[]{:S(2)}, u32[]{:S(2)}) %collective-permute-start.18) | collective-permute-done | bytes 147488 | tf_op jit(solution)/shard_map/ppermute | solution.py:647
  55.0 2.2 %collective-permute-start.23 = (bf16[288,256]{1,0:T(8,128)(2,1)S(1)}, bf16[288,256]{1,0:T(8,128)(2,1)S(1)}, u32[]{:S(2)}, u32[]{:S(2)}) collective-permute-start(bf16[288,256]{1,0:T(8,128)(2,1)S(1)} %get-tuple-element.131), channel_id=1, source_target_pairs={{0,4},{1,5},{8,12},{9,13},{16,20},{17,21},{24,28},{25,29},{2,6},{3... | collective-permute-start | bytes 442376 | tf_op jit(solution)/shard_map/ppermute | solution.py:647
  60.9 1.7 %collective-permute-start.22 = (bf16[512,256]{1,0:T(8,128)(2,1)S(1)}, bf16[512,256]{1,0:T(8,128)(2,1)S(1)}, u32[]{:S(2)}, u32[]{:S(2)}) collective-permute-start(bf16[512,256]{1,0:T(8,128)(2,1)S(1)} %get-tuple-element.128), channel_id=1, source_target_pairs={{0,17},{1,16},{8,25},{9,24},{16,1},{17,0},{24,9},{25,8},{2,19},{3,... | collective-permute-start | bytes 786440 | tf_op jit(solution)/shard_map/ppermute | solution.py:639
  62.7 2.9 %collective-permute-start.24 = (bf16[288,256]{1,0:T(8,128)(2,1)S(1)}, bf16[288,256]{1,0:T(8,128)(2,1)S(1)}, u32[]{:S(2)}, u32[]{:S(2)}) collective-permute-start(bf16[288,256]{1,0:T(8,128)(2,1)S(1)} %get-tuple-element.132), channel_id=1, source_target_pairs={{0,6},{1,7},{8,14},{9,15},{16,22},{17,23},{24,30},{25,31},{2,4},{3... | collective-permute-start | bytes 442376 | tf_op jit(solution)/shard_map/ppermute | solution.py:647
  65.6 5.3 %collective-permute-done.24.refs_3_ = bf16[288,256]{1,0:T(8,128)(2,1)S(1)} collective-permute-done((bf16[288,256]{1,0:T(8,128)(2,1)S(1)}, bf16[288,256]{1,0:T(8,128)(2,1)S(1)}, u32[]{:S(2)}, u32[]{:S(2)}) %collective-permute-start.24) | collective-permute-done | bytes 147488 | tf_op jit(solution)/shard_map/ppermute | solution.py:647
  70.9 1.4 %collective-permute-done.22.refs_3_ = bf16[512,256]{1,0:T(8,128)(2,1)S(1)} collective-permute-done((bf16[512,256]{1,0:T(8,128)(2,1)S(1)}, bf16[512,256]{1,0:T(8,128)(2,1)S(1)}, u32[]{:S(2)}, u32[]{:S(2)}) %collective-permute-start.22) | collective-permute-done | bytes 262176 | tf_op jit(solution)/shard_map/ppermute | solution.py:639
  75.4 1.5 %collective-permute-start.27 = (bf16[512,256]{1,0:T(8,128)(2,1)S(1)}, bf16[512,256]{1,0:T(8,128)(2,1)S(1)}, u32[]{:S(2)}, u32[]{:S(2)}) collective-permute-start(bf16[512,256]{1,0:T(8,128)(2,1)S(1)} %get-tuple-element.140), channel_id=1, source_target_pairs={{0,17},{1,16},{8,25},{9,24},{16,1},{17,0},{24,9},{25,8},{2,19},{3,... | collective-permute-start | bytes 786440 | tf_op jit(solution)/shard_map/ppermute | solution.py:639
  77.0 4.8 %collective-permute-done.25.refs_1_ = bf16[512,256]{1,0:T(8,128)(2,1)S(1)} collective-permute-done((bf16[512,256]{1,0:T(8,128)(2,1)S(1)}, bf16[512,256]{1,0:T(8,128)(2,1)S(1)}, u32[]{:S(2)}, u32[]{:S(2)}) %collective-permute-start.25) | collective-permute-done | bytes 262176 | tf_op jit(solution)/shard_map/ppermute | solution.py:639
  81.8 1.7 %collective-permute-done.26.refs_2_ = bf16[512,256]{1,0:T(8,128)(2,1)S(1)} collective-permute-done((bf16[512,256]{1,0:T(8,128)(2,1)S(1)}, bf16[512,256]{1,0:T(8,128)(2,1)S(1)}, u32[]{:S(2)}, u32[]{:S(2)}) %collective-permute-start.26) | collective-permute-done | bytes 262176 | tf_op jit(solution)/shard_map/ppermute | solution.py:639
  83.4 3.2 %collective-permute-done.27.refs_3_ = bf16[512,256]{1,0:T(8,128)(2,1)S(1)} collective-permute-done((bf16[512,256]{1,0:T(8,128)(2,1)S(1)}, bf16[512,256]{1,0:T(8,128)(2,1)S(1)}, u32[]{:S(2)}, u32[]{:S(2)}) %collective-permute-start.27) | collective-permute-done | bytes 262176 | tf_op jit(solution)/shard_map/ppermute | solution.py:639
  87.4 1.3 %collective-permute-done.30.refs_5_ = bf16[1024,256]{1,0:T(8,128)(2,1)S(1)} collective-permute-done((bf16[1024,256]{1,0:T(8,128)(2,1)S(1)}, bf16[1024,256]{1,0:T(8,128)(2,1)S(1)}, u32[]{:S(2)}, u32[]{:S(2)}) %collective-permute-start.30) | collective-permute-done | bytes 524320 | tf_op jit(solution)/shard_map/ppermute | solution.py:639
  89.4 3.6 %shard_map.59 = f32[32,8,128]{2,1,0:T(8,128)} custom-call(s32[12]{0:T(128)S(1)} %copy-done.3, bf16[1024,256]{1,0:T(8,128)(2,1)S(1)} %get-tuple-element.114.refs_0_, bf16[1024,256]{1,0:T(8,128)(2,1)S(1)} %get-tuple-element.129.refs_1_, bf16[1024,256]{1,0:T(8,128)(2,1)S(1)} %get-tuple-element.141.refs_2_, ...), custom_call_target="tpu_custom_call" | custom-call | flops 4831838208 | bytes 6291456 | tf_op jit(solution)/shard_map/pallas_call | solution.py:749
  93.1 9.0 %all-to-all-start.4 = ((f32[32,8,128]{2,1,0:T(8,128)}), f32[32,8,128]{2,1,0:T(8,128)S(1)}, u32[]{:S(2)}, u32[]{:S(2)}) async-start(f32[32,8,128]{2,1,0:T(8,128)} %shard_map.59), calls=%async_computation.4 | async-start | bytes 262144 | tf_op jit(solution)/shard_map/all_to_all | solution.py:565
  103.2 6.6 %all-to-all-done.4 = f32[32,8,128]{2,1,0:T(8,128)S(1)} async-done(((f32[32,8,128]{2,1,0:T(8,128)}), f32[32,8,128]{2,1,0:T(8,128)S(1)}, u32[]{:S(2)}, u32[]{:S(2)}) %all-to-all-start.4) | async-done | bytes 131104 | tf_op jit(solution)/shard_map/all_to_all | solution.py:565
  109.8 1.4 %shard_map.60 = f32[1,1024]{1,0:T(1,128)S(1)} custom-call(s32[12]{0:T(128)S(1)} %copy-done.3, s32[1,1024]{1,0:T(1,128)S(1)} %bitcast.31, s32[1,1024]{1,0:T(1,128)S(1)} %bitcast.34, f32[256,128]{1,0:T(8,128)S(1)} %bitcast.24), custom_call_target="tpu_custom_call" | custom-call | bytes 16384 | tf_op jit(solution)/shard_map/pallas_call | solution.py:764
  (59 shorter events, 14.0 us)
Async XLA Ops:
  3.5 6.6 %collective-permute-start.3 = (bf16[144,256]{1,0:T(8,128)(2,1)S(1)}, bf16[144,256]{1,0:T(8,128)(2,1)S(1)}, u32[]{:S(2)}, u32[]{:S(2)}) collective-permute-start(bf16[144,256]{1,0:T(8,128)(2,1)S(1)} %get-tuple-element.86), channel_id=1, source_target_pairs={{0,1},{1,0},{8,9},{9,8},{16,17},{17,16},{24,25},{25,24},{2,3},{3,2... | collective-permute-start | bytes 221192 | tf_op jit(solution)/shard_map/ppermute | solution.py:639
  6.6 4.2 %collective-permute-start.4 = (bf16[144,256]{1,0:T(8,128)(2,1)S(1)}, bf16[144,256]{1,0:T(8,128)(2,1)S(1)}, u32[]{:S(2)}, u32[]{:S(2)}) collective-permute-start(bf16[144,256]{1,0:T(8,128)(2,1)S(1)} %get-tuple-element.87), channel_id=1, source_target_pairs={{0,8},{1,9},{8,0},{9,1},{16,24},{17,25},{24,16},{25,17},{2,10},{3,... | collective-permute-start | bytes 221192 | tf_op jit(solution)/shard_map/ppermute | solution.py:639
  6.6 8.4 %collective-permute-start.5 = (bf16[144,256]{1,0:T(8,128)(2,1)S(1)}, bf16[144,256]{1,0:T(8,128)(2,1)S(1)}, u32[]{:S(2)}, u32[]{:S(2)}) collective-permute-start(bf16[144,256]{1,0:T(8,128)(2,1)S(1)} %get-tuple-element.88), channel_id=1, source_target_pairs={{0,9},{1,8},{8,1},{9,0},{16,25},{17,24},{24,17},{25,16},{2,11},{3,... | collective-permute-start | bytes 221192 | tf_op jit(solution)/shard_map/ppermute | solution.py:639
  6.8 8.2 %collective-permute-start.6 = (bf16[144,256]{1,0:T(8,128)(2,1)S(1)}, bf16[144,256]{1,0:T(8,128)(2,1)S(1)}, u32[]{:S(2)}, u32[]{:S(2)}) collective-permute-start(bf16[144,256]{1,0:T(8,128)(2,1)S(1)} %get-tuple-element.89), channel_id=1, source_target_pairs={{0,16},{1,17},{8,24},{9,25},{16,0},{17,1},{24,8},{25,9},{2,18},{3,... | collective-permute-start | bytes 221192 | tf_op jit(solution)/shard_map/ppermute | solution.py:639
  8.7 6.3 %collective-permute-start.7 = (bf16[144,256]{1,0:T(8,128)(2,1)S(1)}, bf16[144,256]{1,0:T(8,128)(2,1)S(1)}, u32[]{:S(2)}, u32[]{:S(2)}) collective-permute-start(bf16[144,256]{1,0:T(8,128)(2,1)S(1)} %get-tuple-element.90), channel_id=1, source_target_pairs={{0,17},{1,16},{8,25},{9,24},{16,1},{17,0},{24,9},{25,8},{2,19},{3,... | collective-permute-start | bytes 221192 | tf_op jit(solution)/shard_map/ppermute | solution.py:639
  10.2 4.8 %collective-permute-start.8 = (bf16[144,256]{1,0:T(8,128)(2,1)S(1)}, bf16[144,256]{1,0:T(8,128)(2,1)S(1)}, u32[]{:S(2)}, u32[]{:S(2)}) collective-permute-start(bf16[144,256]{1,0:T(8,128)(2,1)S(1)} %get-tuple-element.91), channel_id=1, source_target_pairs={{0,24},{1,25},{8,16},{9,17},{16,8},{17,9},{24,0},{25,1},{2,26},{3,... | collective-permute-start | bytes 221192 | tf_op jit(solution)/shard_map/ppermute | solution.py:639
  10.7 6.3 %collective-permute-start.9 = (bf16[144,256]{1,0:T(8,128)(2,1)S(1)}, bf16[144,256]{1,0:T(8,128)(2,1)S(1)}, u32[]{:S(2)}, u32[]{:S(2)}) collective-permute-start(bf16[144,256]{1,0:T(8,128)(2,1)S(1)} %get-tuple-element.92), channel_id=1, source_target_pairs={{0,25},{1,24},{8,17},{9,16},{16,9},{17,8},{24,1},{25,0},{2,27},{3,... | collective-permute-start | bytes 221192 | tf_op jit(solution)/shard_map/ppermute | solution.py:639
  19.2 18.0 %all-to-all-start.3 = ((bf16[8,128,512]{2,1,0:T(8,128)(2,1)}), bf16[8,128,512]{2,1,0:T(8,128)(2,1)S(1)}, u32[]{:S(2)}, u32[]{:S(2)}) async-start(bf16[8,128,512]{2,1,0:T(8,128)(2,1)} %bitcast.16), calls=%async_computation.3 | async-start | bytes 2097152 | tf_op jit(solution)/shard_map/all_to_all | solution.py:699
  22.8 19.5 %collective-permute-start.10 = (bf16[304,256]{1,0:T(8,128)(2,1)S(1)}, bf16[304,256]{1,0:T(8,128)(2,1)S(1)}, u32[]{:S(2)}, u32[]{:S(2)}) collective-permute-start(bf16[304,256]{1,0:T(8,128)(2,1)S(1)} %get-tuple-element.94), channel_id=1, source_target_pairs={{0,2},{1,3},{8,10},{9,11},{16,18},{17,19},{24,26},{25,27},{2,0},{3... | collective-permute-start | bytes 466952 | tf_op jit(solution)/shard_map/ppermute | solution.py:647
  24.4 17.9 %collective-permute-start.11 = (bf16[304,256]{1,0:T(8,128)(2,1)S(1)}, bf16[304,256]{1,0:T(8,128)(2,1)S(1)}, u32[]{:S(2)}, u32[]{:S(2)}) collective-permute-start(bf16[304,256]{1,0:T(8,128)(2,1)S(1)} %get-tuple-element.95), channel_id=1, source_target_pairs={{0,4},{1,5},{8,12},{9,13},{16,20},{17,21},{24,28},{25,29},{2,6},{3... | collective-permute-start | bytes 466952 | tf_op jit(solution)/shard_map/ppermute | solution.py:647
  27.0 15.3 %collective-permute-start.12 = (bf16[304,256]{1,0:T(8,128)(2,1)S(1)}, bf16[304,256]{1,0:T(8,128)(2,1)S(1)}, u32[]{:S(2)}, u32[]{:S(2)}) collective-permute-start(bf16[304,256]{1,0:T(8,128)(2,1)S(1)} %get-tuple-element.96), channel_id=1, source_target_pairs={{0,6},{1,7},{8,14},{9,15},{16,22},{17,23},{24,30},{25,31},{2,4},{3... | collective-permute-start | bytes 466952 | tf_op jit(solution)/shard_map/ppermute | solution.py:647
  38.0 9.0 %collective-permute-start.16 = (bf16[288,256]{1,0:T(8,128)(2,1)S(1)}, bf16[288,256]{1,0:T(8,128)(2,1)S(1)}, u32[]{:S(2)}, u32[]{:S(2)}) collective-permute-start(bf16[288,256]{1,0:T(8,128)(2,1)S(1)} %get-tuple-element.102), channel_id=1, source_target_pairs={{0,2},{1,3},{8,10},{9,11},{16,18},{17,19},{24,26},{25,27},{2,0},{3... | collective-permute-start | bytes 442376 | tf_op jit(solution)/shard_map/ppermute | solution.py:647
  39.7 10.5 %collective-permute-start.17 = (bf16[288,256]{1,0:T(8,128)(2,1)S(1)}, bf16[288,256]{1,0:T(8,128)(2,1)S(1)}, u32[]{:S(2)}, u32[]{:S(2)}) collective-permute-start(bf16[288,256]{1,0:T(8,128)(2,1)S(1)} %get-tuple-element.103), channel_id=1, source_target_pairs={{0,4},{1,5},{8,12},{9,13},{16,20},{17,21},{24,28},{25,29},{2,6},{3... | collective-permute-start | bytes 442376 | tf_op jit(solution)/shard_map/ppermute | solution.py:647
  43.5 13.7 %collective-permute-start.13 = (bf16[512,256]{1,0:T(8,128)(2,1)S(1)}, bf16[512,256]{1,0:T(8,128)(2,1)S(1)}, u32[]{:S(2)}, u32[]{:S(2)}) collective-permute-start(bf16[512,256]{1,0:T(8,128)(2,1)S(1)} %get-tuple-element.111), channel_id=1, source_target_pairs={{0,1},{1,0},{8,9},{9,8},{16,17},{17,16},{24,25},{25,24},{2,3},{3,2... | collective-permute-start | bytes 786440 | tf_op jit(solution)/shard_map/ppermute | solution.py:639
  45.0 12.1 %collective-permute-start.14 = (bf16[512,256]{1,0:T(8,128)(2,1)S(1)}, bf16[512,256]{1,0:T(8,128)(2,1)S(1)}, u32[]{:S(2)}, u32[]{:S(2)}) collective-permute-start(bf16[512,256]{1,0:T(8,128)(2,1)S(1)} %get-tuple-element.112), channel_id=1, source_target_pairs={{0,16},{1,17},{8,24},{9,25},{16,0},{17,1},{24,8},{25,9},{2,18},{3,... | collective-permute-start | bytes 786440 | tf_op jit(solution)/shard_map/ppermute | solution.py:639
  45.6 12.5 %collective-permute-start.15 = (bf16[512,256]{1,0:T(8,128)(2,1)S(1)}, bf16[512,256]{1,0:T(8,128)(2,1)S(1)}, u32[]{:S(2)}, u32[]{:S(2)}) collective-permute-start(bf16[512,256]{1,0:T(8,128)(2,1)S(1)} %get-tuple-element.113), channel_id=1, source_target_pairs={{0,17},{1,16},{8,25},{9,24},{16,1},{17,0},{24,9},{25,8},{2,19},{3,... | collective-permute-start | bytes 786440 | tf_op jit(solution)/shard_map/ppermute | solution.py:639
  47.0 7.9 %collective-permute-start.18 = (bf16[288,256]{1,0:T(8,128)(2,1)S(1)}, bf16[288,256]{1,0:T(8,128)(2,1)S(1)}, u32[]{:S(2)}, u32[]{:S(2)}) collective-permute-start(bf16[288,256]{1,0:T(8,128)(2,1)S(1)} %get-tuple-element.104), channel_id=1, source_target_pairs={{0,6},{1,7},{8,14},{9,15},{16,22},{17,23},{24,30},{25,31},{2,4},{3... | collective-permute-start | bytes 442376 | tf_op jit(solution)/shard_map/ppermute | solution.py:647
  50.2 7.8 %collective-permute-start.19 = (bf16[288,256]{1,0:T(8,128)(2,1)S(1)}, bf16[288,256]{1,0:T(8,128)(2,1)S(1)}, u32[]{:S(2)}, u32[]{:S(2)}) collective-permute-start(bf16[288,256]{1,0:T(8,128)(2,1)S(1)} %get-tuple-element.120), channel_id=1, source_target_pairs={{0,2},{1,3},{8,10},{9,11},{16,18},{17,19},{24,26},{25,27},{2,0},{3... | collective-permute-start | bytes 442376 | tf_op jit(solution)/shard_map/ppermute | solution.py:647
  55.0 7.8 %collective-permute-start.23 = (bf16[288,256]{1,0:T(8,128)(2,1)S(1)}, bf16[288,256]{1,0:T(8,128)(2,1)S(1)}, u32[]{:S(2)}, u32[]{:S(2)}) collective-permute-start(bf16[288,256]{1,0:T(8,128)(2,1)S(1)} %get-tuple-element.131), channel_id=1, source_target_pairs={{0,4},{1,5},{8,12},{9,13},{16,20},{17,21},{24,28},{25,29},{2,6},{3... | collective-permute-start | bytes 442376 | tf_op jit(solution)/shard_map/ppermute | solution.py:647
  59.0 11.9 %collective-permute-start.20 = (bf16[512,256]{1,0:T(8,128)(2,1)S(1)}, bf16[512,256]{1,0:T(8,128)(2,1)S(1)}, u32[]{:S(2)}, u32[]{:S(2)}) collective-permute-start(bf16[512,256]{1,0:T(8,128)(2,1)S(1)} %get-tuple-element.126), channel_id=1, source_target_pairs={{0,1},{1,0},{8,9},{9,8},{16,17},{17,16},{24,25},{25,24},{2,3},{3,2... | collective-permute-start | bytes 786440 | tf_op jit(solution)/shard_map/ppermute | solution.py:639
  60.2 10.7 %collective-permute-start.21 = (bf16[512,256]{1,0:T(8,128)(2,1)S(1)}, bf16[512,256]{1,0:T(8,128)(2,1)S(1)}, u32[]{:S(2)}, u32[]{:S(2)}) collective-permute-start(bf16[512,256]{1,0:T(8,128)(2,1)S(1)} %get-tuple-element.127), channel_id=1, source_target_pairs={{0,16},{1,17},{8,24},{9,25},{16,0},{17,1},{24,8},{25,9},{2,18},{3,... | collective-permute-start | bytes 786440 | tf_op jit(solution)/shard_map/ppermute | solution.py:639
  60.9 11.4 %collective-permute-start.22 = (bf16[512,256]{1,0:T(8,128)(2,1)S(1)}, bf16[512,256]{1,0:T(8,128)(2,1)S(1)}, u32[]{:S(2)}, u32[]{:S(2)}) collective-permute-start(bf16[512,256]{1,0:T(8,128)(2,1)S(1)} %get-tuple-element.128), channel_id=1, source_target_pairs={{0,17},{1,16},{8,25},{9,24},{16,1},{17,0},{24,9},{25,8},{2,19},{3,... | collective-permute-start | bytes 786440 | tf_op jit(solution)/shard_map/ppermute | solution.py:639
  62.7 24.1 %collective-permute-start.28 = (bf16[1024,256]{1,0:T(8,128)(2,1)S(1)}, bf16[1024,256]{1,0:T(8,128)(2,1)S(1)}, u32[]{:S(2)}, u32[]{:S(2)}) collective-permute-start(bf16[1024,256]{1,0:T(8,128)(2,1)S(1)} %get-tuple-element.114.refs_0_), channel_id=1, source_target_pairs={{0,8},{1,9},{8,0},{9,1},{16,24},{17,25},{24,16},{25,17},{2,10},{3,... | collective-permute-start | bytes 1572872 | tf_op jit(solution)/shard_map/ppermute | solution.py:639
  62.7 8.2 %collective-permute-start.24 = (bf16[288,256]{1,0:T(8,128)(2,1)S(1)}, bf16[288,256]{1,0:T(8,128)(2,1)S(1)}, u32[]{:S(2)}, u32[]{:S(2)}) collective-permute-start(bf16[288,256]{1,0:T(8,128)(2,1)S(1)} %get-tuple-element.132), channel_id=1, source_target_pairs={{0,6},{1,7},{8,14},{9,15},{16,22},{17,23},{24,30},{25,31},{2,4},{3... | collective-permute-start | bytes 442376 | tf_op jit(solution)/shard_map/ppermute | solution.py:647
  73.4 8.4 %collective-permute-start.25 = (bf16[512,256]{1,0:T(8,128)(2,1)S(1)}, bf16[512,256]{1,0:T(8,128)(2,1)S(1)}, u32[]{:S(2)}, u32[]{:S(2)}) collective-permute-start(bf16[512,256]{1,0:T(8,128)(2,1)S(1)} %get-tuple-element.138), channel_id=1, source_target_pairs={{0,1},{1,0},{8,9},{9,8},{16,17},{17,16},{24,25},{25,24},{2,3},{3,2... | collective-permute-start | bytes 786440 | tf_op jit(solution)/shard_map/ppermute | solution.py:639
  74.2 9.2 %collective-permute-start.26 = (bf16[512,256]{1,0:T(8,128)(2,1)S(1)}, bf16[512,256]{1,0:T(8,128)(2,1)S(1)}, u32[]{:S(2)}, u32[]{:S(2)}) collective-permute-start(bf16[512,256]{1,0:T(8,128)(2,1)S(1)} %get-tuple-element.139), channel_id=1, source_target_pairs={{0,16},{1,17},{8,24},{9,25},{16,0},{17,1},{24,8},{25,9},{2,18},{3,... | collective-permute-start | bytes 786440 | tf_op jit(solution)/shard_map/ppermute | solution.py:639
  75.4 11.2 %collective-permute-start.27 = (bf16[512,256]{1,0:T(8,128)(2,1)S(1)}, bf16[512,256]{1,0:T(8,128)(2,1)S(1)}, u32[]{:S(2)}, u32[]{:S(2)}) collective-permute-start(bf16[512,256]{1,0:T(8,128)(2,1)S(1)} %get-tuple-element.140), channel_id=1, source_target_pairs={{0,17},{1,16},{8,25},{9,24},{16,1},{17,0},{24,9},{25,8},{2,19},{3,... | collective-permute-start | bytes 786440 | tf_op jit(solution)/shard_map/ppermute | solution.py:639
  76.9 10.4 %collective-permute-start.31 = (bf16[1024,256]{1,0:T(8,128)(2,1)S(1)}, bf16[1024,256]{1,0:T(8,128)(2,1)S(1)}, u32[]{:S(2)}, u32[]{:S(2)}) collective-permute-start(bf16[1024,256]{1,0:T(8,128)(2,1)S(1)} %get-tuple-element.142.refs_6_), channel_id=1, source_target_pairs={{0,8},{1,9},{8,0},{9,1},{16,24},{17,25},{24,16},{25,17},{2,10},{3,... | collective-permute-start | bytes 1572872 | tf_op jit(solution)/shard_map/ppermute | solution.py:639
  81.8 5.6 %collective-permute-start.29 = (bf16[1024,256]{1,0:T(8,128)(2,1)S(1)}, bf16[1024,256]{1,0:T(8,128)(2,1)S(1)}, u32[]{:S(2)}, u32[]{:S(2)}) collective-permute-start(bf16[1024,256]{1,0:T(8,128)(2,1)S(1)} %get-tuple-element.129.refs_1_), channel_id=1, source_target_pairs={{0,8},{1,9},{8,0},{9,1},{16,24},{17,25},{24,16},{25,17},{2,10},{3,... | collective-permute-start | bytes 1572872 | tf_op jit(solution)/shard_map/ppermute | solution.py:639
  83.4 3.9 %collective-permute-start.32 = (bf16[1024,256]{1,0:T(8,128)(2,1)S(1)}, bf16[1024,256]{1,0:T(8,128)(2,1)S(1)}, u32[]{:S(2)}, u32[]{:S(2)}) collective-permute-start(bf16[1024,256]{1,0:T(8,128)(2,1)S(1)} %get-tuple-element.143.refs_7_), channel_id=1, source_target_pairs={{0,8},{1,9},{8,0},{9,1},{16,24},{17,25},{24,16},{25,17},{2,10},{3,... | collective-permute-start | bytes 1572872 | tf_op jit(solution)/shard_map/ppermute | solution.py:639
  86.8 2.6 %collective-permute-start.33 = (bf16[1024,256]{1,0:T(8,128)(2,1)S(1)}, bf16[1024,256]{1,0:T(8,128)(2,1)S(1)}, u32[]{:S(2)}, u32[]{:S(2)}) collective-permute-start(bf16[1024,256]{1,0:T(8,128)(2,1)S(1)} %get-tuple-element.144.refs_8_), channel_id=1, source_target_pairs={{0,8},{1,9},{8,0},{9,1},{16,24},{17,25},{24,16},{25,17},{2,10},{3,... | collective-permute-start | bytes 1572872 | tf_op jit(solution)/shard_map/ppermute | solution.py:639
  93.1 16.7 %all-to-all-start.4 = ((f32[32,8,128]{2,1,0:T(8,128)}), f32[32,8,128]{2,1,0:T(8,128)S(1)}, u32[]{:S(2)}, u32[]{:S(2)}) async-start(f32[32,8,128]{2,1,0:T(8,128)} %shard_map.59), calls=%async_computation.4 | async-start | bytes 262144 | tf_op jit(solution)/shard_map/all_to_all | solution.py:565
  (6 other events, 90.1 us)

commit v8 on v7

--- a/solution.py
+++ b/solution.py
@@ -9,7 +9,7 @@
 
 EPSILON = 1e-06
 AXES = ("ingest", "run")
-TILE = 256
+TILE = 512
 SHARES = (1, 1, 1)
 MIB = 1024 * 1024
 
@@ -274,7 +274,7 @@
     outs, (unit_ref, target_ref) = rest[:-2], rest[-2:]
     step = 128
 
-    @pl.loop(0, plan.rows // step)
+    @pl.loop(0, plan.rows // step, unroll=True)
     def _(number):
         here = pl.ds(pl.multiple_of(number * step, step), step)
         widened = rows_ref[here, :].astype(jnp.float32)
@@ -713,7 +713,7 @@
         if chunk:
             arrived, _ = lax.optimization_barrier((arrived, parts))
         if ahead < len(plan.chunks):
-            arrived, _ = lax.optimization_barrier((arrived, arrivals[ahead][1] if ahead == 2 else routes[ahead]))
+            arrived, _ = lax.optimization_barrier((arrived, arrivals[ahead][1] if ahead + 1 == len(plan.chunks) else routes[ahead]))
         shapes = [wide((4 * plan.part, f), half) for _ in range(plan.lanes // 2)]
         scratch = [pltpu.VMEM((plan.layers * plan.stride, f), half), inputs]
         if chunk == 0:

time: 112 us -> 111 us (level)
  Pallas kernels: 18.1 us -> 16.9 us
  transfers between devices with their start and end apart: 33 -> 33, of which waited for: 12 -> 12; matrix products, arithmetic and copies ran while one was open for 0% -> 0% of each run, Pallas kernels for 6% -> 7%
where the time goes in v8:
time: 111 us
  starting transfers between devices  49.6 us (45%)
  waiting for transfers between devices  42.2 us (38%)
  Pallas kernels  16.9 us (15%)
  local copies, waits for them, and re-layouts  1.12 us (1%)
    ppermute x22, starting transfers between devices, along_lanes(): return lax.ppermute(block, AXES, pairs)  20.5 us
    ppermute x9, starting transfers between devices, along_layers(): return lax.ppermute(block, AXES, pairs)  16.1 us
    ppermute x22, waiting for transfers between devices, along_lanes(): return lax.ppermute(block, AXES, pairs)  16 us
    ppermute x9, waiting for transfers between devices, along_layers(): return lax.ppermute(block, AXES, pairs)  10 us
    all_to_all x1, waiting for transfers between devices, staged(): lax.all_to_all(later, AXES, 0, 0, tiled=True, axis_index_groups=groups)  9.84 us
    all_to_all x1, starting transfers between devices, exchange(): return lax.all_to_all(block, AXES, split_axis=0, concat_axis=0, tiled=True)  9.19 us
    all_to_all x1, waiting for transfers between devices, exchange(): return lax.all_to_all(block, AXES, split_axis=0, concat_axis=0, tiled=True)  6.35 us
    all_to_all x1, starting transfers between devices, staged(): lax.all_to_all(later, AXES, 0, 0, tiled=True, axis_index_groups=groups)  3.74 us
  transfers between devices with their start and end apart: 33, of which 12 were waited for; matrix products, arithmetic and copies ran while one was open for 0% of the time, Pallas kernels for 7%

profile of v8, /device:TPU:0, one launch (start us, length us, event | category | flops | bytes accessed | tf_op | source)
XLA Modules:
  0.0 110.7 jit_solution(14312032454463857099)
XLA Ops:
  0.0 2.8 %shard_map.48 = (bf16[144,256]{1,0:T(8,128)(2,1)S(1)}, bf16[144,256]{1,0:T(8,128)(2,1)S(1)}, bf16[144,256]{1,0:T(8,128)(2,1)S(1)}, bf16[144,256]{1,0:T(8,128)(2,...) custom-call(s32[12]{0:T(128)} %run_len_ref.5, ...), custom_call_target="tpu_custom_call" | custom-call | flops 536870912 | bytes 4718592 | tf_op jit(solution)/shard_map/pallas_call | solution.py:651
  2.8 3.0 %collective-permute-start.3 = (bf16[144,256]{1,0:T(8,128)(2,1)S(1)}, bf16[144,256]{1,0:T(8,128)(2,1)S(1)}, u32[]{:S(2)}, u32[]{:S(2)}) collective-permute-start(bf16[144,256]{1,0:T(8,128)(2,1)S(1)} %get-tuple-element.86), channel_id=1, source_target_pairs={{0,1},{1,0},{8,9},{9,8},{16,17},{17,16},{24,25},{25,24},{2,3},{3,2... | collective-permute-start | bytes 221192 | tf_op jit(solution)/shard_map/ppermute | solution.py:639
  6.0 1.9 %collective-permute-start.6 = (bf16[144,256]{1,0:T(8,128)(2,1)S(1)}, bf16[144,256]{1,0:T(8,128)(2,1)S(1)}, u32[]{:S(2)}, u32[]{:S(2)}) collective-permute-start(bf16[144,256]{1,0:T(8,128)(2,1)S(1)} %get-tuple-element.89), channel_id=1, source_target_pairs={{0,16},{1,17},{8,24},{9,25},{16,0},{17,1},{24,8},{25,9},{2,18},{3,... | collective-permute-start | bytes 221192 | tf_op jit(solution)/shard_map/ppermute | solution.py:639
  7.9 1.5 %collective-permute-start.7 = (bf16[144,256]{1,0:T(8,128)(2,1)S(1)}, bf16[144,256]{1,0:T(8,128)(2,1)S(1)}, u32[]{:S(2)}, u32[]{:S(2)}) collective-permute-start(bf16[144,256]{1,0:T(8,128)(2,1)S(1)} %get-tuple-element.90), channel_id=1, source_target_pairs={{0,17},{1,16},{8,25},{9,24},{16,1},{17,0},{24,9},{25,8},{2,19},{3,... | collective-permute-start | bytes 221192 | tf_op jit(solution)/shard_map/ppermute | solution.py:639
  9.9 2.0 %collective-permute-start.9 = (bf16[144,256]{1,0:T(8,128)(2,1)S(1)}, bf16[144,256]{1,0:T(8,128)(2,1)S(1)}, u32[]{:S(2)}, u32[]{:S(2)}) collective-permute-start(bf16[144,256]{1,0:T(8,128)(2,1)S(1)} %get-tuple-element.92), channel_id=1, source_target_pairs={{0,25},{1,24},{8,17},{9,16},{16,9},{17,8},{24,1},{25,0},{2,27},{3,... | collective-permute-start | bytes 221192 | tf_op jit(solution)/shard_map/ppermute | solution.py:639
  12.0 2.3 %shard_map.50 = bf16[1024,512]{1,0:T(8,128)(2,1)} custom-call(bf16[1024,768]{1,0:T(8,128)(2,1)S(1)} %get-tuple-element.98.unit_ref, s32[1,1024]{1,0:T(1,128)S(1)} %get-tuple-element.99.target_ref), custom_call_target="tpu_custom_call" | custom-call | flops 1073741824 | bytes 4718592 | tf_op jit(solution)/shard_map/pallas_call | solution.py:662
  14.2 2.0 %collective-permute-done.9.refs_7_ = bf16[144,256]{1,0:T(8,128)(2,1)S(1)} collective-permute-done((bf16[144,256]{1,0:T(8,128)(2,1)S(1)}, bf16[144,256]{1,0:T(8,128)(2,1)S(1)}, u32[]{:S(2)}, u32[]{:S(2)}) %collective-permute-start.9) | collective-permute-done | bytes 73760 | tf_op jit(solution)/shard_map/ppermute | solution.py:639
  16.2 2.2 %shard_map.49 = (bf16[304,256]{1,0:T(8,128)(2,1)S(1)}, bf16[304,256]{1,0:T(8,128)(2,1)S(1)}, bf16[304,256]{1,0:T(8,128)(2,1)S(1)}, bf16[304,256]{1,0:T(8,128)(2,1)S(1)}, s32[1,1024]{1,0:T(1,128)S(1)}) custom-call(bf16[144,256]{1,0:T(8,128)(2,1)S(1)} %get-tuple-element.85.refs_0_, bf16[144,256]{1,0:T(8,128)(2,1)S(1)} %collective-permute-done.3.refs_1_, ...), custom_call_target="tpu_custom_call" | custom-call | flops 536870912 | bytes 1572864 | tf_op jit(solution)/shard_map/pallas_call | solution.py:682
  18.4 3.7 %all-to-all-start.3 = ((bf16[8,128,512]{2,1,0:T(8,128)(2,1)}), bf16[8,128,512]{2,1,0:T(8,128)(2,1)S(1)}, u32[]{:S(2)}, u32[]{:S(2)}) async-start(bf16[8,128,512]{2,1,0:T(8,128)(2,1)} %bitcast.16), calls=%async_computation.3 | async-start | bytes 2097152 | tf_op jit(solution)/shard_map/all_to_all | solution.py:699
  22.2 1.6 %collective-permute-start.10 = (bf16[304,256]{1,0:T(8,128)(2,1)S(1)}, bf16[304,256]{1,0:T(8,128)(2,1)S(1)}, u32[]{:S(2)}, u32[]{:S(2)}) collective-permute-start(bf16[304,256]{1,0:T(8,128)(2,1)S(1)} %get-tuple-element.94), channel_id=1, source_target_pairs={{0,2},{1,3},{8,10},{9,11},{16,18},{17,19},{24,26},{25,27},{2,0},{3... | collective-permute-start | bytes 466952 | tf_op jit(solution)/shard_map/ppermute | solution.py:647
  23.8 2.6 %collective-permute-start.11 = (bf16[304,256]{1,0:T(8,128)(2,1)S(1)}, bf16[304,256]{1,0:T(8,128)(2,1)S(1)}, u32[]{:S(2)}, u32[]{:S(2)}) collective-permute-start(bf16[304,256]{1,0:T(8,128)(2,1)S(1)} %get-tuple-element.95), channel_id=1, source_target_pairs={{0,4},{1,5},{8,12},{9,13},{16,20},{17,21},{24,28},{25,29},{2,6},{3... | collective-permute-start | bytes 466952 | tf_op jit(solution)/shard_map/ppermute | solution.py:647
  26.6 9.8 %all-to-all-done.3 = bf16[8,128,512]{2,1,0:T(8,128)(2,1)S(1)} async-done(((bf16[8,128,512]{2,1,0:T(8,128)(2,1)}), bf16[8,128,512]{2,1,0:T(8,128)(2,1)S(1)}, u32[]{:S(2)}, u32[]{:S(2)}) %all-to-all-start.3) | async-done | bytes 1048608 | tf_op jit(solution)/shard_map/all_to_all | solution.py:699
  37.2 1.6 %collective-permute-start.16 = (bf16[288,256]{1,0:T(8,128)(2,1)S(1)}, bf16[288,256]{1,0:T(8,128)(2,1)S(1)}, u32[]{:S(2)}, u32[]{:S(2)}) collective-permute-start(bf16[288,256]{1,0:T(8,128)(2,1)S(1)} %get-tuple-element.102), channel_id=1, source_target_pairs={{0,2},{1,3},{8,10},{9,11},{16,18},{17,19},{24,26},{25,27},{2,0},{3... | collective-permute-start | bytes 442376 | tf_op jit(solution)/shard_map/ppermute | solution.py:647
  38.9 2.6 %collective-permute-start.17 = (bf16[288,256]{1,0:T(8,128)(2,1)S(1)}, bf16[288,256]{1,0:T(8,128)(2,1)S(1)}, u32[]{:S(2)}, u32[]{:S(2)}) collective-permute-start(bf16[288,256]{1,0:T(8,128)(2,1)S(1)} %get-tuple-element.103), channel_id=1, source_target_pairs={{0,4},{1,5},{8,12},{9,13},{16,20},{17,21},{24,28},{25,29},{2,6},{3... | collective-permute-start | bytes 442376 | tf_op jit(solution)/shard_map/ppermute | solution.py:647
  42.7 1.5 %collective-permute-start.13 = (bf16[512,256]{1,0:T(8,128)(2,1)S(1)}, bf16[512,256]{1,0:T(8,128)(2,1)S(1)}, u32[]{:S(2)}, u32[]{:S(2)}) collective-permute-start(bf16[512,256]{1,0:T(8,128)(2,1)S(1)} %get-tuple-element.111), channel_id=1, source_target_pairs={{0,1},{1,0},{8,9},{9,8},{16,17},{17,16},{24,25},{25,24},{2,3},{3,2... | collective-permute-start | bytes 786440 | tf_op jit(solution)/shard_map/ppermute | solution.py:639
  44.8 1.5 %collective-permute-start.15 = (bf16[512,256]{1,0:T(8,128)(2,1)S(1)}, bf16[512,256]{1,0:T(8,128)(2,1)S(1)}, u32[]{:S(2)}, u32[]{:S(2)}) collective-permute-start(bf16[512,256]{1,0:T(8,128)(2,1)S(1)} %get-tuple-element.113), channel_id=1, source_target_pairs={{0,17},{1,16},{8,25},{9,24},{16,1},{17,0},{24,9},{25,8},{2,19},{3,... | collective-permute-start | bytes 786440 | tf_op jit(solution)/shard_map/ppermute | solution.py:639
  46.3 2.3 %collective-permute-start.18 = (bf16[288,256]{1,0:T(8,128)(2,1)S(1)}, bf16[288,256]{1,0:T(8,128)(2,1)S(1)}, u32[]{:S(2)}, u32[]{:S(2)}) collective-permute-start(bf16[288,256]{1,0:T(8,128)(2,1)S(1)} %get-tuple-element.104), channel_id=1, source_target_pairs={{0,6},{1,7},{8,14},{9,15},{16,22},{17,23},{24,30},{25,31},{2,4},{3... | collective-permute-start | bytes 442376 | tf_op jit(solution)/shard_map/ppermute | solution.py:647
  49.5 4.7 %collective-permute-done.18.refs_3_ = bf16[288,256]{1,0:T(8,128)(2,1)S(1)} collective-permute-done((bf16[288,256]{1,0:T(8,128)(2,1)S(1)}, bf16[288,256]{1,0:T(8,128)(2,1)S(1)}, u32[]{:S(2)}, u32[]{:S(2)}) %collective-permute-start.18) | collective-permute-done | bytes 147488 | tf_op jit(solution)/shard_map/ppermute | solution.py:647
  54.2 2.2 %collective-permute-start.23 = (bf16[288,256]{1,0:T(8,128)(2,1)S(1)}, bf16[288,256]{1,0:T(8,128)(2,1)S(1)}, u32[]{:S(2)}, u32[]{:S(2)}) collective-permute-start(bf16[288,256]{1,0:T(8,128)(2,1)S(1)} %get-tuple-element.131), channel_id=1, source_target_pairs={{0,4},{1,5},{8,12},{9,13},{16,20},{17,21},{24,28},{25,29},{2,6},{3... | collective-permute-start | bytes 442376 | tf_op jit(solution)/shard_map/ppermute | solution.py:647
  60.2 1.7 %collective-permute-start.22 = (bf16[512,256]{1,0:T(8,128)(2,1)S(1)}, bf16[512,256]{1,0:T(8,128)(2,1)S(1)}, u32[]{:S(2)}, u32[]{:S(2)}) collective-permute-start(bf16[512,256]{1,0:T(8,128)(2,1)S(1)} %get-tuple-element.128), channel_id=1, source_target_pairs={{0,17},{1,16},{8,25},{9,24},{16,1},{17,0},{24,9},{25,8},{2,19},{3,... | collective-permute-start | bytes 786440 | tf_op jit(solution)/shard_map/ppermute | solution.py:639
  62.0 2.9 %collective-permute-start.24 = (bf16[288,256]{1,0:T(8,128)(2,1)S(1)}, bf16[288,256]{1,0:T(8,128)(2,1)S(1)}, u32[]{:S(2)}, u32[]{:S(2)}) collective-permute-start(bf16[288,256]{1,0:T(8,128)(2,1)S(1)} %get-tuple-element.132), channel_id=1, source_target_pairs={{0,6},{1,7},{8,14},{9,15},{16,22},{17,23},{24,30},{25,31},{2,4},{3... | collective-permute-start | bytes 442376 | tf_op jit(solution)/shard_map/ppermute | solution.py:647
  64.9 5.3 %collective-permute-done.24.refs_3_ = bf16[288,256]{1,0:T(8,128)(2,1)S(1)} collective-permute-done((bf16[288,256]{1,0:T(8,128)(2,1)S(1)}, bf16[288,256]{1,0:T(8,128)(2,1)S(1)}, u32[]{:S(2)}, u32[]{:S(2)}) %collective-permute-start.24) | collective-permute-done | bytes 147488 | tf_op jit(solution)/shard_map/ppermute | solution.py:647
  70.1 1.4 %collective-permute-done.22.refs_3_ = bf16[512,256]{1,0:T(8,128)(2,1)S(1)} collective-permute-done((bf16[512,256]{1,0:T(8,128)(2,1)S(1)}, bf16[512,256]{1,0:T(8,128)(2,1)S(1)}, u32[]{:S(2)}, u32[]{:S(2)}) %collective-permute-start.22) | collective-permute-done | bytes 262176 | tf_op jit(solution)/shard_map/ppermute | solution.py:639
  74.6 1.5 %collective-permute-start.27 = (bf16[512,256]{1,0:T(8,128)(2,1)S(1)}, bf16[512,256]{1,0:T(8,128)(2,1)S(1)}, u32[]{:S(2)}, u32[]{:S(2)}) collective-permute-start(bf16[512,256]{1,0:T(8,128)(2,1)S(1)} %get-tuple-element.140), channel_id=1, source_target_pairs={{0,17},{1,16},{8,25},{9,24},{16,1},{17,0},{24,9},{25,8},{2,19},{3,... | collective-permute-start | bytes 786440 | tf_op jit(solution)/shard_map/ppermute | solution.py:639
  76.2 4.8 %collective-permute-done.25.refs_1_ = bf16[512,256]{1,0:T(8,128)(2,1)S(1)} collective-permute-done((bf16[512,256]{1,0:T(8,128)(2,1)S(1)}, bf16[512,256]{1,0:T(8,128)(2,1)S(1)}, u32[]{:S(2)}, u32[]{:S(2)}) %collective-permute-start.25) | collective-permute-done | bytes 262176 | tf_op jit(solution)/shard_map/ppermute | solution.py:639
  81.0 1.6 %collective-permute-done.26.refs_2_ = bf16[512,256]{1,0:T(8,128)(2,1)S(1)} collective-permute-done((bf16[512,256]{1,0:T(8,128)(2,1)S(1)}, bf16[512,256]{1,0:T(8,128)(2,1)S(1)}, u32[]{:S(2)}, u32[]{:S(2)}) %collective-permute-start.26) | collective-permute-done | bytes 262176 | tf_op jit(solution)/shard_map/ppermute | solution.py:639
  82.7 3.2 %collective-permute-done.27.refs_3_ = bf16[512,256]{1,0:T(8,128)(2,1)S(1)} collective-permute-done((bf16[512,256]{1,0:T(8,128)(2,1)S(1)}, bf16[512,256]{1,0:T(8,128)(2,1)S(1)}, u32[]{:S(2)}, u32[]{:S(2)}) %collective-permute-start.27) | collective-permute-done | bytes 262176 | tf_op jit(solution)/shard_map/ppermute | solution.py:639
  86.6 1.3 %collective-permute-done.30.refs_5_ = bf16[1024,256]{1,0:T(8,128)(2,1)S(1)} collective-permute-done((bf16[1024,256]{1,0:T(8,128)(2,1)S(1)}, bf16[1024,256]{1,0:T(8,128)(2,1)S(1)}, u32[]{:S(2)}, u32[]{:S(2)}) %collective-permute-start.30) | collective-permute-done | bytes 524320 | tf_op jit(solution)/shard_map/ppermute | solution.py:639
  88.7 3.3 %shard_map.59 = f32[32,8,128]{2,1,0:T(8,128)} custom-call(s32[12]{0:T(128)S(1)} %copy-done.3, bf16[1024,256]{1,0:T(8,128)(2,1)S(1)} %get-tuple-element.114.refs_0_, bf16[1024,256]{1,0:T(8,128)(2,1)S(1)} %get-tuple-element.129.refs_1_, bf16[1024,256]{1,0:T(8,128)(2,1)S(1)} %get-tuple-element.141.refs_2_, ...), custom_call_target="tpu_custom_call" | custom-call | flops 4831838208 | bytes 6291456 | tf_op jit(solution)/shard_map/pallas_call | solution.py:749
  91.9 9.2 %all-to-all-start.4 = ((f32[32,8,128]{2,1,0:T(8,128)}), f32[32,8,128]{2,1,0:T(8,128)S(1)}, u32[]{:S(2)}, u32[]{:S(2)}) async-start(f32[32,8,128]{2,1,0:T(8,128)} %shard_map.59), calls=%async_computation.4 | async-start | bytes 262144 | tf_op jit(solution)/shard_map/all_to_all | solution.py:565
  102.3 6.4 %all-to-all-done.4 = f32[32,8,128]{2,1,0:T(8,128)S(1)} async-done(((f32[32,8,128]{2,1,0:T(8,128)}), f32[32,8,128]{2,1,0:T(8,128)S(1)}, u32[]{:S(2)}, u32[]{:S(2)}) %all-to-all-start.4) | async-done | bytes 131104 | tf_op jit(solution)/shard_map/all_to_all | solution.py:565
  108.7 1.4 %shard_map.60 = f32[1,1024]{1,0:T(1,128)S(1)} custom-call(s32[12]{0:T(128)S(1)} %copy-done.3, s32[1,1024]{1,0:T(1,128)S(1)} %bitcast.31, s32[1,1024]{1,0:T(1,128)S(1)} %bitcast.34, f32[256,128]{1,0:T(8,128)S(1)} %bitcast.24), custom_call_target="tpu_custom_call" | custom-call | bytes 16384 | tf_op jit(solution)/shard_map/pallas_call | solution.py:764
  (59 shorter events, 14.0 us)
Async XLA Ops:
  2.8 6.6 %collective-permute-start.3 = (bf16[144,256]{1,0:T(8,128)(2,1)S(1)}, bf16[144,256]{1,0:T(8,128)(2,1)S(1)}, u32[]{:S(2)}, u32[]{:S(2)}) collective-permute-start(bf16[144,256]{1,0:T(8,128)(2,1)S(1)} %get-tuple-element.86), channel_id=1, source_target_pairs={{0,1},{1,0},{8,9},{9,8},{16,17},{17,16},{24,25},{25,24},{2,3},{3,2... | collective-permute-start | bytes 221192 | tf_op jit(solution)/shard_map/ppermute | solution.py:639
  5.8 4.2 %collective-permute-start.4 = (bf16[144,256]{1,0:T(8,128)(2,1)S(1)}, bf16[144,256]{1,0:T(8,128)(2,1)S(1)}, u32[]{:S(2)}, u32[]{:S(2)}) collective-permute-start(bf16[144,256]{1,0:T(8,128)(2,1)S(1)} %get-tuple-element.87), channel_id=1, source_target_pairs={{0,8},{1,9},{8,0},{9,1},{16,24},{17,25},{24,16},{25,17},{2,10},{3,... | collective-permute-start | bytes 221192 | tf_op jit(solution)/shard_map/ppermute | solution.py:639
  5.8 8.4 %collective-permute-start.5 = (bf16[144,256]{1,0:T(8,128)(2,1)S(1)}, bf16[144,256]{1,0:T(8,128)(2,1)S(1)}, u32[]{:S(2)}, u32[]{:S(2)}) collective-permute-start(bf16[144,256]{1,0:T(8,128)(2,1)S(1)} %get-tuple-element.88), channel_id=1, source_target_pairs={{0,9},{1,8},{8,1},{9,0},{16,25},{17,24},{24,17},{25,16},{2,11},{3,... | collective-permute-start | bytes 221192 | tf_op jit(solution)/shard_map/ppermute | solution.py:639
  6.0 8.2 %collective-permute-start.6 = (bf16[144,256]{1,0:T(8,128)(2,1)S(1)}, bf16[144,256]{1,0:T(8,128)(2,1)S(1)}, u32[]{:S(2)}, u32[]{:S(2)}) collective-permute-start(bf16[144,256]{1,0:T(8,128)(2,1)S(1)} %get-tuple-element.89), channel_id=1, source_target_pairs={{0,16},{1,17},{8,24},{9,25},{16,0},{17,1},{24,8},{25,9},{2,18},{3,... | collective-permute-start | bytes 221192 | tf_op jit(solution)/shard_map/ppermute | solution.py:639
  7.9 6.3 %collective-permute-start.7 = (bf16[144,256]{1,0:T(8,128)(2,1)S(1)}, bf16[144,256]{1,0:T(8,128)(2,1)S(1)}, u32[]{:S(2)}, u32[]{:S(2)}) collective-permute-start(bf16[144,256]{1,0:T(8,128)(2,1)S(1)} %get-tuple-element.90), channel_id=1, source_target_pairs={{0,17},{1,16},{8,25},{9,24},{16,1},{17,0},{24,9},{25,8},{2,19},{3,... | collective-permute-start | bytes 221192 | tf_op jit(solution)/shard_map/ppermute | solution.py:639
  9.4 4.8 %collective-permute-start.8 = (bf16[144,256]{1,0:T(8,128)(2,1)S(1)}, bf16[144,256]{1,0:T(8,128)(2,1)S(1)}, u32[]{:S(2)}, u32[]{:S(2)}) collective-permute-start(bf16[144,256]{1,0:T(8,128)(2,1)S(1)} %get-tuple-element.91), channel_id=1, source_target_pairs={{0,24},{1,25},{8,16},{9,17},{16,8},{17,9},{24,0},{25,1},{2,26},{3,... | collective-permute-start | bytes 221192 | tf_op jit(solution)/shard_map/ppermute | solution.py:639
  9.9 6.3 %collective-permute-start.9 = (bf16[144,256]{1,0:T(8,128)(2,1)S(1)}, bf16[144,256]{1,0:T(8,128)(2,1)S(1)}, u32[]{:S(2)}, u32[]{:S(2)}) collective-permute-start(bf16[144,256]{1,0:T(8,128)(2,1)S(1)} %get-tuple-element.92), channel_id=1, source_target_pairs={{0,25},{1,24},{8,17},{9,16},{16,9},{17,8},{24,1},{25,0},{2,27},{3,... | collective-permute-start | bytes 221192 | tf_op jit(solution)/shard_map/ppermute | solution.py:639
  18.4 18.0 %all-to-all-start.3 = ((bf16[8,128,512]{2,1,0:T(8,128)(2,1)}), bf16[8,128,512]{2,1,0:T(8,128)(2,1)S(1)}, u32[]{:S(2)}, u32[]{:S(2)}) async-start(bf16[8,128,512]{2,1,0:T(8,128)(2,1)} %bitcast.16), calls=%async_computation.3 | async-start | bytes 2097152 | tf_op jit(solution)/shard_map/all_to_all | solution.py:699
  22.2 19.3 %collective-permute-start.10 = (bf16[304,256]{1,0:T(8,128)(2,1)S(1)}, bf16[304,256]{1,0:T(8,128)(2,1)S(1)}, u32[]{:S(2)}, u32[]{:S(2)}) collective-permute-start(bf16[304,256]{1,0:T(8,128)(2,1)S(1)} %get-tuple-element.94), channel_id=1, source_target_pairs={{0,2},{1,3},{8,10},{9,11},{16,18},{17,19},{24,26},{25,27},{2,0},{3... | collective-permute-start | bytes 466952 | tf_op jit(solution)/shard_map/ppermute | solution.py:647
  23.8 17.7 %collective-permute-start.11 = (bf16[304,256]{1,0:T(8,128)(2,1)S(1)}, bf16[304,256]{1,0:T(8,128)(2,1)S(1)}, u32[]{:S(2)}, u32[]{:S(2)}) collective-permute-start(bf16[304,256]{1,0:T(8,128)(2,1)S(1)} %get-tuple-element.95), channel_id=1, source_target_pairs={{0,4},{1,5},{8,12},{9,13},{16,20},{17,21},{24,28},{25,29},{2,6},{3... | collective-permute-start | bytes 466952 | tf_op jit(solution)/shard_map/ppermute | solution.py:647
  26.4 15.1 %collective-permute-start.12 = (bf16[304,256]{1,0:T(8,128)(2,1)S(1)}, bf16[304,256]{1,0:T(8,128)(2,1)S(1)}, u32[]{:S(2)}, u32[]{:S(2)}) collective-permute-start(bf16[304,256]{1,0:T(8,128)(2,1)S(1)} %get-tuple-element.96), channel_id=1, source_target_pairs={{0,6},{1,7},{8,14},{9,15},{16,22},{17,23},{24,30},{25,31},{2,4},{3... | collective-permute-start | bytes 466952 | tf_op jit(solution)/shard_map/ppermute | solution.py:647
  37.2 9.0 %collective-permute-start.16 = (bf16[288,256]{1,0:T(8,128)(2,1)S(1)}, bf16[288,256]{1,0:T(8,128)(2,1)S(1)}, u32[]{:S(2)}, u32[]{:S(2)}) collective-permute-start(bf16[288,256]{1,0:T(8,128)(2,1)S(1)} %get-tuple-element.102), channel_id=1, source_target_pairs={{0,2},{1,3},{8,10},{9,11},{16,18},{17,19},{24,26},{25,27},{2,0},{3... | collective-permute-start | bytes 442376 | tf_op jit(solution)/shard_map/ppermute | solution.py:647
  38.9 10.5 %collective-permute-start.17 = (bf16[288,256]{1,0:T(8,128)(2,1)S(1)}, bf16[288,256]{1,0:T(8,128)(2,1)S(1)}, u32[]{:S(2)}, u32[]{:S(2)}) collective-permute-start(bf16[288,256]{1,0:T(8,128)(2,1)S(1)} %get-tuple-element.103), channel_id=1, source_target_pairs={{0,4},{1,5},{8,12},{9,13},{16,20},{17,21},{24,28},{25,29},{2,6},{3... | collective-permute-start | bytes 442376 | tf_op jit(solution)/shard_map/ppermute | solution.py:647
  42.7 13.7 %collective-permute-start.13 = (bf16[512,256]{1,0:T(8,128)(2,1)S(1)}, bf16[512,256]{1,0:T(8,128)(2,1)S(1)}, u32[]{:S(2)}, u32[]{:S(2)}) collective-permute-start(bf16[512,256]{1,0:T(8,128)(2,1)S(1)} %get-tuple-element.111), channel_id=1, source_target_pairs={{0,1},{1,0},{8,9},{9,8},{16,17},{17,16},{24,25},{25,24},{2,3},{3,2... | collective-permute-start | bytes 786440 | tf_op jit(solution)/shard_map/ppermute | solution.py:639
  44.2 12.1 %collective-permute-start.14 = (bf16[512,256]{1,0:T(8,128)(2,1)S(1)}, bf16[512,256]{1,0:T(8,128)(2,1)S(1)}, u32[]{:S(2)}, u32[]{:S(2)}) collective-permute-start(bf16[512,256]{1,0:T(8,128)(2,1)S(1)} %get-tuple-element.112), channel_id=1, source_target_pairs={{0,16},{1,17},{8,24},{9,25},{16,0},{17,1},{24,8},{25,9},{2,18},{3,... | collective-permute-start | bytes 786440 | tf_op jit(solution)/shard_map/ppermute | solution.py:639
  44.8 12.5 %collective-permute-start.15 = (bf16[512,256]{1,0:T(8,128)(2,1)S(1)}, bf16[512,256]{1,0:T(8,128)(2,1)S(1)}, u32[]{:S(2)}, u32[]{:S(2)}) collective-permute-start(bf16[512,256]{1,0:T(8,128)(2,1)S(1)} %get-tuple-element.113), channel_id=1, source_target_pairs={{0,17},{1,16},{8,25},{9,24},{16,1},{17,0},{24,9},{25,8},{2,19},{3,... | collective-permute-start | bytes 786440 | tf_op jit(solution)/shard_map/ppermute | solution.py:639
  46.3 7.9 %collective-permute-start.18 = (bf16[288,256]{1,0:T(8,128)(2,1)S(1)}, bf16[288,256]{1,0:T(8,128)(2,1)S(1)}, u32[]{:S(2)}, u32[]{:S(2)}) collective-permute-start(bf16[288,256]{1,0:T(8,128)(2,1)S(1)} %get-tuple-element.104), channel_id=1, source_target_pairs={{0,6},{1,7},{8,14},{9,15},{16,22},{17,23},{24,30},{25,31},{2,4},{3... | collective-permute-start | bytes 442376 | tf_op jit(solution)/shard_map/ppermute | solution.py:647
  49.4 7.8 %collective-permute-start.19 = (bf16[288,256]{1,0:T(8,128)(2,1)S(1)}, bf16[288,256]{1,0:T(8,128)(2,1)S(1)}, u32[]{:S(2)}, u32[]{:S(2)}) collective-permute-start(bf16[288,256]{1,0:T(8,128)(2,1)S(1)} %get-tuple-element.120), channel_id=1, source_target_pairs={{0,2},{1,3},{8,10},{9,11},{16,18},{17,19},{24,26},{25,27},{2,0},{3... | collective-permute-start | bytes 442376 | tf_op jit(solution)/shard_map/ppermute | solution.py:647
  54.2 7.8 %collective-permute-start.23 = (bf16[288,256]{1,0:T(8,128)(2,1)S(1)}, bf16[288,256]{1,0:T(8,128)(2,1)S(1)}, u32[]{:S(2)}, u32[]{:S(2)}) collective-permute-start(bf16[288,256]{1,0:T(8,128)(2,1)S(1)} %get-tuple-element.131), channel_id=1, source_target_pairs={{0,4},{1,5},{8,12},{9,13},{16,20},{17,21},{24,28},{25,29},{2,6},{3... | collective-permute-start | bytes 442376 | tf_op jit(solution)/shard_map/ppermute | solution.py:647
  58.3 11.9 %collective-permute-start.20 = (bf16[512,256]{1,0:T(8,128)(2,1)S(1)}, bf16[512,256]{1,0:T(8,128)(2,1)S(1)}, u32[]{:S(2)}, u32[]{:S(2)}) collective-permute-start(bf16[512,256]{1,0:T(8,128)(2,1)S(1)} %get-tuple-element.126), channel_id=1, source_target_pairs={{0,1},{1,0},{8,9},{9,8},{16,17},{17,16},{24,25},{25,24},{2,3},{3,2... | collective-permute-start | bytes 786440 | tf_op jit(solution)/shard_map/ppermute | solution.py:639
  59.5 10.7 %collective-permute-start.21 = (bf16[512,256]{1,0:T(8,128)(2,1)S(1)}, bf16[512,256]{1,0:T(8,128)(2,1)S(1)}, u32[]{:S(2)}, u32[]{:S(2)}) collective-permute-start(bf16[512,256]{1,0:T(8,128)(2,1)S(1)} %get-tuple-element.127), channel_id=1, source_target_pairs={{0,16},{1,17},{8,24},{9,25},{16,0},{17,1},{24,8},{25,9},{2,18},{3,... | collective-permute-start | bytes 786440 | tf_op jit(solution)/shard_map/ppermute | solution.py:639
  60.2 11.4 %collective-permute-start.22 = (bf16[512,256]{1,0:T(8,128)(2,1)S(1)}, bf16[512,256]{1,0:T(8,128)(2,1)S(1)}, u32[]{:S(2)}, u32[]{:S(2)}) collective-permute-start(bf16[512,256]{1,0:T(8,128)(2,1)S(1)} %get-tuple-element.128), channel_id=1, source_target_pairs={{0,17},{1,16},{8,25},{9,24},{16,1},{17,0},{24,9},{25,8},{2,19},{3,... | collective-permute-start | bytes 786440 | tf_op jit(solution)/shard_map/ppermute | solution.py:639
  61.9 24.1 %collective-permute-start.28 = (bf16[1024,256]{1,0:T(8,128)(2,1)S(1)}, bf16[1024,256]{1,0:T(8,128)(2,1)S(1)}, u32[]{:S(2)}, u32[]{:S(2)}) collective-permute-start(bf16[1024,256]{1,0:T(8,128)(2,1)S(1)} %get-tuple-element.114.refs_0_), channel_id=1, source_target_pairs={{0,8},{1,9},{8,0},{9,1},{16,24},{17,25},{24,16},{25,17},{2,10},{3,... | collective-permute-start | bytes 1572872 | tf_op jit(solution)/shard_map/ppermute | solution.py:639
  62.0 8.2 %collective-permute-start.24 = (bf16[288,256]{1,0:T(8,128)(2,1)S(1)}, bf16[288,256]{1,0:T(8,128)(2,1)S(1)}, u32[]{:S(2)}, u32[]{:S(2)}) collective-permute-start(bf16[288,256]{1,0:T(8,128)(2,1)S(1)} %get-tuple-element.132), channel_id=1, source_target_pairs={{0,6},{1,7},{8,14},{9,15},{16,22},{17,23},{24,30},{25,31},{2,4},{3... | collective-permute-start | bytes 442376 | tf_op jit(solution)/shard_map/ppermute | solution.py:647
  72.6 8.4 %collective-permute-start.25 = (bf16[512,256]{1,0:T(8,128)(2,1)S(1)}, bf16[512,256]{1,0:T(8,128)(2,1)S(1)}, u32[]{:S(2)}, u32[]{:S(2)}) collective-permute-start(bf16[512,256]{1,0:T(8,128)(2,1)S(1)} %get-tuple-element.138), channel_id=1, source_target_pairs={{0,1},{1,0},{8,9},{9,8},{16,17},{17,16},{24,25},{25,24},{2,3},{3,2... | collective-permute-start | bytes 786440 | tf_op jit(solution)/shard_map/ppermute | solution.py:639
  73.4 9.2 %collective-permute-start.26 = (bf16[512,256]{1,0:T(8,128)(2,1)S(1)}, bf16[512,256]{1,0:T(8,128)(2,1)S(1)}, u32[]{:S(2)}, u32[]{:S(2)}) collective-permute-start(bf16[512,256]{1,0:T(8,128)(2,1)S(1)} %get-tuple-element.139), channel_id=1, source_target_pairs={{0,16},{1,17},{8,24},{9,25},{16,0},{17,1},{24,8},{25,9},{2,18},{3,... | collective-permute-start | bytes 786440 | tf_op jit(solution)/shard_map/ppermute | solution.py:639
  74.6 11.2 %collective-permute-start.27 = (bf16[512,256]{1,0:T(8,128)(2,1)S(1)}, bf16[512,256]{1,0:T(8,128)(2,1)S(1)}, u32[]{:S(2)}, u32[]{:S(2)}) collective-permute-start(bf16[512,256]{1,0:T(8,128)(2,1)S(1)} %get-tuple-element.140), channel_id=1, source_target_pairs={{0,17},{1,16},{8,25},{9,24},{16,1},{17,0},{24,9},{25,8},{2,19},{3,... | collective-permute-start | bytes 786440 | tf_op jit(solution)/shard_map/ppermute | solution.py:639
  76.2 10.4 %collective-permute-start.31 = (bf16[1024,256]{1,0:T(8,128)(2,1)S(1)}, bf16[1024,256]{1,0:T(8,128)(2,1)S(1)}, u32[]{:S(2)}, u32[]{:S(2)}) collective-permute-start(bf16[1024,256]{1,0:T(8,128)(2,1)S(1)} %get-tuple-element.142.refs_6_), channel_id=1, source_target_pairs={{0,8},{1,9},{8,0},{9,1},{16,24},{17,25},{24,16},{25,17},{2,10},{3,... | collective-permute-start | bytes 1572872 | tf_op jit(solution)/shard_map/ppermute | solution.py:639
  81.0 5.6 %collective-permute-start.29 = (bf16[1024,256]{1,0:T(8,128)(2,1)S(1)}, bf16[1024,256]{1,0:T(8,128)(2,1)S(1)}, u32[]{:S(2)}, u32[]{:S(2)}) collective-permute-start(bf16[1024,256]{1,0:T(8,128)(2,1)S(1)} %get-tuple-element.129.refs_1_), channel_id=1, source_target_pairs={{0,8},{1,9},{8,0},{9,1},{16,24},{17,25},{24,16},{25,17},{2,10},{3,... | collective-permute-start | bytes 1572872 | tf_op jit(solution)/shard_map/ppermute | solution.py:639
  82.6 3.9 %collective-permute-start.32 = (bf16[1024,256]{1,0:T(8,128)(2,1)S(1)}, bf16[1024,256]{1,0:T(8,128)(2,1)S(1)}, u32[]{:S(2)}, u32[]{:S(2)}) collective-permute-start(bf16[1024,256]{1,0:T(8,128)(2,1)S(1)} %get-tuple-element.143.refs_7_), channel_id=1, source_target_pairs={{0,8},{1,9},{8,0},{9,1},{16,24},{17,25},{24,16},{25,17},{2,10},{3,... | collective-permute-start | bytes 1572872 | tf_op jit(solution)/shard_map/ppermute | solution.py:639
  86.1 2.6 %collective-permute-start.33 = (bf16[1024,256]{1,0:T(8,128)(2,1)S(1)}, bf16[1024,256]{1,0:T(8,128)(2,1)S(1)}, u32[]{:S(2)}, u32[]{:S(2)}) collective-permute-start(bf16[1024,256]{1,0:T(8,128)(2,1)S(1)} %get-tuple-element.144.refs_8_), channel_id=1, source_target_pairs={{0,8},{1,9},{8,0},{9,1},{16,24},{17,25},{24,16},{25,17},{2,10},{3,... | collective-permute-start | bytes 1572872 | tf_op jit(solution)/shard_map/ppermute | solution.py:639
  91.9 16.7 %all-to-all-start.4 = ((f32[32,8,128]{2,1,0:T(8,128)}), f32[32,8,128]{2,1,0:T(8,128)S(1)}, u32[]{:S(2)}, u32[]{:S(2)}) async-start(f32[32,8,128]{2,1,0:T(8,128)} %shard_map.59), calls=%async_computation.4 | async-start | bytes 262144 | tf_op jit(solution)/shard_map/all_to_all | solution.py:565
  (6 other events, 89.0 us)

commit v9 on v8

--- a/solution.py
+++ b/solution.py
@@ -339,26 +339,26 @@
         owner_ref[number : number + 1, :] = table[0:1, :].astype(jnp.int32)
         block_ref[number : number + 1, :] = table[1:2, :].astype(jnp.int32)
     owner = owner_ref[...]
+    marks = [jnp.where(owner // plan.run == other, 1.0, 0.0) for other in range(plan.layers)]
+    most = functools.reduce(jnp.maximum, [jnp.sum(mark) for mark in marks])
+    stacked = jnp.concatenate(marks, axis=0).astype(jnp.bfloat16)
     shape = (plan.part, plan.part)
     earlier = lax.broadcasted_iota(jnp.int32, shape, 0) < lax.broadcasted_iota(jnp.int32, shape, 1)
-    earlier = jnp.where(earlier, 1.0, 0.0)
-    ones = jnp.ones(shape, jnp.float32)
-    shape = (plan.lanes, plan.lanes)
-    above = lax.broadcasted_iota(jnp.int32, shape, 0) > lax.broadcasted_iota(jnp.int32, shape, 1)
-    above = jnp.where(above, 1.0, 0.0)
+    earlier = jnp.where(earlier, 1.0, 0.0).astype(jnp.bfloat16)
+    shape = (plan.layers * plan.lanes, plan.layers * plan.lanes)
+    line, above = (lax.broadcasted_iota(jnp.int32, shape, axis) for axis in range(2))
+    above = (line > above) & (line // plan.lanes == above // plan.lanes)
+    above = jnp.where(above, 1.0, 0.0).astype(jnp.bfloat16)
+    lines = jnp.dot(above, stacked, preferred_element_type=jnp.float32)
+    counts = jnp.dot(stacked, earlier, preferred_element_type=jnp.float32) + jnp.sum(
+        lines, axis=1, keepdims=True
+    )
+    counts = counts.astype(jnp.int32)
     target = jnp.zeros(owner.shape, jnp.int32)
-    most = jnp.float32(0.0)
     for other in range(plan.layers):
-        chosen = owner // plan.run == other
-        marks = jnp.where(chosen, 1.0, 0.0)
-        lines = jnp.dot(marks, ones, preferred_element_type=jnp.float32)
-        count = jnp.dot(marks, earlier, preferred_element_type=jnp.float32) + jnp.dot(
-            above, lines, preferred_element_type=jnp.float32
-        )
-        count = count.astype(jnp.int32)
+        count = counts[other * plan.lanes : (other + 1) * plan.lanes, :]
         there = jnp.where(count < plan.room, (layer ^ other) * plan.stride + count, -1)
-        target = jnp.where(chosen, there, target)
-        most = jnp.maximum(most, jnp.sum(marks))
+        target = jnp.where(owner // plan.run == other, there, target)
     full = jnp.where(most > plan.room, 1.0, 0.0)
     value = owner % plan.run * plan.blocks + block_ref[...] + 1
     for number in range(plan.lanes):
@@ -534,13 +534,18 @@
     line = plan.device(group, slot) * plan.lanes + core * (plan.lanes // 2) + chip
     column = within // plan.cap * plan.slice + residue % plan.slice
     number = lax.broadcasted_iota(jnp.int32, (plan.devices * plan.lanes, plan.rows), 0)
+    left, pieces = reply_ref[...], []
+    for _ in range(3):
+        pieces.append(left.astype(jnp.bfloat16))
+        left = left - pieces[-1].astype(jnp.float32)
     columns = lax.dot_general(
-        reply_ref[...],
-        jnp.where(number == line, 1.0, 0.0),
+        jnp.concatenate(pieces, axis=1),
+        jnp.where(number == line, 1.0, 0.0).astype(jnp.bfloat16),
         (((0,), (0,)), ((), ())),
-        precision=lax.Precision.HIGHEST,
         preferred_element_type=jnp.float32,
     )
+    high, middle, low = (columns[n * plan.part : (n + 1) * plan.part, :] for n in range(3))
+    columns = high + middle + low
     place = lax.broadcasted_iota(jnp.int32, (plan.part, plan.rows), 0)
     out_ref[...] = jnp.sum(jnp.where(place == column, columns, 0.0), axis=0, keepdims=True)
 
@@ -710,7 +715,7 @@
         inputs = pltpu.VMEM((rows, f), half)
         arrived = arrivals[chunk]
         ahead = chunk + 1
-        if chunk:
+        if chunk == len(plan.chunks) - 1:
             arrived, _ = lax.optimization_barrier((arrived, parts))
         if ahead < len(plan.chunks):
             arrived, _ = lax.optimization_barrier((arrived, arrivals[ahead][1] if ahead + 1 == len(plan.chunks) else routes[ahead]))

time: 111 us -> 110 us (level)
  starting transfers between devices: 49.6 us -> 46.5 us
  waiting for transfers between devices: 42.2 us -> 44.8 us
    ppermute x9, waiting for transfers between devices: 10 us -> 12.8 us  [along_layers(): return lax.ppermute(block, AXES, pairs)]
    ppermute x9, starting transfers between devices: 16.1 us -> 14.5 us  [along_layers(): return lax.ppermute(block, AXES, pairs)]
    all_to_all x1, starting transfers between devices: 9.19 us -> 7.72 us  [exchange(): return lax.all_to_all(block, AXES, split_axis=0, concat_axis=0, tiled=True)]
where the time goes in v9:
time: 110 us
  starting transfers between devices  46.5 us (42%)
  waiting for transfers between devices  44.8 us (41%)
  Pallas kernels  16.3 us (15%)
  local copies, waits for them, and re-layouts  1.12 us (1%)
    ppermute x22, starting transfers between devices, along_lanes(): return lax.ppermute(block, AXES, pairs)  20.6 us
    ppermute x22, waiting for transfers between devices, along_lanes(): return lax.ppermute(block, AXES, pairs)  15.4 us
    ppermute x9, starting transfers between devices, along_layers(): return lax.ppermute(block, AXES, pairs)  14.5 us
    ppermute x9, waiting for transfers between devices, along_layers(): return lax.ppermute(block, AXES, pairs)  12.8 us
    all_to_all x1, waiting for transfers between devices, staged(): lax.all_to_all(later, AXES, 0, 0, tiled=True, axis_index_groups=groups)  10 us
    all_to_all x1, starting transfers between devices, exchange(): return lax.all_to_all(block, AXES, split_axis=0, concat_axis=0, tiled=True)  7.72 us
    all_to_all x1, waiting for transfers between devices, exchange(): return lax.all_to_all(block, AXES, split_axis=0, concat_axis=0, tiled=True)  6.57 us
    all_to_all x1, starting transfers between devices, staged(): lax.all_to_all(later, AXES, 0, 0, tiled=True, axis_index_groups=groups)  3.56 us
  transfers between devices with their start and end apart: 33, of which 12 were waited for; matrix products, arithmetic and copies ran while one was open for 0% of the time, Pallas kernels for 7%

profile of v9, /device:TPU:0, one launch (start us, length us, event | category | flops | bytes accessed | tf_op | source)
XLA Modules:
  0.0 109.6 jit_solution(354501685001063879)
XLA Ops:
  0.0 2.8 %shard_map.48 = (bf16[144,256]{1,0:T(8,128)(2,1)S(1)}, bf16[144,256]{1,0:T(8,128)(2,1)S(1)}, bf16[144,256]{1,0:T(8,128)(2,1)S(1)}, bf16[144,256]{1,0:T(8,128)(2,...) custom-call(s32[12]{0:T(128)} %run_len_ref.5, ...), custom_call_target="tpu_custom_call" | custom-call | flops 536870912 | bytes 4718592 | tf_op jit(solution)/shard_map/pallas_call | solution.py:656
  2.8 3.0 %collective-permute-start.3 = (bf16[144,256]{1,0:T(8,128)(2,1)S(1)}, bf16[144,256]{1,0:T(8,128)(2,1)S(1)}, u32[]{:S(2)}, u32[]{:S(2)}) collective-permute-start(bf16[144,256]{1,0:T(8,128)(2,1)S(1)} %get-tuple-element.82), channel_id=1, source_target_pairs={{0,1},{1,0},{8,9},{9,8},{16,17},{17,16},{24,25},{25,24},{2,3},{3,2... | collective-permute-start | bytes 221192 | tf_op jit(solution)/shard_map/ppermute | solution.py:644
  6.0 1.9 %collective-permute-start.6 = (bf16[144,256]{1,0:T(8,128)(2,1)S(1)}, bf16[144,256]{1,0:T(8,128)(2,1)S(1)}, u32[]{:S(2)}, u32[]{:S(2)}) collective-permute-start(bf16[144,256]{1,0:T(8,128)(2,1)S(1)} %get-tuple-element.85), channel_id=1, source_target_pairs={{0,16},{1,17},{8,24},{9,25},{16,0},{17,1},{24,8},{25,9},{2,18},{3,... | collective-permute-start | bytes 221192 | tf_op jit(solution)/shard_map/ppermute | solution.py:644
  7.9 1.5 %collective-permute-start.7 = (bf16[144,256]{1,0:T(8,128)(2,1)S(1)}, bf16[144,256]{1,0:T(8,128)(2,1)S(1)}, u32[]{:S(2)}, u32[]{:S(2)}) collective-permute-start(bf16[144,256]{1,0:T(8,128)(2,1)S(1)} %get-tuple-element.86), channel_id=1, source_target_pairs={{0,17},{1,16},{8,25},{9,24},{16,1},{17,0},{24,9},{25,8},{2,19},{3,... | collective-permute-start | bytes 221192 | tf_op jit(solution)/shard_map/ppermute | solution.py:644
  9.9 2.0 %collective-permute-start.9 = (bf16[144,256]{1,0:T(8,128)(2,1)S(1)}, bf16[144,256]{1,0:T(8,128)(2,1)S(1)}, u32[]{:S(2)}, u32[]{:S(2)}) collective-permute-start(bf16[144,256]{1,0:T(8,128)(2,1)S(1)} %get-tuple-element.88), channel_id=1, source_target_pairs={{0,25},{1,24},{8,17},{9,16},{16,9},{17,8},{24,1},{25,0},{2,27},{3,... | collective-permute-start | bytes 221192 | tf_op jit(solution)/shard_map/ppermute | solution.py:644
  12.0 2.3 %shard_map.50 = bf16[1024,512]{1,0:T(8,128)(2,1)} custom-call(bf16[1024,768]{1,0:T(8,128)(2,1)S(1)} %get-tuple-element.94.unit_ref, s32[1,1024]{1,0:T(1,128)S(1)} %get-tuple-element.95.target_ref), custom_call_target="tpu_custom_call" | custom-call | flops 1073741824 | bytes 4718592 | tf_op jit(solution)/shard_map/pallas_call | solution.py:667
  14.2 2.0 %collective-permute-done.9.refs_7_ = bf16[144,256]{1,0:T(8,128)(2,1)S(1)} collective-permute-done((bf16[144,256]{1,0:T(8,128)(2,1)S(1)}, bf16[144,256]{1,0:T(8,128)(2,1)S(1)}, u32[]{:S(2)}, u32[]{:S(2)}) %collective-permute-start.9) | collective-permute-done | bytes 73760 | tf_op jit(solution)/shard_map/ppermute | solution.py:644
  16.2 1.8 %shard_map.49 = (bf16[304,256]{1,0:T(8,128)(2,1)S(1)}, bf16[304,256]{1,0:T(8,128)(2,1)S(1)}, bf16[304,256]{1,0:T(8,128)(2,1)S(1)}, bf16[304,256]{1,0:T(8,128)(2,1)S(1)}, s32[1,1024]{1,0:T(1,128)S(1)}) custom-call(bf16[144,256]{1,0:T(8,128)(2,1)S(1)} %get-tuple-element.81.refs_0_, bf16[144,256]{1,0:T(8,128)(2,1)S(1)} %collective-permute-done.3.refs_1_, ...), custom_call_target="tpu_custom_call" | custom-call | flops 536870912 | bytes 1572864 | tf_op jit(solution)/shard_map/pallas_call | solution.py:687
  18.0 3.6 %all-to-all-start.3 = ((bf16[8,128,512]{2,1,0:T(8,128)(2,1)}), bf16[8,128,512]{2,1,0:T(8,128)(2,1)S(1)}, u32[]{:S(2)}, u32[]{:S(2)}) async-start(bf16[8,128,512]{2,1,0:T(8,128)(2,1)} %bitcast.16), calls=%async_computation.3 | async-start | bytes 2097152 | tf_op jit(solution)/shard_map/all_to_all | solution.py:704
  21.6 1.6 %collective-permute-start.10 = (bf16[304,256]{1,0:T(8,128)(2,1)S(1)}, bf16[304,256]{1,0:T(8,128)(2,1)S(1)}, u32[]{:S(2)}, u32[]{:S(2)}) collective-permute-start(bf16[304,256]{1,0:T(8,128)(2,1)S(1)} %get-tuple-element.90), channel_id=1, source_target_pairs={{0,2},{1,3},{8,10},{9,11},{16,18},{17,19},{24,26},{25,27},{2,0},{3... | collective-permute-start | bytes 466952 | tf_op jit(solution)/shard_map/ppermute | solution.py:652
  23.2 2.6 %collective-permute-start.11 = (bf16[304,256]{1,0:T(8,128)(2,1)S(1)}, bf16[304,256]{1,0:T(8,128)(2,1)S(1)}, u32[]{:S(2)}, u32[]{:S(2)}) collective-permute-start(bf16[304,256]{1,0:T(8,128)(2,1)S(1)} %get-tuple-element.91), channel_id=1, source_target_pairs={{0,4},{1,5},{8,12},{9,13},{16,20},{17,21},{24,28},{25,29},{2,6},{3... | collective-permute-start | bytes 466952 | tf_op jit(solution)/shard_map/ppermute | solution.py:652
  26.0 10.0 %all-to-all-done.3 = bf16[8,128,512]{2,1,0:T(8,128)(2,1)S(1)} async-done(((bf16[8,128,512]{2,1,0:T(8,128)(2,1)}), bf16[8,128,512]{2,1,0:T(8,128)(2,1)S(1)}, u32[]{:S(2)}, u32[]{:S(2)}) %all-to-all-start.3) | async-done | bytes 1048608 | tf_op jit(solution)/shard_map/all_to_all | solution.py:704
  36.8 1.6 %collective-permute-start.16 = (bf16[288,256]{1,0:T(8,128)(2,1)S(1)}, bf16[288,256]{1,0:T(8,128)(2,1)S(1)}, u32[]{:S(2)}, u32[]{:S(2)}) collective-permute-start(bf16[288,256]{1,0:T(8,128)(2,1)S(1)} %get-tuple-element.98), channel_id=1, source_target_pairs={{0,2},{1,3},{8,10},{9,11},{16,18},{17,19},{24,26},{25,27},{2,0},{3... | collective-permute-start | bytes 442376 | tf_op jit(solution)/shard_map/ppermute | solution.py:652
  38.5 2.6 %collective-permute-start.17 = (bf16[288,256]{1,0:T(8,128)(2,1)S(1)}, bf16[288,256]{1,0:T(8,128)(2,1)S(1)}, u32[]{:S(2)}, u32[]{:S(2)}) collective-permute-start(bf16[288,256]{1,0:T(8,128)(2,1)S(1)} %get-tuple-element.99), channel_id=1, source_target_pairs={{0,4},{1,5},{8,12},{9,13},{16,20},{17,21},{24,28},{25,29},{2,6},{3... | collective-permute-start | bytes 442376 | tf_op jit(solution)/shard_map/ppermute | solution.py:652
  42.3 1.5 %collective-permute-start.13 = (bf16[512,256]{1,0:T(8,128)(2,1)S(1)}, bf16[512,256]{1,0:T(8,128)(2,1)S(1)}, u32[]{:S(2)}, u32[]{:S(2)}) collective-permute-start(bf16[512,256]{1,0:T(8,128)(2,1)S(1)} %get-tuple-element.107), channel_id=1, source_target_pairs={{0,1},{1,0},{8,9},{9,8},{16,17},{17,16},{24,25},{25,24},{2,3},{3,2... | collective-permute-start | bytes 786440 | tf_op jit(solution)/shard_map/ppermute | solution.py:644
  44.4 1.5 %collective-permute-start.15 = (bf16[512,256]{1,0:T(8,128)(2,1)S(1)}, bf16[512,256]{1,0:T(8,128)(2,1)S(1)}, u32[]{:S(2)}, u32[]{:S(2)}) collective-permute-start(bf16[512,256]{1,0:T(8,128)(2,1)S(1)} %get-tuple-element.109), channel_id=1, source_target_pairs={{0,17},{1,16},{8,25},{9,24},{16,1},{17,0},{24,9},{25,8},{2,19},{3,... | collective-permute-start | bytes 786440 | tf_op jit(solution)/shard_map/ppermute | solution.py:644
  46.6 1.5 %collective-permute-start.18 = (bf16[288,256]{1,0:T(8,128)(2,1)S(1)}, bf16[288,256]{1,0:T(8,128)(2,1)S(1)}, u32[]{:S(2)}, u32[]{:S(2)}) collective-permute-start(bf16[288,256]{1,0:T(8,128)(2,1)S(1)} %get-tuple-element.100), channel_id=1, source_target_pairs={{0,6},{1,7},{8,14},{9,15},{16,22},{17,23},{24,30},{25,31},{2,4},{3... | collective-permute-start | bytes 442376 | tf_op jit(solution)/shard_map/ppermute | solution.py:652
  48.8 5.8 %collective-permute-done.18.refs_3_ = bf16[288,256]{1,0:T(8,128)(2,1)S(1)} collective-permute-done((bf16[288,256]{1,0:T(8,128)(2,1)S(1)}, bf16[288,256]{1,0:T(8,128)(2,1)S(1)}, u32[]{:S(2)}, u32[]{:S(2)}) %collective-permute-start.18) | collective-permute-done | bytes 147488 | tf_op jit(solution)/shard_map/ppermute | solution.py:652
  54.7 1.3 %collective-permute-start.23 = (bf16[288,256]{1,0:T(8,128)(2,1)S(1)}, bf16[288,256]{1,0:T(8,128)(2,1)S(1)}, u32[]{:S(2)}, u32[]{:S(2)}) collective-permute-start(bf16[288,256]{1,0:T(8,128)(2,1)S(1)} %get-tuple-element.123), channel_id=1, source_target_pairs={{0,4},{1,5},{8,12},{9,13},{16,20},{17,21},{24,28},{25,29},{2,6},{3... | collective-permute-start | bytes 442376 | tf_op jit(solution)/shard_map/ppermute | solution.py:652
  58.5 1.5 %collective-permute-start.21 = (bf16[512,256]{1,0:T(8,128)(2,1)S(1)}, bf16[512,256]{1,0:T(8,128)(2,1)S(1)}, u32[]{:S(2)}, u32[]{:S(2)}) collective-permute-start(bf16[512,256]{1,0:T(8,128)(2,1)S(1)} %get-tuple-element.119), channel_id=1, source_target_pairs={{0,16},{1,17},{8,24},{9,25},{16,0},{17,1},{24,8},{25,9},{2,18},{3,... | collective-permute-start | bytes 786440 | tf_op jit(solution)/shard_map/ppermute | solution.py:644
  59.9 1.8 %collective-permute-start.22 = (bf16[512,256]{1,0:T(8,128)(2,1)S(1)}, bf16[512,256]{1,0:T(8,128)(2,1)S(1)}, u32[]{:S(2)}, u32[]{:S(2)}) collective-permute-start(bf16[512,256]{1,0:T(8,128)(2,1)S(1)} %get-tuple-element.120), channel_id=1, source_target_pairs={{0,17},{1,16},{8,25},{9,24},{16,1},{17,0},{24,9},{25,8},{2,19},{3,... | collective-permute-start | bytes 786440 | tf_op jit(solution)/shard_map/ppermute | solution.py:644
  61.9 2.4 %collective-permute-start.24 = (bf16[288,256]{1,0:T(8,128)(2,1)S(1)}, bf16[288,256]{1,0:T(8,128)(2,1)S(1)}, u32[]{:S(2)}, u32[]{:S(2)}) collective-permute-start(bf16[288,256]{1,0:T(8,128)(2,1)S(1)} %get-tuple-element.124), channel_id=1, source_target_pairs={{0,6},{1,7},{8,14},{9,15},{16,22},{17,23},{24,30},{25,31},{2,4},{3... | collective-permute-start | bytes 442376 | tf_op jit(solution)/shard_map/ppermute | solution.py:652
  64.3 5.8 %collective-permute-done.24.refs_3_ = bf16[288,256]{1,0:T(8,128)(2,1)S(1)} collective-permute-done((bf16[288,256]{1,0:T(8,128)(2,1)S(1)}, bf16[288,256]{1,0:T(8,128)(2,1)S(1)}, u32[]{:S(2)}, u32[]{:S(2)}) %collective-permute-start.24) | collective-permute-done | bytes 147488 | tf_op jit(solution)/shard_map/ppermute | solution.py:652
  70.1 2.1 %collective-permute-done.22.refs_3_ = bf16[512,256]{1,0:T(8,128)(2,1)S(1)} collective-permute-done((bf16[512,256]{1,0:T(8,128)(2,1)S(1)}, bf16[512,256]{1,0:T(8,128)(2,1)S(1)}, u32[]{:S(2)}, u32[]{:S(2)}) %collective-permute-start.22) | collective-permute-done | bytes 262176 | tf_op jit(solution)/shard_map/ppermute | solution.py:644
  73.7 1.7 %collective-permute-start.26 = (bf16[512,256]{1,0:T(8,128)(2,1)S(1)}, bf16[512,256]{1,0:T(8,128)(2,1)S(1)}, u32[]{:S(2)}, u32[]{:S(2)}) collective-permute-start(bf16[512,256]{1,0:T(8,128)(2,1)S(1)} %get-tuple-element.131), channel_id=1, source_target_pairs={{0,16},{1,17},{8,24},{9,25},{16,0},{17,1},{24,8},{25,9},{2,18},{3,... | collective-permute-start | bytes 786440 | tf_op jit(solution)/shard_map/ppermute | solution.py:644
  75.4 1.4 %collective-permute-start.27 = (bf16[512,256]{1,0:T(8,128)(2,1)S(1)}, bf16[512,256]{1,0:T(8,128)(2,1)S(1)}, u32[]{:S(2)}, u32[]{:S(2)}) collective-permute-start(bf16[512,256]{1,0:T(8,128)(2,1)S(1)} %get-tuple-element.132), channel_id=1, source_target_pairs={{0,17},{1,16},{8,25},{9,24},{16,1},{17,0},{24,9},{25,8},{2,19},{3,... | collective-permute-start | bytes 786440 | tf_op jit(solution)/shard_map/ppermute | solution.py:644
  76.8 5.3 %collective-permute-done.25.refs_1_ = bf16[512,256]{1,0:T(8,128)(2,1)S(1)} collective-permute-done((bf16[512,256]{1,0:T(8,128)(2,1)S(1)}, bf16[512,256]{1,0:T(8,128)(2,1)S(1)}, u32[]{:S(2)}, u32[]{:S(2)}) %collective-permute-start.25) | collective-permute-done | bytes 262176 | tf_op jit(solution)/shard_map/ppermute | solution.py:644
  82.7 3.5 %collective-permute-done.27.refs_3_ = bf16[512,256]{1,0:T(8,128)(2,1)S(1)} collective-permute-done((bf16[512,256]{1,0:T(8,128)(2,1)S(1)}, bf16[512,256]{1,0:T(8,128)(2,1)S(1)}, u32[]{:S(2)}, u32[]{:S(2)}) %collective-permute-start.27) | collective-permute-done | bytes 262176 | tf_op jit(solution)/shard_map/ppermute | solution.py:644
  86.9 1.3 %collective-permute-done.30.refs_5_ = bf16[1024,256]{1,0:T(8,128)(2,1)S(1)} collective-permute-done((bf16[1024,256]{1,0:T(8,128)(2,1)S(1)}, bf16[1024,256]{1,0:T(8,128)(2,1)S(1)}, u32[]{:S(2)}, u32[]{:S(2)}) %collective-permute-start.30) | collective-permute-done | bytes 524320 | tf_op jit(solution)/shard_map/ppermute | solution.py:644
  89.0 3.5 %shard_map.59 = f32[32,8,128]{2,1,0:T(8,128)} custom-call(s32[12]{0:T(128)S(1)} %copy-done.3, bf16[1024,256]{1,0:T(8,128)(2,1)S(1)} %get-tuple-element.110.refs_0_, bf16[1024,256]{1,0:T(8,128)(2,1)S(1)} %get-tuple-element.121.refs_1_, bf16[1024,256]{1,0:T(8,128)(2,1)S(1)} %get-tuple-element.133.refs_2_, ...), custom_call_target="tpu_custom_call" | custom-call | flops 4831838208 | bytes 6291456 | tf_op jit(solution)/shard_map/pallas_call | solution.py:754
  92.5 7.7 %all-to-all-start.4 = ((f32[32,8,128]{2,1,0:T(8,128)}), f32[32,8,128]{2,1,0:T(8,128)S(1)}, u32[]{:S(2)}, u32[]{:S(2)}) async-start(f32[32,8,128]{2,1,0:T(8,128)} %shard_map.59), calls=%async_computation.4 | async-start | bytes 262144 | tf_op jit(solution)/shard_map/all_to_all | solution.py:570
  101.4 6.6 %all-to-all-done.4 = f32[32,8,128]{2,1,0:T(8,128)S(1)} async-done(((f32[32,8,128]{2,1,0:T(8,128)}), f32[32,8,128]{2,1,0:T(8,128)S(1)}, u32[]{:S(2)}, u32[]{:S(2)}) %all-to-all-start.4) | async-done | bytes 131104 | tf_op jit(solution)/shard_map/all_to_all | solution.py:570
  (59 shorter events, 13.3 us)
Async XLA Ops:
  2.8 6.6 %collective-permute-start.3 = (bf16[144,256]{1,0:T(8,128)(2,1)S(1)}, bf16[144,256]{1,0:T(8,128)(2,1)S(1)}, u32[]{:S(2)}, u32[]{:S(2)}) collective-permute-start(bf16[144,256]{1,0:T(8,128)(2,1)S(1)} %get-tuple-element.82), channel_id=1, source_target_pairs={{0,1},{1,0},{8,9},{9,8},{16,17},{17,16},{24,25},{25,24},{2,3},{3,2... | collective-permute-start | bytes 221192 | tf_op jit(solution)/shard_map/ppermute | solution.py:644
  5.8 4.2 %collective-permute-start.4 = (bf16[144,256]{1,0:T(8,128)(2,1)S(1)}, bf16[144,256]{1,0:T(8,128)(2,1)S(1)}, u32[]{:S(2)}, u32[]{:S(2)}) collective-permute-start(bf16[144,256]{1,0:T(8,128)(2,1)S(1)} %get-tuple-element.83), channel_id=1, source_target_pairs={{0,8},{1,9},{8,0},{9,1},{16,24},{17,25},{24,16},{25,17},{2,10},{3,... | collective-permute-start | bytes 221192 | tf_op jit(solution)/shard_map/ppermute | solution.py:644
  5.8 8.4 %collective-permute-start.5 = (bf16[144,256]{1,0:T(8,128)(2,1)S(1)}, bf16[144,256]{1,0:T(8,128)(2,1)S(1)}, u32[]{:S(2)}, u32[]{:S(2)}) collective-permute-start(bf16[144,256]{1,0:T(8,128)(2,1)S(1)} %get-tuple-element.84), channel_id=1, source_target_pairs={{0,9},{1,8},{8,1},{9,0},{16,25},{17,24},{24,17},{25,16},{2,11},{3,... | collective-permute-start | bytes 221192 | tf_op jit(solution)/shard_map/ppermute | solution.py:644
  6.0 8.2 %collective-permute-start.6 = (bf16[144,256]{1,0:T(8,128)(2,1)S(1)}, bf16[144,256]{1,0:T(8,128)(2,1)S(1)}, u32[]{:S(2)}, u32[]{:S(2)}) collective-permute-start(bf16[144,256]{1,0:T(8,128)(2,1)S(1)} %get-tuple-element.85), channel_id=1, source_target_pairs={{0,16},{1,17},{8,24},{9,25},{16,0},{17,1},{24,8},{25,9},{2,18},{3,... | collective-permute-start | bytes 221192 | tf_op jit(solution)/shard_map/ppermute | solution.py:644
  7.9 6.3 %collective-permute-start.7 = (bf16[144,256]{1,0:T(8,128)(2,1)S(1)}, bf16[144,256]{1,0:T(8,128)(2,1)S(1)}, u32[]{:S(2)}, u32[]{:S(2)}) collective-permute-start(bf16[144,256]{1,0:T(8,128)(2,1)S(1)} %get-tuple-element.86), channel_id=1, source_target_pairs={{0,17},{1,16},{8,25},{9,24},{16,1},{17,0},{24,9},{25,8},{2,19},{3,... | collective-permute-start | bytes 221192 | tf_op jit(solution)/shard_map/ppermute | solution.py:644
  9.4 4.8 %collective-permute-start.8 = (bf16[144,256]{1,0:T(8,128)(2,1)S(1)}, bf16[144,256]{1,0:T(8,128)(2,1)S(1)}, u32[]{:S(2)}, u32[]{:S(2)}) collective-permute-start(bf16[144,256]{1,0:T(8,128)(2,1)S(1)} %get-tuple-element.87), channel_id=1, source_target_pairs={{0,24},{1,25},{8,16},{9,17},{16,8},{17,9},{24,0},{25,1},{2,26},{3,... | collective-permute-start | bytes 221192 | tf_op jit(solution)/shard_map/ppermute | solution.py:644
  9.9 6.3 %collective-permute-start.9 = (bf16[144,256]{1,0:T(8,128)(2,1)S(1)}, bf16[144,256]{1,0:T(8,128)(2,1)S(1)}, u32[]{:S(2)}, u32[]{:S(2)}) collective-permute-start(bf16[144,256]{1,0:T(8,128)(2,1)S(1)} %get-tuple-element.88), channel_id=1, source_target_pairs={{0,25},{1,24},{8,17},{9,16},{16,9},{17,8},{24,1},{25,0},{2,27},{3,... | collective-permute-start | bytes 221192 | tf_op jit(solution)/shard_map/ppermute | solution.py:644
  18.0 18.0 %all-to-all-start.3 = ((bf16[8,128,512]{2,1,0:T(8,128)(2,1)}), bf16[8,128,512]{2,1,0:T(8,128)(2,1)S(1)}, u32[]{:S(2)}, u32[]{:S(2)}) async-start(bf16[8,128,512]{2,1,0:T(8,128)(2,1)} %bitcast.16), calls=%async_computation.3 | async-start | bytes 2097152 | tf_op jit(solution)/shard_map/all_to_all | solution.py:704
  21.6 19.5 %collective-permute-start.10 = (bf16[304,256]{1,0:T(8,128)(2,1)S(1)}, bf16[304,256]{1,0:T(8,128)(2,1)S(1)}, u32[]{:S(2)}, u32[]{:S(2)}) collective-permute-start(bf16[304,256]{1,0:T(8,128)(2,1)S(1)} %get-tuple-element.90), channel_id=1, source_target_pairs={{0,2},{1,3},{8,10},{9,11},{16,18},{17,19},{24,26},{25,27},{2,0},{3... | collective-permute-start | bytes 466952 | tf_op jit(solution)/shard_map/ppermute | solution.py:652
  23.2 17.9 %collective-permute-start.11 = (bf16[304,256]{1,0:T(8,128)(2,1)S(1)}, bf16[304,256]{1,0:T(8,128)(2,1)S(1)}, u32[]{:S(2)}, u32[]{:S(2)}) collective-permute-start(bf16[304,256]{1,0:T(8,128)(2,1)S(1)} %get-tuple-element.91), channel_id=1, source_target_pairs={{0,4},{1,5},{8,12},{9,13},{16,20},{17,21},{24,28},{25,29},{2,6},{3... | collective-permute-start | bytes 466952 | tf_op jit(solution)/shard_map/ppermute | solution.py:652
  25.8 15.3 %collective-permute-start.12 = (bf16[304,256]{1,0:T(8,128)(2,1)S(1)}, bf16[304,256]{1,0:T(8,128)(2,1)S(1)}, u32[]{:S(2)}, u32[]{:S(2)}) collective-permute-start(bf16[304,256]{1,0:T(8,128)(2,1)S(1)} %get-tuple-element.92), channel_id=1, source_target_pairs={{0,6},{1,7},{8,14},{9,15},{16,22},{17,23},{24,30},{25,31},{2,4},{3... | collective-permute-start | bytes 466952 | tf_op jit(solution)/shard_map/ppermute | solution.py:652
  36.8 9.8 %collective-permute-start.16 = (bf16[288,256]{1,0:T(8,128)(2,1)S(1)}, bf16[288,256]{1,0:T(8,128)(2,1)S(1)}, u32[]{:S(2)}, u32[]{:S(2)}) collective-permute-start(bf16[288,256]{1,0:T(8,128)(2,1)S(1)} %get-tuple-element.98), channel_id=1, source_target_pairs={{0,2},{1,3},{8,10},{9,11},{16,18},{17,19},{24,26},{25,27},{2,0},{3... | collective-permute-start | bytes 442376 | tf_op jit(solution)/shard_map/ppermute | solution.py:652
  38.5 9.7 %collective-permute-start.17 = (bf16[288,256]{1,0:T(8,128)(2,1)S(1)}, bf16[288,256]{1,0:T(8,128)(2,1)S(1)}, u32[]{:S(2)}, u32[]{:S(2)}) collective-permute-start(bf16[288,256]{1,0:T(8,128)(2,1)S(1)} %get-tuple-element.99), channel_id=1, source_target_pairs={{0,4},{1,5},{8,12},{9,13},{16,20},{17,21},{24,28},{25,29},{2,6},{3... | collective-permute-start | bytes 442376 | tf_op jit(solution)/shard_map/ppermute | solution.py:652
  42.3 16.2 %collective-permute-start.13 = (bf16[512,256]{1,0:T(8,128)(2,1)S(1)}, bf16[512,256]{1,0:T(8,128)(2,1)S(1)}, u32[]{:S(2)}, u32[]{:S(2)}) collective-permute-start(bf16[512,256]{1,0:T(8,128)(2,1)S(1)} %get-tuple-element.107), channel_id=1, source_target_pairs={{0,1},{1,0},{8,9},{9,8},{16,17},{17,16},{24,25},{25,24},{2,3},{3,2... | collective-permute-start | bytes 786440 | tf_op jit(solution)/shard_map/ppermute | solution.py:644
  43.8 16.1 %collective-permute-start.14 = (bf16[512,256]{1,0:T(8,128)(2,1)S(1)}, bf16[512,256]{1,0:T(8,128)(2,1)S(1)}, u32[]{:S(2)}, u32[]{:S(2)}) collective-permute-start(bf16[512,256]{1,0:T(8,128)(2,1)S(1)} %get-tuple-element.108), channel_id=1, source_target_pairs={{0,16},{1,17},{8,24},{9,25},{16,0},{17,1},{24,8},{25,9},{2,18},{3,... | collective-permute-start | bytes 786440 | tf_op jit(solution)/shard_map/ppermute | solution.py:644
  44.4 17.4 %collective-permute-start.15 = (bf16[512,256]{1,0:T(8,128)(2,1)S(1)}, bf16[512,256]{1,0:T(8,128)(2,1)S(1)}, u32[]{:S(2)}, u32[]{:S(2)}) collective-permute-start(bf16[512,256]{1,0:T(8,128)(2,1)S(1)} %get-tuple-element.109), channel_id=1, source_target_pairs={{0,17},{1,16},{8,25},{9,24},{16,1},{17,0},{24,9},{25,8},{2,19},{3,... | collective-permute-start | bytes 786440 | tf_op jit(solution)/shard_map/ppermute | solution.py:644
  46.6 8.0 %collective-permute-start.18 = (bf16[288,256]{1,0:T(8,128)(2,1)S(1)}, bf16[288,256]{1,0:T(8,128)(2,1)S(1)}, u32[]{:S(2)}, u32[]{:S(2)}) collective-permute-start(bf16[288,256]{1,0:T(8,128)(2,1)S(1)} %get-tuple-element.100), channel_id=1, source_target_pairs={{0,6},{1,7},{8,14},{9,15},{16,22},{17,23},{24,30},{25,31},{2,4},{3... | collective-permute-start | bytes 442376 | tf_op jit(solution)/shard_map/ppermute | solution.py:652
  48.2 9.0 %collective-permute-start.19 = (bf16[288,256]{1,0:T(8,128)(2,1)S(1)}, bf16[288,256]{1,0:T(8,128)(2,1)S(1)}, u32[]{:S(2)}, u32[]{:S(2)}) collective-permute-start(bf16[288,256]{1,0:T(8,128)(2,1)S(1)} %get-tuple-element.112), channel_id=1, source_target_pairs={{0,2},{1,3},{8,10},{9,11},{16,18},{17,19},{24,26},{25,27},{2,0},{3... | collective-permute-start | bytes 442376 | tf_op jit(solution)/shard_map/ppermute | solution.py:652
  54.7 7.2 %collective-permute-start.23 = (bf16[288,256]{1,0:T(8,128)(2,1)S(1)}, bf16[288,256]{1,0:T(8,128)(2,1)S(1)}, u32[]{:S(2)}, u32[]{:S(2)}) collective-permute-start(bf16[288,256]{1,0:T(8,128)(2,1)S(1)} %get-tuple-element.123), channel_id=1, source_target_pairs={{0,4},{1,5},{8,12},{9,13},{16,20},{17,21},{24,28},{25,29},{2,6},{3... | collective-permute-start | bytes 442376 | tf_op jit(solution)/shard_map/ppermute | solution.py:652
  58.2 11.9 %collective-permute-start.20 = (bf16[512,256]{1,0:T(8,128)(2,1)S(1)}, bf16[512,256]{1,0:T(8,128)(2,1)S(1)}, u32[]{:S(2)}, u32[]{:S(2)}) collective-permute-start(bf16[512,256]{1,0:T(8,128)(2,1)S(1)} %get-tuple-element.118), channel_id=1, source_target_pairs={{0,1},{1,0},{8,9},{9,8},{16,17},{17,16},{24,25},{25,24},{2,3},{3,2... | collective-permute-start | bytes 786440 | tf_op jit(solution)/shard_map/ppermute | solution.py:644
  58.5 11.6 %collective-permute-start.21 = (bf16[512,256]{1,0:T(8,128)(2,1)S(1)}, bf16[512,256]{1,0:T(8,128)(2,1)S(1)}, u32[]{:S(2)}, u32[]{:S(2)}) collective-permute-start(bf16[512,256]{1,0:T(8,128)(2,1)S(1)} %get-tuple-element.119), channel_id=1, source_target_pairs={{0,16},{1,17},{8,24},{9,25},{16,0},{17,1},{24,8},{25,9},{2,18},{3,... | collective-permute-start | bytes 786440 | tf_op jit(solution)/shard_map/ppermute | solution.py:644
  59.9 12.3 %collective-permute-start.22 = (bf16[512,256]{1,0:T(8,128)(2,1)S(1)}, bf16[512,256]{1,0:T(8,128)(2,1)S(1)}, u32[]{:S(2)}, u32[]{:S(2)}) collective-permute-start(bf16[512,256]{1,0:T(8,128)(2,1)S(1)} %get-tuple-element.120), channel_id=1, source_target_pairs={{0,17},{1,16},{8,25},{9,24},{16,1},{17,0},{24,9},{25,8},{2,19},{3,... | collective-permute-start | bytes 786440 | tf_op jit(solution)/shard_map/ppermute | solution.py:644
  61.8 24.5 %collective-permute-start.28 = (bf16[1024,256]{1,0:T(8,128)(2,1)S(1)}, bf16[1024,256]{1,0:T(8,128)(2,1)S(1)}, u32[]{:S(2)}, u32[]{:S(2)}) collective-permute-start(bf16[1024,256]{1,0:T(8,128)(2,1)S(1)} %get-tuple-element.110.refs_0_), channel_id=1, source_target_pairs={{0,8},{1,9},{8,0},{9,1},{16,24},{17,25},{24,16},{25,17},{2,10},{3,... | collective-permute-start | bytes 1572872 | tf_op jit(solution)/shard_map/ppermute | solution.py:644
  61.9 8.2 %collective-permute-start.24 = (bf16[288,256]{1,0:T(8,128)(2,1)S(1)}, bf16[288,256]{1,0:T(8,128)(2,1)S(1)}, u32[]{:S(2)}, u32[]{:S(2)}) collective-permute-start(bf16[288,256]{1,0:T(8,128)(2,1)S(1)} %get-tuple-element.124), channel_id=1, source_target_pairs={{0,6},{1,7},{8,14},{9,15},{16,22},{17,23},{24,30},{25,31},{2,4},{3... | collective-permute-start | bytes 442376 | tf_op jit(solution)/shard_map/ppermute | solution.py:652
  73.2 8.9 %collective-permute-start.25 = (bf16[512,256]{1,0:T(8,128)(2,1)S(1)}, bf16[512,256]{1,0:T(8,128)(2,1)S(1)}, u32[]{:S(2)}, u32[]{:S(2)}) collective-permute-start(bf16[512,256]{1,0:T(8,128)(2,1)S(1)} %get-tuple-element.130), channel_id=1, source_target_pairs={{0,1},{1,0},{8,9},{9,8},{16,17},{17,16},{24,25},{25,24},{2,3},{3,2... | collective-permute-start | bytes 786440 | tf_op jit(solution)/shard_map/ppermute | solution.py:644
  73.7 8.9 %collective-permute-start.26 = (bf16[512,256]{1,0:T(8,128)(2,1)S(1)}, bf16[512,256]{1,0:T(8,128)(2,1)S(1)}, u32[]{:S(2)}, u32[]{:S(2)}) collective-permute-start(bf16[512,256]{1,0:T(8,128)(2,1)S(1)} %get-tuple-element.131), channel_id=1, source_target_pairs={{0,16},{1,17},{8,24},{9,25},{16,0},{17,1},{24,8},{25,9},{2,18},{3,... | collective-permute-start | bytes 786440 | tf_op jit(solution)/shard_map/ppermute | solution.py:644
  75.4 10.8 %collective-permute-start.27 = (bf16[512,256]{1,0:T(8,128)(2,1)S(1)}, bf16[512,256]{1,0:T(8,128)(2,1)S(1)}, u32[]{:S(2)}, u32[]{:S(2)}) collective-permute-start(bf16[512,256]{1,0:T(8,128)(2,1)S(1)} %get-tuple-element.132), channel_id=1, source_target_pairs={{0,17},{1,16},{8,25},{9,24},{16,1},{17,0},{24,9},{25,8},{2,19},{3,... | collective-permute-start | bytes 786440 | tf_op jit(solution)/shard_map/ppermute | solution.py:644
  76.8 10.1 %collective-permute-start.31 = (bf16[1024,256]{1,0:T(8,128)(2,1)S(1)}, bf16[1024,256]{1,0:T(8,128)(2,1)S(1)}, u32[]{:S(2)}, u32[]{:S(2)}) collective-permute-start(bf16[1024,256]{1,0:T(8,128)(2,1)S(1)} %get-tuple-element.134.refs_6_), channel_id=1, source_target_pairs={{0,8},{1,9},{8,0},{9,1},{16,24},{17,25},{24,16},{25,17},{2,10},{3,... | collective-permute-start | bytes 1572872 | tf_op jit(solution)/shard_map/ppermute | solution.py:644
  82.2 4.8 %collective-permute-start.29 = (bf16[1024,256]{1,0:T(8,128)(2,1)S(1)}, bf16[1024,256]{1,0:T(8,128)(2,1)S(1)}, u32[]{:S(2)}, u32[]{:S(2)}) collective-permute-start(bf16[1024,256]{1,0:T(8,128)(2,1)S(1)} %get-tuple-element.121.refs_1_), channel_id=1, source_target_pairs={{0,8},{1,9},{8,0},{9,1},{16,24},{17,25},{24,16},{25,17},{2,10},{3,... | collective-permute-start | bytes 1572872 | tf_op jit(solution)/shard_map/ppermute | solution.py:644
  82.6 4.4 %collective-permute-start.32 = (bf16[1024,256]{1,0:T(8,128)(2,1)S(1)}, bf16[1024,256]{1,0:T(8,128)(2,1)S(1)}, u32[]{:S(2)}, u32[]{:S(2)}) collective-permute-start(bf16[1024,256]{1,0:T(8,128)(2,1)S(1)} %get-tuple-element.135.refs_7_), channel_id=1, source_target_pairs={{0,8},{1,9},{8,0},{9,1},{16,24},{17,25},{24,16},{25,17},{2,10},{3,... | collective-permute-start | bytes 1572872 | tf_op jit(solution)/shard_map/ppermute | solution.py:644
  86.4 2.6 %collective-permute-start.33 = (bf16[1024,256]{1,0:T(8,128)(2,1)S(1)}, bf16[1024,256]{1,0:T(8,128)(2,1)S(1)}, u32[]{:S(2)}, u32[]{:S(2)}) collective-permute-start(bf16[1024,256]{1,0:T(8,128)(2,1)S(1)} %get-tuple-element.136.refs_8_), channel_id=1, source_target_pairs={{0,8},{1,9},{8,0},{9,1},{16,24},{17,25},{24,16},{25,17},{2,10},{3,... | collective-permute-start | bytes 1572872 | tf_op jit(solution)/shard_map/ppermute | solution.py:644
  92.5 15.5 %all-to-all-start.4 = ((f32[32,8,128]{2,1,0:T(8,128)}), f32[32,8,128]{2,1,0:T(8,128)S(1)}, u32[]{:S(2)}, u32[]{:S(2)}) async-start(f32[32,8,128]{2,1,0:T(8,128)} %shard_map.59), calls=%async_computation.4 | async-start | bytes 262144 | tf_op jit(solution)/shard_map/all_to_all | solution.py:570
  (6 other events, 85.1 us)

commit v10 on v9

--- a/solution.py
+++ b/solution.py
@@ -466,7 +466,8 @@
     )
     if allowed is not None:
         scores = jnp.where(allowed, scores, -2.0)
-    best_ref[...] = jnp.maximum(best_ref[...], jnp.max(scores, axis=0, keepdims=True))
+    scores = jnp.max(scores.reshape(-1, 8, scores.shape[1]), axis=0)
+    best_ref[...] = jnp.maximum(best_ref[...], scores)
 
 
 def staged_best_kernel(plan, run_len_ref, *refs):
@@ -519,10 +520,10 @@
                 keys = [part[first : first + TILE, :] for part in parts]
                 add_best(jnp.concatenate(keys, axis=1), queries_ref, best_ref)
 
+    best = jnp.max(best_ref[...], axis=0, keepdims=True)
     for number in range(plan.lanes):
-        lines_ref[number : number + 1, :] = best_ref[
-            :, number * plan.part : (number + 1) * plan.part
-        ]
+        here = slice(number * plan.part, (number + 1) * plan.part)
+        lines_ref[number : number + 1, :] = best[:, here]
     for device in range(plan.devices):
         out_ref[device] = lines_ref[...]
 
@@ -757,7 +758,7 @@
         [wide((plan.devices, plan.lanes, 128), jnp.float32)],
         [SMEM] + [VMEM] * (4 * count),
         [
-            pltpu.VMEM((1, rows), jnp.float32),
+            pltpu.VMEM((8, rows), jnp.float32),
             pltpu.VMEM((rows, width), half),
             pltpu.VMEM((plan.lanes, 128), jnp.float32),
         ],

time: 110 us -> 110 us (level)
  no operation moved by 1% of the time
where the time goes in v10:
time: 110 us
  starting transfers between devices  46.4 us (42%)
  waiting for transfers between devices  44.8 us (41%)
  Pallas kernels  16.3 us (15%)
  local copies, waits for them, and re-layouts  1.12 us (1%)
    ppermute x22, starting transfers between devices, along_lanes(): return lax.ppermute(block, AXES, pairs)  20.6 us
    ppermute x22, waiting for transfers between devices, along_lanes(): return lax.ppermute(block, AXES, pairs)  15.4 us
    ppermute x9, starting transfers between devices, along_layers(): return lax.ppermute(block, AXES, pairs)  14.5 us
    ppermute x9, waiting for transfers between devices, along_layers(): return lax.ppermute(block, AXES, pairs)  12.8 us
    all_to_all x1, waiting for transfers between devices, staged(): lax.all_to_all(later, AXES, 0, 0, tiled=True, axis_index_groups=groups)  10 us
    all_to_all x1, starting transfers between devices, exchange(): return lax.all_to_all(block, AXES, split_axis=0, concat_axis=0, tiled=True)  7.71 us
    all_to_all x1, waiting for transfers between devices, exchange(): return lax.all_to_all(block, AXES, split_axis=0, concat_axis=0, tiled=True)  6.57 us
    all_to_all x1, starting transfers between devices, staged(): lax.all_to_all(later, AXES, 0, 0, tiled=True, axis_index_groups=groups)  3.56 us
  transfers between devices with their start and end apart: 33, of which 12 were waited for; matrix products, arithmetic and copies ran while one was open for 0% of the time, Pallas kernels for 7%

profile of v10, /device:TPU:0, one launch (start us, length us, event | category | flops | bytes accessed | tf_op | source)
XLA Modules:
  0.0 109.6 jit_solution(16765092473074084499)
XLA Ops:
  0.0 2.8 %shard_map.48 = (bf16[144,256]{1,0:T(8,128)(2,1)S(1)}, bf16[144,256]{1,0:T(8,128)(2,1)S(1)}, bf16[144,256]{1,0:T(8,128)(2,1)S(1)}, bf16[144,256]{1,0:T(8,128)(2,...) custom-call(s32[12]{0:T(128)} %run_len_ref.5, ...), custom_call_target="tpu_custom_call" | custom-call | flops 536870912 | bytes 4718592 | tf_op jit(solution)/shard_map/pallas_call | solution.py:657
  2.8 3.0 %collective-permute-start.3 = (bf16[144,256]{1,0:T(8,128)(2,1)S(1)}, bf16[144,256]{1,0:T(8,128)(2,1)S(1)}, u32[]{:S(2)}, u32[]{:S(2)}) collective-permute-start(bf16[144,256]{1,0:T(8,128)(2,1)S(1)} %get-tuple-element.82), channel_id=1, source_target_pairs={{0,1},{1,0},{8,9},{9,8},{16,17},{17,16},{24,25},{25,24},{2,3},{3,2... | collective-permute-start | bytes 221192 | tf_op jit(solution)/shard_map/ppermute | solution.py:645
  6.0 1.9 %collective-permute-start.6 = (bf16[144,256]{1,0:T(8,128)(2,1)S(1)}, bf16[144,256]{1,0:T(8,128)(2,1)S(1)}, u32[]{:S(2)}, u32[]{:S(2)}) collective-permute-start(bf16[144,256]{1,0:T(8,128)(2,1)S(1)} %get-tuple-element.85), channel_id=1, source_target_pairs={{0,16},{1,17},{8,24},{9,25},{16,0},{17,1},{24,8},{25,9},{2,18},{3,... | collective-permute-start | bytes 221192 | tf_op jit(solution)/shard_map/ppermute | solution.py:645
  7.9 1.5 %collective-permute-start.7 = (bf16[144,256]{1,0:T(8,128)(2,1)S(1)}, bf16[144,256]{1,0:T(8,128)(2,1)S(1)}, u32[]{:S(2)}, u32[]{:S(2)}) collective-permute-start(bf16[144,256]{1,0:T(8,128)(2,1)S(1)} %get-tuple-element.86), channel_id=1, source_target_pairs={{0,17},{1,16},{8,25},{9,24},{16,1},{17,0},{24,9},{25,8},{2,19},{3,... | collective-permute-start | bytes 221192 | tf_op jit(solution)/shard_map/ppermute | solution.py:645
  9.9 2.0 %collective-permute-start.9 = (bf16[144,256]{1,0:T(8,128)(2,1)S(1)}, bf16[144,256]{1,0:T(8,128)(2,1)S(1)}, u32[]{:S(2)}, u32[]{:S(2)}) collective-permute-start(bf16[144,256]{1,0:T(8,128)(2,1)S(1)} %get-tuple-element.88), channel_id=1, source_target_pairs={{0,25},{1,24},{8,17},{9,16},{16,9},{17,8},{24,1},{25,0},{2,27},{3,... | collective-permute-start | bytes 221192 | tf_op jit(solution)/shard_map/ppermute | solution.py:645
  12.0 2.3 %shard_map.50 = bf16[1024,512]{1,0:T(8,128)(2,1)} custom-call(bf16[1024,768]{1,0:T(8,128)(2,1)S(1)} %get-tuple-element.94.unit_ref, s32[1,1024]{1,0:T(1,128)S(1)} %get-tuple-element.95.target_ref), custom_call_target="tpu_custom_call" | custom-call | flops 1073741824 | bytes 4718592 | tf_op jit(solution)/shard_map/pallas_call | solution.py:668
  14.2 2.0 %collective-permute-done.9.refs_7_ = bf16[144,256]{1,0:T(8,128)(2,1)S(1)} collective-permute-done((bf16[144,256]{1,0:T(8,128)(2,1)S(1)}, bf16[144,256]{1,0:T(8,128)(2,1)S(1)}, u32[]{:S(2)}, u32[]{:S(2)}) %collective-permute-start.9) | collective-permute-done | bytes 73760 | tf_op jit(solution)/shard_map/ppermute | solution.py:645
  16.2 1.8 %shard_map.49 = (bf16[304,256]{1,0:T(8,128)(2,1)S(1)}, bf16[304,256]{1,0:T(8,128)(2,1)S(1)}, bf16[304,256]{1,0:T(8,128)(2,1)S(1)}, bf16[304,256]{1,0:T(8,128)(2,1)S(1)}, s32[1,1024]{1,0:T(1,128)S(1)}) custom-call(bf16[144,256]{1,0:T(8,128)(2,1)S(1)} %get-tuple-element.81.refs_0_, bf16[144,256]{1,0:T(8,128)(2,1)S(1)} %collective-permute-done.3.refs_1_, ...), custom_call_target="tpu_custom_call" | custom-call | flops 536870912 | bytes 1572864 | tf_op jit(solution)/shard_map/pallas_call | solution.py:688
  18.0 3.6 %all-to-all-start.3 = ((bf16[8,128,512]{2,1,0:T(8,128)(2,1)}), bf16[8,128,512]{2,1,0:T(8,128)(2,1)S(1)}, u32[]{:S(2)}, u32[]{:S(2)}) async-start(bf16[8,128,512]{2,1,0:T(8,128)(2,1)} %bitcast.16), calls=%async_computation.3 | async-start | bytes 2097152 | tf_op jit(solution)/shard_map/all_to_all | solution.py:705
  21.6 1.6 %collective-permute-start.10 = (bf16[304,256]{1,0:T(8,128)(2,1)S(1)}, bf16[304,256]{1,0:T(8,128)(2,1)S(1)}, u32[]{:S(2)}, u32[]{:S(2)}) collective-permute-start(bf16[304,256]{1,0:T(8,128)(2,1)S(1)} %get-tuple-element.90), channel_id=1, source_target_pairs={{0,2},{1,3},{8,10},{9,11},{16,18},{17,19},{24,26},{25,27},{2,0},{3... | collective-permute-start | bytes 466952 | tf_op jit(solution)/shard_map/ppermute | solution.py:653
  23.2 2.6 %collective-permute-start.11 = (bf16[304,256]{1,0:T(8,128)(2,1)S(1)}, bf16[304,256]{1,0:T(8,128)(2,1)S(1)}, u32[]{:S(2)}, u32[]{:S(2)}) collective-permute-start(bf16[304,256]{1,0:T(8,128)(2,1)S(1)} %get-tuple-element.91), channel_id=1, source_target_pairs={{0,4},{1,5},{8,12},{9,13},{16,20},{17,21},{24,28},{25,29},{2,6},{3... | collective-permute-start | bytes 466952 | tf_op jit(solution)/shard_map/ppermute | solution.py:653
  26.0 10.0 %all-to-all-done.3 = bf16[8,128,512]{2,1,0:T(8,128)(2,1)S(1)} async-done(((bf16[8,128,512]{2,1,0:T(8,128)(2,1)}), bf16[8,128,512]{2,1,0:T(8,128)(2,1)S(1)}, u32[]{:S(2)}, u32[]{:S(2)}) %all-to-all-start.3) | async-done | bytes 1048608 | tf_op jit(solution)/shard_map/all_to_all | solution.py:705
  36.8 1.6 %collective-permute-start.16 = (bf16[288,256]{1,0:T(8,128)(2,1)S(1)}, bf16[288,256]{1,0:T(8,128)(2,1)S(1)}, u32[]{:S(2)}, u32[]{:S(2)}) collective-permute-start(bf16[288,256]{1,0:T(8,128)(2,1)S(1)} %get-tuple-element.98), channel_id=1, source_target_pairs={{0,2},{1,3},{8,10},{9,11},{16,18},{17,19},{24,26},{25,27},{2,0},{3... | collective-permute-start | bytes 442376 | tf_op jit(solution)/shard_map/ppermute | solution.py:653
  38.5 2.6 %collective-permute-start.17 = (bf16[288,256]{1,0:T(8,128)(2,1)S(1)}, bf16[288,256]{1,0:T(8,128)(2,1)S(1)}, u32[]{:S(2)}, u32[]{:S(2)}) collective-permute-start(bf16[288,256]{1,0:T(8,128)(2,1)S(1)} %get-tuple-element.99), channel_id=1, source_target_pairs={{0,4},{1,5},{8,12},{9,13},{16,20},{17,21},{24,28},{25,29},{2,6},{3... | collective-permute-start | bytes 442376 | tf_op jit(solution)/shard_map/ppermute | solution.py:653
  42.3 1.5 %collective-permute-start.13 = (bf16[512,256]{1,0:T(8,128)(2,1)S(1)}, bf16[512,256]{1,0:T(8,128)(2,1)S(1)}, u32[]{:S(2)}, u32[]{:S(2)}) collective-permute-start(bf16[512,256]{1,0:T(8,128)(2,1)S(1)} %get-tuple-element.107), channel_id=1, source_target_pairs={{0,1},{1,0},{8,9},{9,8},{16,17},{17,16},{24,25},{25,24},{2,3},{3,2... | collective-permute-start | bytes 786440 | tf_op jit(solution)/shard_map/ppermute | solution.py:645
  44.4 1.5 %collective-permute-start.15 = (bf16[512,256]{1,0:T(8,128)(2,1)S(1)}, bf16[512,256]{1,0:T(8,128)(2,1)S(1)}, u32[]{:S(2)}, u32[]{:S(2)}) collective-permute-start(bf16[512,256]{1,0:T(8,128)(2,1)S(1)} %get-tuple-element.109), channel_id=1, source_target_pairs={{0,17},{1,16},{8,25},{9,24},{16,1},{17,0},{24,9},{25,8},{2,19},{3,... | collective-permute-start | bytes 786440 | tf_op jit(solution)/shard_map/ppermute | solution.py:645
  46.6 1.5 %collective-permute-start.18 = (bf16[288,256]{1,0:T(8,128)(2,1)S(1)}, bf16[288,256]{1,0:T(8,128)(2,1)S(1)}, u32[]{:S(2)}, u32[]{:S(2)}) collective-permute-start(bf16[288,256]{1,0:T(8,128)(2,1)S(1)} %get-tuple-element.100), channel_id=1, source_target_pairs={{0,6},{1,7},{8,14},{9,15},{16,22},{17,23},{24,30},{25,31},{2,4},{3... | collective-permute-start | bytes 442376 | tf_op jit(solution)/shard_map/ppermute | solution.py:653
  48.8 5.8 %collective-permute-done.18.refs_3_ = bf16[288,256]{1,0:T(8,128)(2,1)S(1)} collective-permute-done((bf16[288,256]{1,0:T(8,128)(2,1)S(1)}, bf16[288,256]{1,0:T(8,128)(2,1)S(1)}, u32[]{:S(2)}, u32[]{:S(2)}) %collective-permute-start.18) | collective-permute-done | bytes 147488 | tf_op jit(solution)/shard_map/ppermute | solution.py:653
  54.7 1.3 %collective-permute-start.23 = (bf16[288,256]{1,0:T(8,128)(2,1)S(1)}, bf16[288,256]{1,0:T(8,128)(2,1)S(1)}, u32[]{:S(2)}, u32[]{:S(2)}) collective-permute-start(bf16[288,256]{1,0:T(8,128)(2,1)S(1)} %get-tuple-element.123), channel_id=1, source_target_pairs={{0,4},{1,5},{8,12},{9,13},{16,20},{17,21},{24,28},{25,29},{2,6},{3... | collective-permute-start | bytes 442376 | tf_op jit(solution)/shard_map/ppermute | solution.py:653
  58.5 1.5 %collective-permute-start.21 = (bf16[512,256]{1,0:T(8,128)(2,1)S(1)}, bf16[512,256]{1,0:T(8,128)(2,1)S(1)}, u32[]{:S(2)}, u32[]{:S(2)}) collective-permute-start(bf16[512,256]{1,0:T(8,128)(2,1)S(1)} %get-tuple-element.119), channel_id=1, source_target_pairs={{0,16},{1,17},{8,24},{9,25},{16,0},{17,1},{24,8},{25,9},{2,18},{3,... | collective-permute-start | bytes 786440 | tf_op jit(solution)/shard_map/ppermute | solution.py:645
  59.9 1.8 %collective-permute-start.22 = (bf16[512,256]{1,0:T(8,128)(2,1)S(1)}, bf16[512,256]{1,0:T(8,128)(2,1)S(1)}, u32[]{:S(2)}, u32[]{:S(2)}) collective-permute-start(bf16[512,256]{1,0:T(8,128)(2,1)S(1)} %get-tuple-element.120), channel_id=1, source_target_pairs={{0,17},{1,16},{8,25},{9,24},{16,1},{17,0},{24,9},{25,8},{2,19},{3,... | collective-permute-start | bytes 786440 | tf_op jit(solution)/shard_map/ppermute | solution.py:645
  61.9 2.4 %collective-permute-start.24 = (bf16[288,256]{1,0:T(8,128)(2,1)S(1)}, bf16[288,256]{1,0:T(8,128)(2,1)S(1)}, u32[]{:S(2)}, u32[]{:S(2)}) collective-permute-start(bf16[288,256]{1,0:T(8,128)(2,1)S(1)} %get-tuple-element.124), channel_id=1, source_target_pairs={{0,6},{1,7},{8,14},{9,15},{16,22},{17,23},{24,30},{25,31},{2,4},{3... | collective-permute-start | bytes 442376 | tf_op jit(solution)/shard_map/ppermute | solution.py:653
  64.3 5.8 %collective-permute-done.24.refs_3_ = bf16[288,256]{1,0:T(8,128)(2,1)S(1)} collective-permute-done((bf16[288,256]{1,0:T(8,128)(2,1)S(1)}, bf16[288,256]{1,0:T(8,128)(2,1)S(1)}, u32[]{:S(2)}, u32[]{:S(2)}) %collective-permute-start.24) | collective-permute-done | bytes 147488 | tf_op jit(solution)/shard_map/ppermute | solution.py:653
  70.1 2.1 %collective-permute-done.22.refs_3_ = bf16[512,256]{1,0:T(8,128)(2,1)S(1)} collective-permute-done((bf16[512,256]{1,0:T(8,128)(2,1)S(1)}, bf16[512,256]{1,0:T(8,128)(2,1)S(1)}, u32[]{:S(2)}, u32[]{:S(2)}) %collective-permute-start.22) | collective-permute-done | bytes 262176 | tf_op jit(solution)/shard_map/ppermute | solution.py:645
  73.7 1.7 %collective-permute-start.26 = (bf16[512,256]{1,0:T(8,128)(2,1)S(1)}, bf16[512,256]{1,0:T(8,128)(2,1)S(1)}, u32[]{:S(2)}, u32[]{:S(2)}) collective-permute-start(bf16[512,256]{1,0:T(8,128)(2,1)S(1)} %get-tuple-element.131), channel_id=1, source_target_pairs={{0,16},{1,17},{8,24},{9,25},{16,0},{17,1},{24,8},{25,9},{2,18},{3,... | collective-permute-start | bytes 786440 | tf_op jit(solution)/shard_map/ppermute | solution.py:645
  75.4 1.4 %collective-permute-start.27 = (bf16[512,256]{1,0:T(8,128)(2,1)S(1)}, bf16[512,256]{1,0:T(8,128)(2,1)S(1)}, u32[]{:S(2)}, u32[]{:S(2)}) collective-permute-start(bf16[512,256]{1,0:T(8,128)(2,1)S(1)} %get-tuple-element.132), channel_id=1, source_target_pairs={{0,17},{1,16},{8,25},{9,24},{16,1},{17,0},{24,9},{25,8},{2,19},{3,... | collective-permute-start | bytes 786440 | tf_op jit(solution)/shard_map/ppermute | solution.py:645
  76.8 5.3 %collective-permute-done.25.refs_1_ = bf16[512,256]{1,0:T(8,128)(2,1)S(1)} collective-permute-done((bf16[512,256]{1,0:T(8,128)(2,1)S(1)}, bf16[512,256]{1,0:T(8,128)(2,1)S(1)}, u32[]{:S(2)}, u32[]{:S(2)}) %collective-permute-start.25) | collective-permute-done | bytes 262176 | tf_op jit(solution)/shard_map/ppermute | solution.py:645
  82.7 3.5 %collective-permute-done.27.refs_3_ = bf16[512,256]{1,0:T(8,128)(2,1)S(1)} collective-permute-done((bf16[512,256]{1,0:T(8,128)(2,1)S(1)}, bf16[512,256]{1,0:T(8,128)(2,1)S(1)}, u32[]{:S(2)}, u32[]{:S(2)}) %collective-permute-start.27) | collective-permute-done | bytes 262176 | tf_op jit(solution)/shard_map/ppermute | solution.py:645
  86.9 1.3 %collective-permute-done.30.refs_5_ = bf16[1024,256]{1,0:T(8,128)(2,1)S(1)} collective-permute-done((bf16[1024,256]{1,0:T(8,128)(2,1)S(1)}, bf16[1024,256]{1,0:T(8,128)(2,1)S(1)}, u32[]{:S(2)}, u32[]{:S(2)}) %collective-permute-start.30) | collective-permute-done | bytes 524320 | tf_op jit(solution)/shard_map/ppermute | solution.py:645
  89.0 3.5 %shard_map.59 = f32[32,8,128]{2,1,0:T(8,128)} custom-call(s32[12]{0:T(128)S(1)} %copy-done.3, bf16[1024,256]{1,0:T(8,128)(2,1)S(1)} %get-tuple-element.110.refs_0_, bf16[1024,256]{1,0:T(8,128)(2,1)S(1)} %get-tuple-element.121.refs_1_, bf16[1024,256]{1,0:T(8,128)(2,1)S(1)} %get-tuple-element.133.refs_2_, ...), custom_call_target="tpu_custom_call" | custom-call | flops 4831838208 | bytes 6291456 | tf_op jit(solution)/shard_map/pallas_call | solution.py:755
  92.5 7.7 %all-to-all-start.4 = ((f32[32,8,128]{2,1,0:T(8,128)}), f32[32,8,128]{2,1,0:T(8,128)S(1)}, u32[]{:S(2)}, u32[]{:S(2)}) async-start(f32[32,8,128]{2,1,0:T(8,128)} %shard_map.59), calls=%async_computation.4 | async-start | bytes 262144 | tf_op jit(solution)/shard_map/all_to_all | solution.py:571
  101.3 6.6 %all-to-all-done.4 = f32[32,8,128]{2,1,0:T(8,128)S(1)} async-done(((f32[32,8,128]{2,1,0:T(8,128)}), f32[32,8,128]{2,1,0:T(8,128)S(1)}, u32[]{:S(2)}, u32[]{:S(2)}) %all-to-all-start.4) | async-done | bytes 131104 | tf_op jit(solution)/shard_map/all_to_all | solution.py:571
  (59 shorter events, 13.3 us)
Async XLA Ops:
  2.8 6.6 %collective-permute-start.3 = (bf16[144,256]{1,0:T(8,128)(2,1)S(1)}, bf16[144,256]{1,0:T(8,128)(2,1)S(1)}, u32[]{:S(2)}, u32[]{:S(2)}) collective-permute-start(bf16[144,256]{1,0:T(8,128)(2,1)S(1)} %get-tuple-element.82), channel_id=1, source_target_pairs={{0,1},{1,0},{8,9},{9,8},{16,17},{17,16},{24,25},{25,24},{2,3},{3,2... | collective-permute-start | bytes 221192 | tf_op jit(solution)/shard_map/ppermute | solution.py:645
  5.8 4.2 %collective-permute-start.4 = (bf16[144,256]{1,0:T(8,128)(2,1)S(1)}, bf16[144,256]{1,0:T(8,128)(2,1)S(1)}, u32[]{:S(2)}, u32[]{:S(2)}) collective-permute-start(bf16[144,256]{1,0:T(8,128)(2,1)S(1)} %get-tuple-element.83), channel_id=1, source_target_pairs={{0,8},{1,9},{8,0},{9,1},{16,24},{17,25},{24,16},{25,17},{2,10},{3,... | collective-permute-start | bytes 221192 | tf_op jit(solution)/shard_map/ppermute | solution.py:645
  5.8 8.4 %collective-permute-start.5 = (bf16[144,256]{1,0:T(8,128)(2,1)S(1)}, bf16[144,256]{1,0:T(8,128)(2,1)S(1)}, u32[]{:S(2)}, u32[]{:S(2)}) collective-permute-start(bf16[144,256]{1,0:T(8,128)(2,1)S(1)} %get-tuple-element.84), channel_id=1, source_target_pairs={{0,9},{1,8},{8,1},{9,0},{16,25},{17,24},{24,17},{25,16},{2,11},{3,... | collective-permute-start | bytes 221192 | tf_op jit(solution)/shard_map/ppermute | solution.py:645
  6.0 8.2 %collective-permute-start.6 = (bf16[144,256]{1,0:T(8,128)(2,1)S(1)}, bf16[144,256]{1,0:T(8,128)(2,1)S(1)}, u32[]{:S(2)}, u32[]{:S(2)}) collective-permute-start(bf16[144,256]{1,0:T(8,128)(2,1)S(1)} %get-tuple-element.85), channel_id=1, source_target_pairs={{0,16},{1,17},{8,24},{9,25},{16,0},{17,1},{24,8},{25,9},{2,18},{3,... | collective-permute-start | bytes 221192 | tf_op jit(solution)/shard_map/ppermute | solution.py:645
  7.9 6.3 %collective-permute-start.7 = (bf16[144,256]{1,0:T(8,128)(2,1)S(1)}, bf16[144,256]{1,0:T(8,128)(2,1)S(1)}, u32[]{:S(2)}, u32[]{:S(2)}) collective-permute-start(bf16[144,256]{1,0:T(8,128)(2,1)S(1)} %get-tuple-element.86), channel_id=1, source_target_pairs={{0,17},{1,16},{8,25},{9,24},{16,1},{17,0},{24,9},{25,8},{2,19},{3,... | collective-permute-start | bytes 221192 | tf_op jit(solution)/shard_map/ppermute | solution.py:645
  9.4 4.8 %collective-permute-start.8 = (bf16[144,256]{1,0:T(8,128)(2,1)S(1)}, bf16[144,256]{1,0:T(8,128)(2,1)S(1)}, u32[]{:S(2)}, u32[]{:S(2)}) collective-permute-start(bf16[144,256]{1,0:T(8,128)(2,1)S(1)} %get-tuple-element.87), channel_id=1, source_target_pairs={{0,24},{1,25},{8,16},{9,17},{16,8},{17,9},{24,0},{25,1},{2,26},{3,... | collective-permute-start | bytes 221192 | tf_op jit(solution)/shard_map/ppermute | solution.py:645
  9.9 6.3 %collective-permute-start.9 = (bf16[144,256]{1,0:T(8,128)(2,1)S(1)}, bf16[144,256]{1,0:T(8,128)(2,1)S(1)}, u32[]{:S(2)}, u32[]{:S(2)}) collective-permute-start(bf16[144,256]{1,0:T(8,128)(2,1)S(1)} %get-tuple-element.88), channel_id=1, source_target_pairs={{0,25},{1,24},{8,17},{9,16},{16,9},{17,8},{24,1},{25,0},{2,27},{3,... | collective-permute-start | bytes 221192 | tf_op jit(solution)/shard_map/ppermute | solution.py:645
  18.0 18.0 %all-to-all-start.3 = ((bf16[8,128,512]{2,1,0:T(8,128)(2,1)}), bf16[8,128,512]{2,1,0:T(8,128)(2,1)S(1)}, u32[]{:S(2)}, u32[]{:S(2)}) async-start(bf16[8,128,512]{2,1,0:T(8,128)(2,1)} %bitcast.16), calls=%async_computation.3 | async-start | bytes 2097152 | tf_op jit(solution)/shard_map/all_to_all | solution.py:705
  21.6 19.5 %collective-permute-start.10 = (bf16[304,256]{1,0:T(8,128)(2,1)S(1)}, bf16[304,256]{1,0:T(8,128)(2,1)S(1)}, u32[]{:S(2)}, u32[]{:S(2)}) collective-permute-start(bf16[304,256]{1,0:T(8,128)(2,1)S(1)} %get-tuple-element.90), channel_id=1, source_target_pairs={{0,2},{1,3},{8,10},{9,11},{16,18},{17,19},{24,26},{25,27},{2,0},{3... | collective-permute-start | bytes 466952 | tf_op jit(solution)/shard_map/ppermute | solution.py:653
  23.2 17.9 %collective-permute-start.11 = (bf16[304,256]{1,0:T(8,128)(2,1)S(1)}, bf16[304,256]{1,0:T(8,128)(2,1)S(1)}, u32[]{:S(2)}, u32[]{:S(2)}) collective-permute-start(bf16[304,256]{1,0:T(8,128)(2,1)S(1)} %get-tuple-element.91), channel_id=1, source_target_pairs={{0,4},{1,5},{8,12},{9,13},{16,20},{17,21},{24,28},{25,29},{2,6},{3... | collective-permute-start | bytes 466952 | tf_op jit(solution)/shard_map/ppermute | solution.py:653
  25.8 15.3 %collective-permute-start.12 = (bf16[304,256]{1,0:T(8,128)(2,1)S(1)}, bf16[304,256]{1,0:T(8,128)(2,1)S(1)}, u32[]{:S(2)}, u32[]{:S(2)}) collective-permute-start(bf16[304,256]{1,0:T(8,128)(2,1)S(1)} %get-tuple-element.92), channel_id=1, source_target_pairs={{0,6},{1,7},{8,14},{9,15},{16,22},{17,23},{24,30},{25,31},{2,4},{3... | collective-permute-start | bytes 466952 | tf_op jit(solution)/shard_map/ppermute | solution.py:653
  36.8 9.8 %collective-permute-start.16 = (bf16[288,256]{1,0:T(8,128)(2,1)S(1)}, bf16[288,256]{1,0:T(8,128)(2,1)S(1)}, u32[]{:S(2)}, u32[]{:S(2)}) collective-permute-start(bf16[288,256]{1,0:T(8,128)(2,1)S(1)} %get-tuple-element.98), channel_id=1, source_target_pairs={{0,2},{1,3},{8,10},{9,11},{16,18},{17,19},{24,26},{25,27},{2,0},{3... | collective-permute-start | bytes 442376 | tf_op jit(solution)/shard_map/ppermute | solution.py:653
  38.5 9.7 %collective-permute-start.17 = (bf16[288,256]{1,0:T(8,128)(2,1)S(1)}, bf16[288,256]{1,0:T(8,128)(2,1)S(1)}, u32[]{:S(2)}, u32[]{:S(2)}) collective-permute-start(bf16[288,256]{1,0:T(8,128)(2,1)S(1)} %get-tuple-element.99), channel_id=1, source_target_pairs={{0,4},{1,5},{8,12},{9,13},{16,20},{17,21},{24,28},{25,29},{2,6},{3... | collective-permute-start | bytes 442376 | tf_op jit(solution)/shard_map/ppermute | solution.py:653
  42.3 16.2 %collective-permute-start.13 = (bf16[512,256]{1,0:T(8,128)(2,1)S(1)}, bf16[512,256]{1,0:T(8,128)(2,1)S(1)}, u32[]{:S(2)}, u32[]{:S(2)}) collective-permute-start(bf16[512,256]{1,0:T(8,128)(2,1)S(1)} %get-tuple-element.107), channel_id=1, source_target_pairs={{0,1},{1,0},{8,9},{9,8},{16,17},{17,16},{24,25},{25,24},{2,3},{3,2... | collective-permute-start | bytes 786440 | tf_op jit(solution)/shard_map/ppermute | solution.py:645
  43.8 16.1 %collective-permute-start.14 = (bf16[512,256]{1,0:T(8,128)(2,1)S(1)}, bf16[512,256]{1,0:T(8,128)(2,1)S(1)}, u32[]{:S(2)}, u32[]{:S(2)}) collective-permute-start(bf16[512,256]{1,0:T(8,128)(2,1)S(1)} %get-tuple-element.108), channel_id=1, source_target_pairs={{0,16},{1,17},{8,24},{9,25},{16,0},{17,1},{24,8},{25,9},{2,18},{3,... | collective-permute-start | bytes 786440 | tf_op jit(solution)/shard_map/ppermute | solution.py:645
  44.4 17.4 %collective-permute-start.15 = (bf16[512,256]{1,0:T(8,128)(2,1)S(1)}, bf16[512,256]{1,0:T(8,128)(2,1)S(1)}, u32[]{:S(2)}, u32[]{:S(2)}) collective-permute-start(bf16[512,256]{1,0:T(8,128)(2,1)S(1)} %get-tuple-element.109), channel_id=1, source_target_pairs={{0,17},{1,16},{8,25},{9,24},{16,1},{17,0},{24,9},{25,8},{2,19},{3,... | collective-permute-start | bytes 786440 | tf_op jit(solution)/shard_map/ppermute | solution.py:645
  46.6 8.0 %collective-permute-start.18 = (bf16[288,256]{1,0:T(8,128)(2,1)S(1)}, bf16[288,256]{1,0:T(8,128)(2,1)S(1)}, u32[]{:S(2)}, u32[]{:S(2)}) collective-permute-start(bf16[288,256]{1,0:T(8,128)(2,1)S(1)} %get-tuple-element.100), channel_id=1, source_target_pairs={{0,6},{1,7},{8,14},{9,15},{16,22},{17,23},{24,30},{25,31},{2,4},{3... | collective-permute-start | bytes 442376 | tf_op jit(solution)/shard_map/ppermute | solution.py:653
  48.2 9.0 %collective-permute-start.19 = (bf16[288,256]{1,0:T(8,128)(2,1)S(1)}, bf16[288,256]{1,0:T(8,128)(2,1)S(1)}, u32[]{:S(2)}, u32[]{:S(2)}) collective-permute-start(bf16[288,256]{1,0:T(8,128)(2,1)S(1)} %get-tuple-element.112), channel_id=1, source_target_pairs={{0,2},{1,3},{8,10},{9,11},{16,18},{17,19},{24,26},{25,27},{2,0},{3... | collective-permute-start | bytes 442376 | tf_op jit(solution)/shard_map/ppermute | solution.py:653
  54.7 7.2 %collective-permute-start.23 = (bf16[288,256]{1,0:T(8,128)(2,1)S(1)}, bf16[288,256]{1,0:T(8,128)(2,1)S(1)}, u32[]{:S(2)}, u32[]{:S(2)}) collective-permute-start(bf16[288,256]{1,0:T(8,128)(2,1)S(1)} %get-tuple-element.123), channel_id=1, source_target_pairs={{0,4},{1,5},{8,12},{9,13},{16,20},{17,21},{24,28},{25,29},{2,6},{3... | collective-permute-start | bytes 442376 | tf_op jit(solution)/shard_map/ppermute | solution.py:653
  58.2 11.9 %collective-permute-start.20 = (bf16[512,256]{1,0:T(8,128)(2,1)S(1)}, bf16[512,256]{1,0:T(8,128)(2,1)S(1)}, u32[]{:S(2)}, u32[]{:S(2)}) collective-permute-start(bf16[512,256]{1,0:T(8,128)(2,1)S(1)} %get-tuple-element.118), channel_id=1, source_target_pairs={{0,1},{1,0},{8,9},{9,8},{16,17},{17,16},{24,25},{25,24},{2,3},{3,2... | collective-permute-start | bytes 786440 | tf_op jit(solution)/shard_map/ppermute | solution.py:645
  58.5 11.6 %collective-permute-start.21 = (bf16[512,256]{1,0:T(8,128)(2,1)S(1)}, bf16[512,256]{1,0:T(8,128)(2,1)S(1)}, u32[]{:S(2)}, u32[]{:S(2)}) collective-permute-start(bf16[512,256]{1,0:T(8,128)(2,1)S(1)} %get-tuple-element.119), channel_id=1, source_target_pairs={{0,16},{1,17},{8,24},{9,25},{16,0},{17,1},{24,8},{25,9},{2,18},{3,... | collective-permute-start | bytes 786440 | tf_op jit(solution)/shard_map/ppermute | solution.py:645
  59.9 12.3 %collective-permute-start.22 = (bf16[512,256]{1,0:T(8,128)(2,1)S(1)}, bf16[512,256]{1,0:T(8,128)(2,1)S(1)}, u32[]{:S(2)}, u32[]{:S(2)}) collective-permute-start(bf16[512,256]{1,0:T(8,128)(2,1)S(1)} %get-tuple-element.120), channel_id=1, source_target_pairs={{0,17},{1,16},{8,25},{9,24},{16,1},{17,0},{24,9},{25,8},{2,19},{3,... | collective-permute-start | bytes 786440 | tf_op jit(solution)/shard_map/ppermute | solution.py:645
  61.8 24.5 %collective-permute-start.28 = (bf16[1024,256]{1,0:T(8,128)(2,1)S(1)}, bf16[1024,256]{1,0:T(8,128)(2,1)S(1)}, u32[]{:S(2)}, u32[]{:S(2)}) collective-permute-start(bf16[1024,256]{1,0:T(8,128)(2,1)S(1)} %get-tuple-element.110.refs_0_), channel_id=1, source_target_pairs={{0,8},{1,9},{8,0},{9,1},{16,24},{17,25},{24,16},{25,17},{2,10},{3,... | collective-permute-start | bytes 1572872 | tf_op jit(solution)/shard_map/ppermute | solution.py:645
  61.9 8.2 %collective-permute-start.24 = (bf16[288,256]{1,0:T(8,128)(2,1)S(1)}, bf16[288,256]{1,0:T(8,128)(2,1)S(1)}, u32[]{:S(2)}, u32[]{:S(2)}) collective-permute-start(bf16[288,256]{1,0:T(8,128)(2,1)S(1)} %get-tuple-element.124), channel_id=1, source_target_pairs={{0,6},{1,7},{8,14},{9,15},{16,22},{17,23},{24,30},{25,31},{2,4},{3... | collective-permute-start | bytes 442376 | tf_op jit(solution)/shard_map/ppermute | solution.py:653
  73.2 8.9 %collective-permute-start.25 = (bf16[512,256]{1,0:T(8,128)(2,1)S(1)}, bf16[512,256]{1,0:T(8,128)(2,1)S(1)}, u32[]{:S(2)}, u32[]{:S(2)}) collective-permute-start(bf16[512,256]{1,0:T(8,128)(2,1)S(1)} %get-tuple-element.130), channel_id=1, source_target_pairs={{0,1},{1,0},{8,9},{9,8},{16,17},{17,16},{24,25},{25,24},{2,3},{3,2... | collective-permute-start | bytes 786440 | tf_op jit(solution)/shard_map/ppermute | solution.py:645
  73.7 8.9 %collective-permute-start.26 = (bf16[512,256]{1,0:T(8,128)(2,1)S(1)}, bf16[512,256]{1,0:T(8,128)(2,1)S(1)}, u32[]{:S(2)}, u32[]{:S(2)}) collective-permute-start(bf16[512,256]{1,0:T(8,128)(2,1)S(1)} %get-tuple-element.131), channel_id=1, source_target_pairs={{0,16},{1,17},{8,24},{9,25},{16,0},{17,1},{24,8},{25,9},{2,18},{3,... | collective-permute-start | bytes 786440 | tf_op jit(solution)/shard_map/ppermute | solution.py:645
  75.4 10.8 %collective-permute-start.27 = (bf16[512,256]{1,0:T(8,128)(2,1)S(1)}, bf16[512,256]{1,0:T(8,128)(2,1)S(1)}, u32[]{:S(2)}, u32[]{:S(2)}) collective-permute-start(bf16[512,256]{1,0:T(8,128)(2,1)S(1)} %get-tuple-element.132), channel_id=1, source_target_pairs={{0,17},{1,16},{8,25},{9,24},{16,1},{17,0},{24,9},{25,8},{2,19},{3,... | collective-permute-start | bytes 786440 | tf_op jit(solution)/shard_map/ppermute | solution.py:645
  76.8 10.1 %collective-permute-start.31 = (bf16[1024,256]{1,0:T(8,128)(2,1)S(1)}, bf16[1024,256]{1,0:T(8,128)(2,1)S(1)}, u32[]{:S(2)}, u32[]{:S(2)}) collective-permute-start(bf16[1024,256]{1,0:T(8,128)(2,1)S(1)} %get-tuple-element.134.refs_6_), channel_id=1, source_target_pairs={{0,8},{1,9},{8,0},{9,1},{16,24},{17,25},{24,16},{25,17},{2,10},{3,... | collective-permute-start | bytes 1572872 | tf_op jit(solution)/shard_map/ppermute | solution.py:645
  82.2 4.8 %collective-permute-start.29 = (bf16[1024,256]{1,0:T(8,128)(2,1)S(1)}, bf16[1024,256]{1,0:T(8,128)(2,1)S(1)}, u32[]{:S(2)}, u32[]{:S(2)}) collective-permute-start(bf16[1024,256]{1,0:T(8,128)(2,1)S(1)} %get-tuple-element.121.refs_1_), channel_id=1, source_target_pairs={{0,8},{1,9},{8,0},{9,1},{16,24},{17,25},{24,16},{25,17},{2,10},{3,... | collective-permute-start | bytes 1572872 | tf_op jit(solution)/shard_map/ppermute | solution.py:645
  82.6 4.4 %collective-permute-start.32 = (bf16[1024,256]{1,0:T(8,128)(2,1)S(1)}, bf16[1024,256]{1,0:T(8,128)(2,1)S(1)}, u32[]{:S(2)}, u32[]{:S(2)}) collective-permute-start(bf16[1024,256]{1,0:T(8,128)(2,1)S(1)} %get-tuple-element.135.refs_7_), channel_id=1, source_target_pairs={{0,8},{1,9},{8,0},{9,1},{16,24},{17,25},{24,16},{25,17},{2,10},{3,... | collective-permute-start | bytes 1572872 | tf_op jit(solution)/shard_map/ppermute | solution.py:645
  86.4 2.6 %collective-permute-start.33 = (bf16[1024,256]{1,0:T(8,128)(2,1)S(1)}, bf16[1024,256]{1,0:T(8,128)(2,1)S(1)}, u32[]{:S(2)}, u32[]{:S(2)}) collective-permute-start(bf16[1024,256]{1,0:T(8,128)(2,1)S(1)} %get-tuple-element.136.refs_8_), channel_id=1, source_target_pairs={{0,8},{1,9},{8,0},{9,1},{16,24},{17,25},{24,16},{25,17},{2,10},{3,... | collective-permute-start | bytes 1572872 | tf_op jit(solution)/shard_map/ppermute | solution.py:645
  92.5 15.5 %all-to-all-start.4 = ((f32[32,8,128]{2,1,0:T(8,128)}), f32[32,8,128]{2,1,0:T(8,128)S(1)}, u32[]{:S(2)}, u32[]{:S(2)}) async-start(f32[32,8,128]{2,1,0:T(8,128)} %shard_map.59), calls=%async_computation.4 | async-start | bytes 262144 | tf_op jit(solution)/shard_map/all_to_all | solution.py:571
  (6 other events, 85.0 us)
